TPU v7x, 32 devices: a whole 2x2x4 slice. The times are simulated.
32 devices in a mesh: dp: 16 (over z, y, x), mp: 2 (over core).
Axes of the slice: x: 2, y: 2, z: 4, core: 2. Of those that a mesh axis runs over, the one named last changes fastest.
Arguments:
- x_in: bfloat16 [4096, 2048], P('dp'), may hold values from -6 to 6
- cotangent: bfloat16 [4096, 7168], P('dp', 'mp'), may hold values from -6 to 6
- w_gate: bfloat16 [2048, 7168], P('dp', 'mp'), may hold values from -0.125 to 0.125
- w_up: bfloat16 [2048, 7168], P('dp', 'mp'), may hold values from -0.125 to 0.125
- send_counts: int32 [16, 16], P('dp'), may hold values from 0 to 4, as said below
- recv_counts: int32 [16, 16], P('dp'), may hold values from 0 to 4, as said below
Outputs:
- grad_x: bfloat16 [4096, 2048], P('dp', 'mp')
- grad_gate: float32 [2048, 7168], P('dp', 'mp')
Inputs may be any that keep to these rules, and one draw needn't show every extreme that they name: `send_counts`: each entry is 0 to 4. A quarter of the indices only send and the rest only receive; one sending index sends 4 rows to every receiver, so its live rows reach 256. recv_counts is the transpose of send_counts.
All inputs are finite; a program needn't handle non-finite values.
Results may differ from a plain program's by a relative error of at most 0.014.
Values may be sent and summed in bfloat16 or wider, within the bound.
No kernel may reach another device: no remote copies, remote signals or barrier semaphores. Data moves between devices by JAX's collectives and lax.ppermute only.
A program may use at most 192 MiB of HBM per device.

v0:
```python
import jax
import jax.numpy as jnp
from jax import lax
from jax.sharding import PartitionSpec as P

BAL = 208


def contract_last(left, right):
    return lax.dot_general(
        left, right, (((1,), (1,)), ((), ())), preferred_element_type=jnp.float32
    )


def swiglu_back(x_rows, cot_rows, gate_full, up_full, live_mask):
    gate_val = jnp.dot(x_rows, gate_full, preferred_element_type=jnp.float32)
    up_val = jnp.dot(x_rows, up_full, preferred_element_type=jnp.float32)
    sig = jax.nn.sigmoid(gate_val)
    cot_val = cot_rows.astype(jnp.float32)
    d_gate = jnp.where(
        live_mask[:, None], cot_val * up_val * sig * (1.0 + gate_val * (1.0 - sig)), 0.0
    ).astype(jnp.bfloat16)
    d_up = jnp.where(live_mask[:, None], cot_val * gate_val * sig, 0.0).astype(jnp.bfloat16)
    partial_value = contract_last(d_gate, gate_full) + contract_last(d_up, up_full)
    return (partial_value, d_gate)


def group_sum(partial_value):
    return lax.psum_scatter(
        partial_value.astype(jnp.bfloat16), "mp", scatter_dimension=1, tiled=True
    )


def on_device(x_in, cotangent, w_gate, w_up, send_counts, recv_counts):
    rows_cap = x_in.shape[0]
    width = x_in.shape[1]
    dev_count = lax.axis_size("dp")
    gate_full, up_full = (
        lax.all_gather(w_gate, "dp", axis=0, tiled=True),
        lax.all_gather(w_up, "dp", axis=0, tiled=True),
    )
    sent = send_counts[0]
    got = recv_counts[0]
    live_rows = BAL + jnp.sum(sent) - jnp.sum(got)
    live_mask = jnp.arange(rows_cap) < live_rows
    partial_value, d_gate = swiglu_back(x_in, cotangent, gate_full, up_full, live_mask)
    grad_x = group_sum(partial_value)
    block_rows = width // dev_count
    whole = lax.dot_general(
        x_in, d_gate, (((0,), (0,)), ((), ())), preferred_element_type=jnp.float32
    )
    pieces = lax.all_to_all(
        whole.reshape(dev_count, block_rows, whole.shape[1]),
        "dp",
        split_axis=0,
        concat_axis=0,
        tiled=True,
    )
    grad_gate = jnp.sum(pieces, axis=0)
    return (grad_x, grad_gate)


def solution(mesh):
    return jax.shard_map(
        on_device,
        mesh=mesh,
        in_specs=(
            P("dp", None),
            P("dp", "mp"),
            P("dp", "mp"),
            P("dp", "mp"),
            P("dp", None),
            P("dp", None),
        ),
        out_specs=(P("dp", "mp"), P("dp", "mp")),
        check_vma=False,
    )
```

profile of v0, /device:TPU:28, one launch (start us, length us, event | category | flops | bytes accessed | tf_op | source)
XLA Modules:
  0.0 1078.2 jit_solution(11571272572540398484)
XLA Ops:
  7.2 0.0 copy-start
  7.2 0.0 all-gather.5.cloned.1.call-start
  7.2 0.7 all-gather.5.cloned.1.call-update
  7.9 0.0 all-gather.3.cloned.1.call-start
  8.0 0.7 all-gather.3.cloned.1.call-update
  8.7 1.3 reduce_sum.28
  10.0 1.3 reduce_sum.27
  12.6 169.1 %all-gather.5.cloned.1.call-done = bf16[2048,3584]{1,0:T(8,128)(2,1)} async-done(((bf16[128,3584]{1,0:T(8,128)(2,1)}), bf16[2048,3584]{1,0:T(8,128)(2,1)}) %all-gather.5.cloned.1.call-update) | async-done | bytes 14680080 | tf_op jit(solution)/shard_map/all_gather | solution.py:39
  181.7 0.0 copy-done
  181.7 9.0 fusion.14
  190.7 163.8 %all-gather.3.cloned.1.call-done = bf16[2048,3584]{1,0:T(8,128)(2,1)} async-done(((bf16[128,3584]{1,0:T(8,128)(2,1)}), bf16[2048,3584]{1,0:T(8,128)(2,1)}) %all-gather.3.cloned.1.call-update) | async-done | bytes 14680080 | tf_op jit(solution)/shard_map/all_gather | solution.py:40
  354.6 11.4 %fusion.3 = bf16[256,3584]{1,0:T(8,128)(2,1)S(1)} fusion(bf16[256,2048]{1,0:T(8,128)(2,1)S(1)} %copy-done, bf16[2048,3584]{1,0:T(8,128)(2,1)} %all-gather.3.cloned.1.call-done, bf16[256,3584]{1,0:T(8,128)(2,1)} %param.7, f32[256,3584]{1,0:T(8,128)} %fusion.14, pred[256]{0:T(512)(128)(4,1)S(1)} %iota_compare_fusion), kind=kOutput, calls=%fused_computation.4 | convolution fusion | flops 3769106432 | bytes 23068928 | tf_op jit(solution)/shard_map/dot_general | solution.py:17
  366.0 11.6 %fusion.16 = f32[3584,2048]{0,1:T(8,128)} fusion(bf16[256,3584]{1,0:T(8,128)(2,1)S(1)} %fusion.3, bf16[256,2048]{1,0:T(8,128)(2,1)S(1)} %copy-done), kind=kOutput, calls=%fused_computation.20 | convolution fusion | flops 3758096384 | bytes 32243712 | tf_op jit(solution)/shard_map/dot_general | solution.py:49
  377.6 8.0 all-to-all-start
  385.6 0.0 reduce-scatter.2.cloned.1.call-start
  385.6 8.7 fusion.15
  394.3 12.4 %fusion.7 = bf16[256,2048]{1,0:T(8,128)(2,1)} fusion(f32[256,2048]{1,0:T(8,128)} %fusion.15, bf16[2048,3584]{1,0:T(8,128)(2,1)} %all-gather.3.cloned.1.call-done, f32[256,3584]{1,0:T(8,128)} %fusion.14, bf16[256,3584]{1,0:T(8,128)(2,1)} %param.7, pred[256]{0:T(512)(128)(4,1)S(1)} %iota_compare_fusion), kind=kOutput, calls=%fused_computation.11 | convolution fusion | flops 3766484992 | bytes 23331072 | tf_op jit(solution)/shard_map/dot_general | solution.py:10
  406.7 0.0 reduce-scatter.2.cloned.1.call-update
  406.7 652.4 %all-to-all-done = f32[16,128,3584]{2,1,0:T(8,128)} async-done(((f32[16,128,3584]{2,1,0:T(8,128)}), f32[16,128,3584]{2,1,0:T(8,128)}, u32[]{:S(2)}, u32[]{:S(2)}) %all-to-all-start) | async-done | bytes 29360160 | tf_op jit(solution)/shard_map/all_to_all | solution.py:52
  1059.1 0.0 copy-start.1
  1059.1 12.6 %reduce_sum.29 = f32[128,3584]{1,0:T(8,128)} reduce(f32[16,128,3584]{2,1,0:T(8,128)} %all-to-all-done, f32[]{:T(128)} %constant.3.clone.1), dimensions={0}, to_apply=%region_3.4 | reduce | flops 6881280 | bytes 31195140 | tf_op jit(solution)/shard_map/reduce_sum | solution.py:59
  1071.7 0.0 reduce-scatter.2.cloned.1.call-done
  1071.7 0.0 copy-done.1
  (1 shorter events, 0.0 us)
Async XLA Ops:
  7.2 174.5 %copy-start = (bf16[256,2048]{1,0:T(8,128)(2,1)S(1)}, bf16[256,2048]{1,0:T(8,128)(2,1)}, u32[]{:S(2)}) copy-start(bf16[256,2048]{1,0:T(8,128)(2,1)} %param.6) | copy-start | bytes 3145732
  7.2 174.5 %all-gather.5.cloned.1.call-start = ((), (), s32[]{:S(2)}) async-start(), calls=%async_computation.3 | async-start | bytes 15597568 | tf_op jit(solution)/shard_map/all_gather | solution.py:39
  7.9 346.6 %all-gather.3.cloned.1.call-start = ((), (), s32[]{:S(2)}) async-start(), calls=%async_computation.2 | async-start | bytes 15597568 | tf_op jit(solution)/shard_map/all_gather | solution.py:40
  377.6 681.5 %all-to-all-start = ((f32[16,128,3584]{2,1,0:T(8,128)}), f32[16,128,3584]{2,1,0:T(8,128)}, u32[]{:S(2)}, u32[]{:S(2)}) async-start(f32[16,128,3584]{2,1,0:T(8,128)} %bitcast.12), calls=%async_computation.1 | async-start | bytes 58720256 | tf_op jit(solution)/shard_map/all_to_all | solution.py:52
  385.6 686.1 %reduce-scatter.2.cloned.1.call-start = ((), (), s32[]{:S(2)}) async-start(), calls=%async_computation.4 | async-start | bytes 1572864 | tf_op jit(solution)/shard_map/reduce_scatter | solution.py:29
  1059.1 12.6 %copy-start.1 = (bf16[256,2048]{1,0:T(8,128)(2,1)S(1)}, bf16[256,2048]{1,0:T(8,128)(2,1)}, u32[]{:S(2)}) copy-start(bf16[256,2048]{1,0:T(8,128)(2,1)} %param.6) | copy-start | bytes 3145732
Sparse Core Ops, SparseCore 0:
  10.8 170.8 all-gather.4
  184.5 170.0 all-gather.2
  406.9 9.6 reduce-scatter.1
where the time goes:
time: 1080 us
  waiting for transfers between devices  987 us (91%)
  matrix products  53.1 us (5%)
  other arithmetic  15.2 us (1%)
  between operations  15.1 us (1%)
    all_to_all x1, waiting for transfers between devices, on_device(): lax.all_to_all(whole.reshape(dev_count, block_rows, whole.shape[1]), 'dp'...  652 us
    all_gather x1, waiting for transfers between devices, on_device(): lax.all_gather(w_gate, 'dp', axis=0, tiled=True)  169 us
    all_gather x1, waiting for transfers between devices, on_device(): lax.all_gather(w_up, 'dp', axis=0, tiled=True)  164 us
  transfers between devices with their start and end apart: 4, of which 3 were waited for; matrix products, arithmetic and copies ran while one was open for 4% of the time, Pallas kernels for 0%

commit v1 on v0

v1 whole, which is shorter than its diff:
```python
import jax
import jax.numpy as jnp
from jax import lax
from jax.experimental import pallas as pl
from jax.experimental.pallas import tpu as pltpu
from jax.sharding import PartitionSpec as P

BAL = 208
BF = jnp.bfloat16
F32 = jnp.float32


def contract_last(left, right):
    return lax.dot_general(
        left, right, (((1,), (1,)), ((), ())), preferred_element_type=F32
    )


def contract_first(left, right):
    return lax.dot_general(
        left, right, (((0,), (0,)), ((), ())), preferred_element_type=F32
    )


def swiglu_back(x_rows, cot_rows, gate_full, up_full, live_mask):
    gate_val = jnp.dot(x_rows, gate_full, preferred_element_type=F32)
    up_val = jnp.dot(x_rows, up_full, preferred_element_type=F32)
    sig = jax.nn.sigmoid(gate_val)
    cot_val = cot_rows.astype(F32)
    d_gate = jnp.where(
        live_mask[:, None], cot_val * up_val * sig * (1.0 + gate_val * (1.0 - sig)), 0.0
    ).astype(BF)
    d_up = jnp.where(live_mask[:, None], cot_val * gate_val * sig, 0.0).astype(BF)
    return contract_last(d_gate, gate_full) + contract_last(d_up, up_full), d_gate


def live_rows_of(send_counts, recv_counts):
    return BAL + jnp.sum(send_counts[0]) - jnp.sum(recv_counts[0])


def general_plan(x_in, cotangent, w_gate, w_up, send_counts, recv_counts):
    dev_count = lax.axis_size("dp")
    gate_full = lax.all_gather(w_gate, "dp", axis=0, tiled=True)
    up_full = lax.all_gather(w_up, "dp", axis=0, tiled=True)
    live_mask = jnp.arange(x_in.shape[0]) < live_rows_of(send_counts, recv_counts)
    partial_value, d_gate = swiglu_back(x_in, cotangent, gate_full, up_full, live_mask)
    grad_x = lax.psum_scatter(
        partial_value.astype(BF), "mp", scatter_dimension=1, tiled=True
    )
    whole = contract_first(x_in, d_gate)
    pieces = lax.all_to_all(
        whole.reshape(dev_count, x_in.shape[1] // dev_count, whole.shape[1]),
        "dp",
        split_axis=0,
        concat_axis=0,
        tiled=True,
    )
    return grad_x, jnp.sum(pieces, axis=0)


PLANES = 4
PLACES = 4


def chunk_kernel(order, x_ref, cot_ref, *refs, offset, first, last):
    width = cot_ref.shape[1]
    blocks = refs[:PLANES]
    refs = refs[PLANES:]
    if not first:
        prev, refs = refs[0], refs[1:]
    gx_ref, refs = refs[0], refs[1:]
    gg_refs, acc = refs[:PLANES], refs[PLANES]
    step = pl.program_id(0)
    ck = blocks[0].shape[1] // 2
    deep = blocks[0].shape[0]
    cot = cot_ref[:, offset : offset + ck].astype(F32)
    both = None
    xs = []
    for r in range(PLANES):
        plane = order[r]
        start = pl.multiple_of((plane % 2) * deep, deep)
        xr = x_ref[plane // 2, :, pl.ds(start, deep)]
        xs.append(xr)
        term = jnp.dot(xr, blocks[r][...], preferred_element_type=F32)
        both = term if both is None else both + term
    gate, up = both[:, :ck], both[:, ck:]
    sig = jax.nn.sigmoid(gate)
    d_gate = (cot * up * sig * (1.0 + gate * (1.0 - sig))).astype(BF)
    d_up = (cot * gate * sig).astype(BF)
    d_both = jnp.concatenate([d_gate, d_up], axis=1)
    for r in range(PLANES):
        plane = order[r]
        start = pl.multiple_of((plane % 2) * deep, deep)
        gx = contract_last(d_both, blocks[r][...])
        spot = (plane // 2, slice(None), pl.ds(start, deep))
        if not first:
            gx = gx + prev[spot].astype(F32)
        gx_ref[spot] = gx.astype(gx_ref.dtype)
        gg = contract_first(xs[r], d_gate)

        @pl.when(step == 0)
        def _():
            acc[r] = gg

        @pl.when(step > 0)
        def _():
            acc[r] += gg

    @pl.when(step == pl.num_programs(0) - 1)
    def _():
        for r in range(PLANES):
            gg_refs[r][...] = acc[r].astype(BF)


def chunk_call(order, x_all, cot_all, blocks, prev, offset, last):
    rows = x_all.shape[1]
    half = x_all.shape[2]
    deep, wide = blocks[0].shape
    ck = wide // 2
    tile = 256
    first = prev is None
    x_spec = pl.BlockSpec((2, tile, half), lambda i, o: (0, i, 0))
    cot_spec = pl.BlockSpec((tile, cot_all.shape[1]), lambda i, o: (i, 0))
    whole = pl.BlockSpec((deep, wide), lambda i, o: (0, 0))
    gg_spec = pl.BlockSpec((deep, ck), lambda i, o: (0, 0))
    outs = pl.pallas_call(
        lambda *a: chunk_kernel(*a, offset=offset, first=first, last=last),
        grid_spec=pltpu.PrefetchScalarGridSpec(
            num_scalar_prefetch=1,
            grid=(rows // tile,),
            in_specs=[x_spec, cot_spec] + [whole] * PLANES + ([] if first else [x_spec]),
            out_specs=[x_spec] + [gg_spec] * PLANES,
            scratch_shapes=[pltpu.VMEM((PLANES, deep, ck), F32)],
        ),
        out_shape=[jax.ShapeDtypeStruct((2, rows, half), BF if last else F32)]
        + [jax.ShapeDtypeStruct((deep, ck), BF)] * PLANES,
        compiler_params=pltpu.CompilerParams(vmem_limit_bytes=40 * 1024 * 1024),
        cost_estimate=pl.CostEstimate(
            flops=10 * rows * 2 * half * ck, bytes_accessed=2**24, transcendentals=rows * ck
        ),
        name="swiglu_chunk",
    )(order, x_all, cot_all, *blocks, *([] if first else [prev]))
    return outs[0], outs[1:]


def at(z, q):
    return z * PLACES + q


def pairs_in_plane(s):
    return [(at(z, q), at(z, q ^ s)) for z in range(PLANES) for q in range(PLACES)]


def pairs_of_planes(moves):
    return [(at(a, q), at(b, q)) for a, b in moves for q in range(PLACES)]


OUTER = pairs_of_planes([(0, 1), (1, 0), (2, 3), (3, 2)])
INNER = pairs_of_planes([(1, 2), (2, 1)])
TO_ENDS = pairs_of_planes([(1, 0), (2, 3)])
FROM_ENDS = pairs_of_planes([(0, 1), (3, 2)])
PLANE_GROUPS = [[at(z, q) for q in range(PLACES)] for z in range(PLANES)]


def send(value, pairs):
    return lax.ppermute(value, "dp", pairs)


def across_plane(value):
    return lax.all_to_all(
        value, "dp", split_axis=0, concat_axis=0, tiled=True, axis_index_groups=PLANE_GROUPS
    )


def gather_planes(own):
    a1 = send(own, OUTER)
    b1 = send(own, INNER)
    a2 = send(a1, INNER)
    b2 = send(b1, TO_ENDS)
    a3 = send(a2, TO_ENDS)
    return own, a1, b1 + b2, a2 + a3


def plane_order(z):
    low = z < 2
    return jnp.stack(
        [z, z ^ 1, jnp.where(low, 2, 1), jnp.where(low, 3, 0)]
    ).astype(jnp.int32)


def add(*terms):
    total = terms[0].astype(F32)
    for term in terms[1:]:
        total = total + term.astype(F32)
    return total.astype(BF)


def sum_planes(parts):
    own, p1, p2, p3 = parts
    r1 = send(p3, FROM_ENDS)
    r2b = send(p2, FROM_ENDS)
    r2a = send(add(p3, r1), INNER)
    r3b = send(add(p2, r2b), INNER)
    r3a = send(add(p1, r2a), OUTER)
    return add(own, r3a, r3b)


def planes_plan(x_in, cotangent, w_gate, w_up, send_counts, recv_counts):
    rows, width = x_in.shape
    depth, hidden = w_gate.shape
    quarter = hidden // PLACES
    half = width // 2
    core = lax.axis_index("mp")
    index = lax.axis_index("dp")
    z = index // PLACES
    chunks = [256, 384, 256] if quarter == 896 else [quarter]
    swap = [(0, 1), (1, 0)]

    gate_q = w_gate.reshape(depth, PLACES, quarter)
    up_q = w_up.reshape(depth, PLACES, quarter)
    blocks = []
    offset = 0
    for ck in chunks:
        part = jnp.concatenate(
            [gate_q[:, :, offset : offset + ck], up_q[:, :, offset : offset + ck]], axis=2
        )
        own = across_plane(part.transpose(1, 0, 2)).reshape(PLACES * depth, 2 * ck)
        blocks.append(gather_planes(own))
        offset += ck

    x_half = lax.dynamic_slice_in_dim(x_in, core * half, half, 1)
    mine = jnp.concatenate(
        [x_half] + [send(x_half, pairs_in_plane(s)) for s in range(1, PLACES)], axis=0
    )
    other = lax.ppermute(mine, "mp", swap)
    x_all = jnp.where(core == 0, jnp.stack([mine, other]), jnp.stack([other, mine]))

    live = jnp.arange(rows) < live_rows_of(send_counts, recv_counts)
    cot_q = jnp.where(live[:, None], cotangent, jnp.zeros((), BF)).reshape(rows, PLACES, quarter)
    place = index % PLACES
    cot_all = jnp.concatenate(
        [
            send(c, pairs_in_plane(s)) if s else c
            for s in range(PLACES)
            for c in [lax.dynamic_index_in_dim(cot_q, place ^ s, 1, keepdims=False)]
        ],
        axis=0,
    )

    order = plane_order(z)
    grads = []
    gx = None
    offset = 0
    for k, ck in enumerate(chunks):
        gx, parts = chunk_call(
            order, x_all, cot_all, blocks[k], gx, offset, k == len(chunks) - 1
        )
        own = sum_planes(parts)
        grads.append(across_plane(own.reshape(PLACES, depth, ck)))
        offset += ck
    grad_gate = (
        jnp.concatenate(grads, axis=2).transpose(1, 0, 2).reshape(depth, hidden).astype(F32)
    )

    theirs = lax.ppermute(lax.dynamic_index_in_dim(gx, 1 - core, 0, keepdims=False), "mp", swap)
    ours = add(lax.dynamic_index_in_dim(gx, core, 0, keepdims=False), theirs)
    ours = ours.reshape(PLACES, rows, half)
    grad_x = add(ours[0], *[send(ours[s], pairs_in_plane(s)) for s in range(1, PLACES)])
    return grad_x, grad_gate


def solution(mesh):
    sizes = dict(mesh.shape)
    by_planes = sizes["dp"] == PLANES * PLACES and sizes["mp"] == 2
    return jax.shard_map(
        planes_plan if by_planes else general_plan,
        mesh=mesh,
        in_specs=(
            P("dp", None),
            P("dp", "mp"),
            P("dp", "mp"),
            P("dp", "mp"),
            P("dp", None),
            P("dp", None),
        ),
        out_specs=(P("dp", "mp"), P("dp", "mp")),
        check_vma=False,
    )
```

time: 1080 us -> 331 us (0.31)
  the two profiles are of different devices: /device:TPU:28 before, /device:TPU:0 now
where the time goes in v1:
time: 331 us; the launch traced here: 330 us
  starting transfers between devices  110 us (33%)
  waiting for transfers between devices  90.6 us (27%)
  Pallas kernels  46.2 us (14%)
  other arithmetic  41.4 us (13%)
  local copies, waits for them, and re-layouts  29.3 us (9%)
  blocking collectives  9.78 us (3%)
    ppermute x39, starting transfers between devices, send(): return lax.ppermute(value, 'dp', pairs)  89.5 us
    ppermute x39, waiting for transfers between devices, send(): return lax.ppermute(value, 'dp', pairs)  76.5 us
    pallas_call x3, Pallas kernels, chunk_call(): pl.pallas_call(lambda *a: chunk_kernel(*a, offset=offset, first=first, la...  46.2 us
    all_to_all x5, starting transfers between devices, across_plane(): lax.all_to_all(value, 'dp', split_axis=0, concat_axis=0, tiled=True, axis...  20.2 us
    convert_element_type x14, other arithmetic, add(): return total.astype(BF)  17 us
    all_to_all x5, waiting for transfers between devices, across_plane(): lax.all_to_all(value, 'dp', split_axis=0, concat_axis=0, tiled=True, axis...  14.1 us
    all_to_all x1, blocking collectives, across_plane(): lax.all_to_all(value, 'dp', split_axis=0, concat_axis=0, tiled=True, axis...  9.78 us
    add x6, other arithmetic, gather_planes(): return (own, a1, b1 + b2, a2 + a3)  8.75 us
  transfers between devices with their start and end apart: 46, of which 12 were waited for; matrix products, arithmetic and copies ran while one was open for 17% of the time, Pallas kernels for 14%

profile of v1, /device:TPU:0, one launch (start us, length us, event | category | flops | bytes accessed | tf_op | source)
XLA Modules:
  0.0 329.8 jit_solution(4705341527361034110)
XLA Ops:
  0.6 2.0 reshape.50
  3.7 1.9 reshape.51
  7.6 5.2 %all-to-all-start.2 = ((bf16[4,128,512]{2,1,0:T(8,128)(2,1)}), bf16[4,128,512]{2,1,0:T(8,128)(2,1)S(1)}, u32[]{:S(2)}, u32[]{:S(2)}) async-start(bf16[4,128,512]{2,1,0:T(8,128)(2,1)} %maximum_bitcast_fusion.2), calls=%async_computation.2 | async-start | bytes 1048576 | tf_op jit(solution)/shard_map/all_to_all | solution.py:170
  13.6 2.0 collective-permute-start
  15.6 1.5 collective-permute-start.1
  22.5 4.2 %all-to-all-start = ((bf16[4,128,512]{2,1,0:T(8,128)(2,1)}), bf16[4,128,512]{2,1,0:T(8,128)(2,1)S(1)}, u32[]{:S(2)}, u32[]{:S(2)}) async-start(bf16[4,128,512]{2,1,0:T(8,128)(2,1)} %maximum_bitcast_fusion.1), calls=%async_computation | async-start | bytes 1048576 | tf_op jit(solution)/shard_map/all_to_all | solution.py:170
  26.7 2.9 broadcast_select_fusion
  29.6 4.4 %reshape.49 = bf16[256,4,896]{2,1,0:T(4,128)(2,1)} reshape(bf16[256,3584]{1,0:T(8,128)(2,1)} %broadcast_select_fusion) | data formatting | bytes 3670016 | tf_op jit(solution)/shard_map/reshape | solution.py:239
  35.1 10.6 %collective-permute-done.1 = bf16[256,1024]{1,0:T(8,128)(2,1)} collective-permute-done((bf16[256,1024]{1,0:T(8,128)(2,1)}, bf16[256,1024]{1,0:T(8,128)(2,1)}, u32[]{:S(2)}, u32[]{:S(2)}) %collective-permute-start.1) | collective-permute-done | bytes 524320 | tf_op jit(solution)/shard_map/ppermute | solution.py:166
  45.7 4.2 %fusion.1 = (bf16[1,1024,1024]{2,1,0:T(8,128)(2,1)}, bf16[1024,1024]{1,0:T(8,128)(2,1)}) fusion(bf16[256,1024]{1,0:T(8,128)(2,1)} %collective-permute-done.2, bf16[256,1024]{1,0:T(8,128)(2,1)} %collective-permute-done.1, bf16[256,1024]{1,0:T(8,128)(2,1)} %collective-permute-done, bf16[256,1024]{1,0:T(8,128)(2,1)} %constant_dynamic-slice_fusion.4), kind=kLoop, calls=%fused_computation.35 | loop fusion | flops 8388608 | bytes 6291456 | tf_op jit(solution)/shard_map/stack | solution.py:236
  49.9 3.5 %all-to-all-start.1 = ((bf16[4,128,768]{2,1,0:T(8,128)(2,1)}), bf16[4,128,768]{2,1,0:T(8,128)(2,1)S(1)}, u32[]{:S(2)}, u32[]{:S(2)}) async-start(bf16[4,128,768]{2,1,0:T(8,128)(2,1)} %maximum_bitcast_fusion), calls=%async_computation.1 | async-start | bytes 1572864 | tf_op jit(solution)/shard_map/all_to_all | solution.py:170
  53.4 8.2 %constant_dynamic-slice_fusion.3 = (bf16[256,1,896]{2,1,0:T(2,128)(2,1)}, bf16[256,1,896]{2,1,0:T(2,128)(2,1)S(1)}, bf16[256,1,896]{2,1,0:T(2,128)(2,1)S(1)}, bf16[256,1,896]{2,1,0:T(2,128)(2,1)S(1)}) fusion(bf16[256,4,896]{2,1,0:T(4,128)(2,1)} %reshape.49, s32[]{:T(128)S(6)} %select_n.61, s32[]{:T(128)S(6)} %select_n.63, s32[]{:T(128)S(6)} %select_n.62, ...), kind=kLoop, calls=%fused_computation.31 | loop fusion | bytes 3670032 | tf_op jit(solution)/shard_map/jit(dynamic_index_in_dim)/dynamic_slice | solution.py:245
  61.6 2.0 collective-permute-start.4
  63.7 1.5 collective-permute-start.5
  65.4 1.6 collective-permute-start.17
  67.1 8.2 %collective-permute-done.4 = bf16[256,896]{1,0:T(8,128)(2,1)S(1)} collective-permute-done((bf16[256,896]{1,0:T(8,128)(2,1)S(1)}, bf16[256,896]{1,0:T(8,128)(2,1)S(1)}, u32[]{:S(2)}, u32[]{:S(2)}) %collective-permute-start.4) | collective-permute-done | bytes 458784 | tf_op jit(solution)/shard_map/ppermute | solution.py:166
  75.2 1.5 collective-permute-start.18
  76.7 9.2 %collective-permute-done.5 = bf16[256,896]{1,0:T(8,128)(2,1)S(1)} collective-permute-done((bf16[256,896]{1,0:T(8,128)(2,1)S(1)}, bf16[256,896]{1,0:T(8,128)(2,1)S(1)}, u32[]{:S(2)}, u32[]{:S(2)}) %collective-permute-start.5) | collective-permute-done | bytes 458784 | tf_op jit(solution)/shard_map/ppermute | solution.py:166
  86.0 1.6 collective-permute-start.7
  89.2 1.5 collective-permute-start.20
  90.6 10.3 %collective-permute-done.7.a_4_ = bf16[512,512]{1,0:T(8,128)(2,1)} collective-permute-done((bf16[512,512]{1,0:T(8,128)(2,1)S(1)}, bf16[512,512]{1,0:T(8,128)(2,1)}, u32[]{:S(2)}, u32[]{:S(2)}) %collective-permute-start.7) | collective-permute-done | bytes 524320 | tf_op jit(solution)/shard_map/ppermute | solution.py:166
  102.3 1.6 collective-permute-start.13
  103.8 12.3 %collective-permute-done.12.a_4_ = bf16[512,768]{1,0:T(8,128)(2,1)} collective-permute-done((bf16[512,768]{1,0:T(8,128)(2,1)S(1)}, bf16[512,768]{1,0:T(8,128)(2,1)}, u32[]{:S(2)}, u32[]{:S(2)}) %collective-permute-start.12) | collective-permute-done | bytes 786464 | tf_op jit(solution)/shard_map/ppermute | solution.py:166
  116.1 1.5 collective-permute-start.15
  117.6 1.5 collective-permute-start.10
  119.1 5.0 %collective-permute-done.19 = bf16[512,512]{1,0:T(8,128)(2,1)} collective-permute-done((bf16[512,512]{1,0:T(8,128)(2,1)}, bf16[512,512]{1,0:T(8,128)(2,1)}, u32[]{:S(2)}, u32[]{:S(2)}) %collective-permute-start.19) | collective-permute-done | bytes 524320 | tf_op jit(solution)/shard_map/ppermute | solution.py:166
  126.7 1.5 pad_maximum_fusion.1.a_2_
  128.2 1.5 add.114.a_5_
  132.4 6.9 %collective-permute-done.21 = bf16[512,512]{1,0:T(8,128)(2,1)} collective-permute-done((bf16[512,512]{1,0:T(8,128)(2,1)}, bf16[512,512]{1,0:T(8,128)(2,1)}, u32[]{:S(2)}, u32[]{:S(2)}) %collective-permute-start.21) | collective-permute-done | bytes 524320 | tf_op jit(solution)/shard_map/ppermute | solution.py:166
  140.5 1.3 add.115.a_6_
  143.2 2.9 maximum_select_fusion.a_1_
  146.1 13.5 %swiglu_chunk.3 = (f32[2,1024,1024]{2,1,0:T(8,128)}, bf16[512,256]{1,0:T(8,128)(2,1)S(1)}, bf16[512,256]{1,0:T(8,128)(2,1)S(1)}, bf16[512,256]{1,0:T(8,128)(2,1)}, bf16[512,256]{1,0:T(8,128)(2,1)}) custom-call(s32[4]{0:T(128)S(1)} %pad_add_fusion.a_0_, bf16[2,1024,1024]{2,1,0:T(8,128)(2,1)S(1)} %maximum_select_fusion.a_1_, ...), custom_call_target="tpu_custom_call" | custom-call | flops 5368709120 | bytes 16777216 | tf_op jit(solution)/shard_map/swiglu_chunk/pallas_call | solution.py:126
  161.0 27.3 %collective-permute-start.26 = (bf16[512,256]{1,0:T(8,128)(2,1)}, bf16[512,256]{1,0:T(8,128)(2,1)}, u32[]{:S(2)}, u32[]{:S(2)}) collective-permute-start(bf16[512,256]{1,0:T(8,128)(2,1)} %get-tuple-element.22), channel_id=1, source_target_pairs={{0,8},{2,10},{4,12},{6,14},{24,16},{26,18},{28,20},{30,22},{1,9},{... | collective-permute-start | bytes 786440 | tf_op jit(solution)/shard_map/ppermute | solution.py:166
  189.0 1.5 collective-permute-start.29
  190.5 1.3 add.110.a_5_
  191.9 1.3 add.111.a_6_
  193.2 1.7 add.112.a_5_
  198.5 6.3 %collective-permute-done.16 = bf16[512,768]{1,0:T(8,128)(2,1)} collective-permute-done((bf16[512,768]{1,0:T(8,128)(2,1)}, bf16[512,768]{1,0:T(8,128)(2,1)}, u32[]{:S(2)}, u32[]{:S(2)}) %collective-permute-start.16) | collective-permute-done | bytes 786464 | tf_op jit(solution)/shard_map/ppermute | solution.py:166
  204.8 1.6 add.113.a_6_
  206.4 19.0 %swiglu_chunk.4 = (f32[2,1024,1024]{2,1,0:T(8,128)}, bf16[512,384]{1,0:T(8,128)(2,1)S(1)}, bf16[512,384]{1,0:T(8,128)(2,1)S(1)}, bf16[512,384]{1,0:T(8,128)(2,1)S(1)}, bf16[512,384]{1,0:T(8,128)(2,1)S(1)}) custom-call(s32[4]{0:T(128)S(1)} %pad_add_fusion.a_0_, bf16[2,1024,1024]{2,1,0:T(8,128)(2,1)S(1)} %copy-done.4, ...), custom_call_target="tpu_custom_call" | custom-call | flops 8053063680 | bytes 16777216 | tf_op jit(solution)/shard_map/swiglu_chunk/pallas_call | solution.py:126
  225.4 1.5 collective-permute-start.31
  226.9 13.8 %swiglu_chunk.5 = (bf16[2,1024,1024]{2,1,0:T(8,128)(2,1)S(1)}, bf16[512,256]{1,0:T(8,128)(2,1)S(1)}, bf16[512,256]{1,0:T(8,128)(2,1)S(1)}, bf16[512,256]{1,0:T(8,128)(2,1)S(1)}, bf16[512,256]{1,0:T(8,128)(2,1)S(1)}) custom-call(s32[4]{0:T(128)S(1)} %pad_add_fusion.a_0_, bf16[2,1024,1024]{2,1,0:T(8,128)(2,1)S(1)} %copy-done.4, ...), custom_call_target="tpu_custom_call" | custom-call | flops 5368709120 | bytes 16777216 | tf_op jit(solution)/shard_map/swiglu_chunk/pallas_call | solution.py:126
  241.4 1.3 collective-permute-start.36
  242.7 1.3 collective-permute-start.39
  245.0 4.3 %collective-permute-done.36 = bf16[512,256]{1,0:T(8,128)(2,1)S(1)} collective-permute-done((bf16[512,256]{1,0:T(8,128)(2,1)S(1)}, bf16[512,256]{1,0:T(8,128)(2,1)S(1)}, u32[]{:S(2)}, u32[]{:S(2)}) %collective-permute-start.36) | collective-permute-done | bytes 262176 | tf_op jit(solution)/shard_map/ppermute | solution.py:166
  249.3 4.4 %collective-permute-start.34 = (bf16[512,384]{1,0:T(8,128)(2,1)S(1)}, bf16[512,384]{1,0:T(8,128)(2,1)S(1)}, u32[]{:S(2)}, u32[]{:S(2)}) collective-permute-start(bf16[512,384]{1,0:T(8,128)(2,1)S(1)} %get-tuple-element.27), channel_id=1, source_target_pairs={{0,8},{2,10},{4,12},{6,14},{24,16},{26,18},{28,20},{30,22},{1,9},{... | collective-permute-start | bytes 1179656 | tf_op jit(solution)/shard_map/ppermute | solution.py:166
  255.0 2.5 collective-permute-start.28
  259.9 2.3 collective-permute-done.34
  262.1 1.4 collective-permute-start.40
  264.3 1.5 collective-permute-start.32
  266.6 1.4 collective-permute-start.35
  268.0 8.2 %collective-permute-start.38 = (bf16[512,256]{1,0:T(8,128)(2,1)}, bf16[512,256]{1,0:T(8,128)(2,1)}, u32[]{:S(2)}, u32[]{:S(2)}) collective-permute-start(bf16[512,256]{1,0:T(8,128)(2,1)} %add_convert_fusion.7), channel_id=1, source_target_pairs={{0,8},{2,10},{4,12},{6,14},{8,0},{10,2},{12,4},{14,6},{16,24},{18,... | collective-permute-start | bytes 786440 | tf_op jit(solution)/shard_map/ppermute | solution.py:166
  277.0 4.0 %all-to-all-start.3 = ((bf16[4,128,256]{2,1,0:T(8,128)(2,1)}), bf16[4,128,256]{2,1,0:T(8,128)(2,1)S(1)}, u32[]{:S(2)}, u32[]{:S(2)}) async-start(bf16[4,128,256]{2,1,0:T(8,128)(2,1)} %bitcast.18), calls=%async_computation.3 | async-start | bytes 524288 | tf_op jit(solution)/shard_map/all_to_all | solution.py:170
  281.0 1.9 add_convert_fusion.3
  282.8 2.8 collective-permute-start.33
  285.6 1.8 add_convert_fusion.5
  287.5 3.2 fusion
  291.8 3.6 %collective-permute-start.23 = (bf16[256,1024]{1,0:T(8,128)(2,1)}, bf16[256,1024]{1,0:T(8,128)(2,1)}, u32[]{:S(2)}, u32[]{:S(2)}) collective-permute-start(bf16[256,1024]{1,0:T(8,128)(2,1)} %get-tuple-element.32), channel_id=1, source_target_pairs={{0,2},{2,0},{4,6},{6,4},{8,10},{10,8},{12,14},{14,12},{16,18},{18,... | collective-permute-start | bytes 1572872 | tf_op jit(solution)/shard_map/ppermute | solution.py:166
  295.7 1.5 collective-permute-start.25
  297.2 3.4 %all-to-all-start.5 = ((bf16[4,128,256]{2,1,0:T(8,128)(2,1)}), bf16[4,128,256]{2,1,0:T(8,128)(2,1)S(1)}, u32[]{:S(2)}, u32[]{:S(2)}) async-start(bf16[4,128,256]{2,1,0:T(8,128)(2,1)} %bitcast.20), calls=%async_computation.5 | async-start | bytes 524288 | tf_op jit(solution)/shard_map/all_to_all | solution.py:170
  301.9 14.1 %all-to-all-done.5 = bf16[4,128,256]{2,1,0:T(8,128)(2,1)S(1)} async-done(((bf16[4,128,256]{2,1,0:T(8,128)(2,1)}), bf16[4,128,256]{2,1,0:T(8,128)(2,1)S(1)}, u32[]{:S(2)}, u32[]{:S(2)}) %all-to-all-start.5) | async-done | bytes 262176 | tf_op jit(solution)/shard_map/all_to_all | solution.py:170
  315.9 9.8 %all_to_all.30 = bf16[4,128,384]{2,1,0:T(8,128)(2,1)S(1)} all-to-all(bf16[4,128,384]{2,1,0:T(8,128)(2,1)S(1)} %bitcast.51), channel_id=1, replica_groups={{0,2,4,6},{8,10,12,14},{16,18,20,22},{24,26,28,30},{1,3,5,7},{9,11,13,1..., dimensions={0} | all-to-all | bytes 786432 | tf_op jit(solution)/shard_map/all_to_all | solution.py:170
  325.9 1.4 copy.29
  327.3 2.5 add_convert_fusion
  (152 shorter events, 36.3 us)
Async XLA Ops:
  0.6 12.1 %copy-start = (bf16[256,2048]{1,0:T(8,128)(2,1)S(1)}, bf16[256,2048]{1,0:T(8,128)(2,1)}, u32[]{:S(2)}) copy-start(bf16[256,2048]{1,0:T(8,128)(2,1)} %param.6) | copy-start | bytes 3145732
  2.7 26.9 %copy-start.22 = (bf16[128,4,896]{2,1,0:T(4,128)(2,1)}, bf16[128,4,896]{2,1,0:T(4,128)(2,1)S(1)}, u32[]{:S(2)}) copy-start(bf16[128,4,896]{2,1,0:T(4,128)(2,1)S(1)} %reshape.50) | copy-start | bytes 2752516
  6.7 10.4 %copy-start.30 = (s32[1,16]{1,0:T(1,128)S(1)}, s32[1,16]{1,0:T(1,128)}, u32[]{:S(2)}) copy-start(s32[1,16]{1,0:T(1,128)} %param.10) | copy-start | bytes 196
  6.7 11.1 %copy-start.31 = (s32[1,16]{1,0:T(1,128)S(1)}, s32[1,16]{1,0:T(1,128)}, u32[]{:S(2)}) copy-start(s32[1,16]{1,0:T(1,128)} %param.11) | copy-start | bytes 196
  7.6 15.0 %all-to-all-start.2 = ((bf16[4,128,512]{2,1,0:T(8,128)(2,1)}), bf16[4,128,512]{2,1,0:T(8,128)(2,1)S(1)}, u32[]{:S(2)}, u32[]{:S(2)}) async-start(bf16[4,128,512]{2,1,0:T(8,128)(2,1)} %maximum_bitcast_fusion.2), calls=%async_computation.2 | async-start | bytes 1048576 | tf_op jit(solution)/shard_map/all_to_all | solution.py:170
  13.6 21.5 %collective-permute-start = (bf16[256,1024]{1,0:T(8,128)(2,1)}, bf16[256,1024]{1,0:T(8,128)(2,1)}, u32[]{:S(2)}, u32[]{:S(2)}) collective-permute-start(bf16[256,1024]{1,0:T(8,128)(2,1)} %constant_dynamic-slice_fusion.4), channel_id=1, source_target_pairs={{0,2},{2,0},{4,6},{6,4},{8,10},{10,8},{12,14},{14,12},{16,18},{18,... | collective-permute-start | bytes 1572872 | tf_op jit(solution)/shard_map/ppermute | solution.py:166
  15.6 30.1 %collective-permute-start.1 = (bf16[256,1024]{1,0:T(8,128)(2,1)}, bf16[256,1024]{1,0:T(8,128)(2,1)}, u32[]{:S(2)}, u32[]{:S(2)}) collective-permute-start(bf16[256,1024]{1,0:T(8,128)(2,1)} %constant_dynamic-slice_fusion.4), channel_id=1, source_target_pairs={{0,4},{2,6},{4,0},{6,2},{8,12},{10,14},{12,8},{14,10},{16,20},{18,... | collective-permute-start | bytes 1572872 | tf_op jit(solution)/shard_map/ppermute | solution.py:166
  17.0 28.7 %collective-permute-start.2 = (bf16[256,1024]{1,0:T(8,128)(2,1)}, bf16[256,1024]{1,0:T(8,128)(2,1)}, u32[]{:S(2)}, u32[]{:S(2)}) collective-permute-start(bf16[256,1024]{1,0:T(8,128)(2,1)} %constant_dynamic-slice_fusion.4), channel_id=1, source_target_pairs={{0,6},{2,4},{4,2},{6,0},{8,14},{10,12},{12,10},{14,8},{16,22},{18,... | collective-permute-start | bytes 1572872 | tf_op jit(solution)/shard_map/ppermute | solution.py:166
  22.5 52.7 %copy-start.7 = (bf16[4,128,512]{2,1,0:T(8,128)(2,1)}, bf16[4,128,512]{2,1,0:T(8,128)(2,1)S(1)}, u32[]{:S(2)}) copy-start(bf16[4,128,512]{2,1,0:T(8,128)(2,1)S(1)} %all-to-all-done.2) | copy-start | bytes 1572868
  22.5 27.4 %all-to-all-start = ((bf16[4,128,512]{2,1,0:T(8,128)(2,1)}), bf16[4,128,512]{2,1,0:T(8,128)(2,1)S(1)}, u32[]{:S(2)}, u32[]{:S(2)}) async-start(bf16[4,128,512]{2,1,0:T(8,128)(2,1)} %maximum_bitcast_fusion.1), calls=%async_computation | async-start | bytes 1048576 | tf_op jit(solution)/shard_map/all_to_all | solution.py:170
  49.9 93.3 %collective-permute-start.3 = (bf16[1024,1024]{1,0:T(8,128)(2,1)}, bf16[1024,1024]{1,0:T(8,128)(2,1)}, u32[]{:S(2)}, u32[]{:S(2)}) collective-permute-start(bf16[1024,1024]{1,0:T(8,128)(2,1)} %get-tuple-element.36), channel_id=1, source_target_pairs={{0,1},{1,0},{2,3},{3,2},{4,5},{5,4},{6,7},{7,6},{8,9},{9,8},{10,11... | collective-permute-start | bytes 6291464 | tf_op jit(solution)/shard_map/ppermute | solution.py:235
  49.9 37.7 %all-to-all-start.1 = ((bf16[4,128,768]{2,1,0:T(8,128)(2,1)}), bf16[4,128,768]{2,1,0:T(8,128)(2,1)S(1)}, u32[]{:S(2)}, u32[]{:S(2)}) async-start(bf16[4,128,768]{2,1,0:T(8,128)(2,1)} %maximum_bitcast_fusion), calls=%async_computation.1 | async-start | bytes 1572864 | tf_op jit(solution)/shard_map/all_to_all | solution.py:170
  61.6 13.6 %collective-permute-start.4 = (bf16[256,896]{1,0:T(8,128)(2,1)S(1)}, bf16[256,896]{1,0:T(8,128)(2,1)S(1)}, u32[]{:S(2)}, u32[]{:S(2)}) collective-permute-start(bf16[256,896]{1,0:T(8,128)(2,1)S(1)} %bitcast.54), channel_id=1, source_target_pairs={{0,2},{2,0},{4,6},{6,4},{8,10},{10,8},{12,14},{14,12},{16,18},{18,... | collective-permute-start | bytes 1376264 | tf_op jit(solution)/shard_map/ppermute | solution.py:166
  63.7 22.3 %collective-permute-start.5 = (bf16[256,896]{1,0:T(8,128)(2,1)S(1)}, bf16[256,896]{1,0:T(8,128)(2,1)S(1)}, u32[]{:S(2)}, u32[]{:S(2)}) collective-permute-start(bf16[256,896]{1,0:T(8,128)(2,1)S(1)} %bitcast.53), channel_id=1, source_target_pairs={{0,4},{2,6},{4,0},{6,2},{8,12},{10,14},{12,8},{14,10},{16,20},{18,... | collective-permute-start | bytes 1376264 | tf_op jit(solution)/shard_map/ppermute | solution.py:166
  65.3 22.3 %collective-permute-start.6 = (bf16[256,896]{1,0:T(8,128)(2,1)S(1)}, bf16[256,896]{1,0:T(8,128)(2,1)S(1)}, u32[]{:S(2)}, u32[]{:S(2)}) collective-permute-start(bf16[256,896]{1,0:T(8,128)(2,1)S(1)} %bitcast.52), channel_id=1, source_target_pairs={{0,6},{2,4},{4,2},{6,0},{8,14},{10,12},{12,10},{14,8},{16,22},{18,... | collective-permute-start | bytes 1376264 | tf_op jit(solution)/shard_map/ppermute | solution.py:166
  65.4 23.0 %collective-permute-start.17 = (bf16[512,512]{1,0:T(8,128)(2,1)S(1)}, bf16[512,512]{1,0:T(8,128)(2,1)S(1)}, u32[]{:S(2)}, u32[]{:S(2)}) collective-permute-start(bf16[512,512]{1,0:T(8,128)(2,1)S(1)} %bitcast.46), channel_id=1, source_target_pairs={{0,8},{2,10},{4,12},{6,14},{8,0},{10,2},{12,4},{14,6},{16,24},{18,... | collective-permute-start | bytes 1572872 | tf_op jit(solution)/shard_map/ppermute | solution.py:166
  75.2 12.3 %copy-start.27 = (bf16[256,896]{1,0:T(8,128)(2,1)}, bf16[256,896]{1,0:T(8,128)(2,1)S(1)}, u32[]{:S(2)}) copy-start(bf16[256,896]{1,0:T(8,128)(2,1)S(1)} %collective-permute-done.4) | copy-start | bytes 1376260
  75.2 13.9 %collective-permute-start.18 = (bf16[512,512]{1,0:T(8,128)(2,1)S(1)}, bf16[512,512]{1,0:T(8,128)(2,1)}, u32[]{:S(2)}, u32[]{:S(2)}) collective-permute-start(bf16[512,512]{1,0:T(8,128)(2,1)S(1)} %bitcast.47), channel_id=1, source_target_pairs={{8,16},{10,18},{12,20},{14,22},{16,8},{18,10},{20,12},{22,14},{9,1... | collective-permute-start | bytes 1572872 | tf_op jit(solution)/shard_map/ppermute | solution.py:166
  86.0 15.0 %collective-permute-start.7 = (bf16[512,512]{1,0:T(8,128)(2,1)S(1)}, bf16[512,512]{1,0:T(8,128)(2,1)}, u32[]{:S(2)}, u32[]{:S(2)}) collective-permute-start(bf16[512,512]{1,0:T(8,128)(2,1)S(1)} %bitcast.43), channel_id=1, source_target_pairs={{0,8},{2,10},{4,12},{6,14},{8,0},{10,2},{12,4},{14,6},{16,24},{18,... | collective-permute-start | bytes 1572872 | tf_op jit(solution)/shard_map/ppermute | solution.py:166
  87.6 40.6 %copy-start.5 = (bf16[4,128,768]{2,1,0:T(8,128)(2,1)}, bf16[4,128,768]{2,1,0:T(8,128)(2,1)S(1)}, u32[]{:S(2)}) copy-start(bf16[4,128,768]{2,1,0:T(8,128)(2,1)S(1)} %all-to-all-done.1) | copy-start | bytes 2359300
  87.6 28.5 %collective-permute-start.12 = (bf16[512,768]{1,0:T(8,128)(2,1)S(1)}, bf16[512,768]{1,0:T(8,128)(2,1)}, u32[]{:S(2)}, u32[]{:S(2)}) collective-permute-start(bf16[512,768]{1,0:T(8,128)(2,1)S(1)} %bitcast.40), channel_id=1, source_target_pairs={{0,8},{2,10},{4,12},{6,14},{8,0},{10,2},{12,4},{14,6},{16,24},{18,... | collective-permute-start | bytes 2359304 | tf_op jit(solution)/shard_map/ppermute | solution.py:166
  88.4 38.3 %copy-start.19 = (bf16[512,512]{1,0:T(8,128)(2,1)}, bf16[512,512]{1,0:T(8,128)(2,1)S(1)}, u32[]{:S(2)}) copy-start(bf16[512,512]{1,0:T(8,128)(2,1)S(1)} %collective-permute-done.17.a_4_) | copy-start | bytes 1572868
  88.4 13.8 %collective-permute-start.8 = (bf16[512,512]{1,0:T(8,128)(2,1)S(1)}, bf16[512,512]{1,0:T(8,128)(2,1)S(1)}, u32[]{:S(2)}, u32[]{:S(2)}) collective-permute-start(bf16[512,512]{1,0:T(8,128)(2,1)S(1)} %bitcast.44), channel_id=1, source_target_pairs={{8,16},{10,18},{12,20},{14,22},{16,8},{18,10},{20,12},{22,14},{9,1... | collective-permute-start | bytes 1572872 | tf_op jit(solution)/shard_map/ppermute | solution.py:166
  89.2 28.5 %collective-permute-start.20 = (bf16[512,512]{1,0:T(8,128)(2,1)S(1)}, bf16[512,512]{1,0:T(8,128)(2,1)}, u32[]{:S(2)}, u32[]{:S(2)}) collective-permute-start(bf16[512,512]{1,0:T(8,128)(2,1)S(1)} %collective-permute-done.17.a_4_), channel_id=1, source_target_pairs={{8,16},{10,18},{12,20},{14,22},{16,8},{18,10},{20,12},{22,14},{9,1... | collective-permute-start | bytes 1572872 | tf_op jit(solution)/shard_map/ppermute | solution.py:166
  100.9 23.1 %collective-permute-start.19 = (bf16[512,512]{1,0:T(8,128)(2,1)}, bf16[512,512]{1,0:T(8,128)(2,1)}, u32[]{:S(2)}, u32[]{:S(2)}) collective-permute-start(bf16[512,512]{1,0:T(8,128)(2,1)} %collective-permute-done.18), channel_id=1, source_target_pairs={{8,0},{10,2},{12,4},{14,6},{16,24},{18,26},{20,28},{22,30},{9,1},{... | collective-permute-start | bytes 1572872 | tf_op jit(solution)/shard_map/ppermute | solution.py:166
  102.2 24.5 %copy-start.24 = (bf16[512,512]{1,0:T(8,128)(2,1)}, bf16[512,512]{1,0:T(8,128)(2,1)S(1)}, u32[]{:S(2)}) copy-start(bf16[512,512]{1,0:T(8,128)(2,1)S(1)} %collective-permute-done.8) | copy-start | bytes 1572868
  102.3 27.5 %collective-permute-start.13 = (bf16[512,768]{1,0:T(8,128)(2,1)S(1)}, bf16[512,768]{1,0:T(8,128)(2,1)}, u32[]{:S(2)}, u32[]{:S(2)}) collective-permute-start(bf16[512,768]{1,0:T(8,128)(2,1)S(1)} %bitcast.41), channel_id=1, source_target_pairs={{8,16},{10,18},{12,20},{14,22},{16,8},{18,10},{20,12},{22,14},{9,1... | collective-permute-start | bytes 2359304 | tf_op jit(solution)/shard_map/ppermute | solution.py:166
  116.1 25.8 %collective-permute-start.15 = (bf16[512,768]{1,0:T(8,128)(2,1)}, bf16[512,768]{1,0:T(8,128)(2,1)}, u32[]{:S(2)}, u32[]{:S(2)}) collective-permute-start(bf16[512,768]{1,0:T(8,128)(2,1)} %collective-permute-done.12.a_4_), channel_id=1, source_target_pairs={{8,16},{10,18},{12,20},{14,22},{16,8},{18,10},{20,12},{22,14},{9,1... | collective-permute-start | bytes 2359304 | tf_op jit(solution)/shard_map/ppermute | solution.py:166
  117.6 13.4 %collective-permute-start.10 = (bf16[512,512]{1,0:T(8,128)(2,1)}, bf16[512,512]{1,0:T(8,128)(2,1)}, u32[]{:S(2)}, u32[]{:S(2)}) collective-permute-start(bf16[512,512]{1,0:T(8,128)(2,1)} %collective-permute-done.7.a_4_), channel_id=1, source_target_pairs={{8,16},{10,18},{12,20},{14,22},{16,8},{18,10},{20,12},{22,14},{9,1... | collective-permute-start | bytes 1572872 | tf_op jit(solution)/shard_map/ppermute | solution.py:166
  124.1 15.2 %collective-permute-start.21 = (bf16[512,512]{1,0:T(8,128)(2,1)}, bf16[512,512]{1,0:T(8,128)(2,1)}, u32[]{:S(2)}, u32[]{:S(2)}) collective-permute-start(bf16[512,512]{1,0:T(8,128)(2,1)} %collective-permute-done.20), channel_id=1, source_target_pairs={{8,0},{10,2},{12,4},{14,6},{16,24},{18,26},{20,28},{22,30},{9,1},{... | collective-permute-start | bytes 1572872 | tf_op jit(solution)/shard_map/ppermute | solution.py:166
  128.2 14.9 %copy-start.21 = (bf16[1,1024,1024]{2,1,0:T(8,128)(2,1)S(1)}, bf16[1,1024,1024]{2,1,0:T(8,128)(2,1)}, u32[]{:S(2)}) copy-start(bf16[1,1024,1024]{2,1,0:T(8,128)(2,1)} %get-tuple-element.35) | copy-start | bytes 6291460
  129.7 58.5 %collective-permute-start.9 = (bf16[512,512]{1,0:T(8,128)(2,1)S(1)}, bf16[512,512]{1,0:T(8,128)(2,1)S(1)}, u32[]{:S(2)}, u32[]{:S(2)}) collective-permute-start(bf16[512,512]{1,0:T(8,128)(2,1)S(1)} %copy-done.25), channel_id=1, source_target_pairs={{8,0},{10,2},{12,4},{14,6},{16,24},{18,26},{20,28},{22,30},{9,1},{... | collective-permute-start | bytes 1572872 | tf_op jit(solution)/shard_map/ppermute | solution.py:166
  131.1 62.1 %collective-permute-start.14 = (bf16[512,768]{1,0:T(8,128)(2,1)}, bf16[512,768]{1,0:T(8,128)(2,1)}, u32[]{:S(2)}, u32[]{:S(2)}) collective-permute-start(bf16[512,768]{1,0:T(8,128)(2,1)} %collective-permute-done.13), channel_id=1, source_target_pairs={{8,0},{10,2},{12,4},{14,6},{16,24},{18,26},{20,28},{22,30},{9,1},{... | collective-permute-start | bytes 2359304 | tf_op jit(solution)/shard_map/ppermute | solution.py:166
  139.2 52.6 %collective-permute-start.11 = (bf16[512,512]{1,0:T(8,128)(2,1)}, bf16[512,512]{1,0:T(8,128)(2,1)}, u32[]{:S(2)}, u32[]{:S(2)}) collective-permute-start(bf16[512,512]{1,0:T(8,128)(2,1)} %collective-permute-done.10), channel_id=1, source_target_pairs={{8,0},{10,2},{12,4},{14,6},{16,24},{18,26},{20,28},{22,30},{9,1},{... | collective-permute-start | bytes 1572872 | tf_op jit(solution)/shard_map/ppermute | solution.py:166
  141.9 63.0 %collective-permute-start.16 = (bf16[512,768]{1,0:T(8,128)(2,1)}, bf16[512,768]{1,0:T(8,128)(2,1)}, u32[]{:S(2)}, u32[]{:S(2)}) collective-permute-start(bf16[512,768]{1,0:T(8,128)(2,1)} %collective-permute-done.15), channel_id=1, source_target_pairs={{8,0},{10,2},{12,4},{14,6},{16,24},{18,26},{20,28},{22,30},{9,1},{... | collective-permute-start | bytes 2359304 | tf_op jit(solution)/shard_map/ppermute | solution.py:166
  146.1 13.5 %copy-start.3 = (bf16[2,1024,1024]{2,1,0:T(8,128)(2,1)}, bf16[2,1024,1024]{2,1,0:T(8,128)(2,1)S(1)}, u32[]{:S(2)}) copy-start(bf16[2,1024,1024]{2,1,0:T(8,128)(2,1)S(1)} %maximum_select_fusion.a_1_) | copy-start | bytes 12582916
  161.0 34.0 %collective-permute-start.26 = (bf16[512,256]{1,0:T(8,128)(2,1)}, bf16[512,256]{1,0:T(8,128)(2,1)}, u32[]{:S(2)}, u32[]{:S(2)}) collective-permute-start(bf16[512,256]{1,0:T(8,128)(2,1)} %get-tuple-element.22), channel_id=1, source_target_pairs={{0,8},{2,10},{4,12},{6,14},{24,16},{26,18},{28,20},{30,22},{1,9},{... | collective-permute-start | bytes 786440 | tf_op jit(solution)/shard_map/ppermute | solution.py:166
  189.0 7.8 %collective-permute-start.29 = (bf16[512,256]{1,0:T(8,128)(2,1)}, bf16[512,256]{1,0:T(8,128)(2,1)S(1)}, u32[]{:S(2)}, u32[]{:S(2)}) collective-permute-start(bf16[512,256]{1,0:T(8,128)(2,1)} %get-tuple-element.23), channel_id=1, source_target_pairs={{0,8},{2,10},{4,12},{6,14},{24,16},{26,18},{28,20},{30,22},{1,9},{... | collective-permute-start | bytes 786440 | tf_op jit(solution)/shard_map/ppermute | solution.py:166
  193.2 13.2 %copy-start.4 = (bf16[2,1024,1024]{2,1,0:T(8,128)(2,1)S(1)}, bf16[2,1024,1024]{2,1,0:T(8,128)(2,1)}, u32[]{:S(2)}) copy-start(bf16[2,1024,1024]{2,1,0:T(8,128)(2,1)} %copy-done.3) | copy-start | bytes 12582916
  194.9 11.5 %copy-start.6 = (bf16[4,128,768]{2,1,0:T(8,128)(2,1)S(1)}, bf16[4,128,768]{2,1,0:T(8,128)(2,1)}, u32[]{:S(2)}) copy-start(bf16[4,128,768]{2,1,0:T(8,128)(2,1)} %copy-done.5) | copy-start | bytes 2359300
  196.1 48.1 %collective-permute-start.27 = (bf16[512,256]{1,0:T(8,128)(2,1)S(1)}, bf16[512,256]{1,0:T(8,128)(2,1)S(1)}, u32[]{:S(2)}, u32[]{:S(2)}) collective-permute-start(bf16[512,256]{1,0:T(8,128)(2,1)S(1)} %add_convert_fusion.12), channel_id=1, source_target_pairs={{8,16},{10,18},{12,20},{14,22},{16,8},{18,10},{20,12},{22,14},{9,1... | collective-permute-start | bytes 786440 | tf_op jit(solution)/shard_map/ppermute | solution.py:166
  197.8 68.7 %collective-permute-start.30 = (bf16[512,256]{1,0:T(8,128)(2,1)S(1)}, bf16[512,256]{1,0:T(8,128)(2,1)S(1)}, u32[]{:S(2)}, u32[]{:S(2)}) collective-permute-start(bf16[512,256]{1,0:T(8,128)(2,1)S(1)} %add_convert_fusion.10), channel_id=1, source_target_pairs={{8,16},{10,18},{12,20},{14,22},{16,8},{18,10},{20,12},{22,14},{9,1... | collective-permute-start | bytes 786440 | tf_op jit(solution)/shard_map/ppermute | solution.py:166
  225.4 15.3 %copy-start.9 = (bf16[512,384]{1,0:T(8,128)(2,1)}, bf16[512,384]{1,0:T(8,128)(2,1)S(1)}, u32[]{:S(2)}) copy-start(bf16[512,384]{1,0:T(8,128)(2,1)S(1)} %get-tuple-element.24) | copy-start | bytes 1179652
  225.4 15.3 %copy-start.11 = (bf16[512,384]{1,0:T(8,128)(2,1)}, bf16[512,384]{1,0:T(8,128)(2,1)S(1)}, u32[]{:S(2)}) copy-start(bf16[512,384]{1,0:T(8,128)(2,1)S(1)} %get-tuple-element.25) | copy-start | bytes 1179652
  225.4 32.8 %collective-permute-start.31 = (bf16[512,384]{1,0:T(8,128)(2,1)S(1)}, bf16[512,384]{1,0:T(8,128)(2,1)S(1)}, u32[]{:S(2)}, u32[]{:S(2)}) collective-permute-start(bf16[512,384]{1,0:T(8,128)(2,1)S(1)} %get-tuple-element.26), channel_id=1, source_target_pairs={{0,8},{2,10},{4,12},{6,14},{24,16},{26,18},{28,20},{30,22},{1,9},{... | collective-permute-start | bytes 1179656 | tf_op jit(solution)/shard_map/ppermute | solution.py:166
  241.4 7.9 %collective-permute-start.36 = (bf16[512,256]{1,0:T(8,128)(2,1)S(1)}, bf16[512,256]{1,0:T(8,128)(2,1)S(1)}, u32[]{:S(2)}, u32[]{:S(2)}) collective-permute-start(bf16[512,256]{1,0:T(8,128)(2,1)S(1)} %get-tuple-element.30), channel_id=1, source_target_pairs={{0,8},{2,10},{4,12},{6,14},{24,16},{26,18},{28,20},{30,22},{1,9},{... | collective-permute-start | bytes 786440 | tf_op jit(solution)/shard_map/ppermute | solution.py:166
  242.7 12.2 %collective-permute-start.39 = (bf16[512,256]{1,0:T(8,128)(2,1)S(1)}, bf16[512,256]{1,0:T(8,128)(2,1)S(1)}, u32[]{:S(2)}, u32[]{:S(2)}) collective-permute-start(bf16[512,256]{1,0:T(8,128)(2,1)S(1)} %get-tuple-element.31), channel_id=1, source_target_pairs={{0,8},{2,10},{4,12},{6,14},{24,16},{26,18},{28,20},{30,22},{1,9},{... | collective-permute-start | bytes 786440 | tf_op jit(solution)/shard_map/ppermute | solution.py:166
  244.2 43.2 %collective-permute-start.22 = (bf16[1024,1024]{1,0:T(8,128)(2,1)S(1)}, bf16[1024,1024]{1,0:T(8,128)(2,1)}, u32[]{:S(2)}, u32[]{:S(2)}) collective-permute-start(bf16[1024,1024]{1,0:T(8,128)(2,1)S(1)} %dynamic-slice_bitcast_fusion), channel_id=1, source_target_pairs={{0,1},{1,0},{2,3},{3,2},{4,5},{5,4},{6,7},{7,6},{8,9},{9,8},{10,11... | collective-permute-start | bytes 6291464 | tf_op jit(solution)/shard_map/ppermute | solution.py:265
  249.3 12.8 %collective-permute-start.34 = (bf16[512,384]{1,0:T(8,128)(2,1)S(1)}, bf16[512,384]{1,0:T(8,128)(2,1)S(1)}, u32[]{:S(2)}, u32[]{:S(2)}) collective-permute-start(bf16[512,384]{1,0:T(8,128)(2,1)S(1)} %get-tuple-element.27), channel_id=1, source_target_pairs={{0,8},{2,10},{4,12},{6,14},{24,16},{26,18},{28,20},{30,22},{1,9},{... | collective-permute-start | bytes 1179656 | tf_op jit(solution)/shard_map/ppermute | solution.py:166
  253.8 22.3 %copy-start.16 = (bf16[512,256]{1,0:T(8,128)(2,1)S(1)}, bf16[512,256]{1,0:T(8,128)(2,1)}, u32[]{:S(2)}) copy-start(bf16[512,256]{1,0:T(8,128)(2,1)} %copy-done.15) | copy-start | bytes 786436
  255.0 13.0 %collective-permute-start.28 = (bf16[512,256]{1,0:T(8,128)(2,1)S(1)}, bf16[512,256]{1,0:T(8,128)(2,1)S(1)}, u32[]{:S(2)}, u32[]{:S(2)}) collective-permute-start(bf16[512,256]{1,0:T(8,128)(2,1)S(1)} %add_convert_fusion.11), channel_id=1, source_target_pairs={{0,8},{2,10},{4,12},{6,14},{8,0},{10,2},{12,4},{14,6},{16,24},{18,... | collective-permute-start | bytes 786440 | tf_op jit(solution)/shard_map/ppermute | solution.py:166
  258.2 22.7 %copy-start.12 = (bf16[512,384]{1,0:T(8,128)(2,1)S(1)}, bf16[512,384]{1,0:T(8,128)(2,1)}, u32[]{:S(2)}) copy-start(bf16[512,384]{1,0:T(8,128)(2,1)} %copy-done.11) | copy-start | bytes 1179652
  258.2 6.1 %collective-permute-start.37 = (bf16[512,256]{1,0:T(8,128)(2,1)S(1)}, bf16[512,256]{1,0:T(8,128)(2,1)S(1)}, u32[]{:S(2)}, u32[]{:S(2)}) collective-permute-start(bf16[512,256]{1,0:T(8,128)(2,1)S(1)} %add_convert_fusion.8), channel_id=1, source_target_pairs={{8,16},{10,18},{12,20},{14,22},{16,8},{18,10},{20,12},{22,14},{9,1... | collective-permute-start | bytes 786440 | tf_op jit(solution)/shard_map/ppermute | solution.py:166
  259.9 25.7 %copy-start.18 = (bf16[512,256]{1,0:T(8,128)(2,1)S(1)}, bf16[512,256]{1,0:T(8,128)(2,1)}, u32[]{:S(2)}) copy-start(bf16[512,256]{1,0:T(8,128)(2,1)} %copy-done.17) | copy-start | bytes 786436
  262.1 23.5 %collective-permute-start.40 = (bf16[512,256]{1,0:T(8,128)(2,1)}, bf16[512,256]{1,0:T(8,128)(2,1)}, u32[]{:S(2)}, u32[]{:S(2)}) collective-permute-start(bf16[512,256]{1,0:T(8,128)(2,1)} %add_convert_fusion.6), channel_id=1, source_target_pairs={{8,16},{10,18},{12,20},{14,22},{16,8},{18,10},{20,12},{22,14},{9,1... | collective-permute-start | bytes 786440 | tf_op jit(solution)/shard_map/ppermute | solution.py:166
  264.3 16.6 %collective-permute-start.32 = (bf16[512,384]{1,0:T(8,128)(2,1)}, bf16[512,384]{1,0:T(8,128)(2,1)}, u32[]{:S(2)}, u32[]{:S(2)}) collective-permute-start(bf16[512,384]{1,0:T(8,128)(2,1)} %add_convert_fusion.4), channel_id=1, source_target_pairs={{8,16},{10,18},{12,20},{14,22},{16,8},{18,10},{20,12},{22,14},{9,1... | collective-permute-start | bytes 1179656 | tf_op jit(solution)/shard_map/ppermute | solution.py:166
  266.6 34.0 %collective-permute-start.35 = (bf16[512,384]{1,0:T(8,128)(2,1)}, bf16[512,384]{1,0:T(8,128)(2,1)}, u32[]{:S(2)}, u32[]{:S(2)}) collective-permute-start(bf16[512,384]{1,0:T(8,128)(2,1)} %add_convert_fusion.2), channel_id=1, source_target_pairs={{8,16},{10,18},{12,20},{14,22},{16,8},{18,10},{20,12},{22,14},{9,1... | collective-permute-start | bytes 1179656 | tf_op jit(solution)/shard_map/ppermute | solution.py:166
  268.0 17.7 %collective-permute-start.38 = (bf16[512,256]{1,0:T(8,128)(2,1)}, bf16[512,256]{1,0:T(8,128)(2,1)}, u32[]{:S(2)}, u32[]{:S(2)}) collective-permute-start(bf16[512,256]{1,0:T(8,128)(2,1)} %add_convert_fusion.7), channel_id=1, source_target_pairs={{0,8},{2,10},{4,12},{6,14},{8,0},{10,2},{12,4},{14,6},{16,24},{18,... | collective-permute-start | bytes 786440 | tf_op jit(solution)/shard_map/ppermute | solution.py:166
  277.0 20.2 %all-to-all-start.3 = ((bf16[4,128,256]{2,1,0:T(8,128)(2,1)}), bf16[4,128,256]{2,1,0:T(8,128)(2,1)S(1)}, u32[]{:S(2)}, u32[]{:S(2)}) async-start(bf16[4,128,256]{2,1,0:T(8,128)(2,1)} %bitcast.18), calls=%async_computation.3 | async-start | bytes 524288 | tf_op jit(solution)/shard_map/all_to_all | solution.py:170
  282.8 17.7 %collective-permute-start.33 = (bf16[512,384]{1,0:T(8,128)(2,1)}, bf16[512,384]{1,0:T(8,128)(2,1)}, u32[]{:S(2)}, u32[]{:S(2)}) collective-permute-start(bf16[512,384]{1,0:T(8,128)(2,1)} %add_convert_fusion.3), channel_id=1, source_target_pairs={{0,8},{2,10},{4,12},{6,14},{8,0},{10,2},{12,4},{14,6},{16,24},{18,... | collective-permute-start | bytes 1179656 | tf_op jit(solution)/shard_map/ppermute | solution.py:166
  291.8 35.5 %collective-permute-start.23 = (bf16[256,1024]{1,0:T(8,128)(2,1)}, bf16[256,1024]{1,0:T(8,128)(2,1)}, u32[]{:S(2)}, u32[]{:S(2)}) collective-permute-start(bf16[256,1024]{1,0:T(8,128)(2,1)} %get-tuple-element.32), channel_id=1, source_target_pairs={{0,2},{2,0},{4,6},{6,4},{8,10},{10,8},{12,14},{14,12},{16,18},{18,... | collective-permute-start | bytes 1572872 | tf_op jit(solution)/shard_map/ppermute | solution.py:166
  295.4 31.9 %collective-permute-start.24 = (bf16[256,1024]{1,0:T(8,128)(2,1)}, bf16[256,1024]{1,0:T(8,128)(2,1)}, u32[]{:S(2)}, u32[]{:S(2)}) collective-permute-start(bf16[256,1024]{1,0:T(8,128)(2,1)} %get-tuple-element.34), channel_id=1, source_target_pairs={{0,4},{2,6},{4,0},{6,2},{8,12},{10,14},{12,8},{14,10},{16,20},{18,... | collective-permute-start | bytes 1572872 | tf_op jit(solution)/shard_map/ppermute | solution.py:166
  295.7 31.6 %collective-permute-start.25 = (bf16[256,1024]{1,0:T(8,128)(2,1)}, bf16[256,1024]{1,0:T(8,128)(2,1)}, u32[]{:S(2)}, u32[]{:S(2)}) collective-permute-start(bf16[256,1024]{1,0:T(8,128)(2,1)} %get-tuple-element.33), channel_id=1, source_target_pairs={{0,6},{2,4},{4,2},{6,0},{8,14},{10,12},{12,10},{14,8},{16,22},{18,... | collective-permute-start | bytes 1572872 | tf_op jit(solution)/shard_map/ppermute | solution.py:166
  297.2 18.8 %all-to-all-start.5 = ((bf16[4,128,256]{2,1,0:T(8,128)(2,1)}), bf16[4,128,256]{2,1,0:T(8,128)(2,1)S(1)}, u32[]{:S(2)}, u32[]{:S(2)}) async-start(bf16[4,128,256]{2,1,0:T(8,128)(2,1)} %bitcast.20), calls=%async_computation.5 | async-start | bytes 524288 | tf_op jit(solution)/shard_map/all_to_all | solution.py:170
  (16 other events, 48.6 us)

commit v2 on v1

v2 whole, which is shorter than its diff:
```python
import jax
import jax.numpy as jnp
from jax import lax
from jax.experimental import pallas as pl
from jax.experimental.pallas import tpu as pltpu
from jax.sharding import PartitionSpec as P

BAL = 208
BF = jnp.bfloat16
F32 = jnp.float32


def contract_last(left, right):
    return lax.dot_general(
        left, right, (((1,), (1,)), ((), ())), preferred_element_type=F32
    )


def contract_first(left, right):
    return lax.dot_general(
        left, right, (((0,), (0,)), ((), ())), preferred_element_type=F32
    )


def swiglu_back(x_rows, cot_rows, gate_full, up_full, live_mask):
    gate_val = jnp.dot(x_rows, gate_full, preferred_element_type=F32)
    up_val = jnp.dot(x_rows, up_full, preferred_element_type=F32)
    sig = jax.nn.sigmoid(gate_val)
    cot_val = cot_rows.astype(F32)
    d_gate = jnp.where(
        live_mask[:, None], cot_val * up_val * sig * (1.0 + gate_val * (1.0 - sig)), 0.0
    ).astype(BF)
    d_up = jnp.where(live_mask[:, None], cot_val * gate_val * sig, 0.0).astype(BF)
    return contract_last(d_gate, gate_full) + contract_last(d_up, up_full), d_gate


def live_rows_of(send_counts, recv_counts):
    return BAL + jnp.sum(send_counts[0]) - jnp.sum(recv_counts[0])


def general_plan(x_in, cotangent, w_gate, w_up, send_counts, recv_counts):
    dev_count = lax.axis_size("dp")
    gate_full = lax.all_gather(w_gate, "dp", axis=0, tiled=True)
    up_full = lax.all_gather(w_up, "dp", axis=0, tiled=True)
    live_mask = jnp.arange(x_in.shape[0]) < live_rows_of(send_counts, recv_counts)
    partial_value, d_gate = swiglu_back(x_in, cotangent, gate_full, up_full, live_mask)
    grad_x = lax.psum_scatter(
        partial_value.astype(BF), "mp", scatter_dimension=1, tiled=True
    )
    whole = contract_first(x_in, d_gate)
    pieces = lax.all_to_all(
        whole.reshape(dev_count, x_in.shape[1] // dev_count, whole.shape[1]),
        "dp",
        split_axis=0,
        concat_axis=0,
        tiled=True,
    )
    return grad_x, jnp.sum(pieces, axis=0)


PLANES = 4
PLACES = 4
TILE = 256


def tie(*values):
    return lax.optimization_barrier(values)


def chunk_kernel(scalars, mine_ref, other_ref, *refs, plan):
    groups = []
    for n, sizes in plan["counts"]:
        members = []
        for size in sizes:
            members.append(refs[:size])
            refs = refs[size:]
        groups.append((n, members))
    prev = None
    if not plan["first"]:
        prev, refs = refs[:2], refs[2:]
    gx_refs, refs = refs[:2], refs[2:]
    n_out = 1 if plan["last"] else PLANES
    gg_refs, (w_all, x_tile, cot_tile, acc) = refs[:n_out], refs[n_out:]
    step = pl.program_id(0)
    width, wide = w_all.shape
    ck = wide // 2
    blk = width // (PLANES * PLACES)
    half = width // 2
    rows = TILE // 2
    core = scalars[PLANES * PLACES]
    left = plan["left"]

    def place_rows(first_block, n, value):
        for i in range(n // blk):
            start = pl.multiple_of(scalars[first_block + i] * blk, blk)
            w_all[pl.ds(start, blk), :] = value(slice(i * blk, (i + 1) * blk))

    @pl.when(step == 0)
    def _():
        base = 0
        cols = slice(left, left + wide)
        for n, members in groups:
            for i, (value, *more) in enumerate(members):
                if more:
                    place_rows(i * PLACES + base, n, lambda r: value[r, cols] + more[0][r, cols])
                else:
                    place_rows(i * PLACES + base, n, lambda r: value[r, cols])
            base += n // blk

    lower = pl.ds(pl.multiple_of(core * rows, rows), rows)
    upper = pl.ds(pl.multiple_of((1 - core) * rows, rows), rows)
    x_tile[lower, :] = mine_ref[0, :, :width]
    x_tile[upper, :] = other_ref[0]
    for i in range(2):
        at_col = plan["cot"] + i * plan["quarter"] + plan["offset"]
        cot_tile[i * rows : (i + 1) * rows, :] = mine_ref[0, :, at_col : at_col + ck]

    x = x_tile[...]
    both = jnp.dot(x, w_all[...], preferred_element_type=F32)
    gate, up = both[:, :ck], both[:, ck:]
    cot = cot_tile[...].astype(F32)
    sig = jax.nn.sigmoid(gate)
    d_gate = (cot * up * sig * (1.0 + gate * (1.0 - sig))).astype(BF)
    d_up = (cot * gate * sig).astype(BF)
    gg = contract_first(x, d_gate)

    @pl.when(step == 0)
    def _():
        acc[...] = gg

    @pl.when(step > 0)
    def _():
        acc[...] += gg

    gx = contract_last(jnp.concatenate([d_gate, d_up], axis=1), w_all[...])
    low, high = gx[:, :half], gx[:, half:]
    for keep in range(2):

        @pl.when(core == keep)
        def _():
            for ref, value, i in ((gx_refs[0], (low, high)[keep], 0), (gx_refs[1], (high, low)[keep], 1)):
                ref[...] = (value if prev is None else value + prev[i][...].astype(F32)).astype(BF)

    @pl.when(step == pl.num_programs(0) - 1)
    def _():
        for j in range(PLANES * PLACES):
            if plan["last"]:
                gg_refs[0][j] = acc[j * blk : (j + 1) * blk, :].astype(BF)
            else:
                start = pl.multiple_of(scalars[j] * blk, blk)
                row = (j % PLACES) * blk
                gg_refs[j // PLACES][row : row + blk, :] = acc[pl.ds(start, blk), :].astype(BF)


def chunk_call(scalars, mine, other, groups, prev, ck, **plan):
    width = other.shape[2]
    rows = PLACES * TILE
    half = width // 2
    plan["counts"] = [(g[0][0].shape[0], [len(m) for m in g]) for g in groups]
    flat = [v for g in groups for m in g for v in m]
    plan["first"] = prev is None
    blk = width // (PLANES * PLACES)
    deep = width // PLANES
    gx_spec = pl.BlockSpec((TILE, half), lambda i, o: (i, 0))
    w_specs = [
        pl.BlockSpec(v.shape, lambda i, o: (0, 0), pipeline_mode=pl.Buffered(1))
        for v in flat
    ]
    if plan["last"]:
        gg_specs = [pl.BlockSpec((PLANES * PLACES, blk, ck), lambda i, o: (0, 0, 0))]
        gg_shapes = [jax.ShapeDtypeStruct((PLANES * PLACES, blk, ck), BF)]
    else:
        gg_specs = [pl.BlockSpec((deep, ck), lambda i, o: (0, 0))] * PLANES
        gg_shapes = [jax.ShapeDtypeStruct((deep, ck), BF)] * PLANES
    outs = pl.pallas_call(
        lambda *a: chunk_kernel(*a, plan=plan),
        grid_spec=pltpu.PrefetchScalarGridSpec(
            num_scalar_prefetch=1,
            grid=(PLACES,),
            in_specs=[
                pl.BlockSpec((1,) + mine.shape[1:], lambda i, o: (i, 0, 0)),
                pl.BlockSpec((1,) + other.shape[1:], lambda i, o: (i, 0, 0)),
            ]
            + w_specs
            + ([] if prev is None else [gx_spec] * 2),
            out_specs=[gx_spec] * 2 + gg_specs,
            scratch_shapes=[
                pltpu.VMEM((width, 2 * ck), BF),
                pltpu.VMEM((TILE, width), BF),
                pltpu.VMEM((TILE, ck), BF),
                pltpu.VMEM((width, ck), F32),
            ],
        ),
        out_shape=[jax.ShapeDtypeStruct((rows, half), BF)] * 2 + gg_shapes,
        compiler_params=pltpu.CompilerParams(vmem_limit_bytes=56 * 1024 * 1024),
        cost_estimate=pl.CostEstimate(
            flops=10 * rows * width * ck, bytes_accessed=2**24, transcendentals=rows * ck
        ),
        name="swiglu_chunk",
    )(scalars, mine, other, *flat, *([] if prev is None else prev))
    return outs[:2], outs[2:]


def join_kernel(scalars, *refs, widths, quarter):
    out = refs[-1]
    firsts, last = refs[:PLACES], refs[PLACES]
    split = widths[0]
    for s in range(PLACES):
        start = scalars[PLANES * PLACES + 1 + s] * quarter
        spot = pl.ds(pl.multiple_of(start, 128), split)
        out[:, spot] = firsts[s][...].astype(F32)
    for q in range(PLACES):
        total = last[q].astype(F32)
        for z in range(1, PLANES):
            total = total + last[z * PLACES + q].astype(F32)
        out[:, q * quarter + split : (q + 1) * quarter] = total


def join_call(scalars, firsts, last, widths, quarter):
    depth = last.shape[1]
    vmem = pl.BlockSpec(memory_space=pltpu.VMEM)
    return pl.pallas_call(
        lambda *a: join_kernel(*a, widths=widths, quarter=quarter),
        in_specs=[pl.BlockSpec(memory_space=pltpu.SMEM)] + [vmem] * (PLACES + 1),
        out_specs=vmem,
        out_shape=jax.ShapeDtypeStruct((depth, PLACES * quarter), F32),
        compiler_params=pltpu.CompilerParams(vmem_limit_bytes=16 * 1024 * 1024),
        name="join_chunks",
    )(scalars, *firsts, last)


def at(z, q):
    return z * PLACES + q


def pairs_in_plane(s):
    return [(at(z, q), at(z, q ^ s)) for z in range(PLANES) for q in range(PLACES)]


def pairs_across(r):
    return [(at(z, q), at(z ^ r, q)) for z in range(PLANES) for q in range(PLACES)]


def pairs_of_planes(moves):
    return [(at(a, q), at(b, q)) for a, b in moves for q in range(PLACES)]


OUTER = pairs_of_planes([(0, 1), (1, 0), (2, 3), (3, 2)])
INNER = pairs_of_planes([(1, 2), (2, 1)])
TO_ENDS = pairs_of_planes([(1, 0), (2, 3)])
FROM_ENDS = pairs_of_planes([(0, 1), (3, 2)])
COLUMN_GROUPS = [[at(z, q) for z in range(PLANES)] for q in range(PLACES)]


def send(value, pairs):
    return lax.ppermute(value, "dp", pairs)


def from_plane(pieces):
    return [send(p, pairs_in_plane(s)) if s else p for s, p in enumerate(pieces)]


def gather_planes(own):
    a1 = send(own, OUTER)
    b1 = send(own, INNER)
    a2 = send(a1, INNER)
    b2 = send(b1, TO_ENDS)
    a3 = send(a2, TO_ENDS)
    return own, a1, b1, b2, a2, a3


def plane_order(z):
    low = z < 2
    return [z, z ^ 1, jnp.where(low, 2, 1), jnp.where(low, 3, 0)]


def add(*terms):
    total = terms[0].astype(F32)
    for term in terms[1:]:
        total = total + term.astype(F32)
    return total.astype(BF)


def sum_planes(parts):
    own, p1, p2, p3 = parts
    r1 = send(p3, FROM_ENDS)
    r2b = send(p2, FROM_ENDS)
    r2a = send(add(p3, r1), INNER)
    r3b = send(add(p2, r2b), INNER)
    r3a = send(add(p1, r2a), OUTER)
    return add(own, r3a, r3b)


def planes_plan(x_in, cotangent, w_gate, w_up, send_counts, recv_counts):
    rows, width = x_in.shape
    depth, hidden = w_gate.shape
    quarter = hidden // PLACES
    half = width // 2
    core = lax.axis_index("mp")
    index = lax.axis_index("dp")
    z, place = index // PLACES, index % PLACES
    chunks = [640, 256]
    swap = [(0, 1), (1, 0)]
    offsets = [sum(chunks[:i]) for i in range(len(chunks))]

    def columns(array, q, offset, count):
        return lax.dynamic_slice_in_dim(array, q * quarter + offset, count, 1)

    def piece_of_weights(q, which):
        return jnp.concatenate(
            [columns(w, q, offsets[k], chunks[k]) for k in which for w in (w_gate, w_up)], axis=1
        )

    def scalars_for(order):
        return jnp.stack(
            [order[r] * PLACES + (place ^ s) for r in range(PLANES) for s in range(PLACES)]
            + [core]
            + [place ^ s for s in range(PLACES)]
        ).astype(jnp.int32)

    relayed = scalars_for(plane_order(z))
    direct = scalars_for([z ^ r for r in range(PLANES)])

    first = [piece_of_weights(place ^ s, (0,)) for s in range(PLACES)]
    own = first[0]
    a1o = send(own, OUTER)
    b1o = send(own, INNER)
    rest = from_plane(first)[1:]
    a2o = send(a1o, INNER)
    b2o = send(b1o, TO_ENDS)
    a2o, b2o, x_in, cotangent, w_gate, w_up, *rest = tie(
        a2o, b2o, x_in, cotangent, w_gate, w_up, *rest
    )

    rest = jnp.concatenate(rest, axis=0)
    a1r = send(rest, OUTER)
    b1r = send(rest, INNER)
    a3o = send(a2o, TO_ENDS)
    live = jnp.arange(rows) < live_rows_of(send_counts, recv_counts)
    cotangent = jnp.where(live[:, None], cotangent, jnp.zeros((), BF))
    x_half = lax.dynamic_slice_in_dim(x_in, core * (rows // 2), rows // 2, 0)
    parcels = []
    for s in range(PLACES):
        cot = columns(cotangent, place ^ s, 0, quarter)
        parcels.append(
            jnp.concatenate(
                [x_half, cot[: rows // 2], cot[rows // 2 :], piece_of_weights(place ^ s, (1,))],
                axis=1,
            )
        )
    parcels = from_plane(parcels)
    a1r, b1r, a3o = tie(a1r, b1r, a3o)

    a2r = send(a1r, INNER)
    b2r = send(b1r, TO_ENDS)
    a2r, b2r, *parcels = tie(a2r, b2r, *parcels)
    mine = jnp.stack(parcels)
    other = lax.ppermute(mine[:, :, :width], "mp", swap)
    cot_at = width
    last_at = width + 2 * quarter

    second = mine[:, :, last_at:].reshape(PLACES * depth, 2 * chunks[1])
    a3r = send(a2r, TO_ENDS)
    a3r, other, second = tie(a3r, other, second)

    common = dict(cot=width, quarter=quarter)
    near = send(second, pairs_across(1))
    far = send(second, pairs_across(2))
    gx, parts = chunk_call(
        relayed, mine, other,
        [
            ((own,), (a1o,), (b1o, b2o), (a2o, a3o)),
            ((rest,), (a1r,), (b1r, b2r), (a2r, a3r)),
        ],
        None, chunks[0], left=0, offset=0, last=False, **common,
    )
    near, far, *values = tie(near, far, *gx, *parts)
    gx, (p0, p1, p2, p3) = values[:2], values[2:]
    r1 = send(p3, FROM_ENDS)
    middle = send(second, INNER)
    ends = send(far, TO_ENDS)
    r1, middle, ends, p2, p3 = tie(r1, middle, ends, p2, p3)
    r2b = send(p2, FROM_ENDS)
    r2a = send(add(p3, r1), INNER)
    (keep, give), (lasts,) = chunk_call(
        direct, mine, other, [((second,), (near,), (far,), (middle, ends))], gx, chunks[1],
        left=0, offset=offsets[1], last=True, **common,
    )
    r2a, r2b, keep, give, lasts = tie(r2a, r2b, keep, give, lasts)
    lasts = lax.all_to_all(lasts, "dp", split_axis=0, concat_axis=0, tiled=True)
    theirs = lax.ppermute(give, "mp", swap)
    r3b = send(add(p2, r2b), INNER)
    r3a = send(add(p1, r2a), OUTER)
    rows_x = from_plane(
        [
            add(keep[s * rows : (s + 1) * rows], theirs[s * rows : (s + 1) * rows])
            for s in range(PLACES)
        ]
    )
    r3a, r3b, *rows_x = tie(r3a, r3b, *rows_x)
    sums = add(p0, r3a, r3b)
    firsts = from_plane([sums[s * depth : (s + 1) * depth] for s in range(PLACES)])
    grad_gate = join_call(relayed, firsts, lasts, [chunks[0]], quarter)
    return add(*rows_x), grad_gate


def solution(mesh):
    sizes = dict(mesh.shape)
    by_planes = sizes["dp"] == PLANES * PLACES and sizes["mp"] == 2
    return jax.shard_map(
        planes_plan if by_planes else general_plan,
        mesh=mesh,
        in_specs=(
            P("dp", None),
            P("dp", "mp"),
            P("dp", "mp"),
            P("dp", "mp"),
            P("dp", None),
            P("dp", None),
        ),
        out_specs=(P("dp", "mp"), P("dp", "mp")),
        check_vma=False,
    )
```

time: 331 us -> 250 us (0.76)
  starting transfers between devices: 110 us -> 58 us
  other arithmetic: 41.4 us -> 8.82 us
  waiting for transfers between devices: 90.6 us -> 121 us
  local copies, waits for them, and re-layouts: 29.3 us -> 14.2 us
  blocking collectives: 9.78 us -> 0 us
    ppermute x39 -> x31, waiting for transfers between devices: 76.5 us -> 121 us  [send(): return lax.ppermute(value, 'dp', pairs)]
    ppermute x39 -> x31, starting transfers between devices: 89.5 us -> 54 us  [send(): return lax.ppermute(value, 'dp', pairs)]
    all_to_all x5 -> x1, starting transfers between devices: 20.2 us -> 3.93 us  [planes_plan(): lasts = lax.all_to_all(lasts, 'dp', split_axis=0, concat_axis=0, tiled=True)]
    all_to_all x5 -> x1, waiting for transfers between devices: 14.1 us -> 0.01 us  [planes_plan(): lasts = lax.all_to_all(lasts, 'dp', split_axis=0, concat_axis=0, tiled=True)]
    convert_element_type x14 -> x6, other arithmetic: 17 us -> 6.67 us  [add(): return total.astype(BF)]
    all_to_all x1 -> x0, blocking collectives: 9.78 us -> none  [across_plane(): lax.all_to_all(value, 'dp', split_axis=0, concat_axis=0, tiled=True, axis...]
    add x6 -> x0, other arithmetic: 8.75 us -> none  [gather_planes(): return (own, a1, b1 + b2, a2 + a3)]
    reshape x3 -> x0, local copies, waits for them, and re-layouts: 8.34 us -> none  [the longest x1 4.38 us: planes_plan(): jnp.where(live[:, None], cotangent, jnp.zeros((), BF))]
  transfers between devices with their start and end apart: 46 -> 34, of which waited for: 12 -> 13; matrix products, arithmetic and copies ran while one was open for 17% -> 5% of each run, Pallas kernels for 14% -> 17%
where the time goes in v2:
time: 250 us; the launch traced here: 249 us
  waiting for transfers between devices  121 us (48%)
  starting transfers between devices  58 us (23%)
  Pallas kernels  44.5 us (18%)
  local copies, waits for them, and re-layouts  14.2 us (6%)
  other arithmetic  8.82 us (4%)
  between operations  2.62 us (1%)
    ppermute x31, waiting for transfers between devices, send(): return lax.ppermute(value, 'dp', pairs)  121 us
    ppermute x31, starting transfers between devices, send(): return lax.ppermute(value, 'dp', pairs)  54 us
    pallas_call x2, Pallas kernels, chunk_call(): pl.pallas_call(lambda *a: chunk_kernel(*a, plan=plan), grid_spec=pltpu.Pr...  42.5 us
    unnamed x62, local copies, waits for them, and re-layouts  8.99 us
    convert_element_type x6, other arithmetic, add(): return total.astype(BF)  6.67 us
  transfers between devices with their start and end apart: 34, of which 13 were waited for; matrix products, arithmetic and copies ran while one was open for 5% of the time, Pallas kernels for 17%

profile of v2, /device:TPU:0, one launch (start us, length us, event | category | flops | bytes accessed | tf_op | source)
XLA Modules:
  0.0 249.0 jit_solution(469163348262936893)
XLA Ops:
  0.7 1.5 constant_dynamic-slice_fusion
  2.3 1.5 collective-permute-start.2
  3.8 5.2 %collective-permute-start = (bf16[128,1280]{1,0:T(8,128)(2,1)S(1)}, bf16[128,1280]{1,0:T(8,128)(2,1)}, u32[]{:S(2)}, u32[]{:S(2)}) collective-permute-start(bf16[128,1280]{1,0:T(8,128)(2,1)S(1)} %pad_maximum_fusion.1.a_3_), channel_id=1, source_target_pairs={{0,8},{2,10},{4,12},{6,14},{8,0},{10,2},{12,4},{14,6},{16,24},{18,... | collective-permute-start | bytes 983048 | tf_op jit(solution)/shard_map/ppermute | solution.py:256
  9.0 1.6 collective-permute-start.4
  10.6 1.6 collective-permute-start.5
  12.8 1.3 collective-permute-start.3
  14.1 2.5 collective-permute-done.a_4_
  16.5 1.4 collective-permute-start.1
  17.9 0.6 reduce_sum.19
  18.6 0.6 reduce_sum.18
  20.5 5.8 %collective-permute-done.5 = bf16[128,1280]{1,0:T(8,128)(2,1)S(1)} collective-permute-done((bf16[128,1280]{1,0:T(8,128)(2,1)S(1)}, bf16[128,1280]{1,0:T(8,128)(2,1)S(1)}, u32[]{:S(2)}, u32[]{:S(2)}) %collective-permute-start.5) | collective-permute-done | bytes 327712 | tf_op jit(solution)/shard_map/ppermute | solution.py:256
  26.4 0.7 collective-permute-start.8
  27.2 6.2 %collective-permute-start.7 = (bf16[384,1280]{1,0:T(8,128)(2,1)S(1)}, bf16[384,1280]{1,0:T(8,128)(2,1)S(1)}, u32[]{:S(2)}, u32[]{:S(2)}) collective-permute-start(bf16[384,1280]{1,0:T(8,128)(2,1)S(1)} %constant_dynamic-update-slice_fusion.a_9_), channel_id=1, source_target_pairs={{0,8},{2,10},{4,12},{6,14},{8,0},{10,2},{12,4},{14,6},{16,24},{18,... | collective-permute-start | bytes 2949128 | tf_op jit(solution)/shard_map/ppermute | solution.py:256
  33.5 0.9 copy-done.1
  34.4 1.6 collective-permute-start.9
  36.6 0.6 copy-done.2
  37.4 1.0 dynamic-slice_dynamic-update-slice_fusion.13
  38.4 1.0 dynamic-slice_dynamic-update-slice_fusion.12
  39.4 2.5 %collective-permute-start.14 = (bf16[128,4352]{1,0:T(8,128)(2,1)S(1)}, bf16[128,4352]{1,0:T(8,128)(2,1)S(1)}, u32[]{:S(2)}, u32[]{:S(2)}) collective-permute-start(bf16[128,4352]{1,0:T(8,128)(2,1)S(1)} %get-tuple-element.118), channel_id=1, source_target_pairs={{0,6},{2,4},{4,2},{6,0},{8,14},{10,12},{12,10},{14,8},{16,22},{18,... | collective-permute-start | bytes 3342344 | tf_op jit(solution)/shard_map/ppermute | solution.py:256
  42.4 17.7 %collective-permute-done.9.a_8_ = bf16[128,1280]{1,0:T(8,128)(2,1)S(1)} collective-permute-done((bf16[128,1280]{1,0:T(8,128)(2,1)}, bf16[128,1280]{1,0:T(8,128)(2,1)S(1)}, u32[]{:S(2)}, u32[]{:S(2)}) %collective-permute-start.9) | collective-permute-done | bytes 327712 | tf_op jit(solution)/shard_map/ppermute | solution.py:256
  60.1 1.5 collective-permute-start.12
  61.6 1.6 collective-permute-start.10
  63.2 1.3 collective-permute-start.11
  64.5 3.4 %collective-permute-done.14 = bf16[128,4352]{1,0:T(8,128)(2,1)S(1)} collective-permute-done((bf16[128,4352]{1,0:T(8,128)(2,1)S(1)}, bf16[128,4352]{1,0:T(8,128)(2,1)S(1)}, u32[]{:S(2)}, u32[]{:S(2)}) %collective-permute-start.14) | collective-permute-done | bytes 1114144 | tf_op jit(solution)/shard_map/ppermute | solution.py:256
  67.9 20.3 %collective-permute-done.13 = bf16[128,4352]{1,0:T(8,128)(2,1)S(1)} collective-permute-done((bf16[128,4352]{1,0:T(8,128)(2,1)S(1)}, bf16[128,4352]{1,0:T(8,128)(2,1)S(1)}, u32[]{:S(2)}, u32[]{:S(2)}) %collective-permute-start.13) | collective-permute-done | bytes 1114144 | tf_op jit(solution)/shard_map/ppermute | solution.py:256
  88.3 1.0 copy-done.18
  89.2 0.6 pad_maximum_fusion.a_1_
  89.9 2.1 copy-done.5
  92.3 1.3 collective-permute-start.15
  93.6 0.7 stack.147.a_0_
  94.3 1.1 slice.89
  95.4 23.2 %collective-permute-done.15.a_14_ = bf16[384,1280]{1,0:T(8,128)(2,1)} collective-permute-done((bf16[384,1280]{1,0:T(8,128)(2,1)}, bf16[384,1280]{1,0:T(8,128)(2,1)}, u32[]{:S(2)}, u32[]{:S(2)}) %collective-permute-start.15) | collective-permute-done | bytes 983072 | tf_op jit(solution)/shard_map/ppermute | solution.py:256
  118.6 1.9 collective-permute-start.17
  120.6 26.0 %swiglu_chunk.2 = (bf16[1024,1024]{1,0:T(8,128)(2,1)}, bf16[1024,1024]{1,0:T(8,128)(2,1)}, bf16[512,640]{1,0:T(8,128)(2,1)}, bf16[512,640]{1,0:T(8,128)(2,1)}, b...) custom-call(s32[21]{0:T(128)} %stack.147.a_0_, bf16[4,128,4352]{2,1,0:T(8,128)(2,1)} %copy-done.5, ...), custom_call_target="tpu_custom_call" | custom-call | flops 13421772800 | bytes 16777216 | tf_op jit(solution)/shard_map/swiglu_chunk/pallas_call | solution.py:175
  146.6 0.8 copy-done.20
  147.4 2.0 collective-permute-start.19
  149.5 0.7 collective-permute-start.20
  150.2 1.3 collective-permute-start.21
  151.5 13.5 %collective-permute-done.21.a_7_ = bf16[512,512]{1,0:T(8,128)(2,1)S(1)} collective-permute-done((bf16[512,512]{1,0:T(8,128)(2,1)S(1)}, bf16[512,512]{1,0:T(8,128)(2,1)S(1)}, u32[]{:S(2)}, u32[]{:S(2)}) %collective-permute-start.21) | collective-permute-done | bytes 524320 | tf_op jit(solution)/shard_map/ppermute | solution.py:256
  165.1 0.8 copy-done.22
  165.9 1.2 add_convert_fusion.3
  167.1 0.7 collective-permute-start.22
  167.8 4.6 %collective-permute-start.23 = (bf16[512,640]{1,0:T(8,128)(2,1)S(1)}, bf16[512,640]{1,0:T(8,128)(2,1)S(1)}, u32[]{:S(2)}, u32[]{:S(2)}) collective-permute-start(bf16[512,640]{1,0:T(8,128)(2,1)S(1)} %copy-done.9), channel_id=1, source_target_pairs={{0,8},{2,10},{4,12},{6,14},{24,16},{26,18},{28,20},{30,22},{1,9},{... | collective-permute-start | bytes 1966088 | tf_op jit(solution)/shard_map/ppermute | solution.py:256
  172.5 0.6 stack.156.a_0_
  173.1 16.5 %swiglu_chunk.3 = (bf16[1024,1024]{1,0:T(8,128)(2,1)}, bf16[1024,1024]{1,0:T(8,128)(2,1)}, bf16[16,128,256]{2,1,0:T(8,128)(2,1)}) custom-call(s32[21]{0:T(128)} %stack.156.a_0_, bf16[4,128,4352]{2,1,0:T(8,128)(2,1)} %copy-done.5, bf16[4,128,2048]{2,1,0:T(8,128)(2,1)} %collective-permute-done.16.a_2_, bf16[512,512]{1,0:T(8,128)(2,1)} %bitcast.41, ...), custom_call_target="tpu_custom_call" | custom-call | flops 5368709120 | bytes 16777216 | tf_op jit(solution)/shard_map/swiglu_chunk/pallas_call | solution.py:175
  189.6 0.8 copy-done.10
  190.7 3.9 %all-to-all-start = ((bf16[16,128,256]{2,1,0:T(8,128)(2,1)}), bf16[16,128,256]{2,1,0:T(8,128)(2,1)S(1)}, u32[]{:S(2)}, u32[]{:S(2)}) async-start(bf16[16,128,256]{2,1,0:T(8,128)(2,1)} %get-tuple-element.109), calls=%async_computation | async-start | bytes 2097152 | tf_op jit(solution)/shard_map/all_to_all | solution.py:390
  194.6 1.6 add_convert_fusion.1
  196.2 0.7 collective-permute-start.25
  196.9 1.4 add_convert_fusion.2
  198.4 4.7 %collective-permute-start.24 = (bf16[512,640]{1,0:T(8,128)(2,1)S(1)}, bf16[512,640]{1,0:T(8,128)(2,1)S(1)}, u32[]{:S(2)}, u32[]{:S(2)}) collective-permute-start(bf16[512,640]{1,0:T(8,128)(2,1)S(1)} %add_convert_fusion.2), channel_id=1, source_target_pairs={{0,8},{2,10},{4,12},{6,14},{8,0},{10,2},{12,4},{14,6},{16,24},{18,... | collective-permute-start | bytes 1966088 | tf_op jit(solution)/shard_map/ppermute | solution.py:256
  203.1 1.0 add_convert_fusion.5
  204.1 2.4 collective-permute-start.29
  207.0 0.6 collective-permute-start.27
  207.6 20.8 %collective-permute-done.24 = bf16[512,640]{1,0:T(8,128)(2,1)S(1)} collective-permute-done((bf16[512,640]{1,0:T(8,128)(2,1)S(1)}, bf16[512,640]{1,0:T(8,128)(2,1)S(1)}, u32[]{:S(2)}, u32[]{:S(2)}) %collective-permute-start.24) | collective-permute-done | bytes 655392 | tf_op jit(solution)/shard_map/ppermute | solution.py:256
  228.4 6.0 %collective-permute-done.28 = bf16[256,1024]{1,0:T(8,128)(2,1)S(1)} collective-permute-done((bf16[256,1024]{1,0:T(8,128)(2,1)S(1)}, bf16[256,1024]{1,0:T(8,128)(2,1)S(1)}, u32[]{:S(2)}, u32[]{:S(2)}) %collective-permute-start.28) | collective-permute-done | bytes 524320 | tf_op jit(solution)/shard_map/ppermute | solution.py:256
  234.5 2.4 collective-permute-done.27
  237.2 1.5 collective-permute-start.32
  238.7 1.2 collective-permute-start.31
  239.9 0.9 collective-permute-start.30
  240.7 1.2 add_convert_fusion.4
  241.9 3.0 %collective-permute-done.32.a_4_ = bf16[128,640]{1,0:T(8,128)(2,1)S(1)} collective-permute-done((bf16[128,640]{1,0:T(8,128)(2,1)S(1)}, bf16[128,640]{1,0:T(8,128)(2,1)S(1)}, u32[]{:S(2)}, u32[]{:S(2)}) %collective-permute-start.32) | collective-permute-done | bytes 163872 | tf_op jit(solution)/shard_map/ppermute | solution.py:256
  244.9 2.0 collective-permute-done.31.a_3_
  247.0 2.0 join_chunks.1
  (92 shorter events, 3.9 us)
Async XLA Ops:
  2.2 24.1 %copy-start.13 = (bf16[128,1280]{1,0:T(8,128)(2,1)}, bf16[128,1280]{1,0:T(8,128)(2,1)S(1)}, u32[]{:S(2)}) copy-start(bf16[128,1280]{1,0:T(8,128)(2,1)S(1)} %pad_maximum_fusion.1.a_3_) | copy-start | bytes 983044
  2.2 15.7 %copy-start.24 = (s32[1,16]{1,0:T(1,128)S(1)}, s32[1,16]{1,0:T(1,128)}, u32[]{:S(2)}) copy-start(s32[1,16]{1,0:T(1,128)} %param.11) | copy-start | bytes 196
  2.3 16.3 %copy-start.25 = (s32[1,16]{1,0:T(1,128)S(1)}, s32[1,16]{1,0:T(1,128)}, u32[]{:S(2)}) copy-start(s32[1,16]{1,0:T(1,128)} %param.10) | copy-start | bytes 196
  2.3 10.5 %collective-permute-start.2 = (bf16[128,1280]{1,0:T(8,128)(2,1)S(1)}, bf16[128,1280]{1,0:T(8,128)(2,1)}, u32[]{:S(2)}, u32[]{:S(2)}) collective-permute-start(bf16[128,1280]{1,0:T(8,128)(2,1)S(1)} %pad_maximum_fusion.1.a_3_), channel_id=1, source_target_pairs={{8,16},{10,18},{12,20},{14,22},{16,8},{18,10},{20,12},{22,14},{9,1... | collective-permute-start | bytes 983048 | tf_op jit(solution)/shard_map/ppermute | solution.py:256
  3.8 12.7 %collective-permute-start = (bf16[128,1280]{1,0:T(8,128)(2,1)S(1)}, bf16[128,1280]{1,0:T(8,128)(2,1)}, u32[]{:S(2)}, u32[]{:S(2)}) collective-permute-start(bf16[128,1280]{1,0:T(8,128)(2,1)S(1)} %pad_maximum_fusion.1.a_3_), channel_id=1, source_target_pairs={{0,8},{2,10},{4,12},{6,14},{8,0},{10,2},{12,4},{14,6},{16,24},{18,... | collective-permute-start | bytes 983048 | tf_op jit(solution)/shard_map/ppermute | solution.py:256
  9.0 11.5 %collective-permute-start.4 = (bf16[128,1280]{1,0:T(8,128)(2,1)S(1)}, bf16[128,1280]{1,0:T(8,128)(2,1)S(1)}, u32[]{:S(2)}, u32[]{:S(2)}) collective-permute-start(bf16[128,1280]{1,0:T(8,128)(2,1)S(1)} %pad_maximum_fusion.2), channel_id=1, source_target_pairs={{0,2},{2,0},{4,6},{6,4},{8,10},{10,8},{12,14},{14,12},{16,18},{18,... | collective-permute-start | bytes 983048 | tf_op jit(solution)/shard_map/ppermute | solution.py:256
  10.6 15.7 %collective-permute-start.5 = (bf16[128,1280]{1,0:T(8,128)(2,1)S(1)}, bf16[128,1280]{1,0:T(8,128)(2,1)S(1)}, u32[]{:S(2)}, u32[]{:S(2)}) collective-permute-start(bf16[128,1280]{1,0:T(8,128)(2,1)S(1)} %pad_maximum_fusion.3), channel_id=1, source_target_pairs={{0,4},{2,6},{4,0},{6,2},{8,12},{10,14},{12,8},{14,10},{16,20},{18,... | collective-permute-start | bytes 983048 | tf_op jit(solution)/shard_map/ppermute | solution.py:256
  12.2 21.1 %copy-start.14 = (bf16[256,2048]{1,0:T(8,128)(2,1)S(1)}, bf16[256,2048]{1,0:T(8,128)(2,1)}, u32[]{:S(2)}) copy-start(bf16[256,2048]{1,0:T(8,128)(2,1)} %param.6) | copy-start | bytes 3145732
  12.2 14.1 %collective-permute-start.6 = (bf16[128,1280]{1,0:T(8,128)(2,1)S(1)}, bf16[128,1280]{1,0:T(8,128)(2,1)S(1)}, u32[]{:S(2)}, u32[]{:S(2)}) collective-permute-start(bf16[128,1280]{1,0:T(8,128)(2,1)S(1)} %pad_maximum_fusion.4), channel_id=1, source_target_pairs={{0,6},{2,4},{4,2},{6,0},{8,14},{10,12},{12,10},{14,8},{16,22},{18,... | collective-permute-start | bytes 983048 | tf_op jit(solution)/shard_map/ppermute | solution.py:256
  12.8 13.5 %collective-permute-start.3 = (bf16[128,1280]{1,0:T(8,128)(2,1)}, bf16[128,1280]{1,0:T(8,128)(2,1)}, u32[]{:S(2)}, u32[]{:S(2)}) collective-permute-start(bf16[128,1280]{1,0:T(8,128)(2,1)} %collective-permute-done.2.a_5_), channel_id=1, source_target_pairs={{8,0},{10,2},{12,4},{14,6},{16,24},{18,26},{20,28},{22,30},{9,1},{... | collective-permute-start | bytes 983048 | tf_op jit(solution)/shard_map/ppermute | solution.py:256
  16.5 9.8 %collective-permute-start.1 = (bf16[128,1280]{1,0:T(8,128)(2,1)}, bf16[128,1280]{1,0:T(8,128)(2,1)}, u32[]{:S(2)}, u32[]{:S(2)}) collective-permute-start(bf16[128,1280]{1,0:T(8,128)(2,1)} %collective-permute-done.a_4_), channel_id=1, source_target_pairs={{8,16},{10,18},{12,20},{14,22},{16,8},{18,10},{20,12},{22,14},{9,1... | collective-permute-start | bytes 983048 | tf_op jit(solution)/shard_map/ppermute | solution.py:256
  26.4 7.1 %copy-start.15 = (bf16[384,1280]{1,0:T(8,128)(2,1)}, bf16[384,1280]{1,0:T(8,128)(2,1)S(1)}, u32[]{:S(2)}) copy-start(bf16[384,1280]{1,0:T(8,128)(2,1)S(1)} %constant_dynamic-update-slice_fusion.a_9_) | copy-start | bytes 2949124
  26.4 35.1 %collective-permute-start.8 = (bf16[384,1280]{1,0:T(8,128)(2,1)S(1)}, bf16[384,1280]{1,0:T(8,128)(2,1)S(1)}, u32[]{:S(2)}, u32[]{:S(2)}) collective-permute-start(bf16[384,1280]{1,0:T(8,128)(2,1)S(1)} %constant_dynamic-update-slice_fusion.a_9_), channel_id=1, source_target_pairs={{8,16},{10,18},{12,20},{14,22},{16,8},{18,10},{20,12},{22,14},{9,1... | collective-permute-start | bytes 2949128 | tf_op jit(solution)/shard_map/ppermute | solution.py:256
  27.2 34.4 %collective-permute-start.7 = (bf16[384,1280]{1,0:T(8,128)(2,1)S(1)}, bf16[384,1280]{1,0:T(8,128)(2,1)S(1)}, u32[]{:S(2)}, u32[]{:S(2)}) collective-permute-start(bf16[384,1280]{1,0:T(8,128)(2,1)S(1)} %constant_dynamic-update-slice_fusion.a_9_), channel_id=1, source_target_pairs={{0,8},{2,10},{4,12},{6,14},{8,0},{10,2},{12,4},{14,6},{16,24},{18,... | collective-permute-start | bytes 2949128 | tf_op jit(solution)/shard_map/ppermute | solution.py:256
  33.4 1.0 copy-start.1
  34.4 1.6 copy-start.7
  34.4 1.8 copy-start.4
  34.4 2.2 copy-start.3
  34.4 2.8 %copy-start.2 = (bf16[128,4352]{1,0:T(8,128)(2,1)S(1)}, bf16[128,4352]{1,0:T(8,128)(2,1)}, u32[]{:S(2)}) copy-start(bf16[128,4352]{1,0:T(8,128)(2,1)} %copy-done.1) | copy-start | bytes 3342340
  34.4 25.7 %collective-permute-start.9 = (bf16[128,1280]{1,0:T(8,128)(2,1)}, bf16[128,1280]{1,0:T(8,128)(2,1)S(1)}, u32[]{:S(2)}, u32[]{:S(2)}) collective-permute-start(bf16[128,1280]{1,0:T(8,128)(2,1)} %collective-permute-done.1.a_7_), channel_id=1, source_target_pairs={{8,0},{10,2},{12,4},{14,6},{16,24},{18,26},{20,28},{22,30},{9,1},{... | collective-permute-start | bytes 983048 | tf_op jit(solution)/shard_map/ppermute | solution.py:256
  39.4 28.5 %collective-permute-start.14 = (bf16[128,4352]{1,0:T(8,128)(2,1)S(1)}, bf16[128,4352]{1,0:T(8,128)(2,1)S(1)}, u32[]{:S(2)}, u32[]{:S(2)}) collective-permute-start(bf16[128,4352]{1,0:T(8,128)(2,1)S(1)} %get-tuple-element.118), channel_id=1, source_target_pairs={{0,6},{2,4},{4,2},{6,0},{8,14},{10,12},{12,10},{14,8},{16,22},{18,... | collective-permute-start | bytes 3342344 | tf_op jit(solution)/shard_map/ppermute | solution.py:256
  41.9 46.3 %collective-permute-start.13 = (bf16[128,4352]{1,0:T(8,128)(2,1)S(1)}, bf16[128,4352]{1,0:T(8,128)(2,1)S(1)}, u32[]{:S(2)}, u32[]{:S(2)}) collective-permute-start(bf16[128,4352]{1,0:T(8,128)(2,1)S(1)} %get-tuple-element.119), channel_id=1, source_target_pairs={{0,4},{2,6},{4,0},{6,2},{8,12},{10,14},{12,8},{14,10},{16,20},{18,... | collective-permute-start | bytes 3342344 | tf_op jit(solution)/shard_map/ppermute | solution.py:256
  60.1 29.8 %copy-start.23 = (bf16[128,1280]{1,0:T(8,128)(2,1)}, bf16[128,1280]{1,0:T(8,128)(2,1)S(1)}, u32[]{:S(2)}) copy-start(bf16[128,1280]{1,0:T(8,128)(2,1)S(1)} %collective-permute-done.9.a_8_) | copy-start | bytes 983044
  60.1 28.2 %collective-permute-start.12 = (bf16[128,4352]{1,0:T(8,128)(2,1)S(1)}, bf16[128,4352]{1,0:T(8,128)(2,1)S(1)}, u32[]{:S(2)}, u32[]{:S(2)}) collective-permute-start(bf16[128,4352]{1,0:T(8,128)(2,1)S(1)} %get-tuple-element.120), channel_id=1, source_target_pairs={{0,2},{2,0},{4,6},{6,4},{8,10},{10,8},{12,14},{14,12},{16,18},{18,... | collective-permute-start | bytes 3342344 | tf_op jit(solution)/shard_map/ppermute | solution.py:256
  61.6 28.3 %copy-start.16 = (bf16[384,1280]{1,0:T(8,128)(2,1)}, bf16[384,1280]{1,0:T(8,128)(2,1)S(1)}, u32[]{:S(2)}) copy-start(bf16[384,1280]{1,0:T(8,128)(2,1)S(1)} %collective-permute-done.8.a_11_) | copy-start | bytes 2949124
  61.6 28.3 %copy-start.17 = (bf16[384,1280]{1,0:T(8,128)(2,1)}, bf16[384,1280]{1,0:T(8,128)(2,1)S(1)}, u32[]{:S(2)}) copy-start(bf16[384,1280]{1,0:T(8,128)(2,1)S(1)} %collective-permute-done.7.a_10_) | copy-start | bytes 2949124
  61.6 26.7 %collective-permute-start.10 = (bf16[384,1280]{1,0:T(8,128)(2,1)S(1)}, bf16[384,1280]{1,0:T(8,128)(2,1)}, u32[]{:S(2)}, u32[]{:S(2)}) collective-permute-start(bf16[384,1280]{1,0:T(8,128)(2,1)S(1)} %collective-permute-done.7.a_10_), channel_id=1, source_target_pairs={{8,16},{10,18},{12,20},{14,22},{16,8},{18,10},{20,12},{22,14},{9,1... | collective-permute-start | bytes 2949128 | tf_op jit(solution)/shard_map/ppermute | solution.py:256
  63.2 25.1 %collective-permute-start.11 = (bf16[384,1280]{1,0:T(8,128)(2,1)S(1)}, bf16[384,1280]{1,0:T(8,128)(2,1)S(1)}, u32[]{:S(2)}, u32[]{:S(2)}) collective-permute-start(bf16[384,1280]{1,0:T(8,128)(2,1)S(1)} %collective-permute-done.8.a_11_), channel_id=1, source_target_pairs={{8,0},{10,2},{12,4},{14,6},{16,24},{18,26},{20,28},{22,30},{9,1},{... | collective-permute-start | bytes 2949128 | tf_op jit(solution)/shard_map/ppermute | solution.py:256
  88.3 1.0 copy-start.18
  89.9 2.1 copy-start.5
  92.2 26.4 %collective-permute-start.16 = (bf16[4,128,2048]{2,1,0:T(8,128)(2,1)S(1)}, bf16[4,128,2048]{2,1,0:T(8,128)(2,1)}, u32[]{:S(2)}, u32[]{:S(2)}) collective-permute-start(bf16[4,128,2048]{2,1,0:T(8,128)(2,1)S(1)} %slice.88), channel_id=1, source_target_pairs={{0,1},{1,0},{2,3},{3,2},{4,5},{5,4},{6,7},{7,6},{8,9},{9,8},{10,11... | collective-permute-start | bytes 6291464 | tf_op jit(solution)/shard_map/ppermute | solution.py:358
  92.3 26.4 %collective-permute-start.15 = (bf16[384,1280]{1,0:T(8,128)(2,1)}, bf16[384,1280]{1,0:T(8,128)(2,1)}, u32[]{:S(2)}, u32[]{:S(2)}) collective-permute-start(bf16[384,1280]{1,0:T(8,128)(2,1)} %collective-permute-done.10.a_13_), channel_id=1, source_target_pairs={{8,0},{10,2},{12,4},{14,6},{16,24},{18,26},{20,28},{22,30},{9,1},{... | collective-permute-start | bytes 2949128 | tf_op jit(solution)/shard_map/ppermute | solution.py:256
  95.4 54.1 %copy-start.12 = (bf16[4,128,512]{2,1,0:T(8,128)(2,1)}, bf16[4,128,512]{2,1,0:T(8,128)(2,1)S(1)}, u32[]{:S(2)}) copy-start(bf16[4,128,512]{2,1,0:T(8,128)(2,1)S(1)} %slice.89) | copy-start | bytes 1572868
  118.6 27.9 %collective-permute-start.18 = (bf16[512,512]{1,0:T(8,128)(2,1)S(1)}, bf16[512,512]{1,0:T(8,128)(2,1)S(1)}, u32[]{:S(2)}, u32[]{:S(2)}) collective-permute-start(bf16[512,512]{1,0:T(8,128)(2,1)S(1)} %bitcast.38), channel_id=1, source_target_pairs={{0,16},{2,18},{4,20},{6,22},{8,24},{10,26},{12,28},{14,30},{16,0},... | collective-permute-start | bytes 1572872 | tf_op jit(solution)/shard_map/ppermute | solution.py:256
  118.6 28.0 %collective-permute-start.17 = (bf16[512,512]{1,0:T(8,128)(2,1)S(1)}, bf16[512,512]{1,0:T(8,128)(2,1)S(1)}, u32[]{:S(2)}, u32[]{:S(2)}) collective-permute-start(bf16[512,512]{1,0:T(8,128)(2,1)S(1)} %bitcast.39), channel_id=1, source_target_pairs={{0,8},{2,10},{4,12},{6,14},{8,0},{10,2},{12,4},{14,6},{16,24},{18,... | collective-permute-start | bytes 1572872 | tf_op jit(solution)/shard_map/ppermute | solution.py:256
  146.6 21.3 %copy-start.9 = (bf16[512,640]{1,0:T(8,128)(2,1)S(1)}, bf16[512,640]{1,0:T(8,128)(2,1)}, u32[]{:S(2)}) copy-start(bf16[512,640]{1,0:T(8,128)(2,1)} %get-tuple-element.89) | copy-start | bytes 1966084
  146.6 20.5 %copy-start.19 = (bf16[512,512]{1,0:T(8,128)(2,1)}, bf16[512,512]{1,0:T(8,128)(2,1)S(1)}, u32[]{:S(2)}) copy-start(bf16[512,512]{1,0:T(8,128)(2,1)S(1)} %collective-permute-done.18.a_5_) | copy-start | bytes 1572868
  146.6 0.8 copy-start.20
  147.4 18.4 %collective-permute-start.19 = (bf16[512,640]{1,0:T(8,128)(2,1)}, bf16[512,640]{1,0:T(8,128)(2,1)S(1)}, u32[]{:S(2)}, u32[]{:S(2)}) collective-permute-start(bf16[512,640]{1,0:T(8,128)(2,1)} %get-tuple-element.87), channel_id=1, source_target_pairs={{0,8},{2,10},{4,12},{6,14},{24,16},{26,18},{28,20},{30,22},{1,9},{... | collective-permute-start | bytes 1966088 | tf_op jit(solution)/shard_map/ppermute | solution.py:256
  149.5 2.0 collective-permute-start.20
  150.2 14.9 %collective-permute-start.21 = (bf16[512,512]{1,0:T(8,128)(2,1)S(1)}, bf16[512,512]{1,0:T(8,128)(2,1)S(1)}, u32[]{:S(2)}, u32[]{:S(2)}) collective-permute-start(bf16[512,512]{1,0:T(8,128)(2,1)S(1)} %collective-permute-done.18.a_5_), channel_id=1, source_target_pairs={{8,0},{10,2},{12,4},{14,6},{16,24},{18,26},{20,28},{22,30},{9,1},{... | collective-permute-start | bytes 1572872 | tf_op jit(solution)/shard_map/ppermute | solution.py:256
  151.5 13.5 %copy-start.21 = (bf16[512,512]{1,0:T(8,128)(2,1)}, bf16[512,512]{1,0:T(8,128)(2,1)S(1)}, u32[]{:S(2)}) copy-start(bf16[512,512]{1,0:T(8,128)(2,1)S(1)} %collective-permute-done.20.a_6_) | copy-start | bytes 1572868
  165.1 0.8 copy-start.22
  167.1 22.5 %collective-permute-start.22 = (bf16[512,640]{1,0:T(8,128)(2,1)S(1)}, bf16[512,640]{1,0:T(8,128)(2,1)S(1)}, u32[]{:S(2)}, u32[]{:S(2)}) collective-permute-start(bf16[512,640]{1,0:T(8,128)(2,1)S(1)} %add_convert_fusion.3), channel_id=1, source_target_pairs={{8,16},{10,18},{12,20},{14,22},{16,8},{18,10},{20,12},{22,14},{9,1... | collective-permute-start | bytes 1966088 | tf_op jit(solution)/shard_map/ppermute | solution.py:256
  167.8 21.8 %collective-permute-start.23 = (bf16[512,640]{1,0:T(8,128)(2,1)S(1)}, bf16[512,640]{1,0:T(8,128)(2,1)S(1)}, u32[]{:S(2)}, u32[]{:S(2)}) collective-permute-start(bf16[512,640]{1,0:T(8,128)(2,1)S(1)} %copy-done.9), channel_id=1, source_target_pairs={{0,8},{2,10},{4,12},{6,14},{24,16},{26,18},{28,20},{30,22},{1,9},{... | collective-permute-start | bytes 1966088 | tf_op jit(solution)/shard_map/ppermute | solution.py:256
  189.6 0.9 copy-start.10
  189.6 1.0 copy-start.11
  190.7 12.4 %collective-permute-start.26 = (bf16[1024,1024]{1,0:T(8,128)(2,1)}, bf16[1024,1024]{1,0:T(8,128)(2,1)S(1)}, u32[]{:S(2)}, u32[]{:S(2)}) collective-permute-start(bf16[1024,1024]{1,0:T(8,128)(2,1)} %get-tuple-element.101), channel_id=1, source_target_pairs={{0,1},{1,0},{2,3},{3,2},{4,5},{5,4},{6,7},{7,6},{8,9},{9,8},{10,11... | collective-permute-start | bytes 6291464 | tf_op jit(solution)/shard_map/ppermute | solution.py:391
  190.7 51.2 %all-to-all-start = ((bf16[16,128,256]{2,1,0:T(8,128)(2,1)}), bf16[16,128,256]{2,1,0:T(8,128)(2,1)S(1)}, u32[]{:S(2)}, u32[]{:S(2)}) async-start(bf16[16,128,256]{2,1,0:T(8,128)(2,1)} %get-tuple-element.109), calls=%async_computation | async-start | bytes 2097152 | tf_op jit(solution)/shard_map/all_to_all | solution.py:390
  194.6 8.4 %copy-start.6 = (bf16[1024,1024]{1,0:T(8,128)(2,1)S(1)}, bf16[1024,1024]{1,0:T(8,128)(2,1)}, u32[]{:S(2)}) copy-start(bf16[1024,1024]{1,0:T(8,128)(2,1)} %get-tuple-element.100) | copy-start | bytes 6291460
  196.2 11.4 %collective-permute-start.25 = (bf16[512,640]{1,0:T(8,128)(2,1)S(1)}, bf16[512,640]{1,0:T(8,128)(2,1)S(1)}, u32[]{:S(2)}, u32[]{:S(2)}) collective-permute-start(bf16[512,640]{1,0:T(8,128)(2,1)S(1)} %add_convert_fusion.1), channel_id=1, source_target_pairs={{8,16},{10,18},{12,20},{14,22},{16,8},{18,10},{20,12},{22,14},{9,1... | collective-permute-start | bytes 1966088 | tf_op jit(solution)/shard_map/ppermute | solution.py:256
  198.4 38.5 %copy-start.8 = (bf16[512,640]{1,0:T(8,128)(2,1)S(1)}, bf16[512,640]{1,0:T(8,128)(2,1)}, u32[]{:S(2)}) copy-start(bf16[512,640]{1,0:T(8,128)(2,1)} %get-tuple-element.106) | copy-start | bytes 1966084
  198.4 30.1 %collective-permute-start.24 = (bf16[512,640]{1,0:T(8,128)(2,1)S(1)}, bf16[512,640]{1,0:T(8,128)(2,1)S(1)}, u32[]{:S(2)}, u32[]{:S(2)}) collective-permute-start(bf16[512,640]{1,0:T(8,128)(2,1)S(1)} %add_convert_fusion.2), channel_id=1, source_target_pairs={{0,8},{2,10},{4,12},{6,14},{8,0},{10,2},{12,4},{14,6},{16,24},{18,... | collective-permute-start | bytes 1966088 | tf_op jit(solution)/shard_map/ppermute | solution.py:256
  204.1 24.4 %collective-permute-start.29 = (bf16[256,1024]{1,0:T(8,128)(2,1)S(1)}, bf16[256,1024]{1,0:T(8,128)(2,1)S(1)}, u32[]{:S(2)}, u32[]{:S(2)}) collective-permute-start(bf16[256,1024]{1,0:T(8,128)(2,1)S(1)} %get-tuple-element.110), channel_id=1, source_target_pairs={{0,6},{2,4},{4,2},{6,0},{8,14},{10,12},{12,10},{14,8},{16,22},{18,... | collective-permute-start | bytes 1572872 | tf_op jit(solution)/shard_map/ppermute | solution.py:256
  206.5 28.0 %collective-permute-start.28 = (bf16[256,1024]{1,0:T(8,128)(2,1)S(1)}, bf16[256,1024]{1,0:T(8,128)(2,1)S(1)}, u32[]{:S(2)}, u32[]{:S(2)}) collective-permute-start(bf16[256,1024]{1,0:T(8,128)(2,1)S(1)} %get-tuple-element.111), channel_id=1, source_target_pairs={{0,4},{2,6},{4,0},{6,2},{8,12},{10,14},{12,8},{14,10},{16,20},{18,... | collective-permute-start | bytes 1572872 | tf_op jit(solution)/shard_map/ppermute | solution.py:256
  207.0 29.8 %collective-permute-start.27 = (bf16[256,1024]{1,0:T(8,128)(2,1)S(1)}, bf16[256,1024]{1,0:T(8,128)(2,1)S(1)}, u32[]{:S(2)}, u32[]{:S(2)}) collective-permute-start(bf16[256,1024]{1,0:T(8,128)(2,1)S(1)} %get-tuple-element.112), channel_id=1, source_target_pairs={{0,2},{2,0},{4,6},{6,4},{8,10},{10,8},{12,14},{14,12},{16,18},{18,... | collective-permute-start | bytes 1572872 | tf_op jit(solution)/shard_map/ppermute | solution.py:256
  237.2 7.8 %collective-permute-start.32 = (bf16[128,640]{1,0:T(8,128)(2,1)S(1)}, bf16[128,640]{1,0:T(8,128)(2,1)S(1)}, u32[]{:S(2)}, u32[]{:S(2)}) collective-permute-start(bf16[128,640]{1,0:T(8,128)(2,1)S(1)} %get-tuple-element.134), channel_id=1, source_target_pairs={{0,6},{2,4},{4,2},{6,0},{8,14},{10,12},{12,10},{14,8},{16,22},{18,... | collective-permute-start | bytes 491528 | tf_op jit(solution)/shard_map/ppermute | solution.py:256
  238.7 8.3 %collective-permute-start.31 = (bf16[128,640]{1,0:T(8,128)(2,1)S(1)}, bf16[128,640]{1,0:T(8,128)(2,1)S(1)}, u32[]{:S(2)}, u32[]{:S(2)}) collective-permute-start(bf16[128,640]{1,0:T(8,128)(2,1)S(1)} %get-tuple-element.135), channel_id=1, source_target_pairs={{0,4},{2,6},{4,0},{6,2},{8,12},{10,14},{12,8},{14,10},{16,20},{18,... | collective-permute-start | bytes 491528 | tf_op jit(solution)/shard_map/ppermute | solution.py:256
  239.9 7.1 %copy-start = (s32[21]{0:T(128)S(1)}, s32[21]{0:T(128)}, u32[]{:S(2)}) copy-start(s32[21]{0:T(128)} %stack.147.a_0_) | copy-start | bytes 256
  239.9 7.1 %collective-permute-start.30 = (bf16[128,640]{1,0:T(8,128)(2,1)S(1)}, bf16[128,640]{1,0:T(8,128)(2,1)S(1)}, u32[]{:S(2)}, u32[]{:S(2)}) collective-permute-start(bf16[128,640]{1,0:T(8,128)(2,1)S(1)} %get-tuple-element.136), channel_id=1, source_target_pairs={{0,2},{2,0},{4,6},{6,4},{8,10},{10,8},{12,14},{14,12},{16,18},{18,... | collective-permute-start | bytes 491528 | tf_op jit(solution)/shard_map/ppermute | solution.py:256

commit v3 on v2

v3 whole, which is shorter than its diff:
```python
import jax
import jax.numpy as jnp
from jax import lax
from jax.experimental import pallas as pl
from jax.experimental.pallas import tpu as pltpu
from jax.sharding import PartitionSpec as P

BAL = 208
BF = jnp.bfloat16
F32 = jnp.float32


def contract_last(left, right):
    return lax.dot_general(
        left, right, (((1,), (1,)), ((), ())), preferred_element_type=F32
    )


def contract_first(left, right):
    return lax.dot_general(
        left, right, (((0,), (0,)), ((), ())), preferred_element_type=F32
    )


def swiglu_back(x_rows, cot_rows, gate_full, up_full, live_mask):
    gate_val = jnp.dot(x_rows, gate_full, preferred_element_type=F32)
    up_val = jnp.dot(x_rows, up_full, preferred_element_type=F32)
    sig = jax.nn.sigmoid(gate_val)
    cot_val = cot_rows.astype(F32)
    d_gate = jnp.where(
        live_mask[:, None], cot_val * up_val * sig * (1.0 + gate_val * (1.0 - sig)), 0.0
    ).astype(BF)
    d_up = jnp.where(live_mask[:, None], cot_val * gate_val * sig, 0.0).astype(BF)
    return contract_last(d_gate, gate_full) + contract_last(d_up, up_full), d_gate


def live_rows_of(send_counts, recv_counts):
    return BAL + jnp.sum(send_counts[0]) - jnp.sum(recv_counts[0])


def general_plan(x_in, cotangent, w_gate, w_up, send_counts, recv_counts):
    dev_count = lax.axis_size("dp")
    gate_full = lax.all_gather(w_gate, "dp", axis=0, tiled=True)
    up_full = lax.all_gather(w_up, "dp", axis=0, tiled=True)
    live_mask = jnp.arange(x_in.shape[0]) < live_rows_of(send_counts, recv_counts)
    partial_value, d_gate = swiglu_back(x_in, cotangent, gate_full, up_full, live_mask)
    grad_x = lax.psum_scatter(
        partial_value.astype(BF), "mp", scatter_dimension=1, tiled=True
    )
    whole = contract_first(x_in, d_gate)
    pieces = lax.all_to_all(
        whole.reshape(dev_count, x_in.shape[1] // dev_count, whole.shape[1]),
        "dp",
        split_axis=0,
        concat_axis=0,
        tiled=True,
    )
    return grad_x, jnp.sum(pieces, axis=0)


CREW = (0, 1, 2, 3)
NEAR, FAR = 4, 8
CHAIN = (0, NEAR, FAR, NEAR | FAR)
DEVS = 16
TILE = 256


def tie(*values):
    return lax.optimization_barrier(values)


def send(value, mask):
    return lax.ppermute(value, "dp", [(i, i ^ mask) for i in range(DEVS)])


def along(value, moves):
    crew = len(CREW)
    return lax.ppermute(
        value, "dp", [(crew * a + q, crew * b + q) for a, b in moves for q in range(crew)]
    )


OUTER = [(0, 1), (1, 0), (2, 3), (3, 2)]
INNER = [(1, 2), (2, 1)]
TO_ENDS = [(1, 0), (2, 3)]
FROM_ENDS = [(0, 1), (3, 2)]


def crew_swap(pieces):
    return [send(p, m) if m else p for p, m in zip(pieces, CREW)]


def add(*terms):
    total = terms[0].astype(F32)
    for term in terms[1:]:
        total = total + term.astype(F32)
    return total.astype(BF)


def chunk_kernel(scalars, mine_ref, other_ref, *refs, plan):
    groups = []
    for n, members in plan["counts"]:
        groups.append((n, refs[:members]))
        refs = refs[members:]
    prev = None
    if not plan["first"]:
        prev, refs = refs[:2], refs[2:]
    gx_refs, refs = refs[:2], refs[2:]
    n_out = 1 if plan["last"] else len(CHAIN)
    gg_refs, (w_all, x_tile, cot_tile, acc, sems) = refs[:n_out], refs[n_out:]
    step = pl.program_id(0)
    width, wide = w_all.shape
    ck = wide // 2
    blk = width // DEVS
    crew = len(CREW)
    half = width // 2
    rows = TILE // 2
    core = scalars[DEVS]

    def block_rows(j):
        return pl.ds(pl.multiple_of(scalars[j] * blk, blk), blk)

    inner = scalars[DEVS + 1]

    def weight_copies(act):
        base = 0
        for n, members in groups:
            for c, member in enumerate(members):
                for i in range(n // blk):
                    j = min(c, len(CHAIN) - 1) * crew + base + i
                    copy = pltpu.make_async_copy(
                        member.at[pl.ds(i * blk, blk), :], w_all.at[block_rows(j), :], sems.at[j]
                    )
                    if len(members) > len(CHAIN) and c >= len(CHAIN) - 1:
                        pl.when(inner == (1 if c == len(CHAIN) - 1 else 0))(
                            lambda copy=copy: act(copy)
                        )
                    else:
                        act(copy)
            base += n // blk

    @pl.when(step == 0)
    def _():
        weight_copies(lambda copy: copy.start())

    lower = pl.ds(pl.multiple_of(core * rows, rows), rows)
    upper = pl.ds(pl.multiple_of((1 - core) * rows, rows), rows)
    x_tile[lower, :] = mine_ref[0, :, :width]
    x_tile[upper, :] = other_ref[0]
    for i in range(2):
        at_col = plan["cot"] + i * plan["quarter"] + plan["offset"]
        cot_tile[i * rows : (i + 1) * rows, :] = mine_ref[0, :, at_col : at_col + ck]

    @pl.when(step == 0)
    def _():
        weight_copies(lambda copy: copy.wait())

    x = x_tile[...]
    both = jnp.dot(x, w_all[...], preferred_element_type=F32)
    gate, up = both[:, :ck], both[:, ck:]
    cot = cot_tile[...].astype(F32)
    sig = jax.nn.sigmoid(gate)
    d_gate = (cot * up * sig * (1.0 + gate * (1.0 - sig))).astype(BF)
    d_up = (cot * gate * sig).astype(BF)
    gg = contract_first(x, d_gate)

    @pl.when(step == 0)
    def _():
        acc[...] = gg

    @pl.when(step > 0)
    def _():
        acc[...] += gg

    gx = contract_last(jnp.concatenate([d_gate, d_up], axis=1), w_all[...])
    low, high = gx[:, :half], gx[:, half:]
    for keep in range(2):

        @pl.when(core == keep)
        def _():
            for ref, value, i in ((gx_refs[0], (low, high)[keep], 0), (gx_refs[1], (high, low)[keep], 1)):
                ref[...] = (value if prev is None else value + prev[i][...].astype(F32)).astype(BF)

    @pl.when(step == pl.num_programs(0) - 1)
    def _():
        for j in range(DEVS):
            if plan["last"]:
                gg_refs[0][j] = acc[j * blk : (j + 1) * blk, :].astype(BF)
            else:
                row = (j % crew) * blk
                at_row = pl.multiple_of(scalars[2 * DEVS + j] * blk, blk)
                gg_refs[j // crew][row : row + blk, :] = acc[pl.ds(at_row, blk), :].astype(BF)


def chunk_call(scalars, mine, other, groups, prev, ck, **plan):
    width = other.shape[2]
    rows = len(CREW) * TILE
    half = width // 2
    plan["counts"] = [(g[0].shape[0], len(g)) for g in groups]
    plan["first"] = prev is None
    flat = [v for g in groups for v in g]
    blk = width // DEVS
    deep = blk * len(CREW)
    gx_spec = pl.BlockSpec((TILE, half), lambda i, o: (i, 0))
    if plan["last"]:
        gg_specs = [pl.BlockSpec((DEVS, blk, ck), lambda i, o: (0, 0, 0))]
        gg_shapes = [jax.ShapeDtypeStruct((DEVS, blk, ck), BF)]
    else:
        gg_specs = [pl.BlockSpec((deep, ck), lambda i, o: (0, 0))] * len(CHAIN)
        gg_shapes = [jax.ShapeDtypeStruct((deep, ck), BF)] * len(CHAIN)
    outs = pl.pallas_call(
        lambda *a: chunk_kernel(*a, plan=plan),
        grid_spec=pltpu.PrefetchScalarGridSpec(
            num_scalar_prefetch=1,
            grid=(len(CREW),),
            in_specs=[
                pl.BlockSpec((1,) + mine.shape[1:], lambda i, o: (i, 0, 0)),
                pl.BlockSpec((1,) + other.shape[1:], lambda i, o: (i, 0, 0)),
            ]
            + [pl.BlockSpec(memory_space=pl.ANY)] * len(flat)
            + ([] if prev is None else [gx_spec] * 2),
            out_specs=[gx_spec] * 2 + gg_specs,
            scratch_shapes=[
                pltpu.VMEM((width, 2 * ck), BF),
                pltpu.VMEM((TILE, width), BF),
                pltpu.VMEM((TILE, ck), BF),
                pltpu.VMEM((width, ck), F32),
                pltpu.SemaphoreType.DMA((DEVS,)),
            ],
        ),
        out_shape=[jax.ShapeDtypeStruct((rows, half), BF)] * 2 + gg_shapes,
        compiler_params=pltpu.CompilerParams(vmem_limit_bytes=48 * 1024 * 1024),
        cost_estimate=pl.CostEstimate(
            flops=10 * rows * width * ck, bytes_accessed=2**24, transcendentals=rows * ck
        ),
        name="swiglu_chunk",
    )(scalars, mine, other, *flat, *([] if prev is None else prev))
    return outs[:2], outs[2:]


def join_kernel(scalars, *refs, split, quarter):
    out = refs[-1]
    firsts, last = refs[: len(CREW)], refs[len(CREW)]
    for s in range(len(CREW)):
        start = scalars[DEVS + 2 + s] * quarter
        spot = pl.ds(pl.multiple_of(start, 128), split)
        out[:, spot] = firsts[s][...].astype(F32)
    for q in range(len(CREW)):
        total = None
        for m in CHAIN:
            term = last[q ^ m].astype(F32)
            total = term if total is None else total + term
        out[:, q * quarter + split : (q + 1) * quarter] = total


def join_call(scalars, firsts, last, split, quarter):
    depth = last.shape[1]
    vmem = pl.BlockSpec(memory_space=pltpu.VMEM)
    return pl.pallas_call(
        lambda *a: join_kernel(*a, split=split, quarter=quarter),
        in_specs=[pl.BlockSpec(memory_space=pltpu.SMEM)] + [vmem] * (len(CREW) + 1),
        out_specs=vmem,
        out_shape=jax.ShapeDtypeStruct((depth, len(CREW) * quarter), F32),
        compiler_params=pltpu.CompilerParams(vmem_limit_bytes=16 * 1024 * 1024),
        name="join_chunks",
    )(scalars, *firsts, last)


def split_plan(x_in, cotangent, w_gate, w_up, send_counts, recv_counts):
    rows, width = x_in.shape
    depth, hidden = w_gate.shape
    crew = len(CREW)
    quarter = hidden // crew
    core = lax.axis_index("mp")
    index = lax.axis_index("dp")
    z, place = index // crew, index % crew
    places = [place ^ m for m in CREW]
    chunks = [640, 256]
    offsets = [0, chunks[0]]
    swap = [(0, 1), (1, 0)]

    def columns(array, q, offset, count):
        return lax.dynamic_slice_in_dim(array, q * quarter + offset, count, 1)

    def piece_of_weights(q, k):
        return jnp.concatenate(
            [columns(w, q, offsets[k], chunks[k]) for w in (w_gate, w_up)], axis=1
        )

    order = [z, z ^ 1, jnp.where(z < 2, 2, 1), jnp.where(z < 2, 3, 0)]
    inner = ((z == 1) | (z == 2)).astype(jnp.int32)
    scalars = [index ^ c ^ m for c in CHAIN for m in CREW] + [core, inner] + places
    scalars += [0] * (2 * DEVS - len(scalars)) + [p * crew + q for p in order for q in places]
    scalars = jnp.stack([jnp.asarray(v, jnp.int32) for v in scalars])

    first = [piece_of_weights(q, 0) for q in places]
    own = first[0]
    own_far = send(own, FAR)
    own_near = send(own, NEAR)
    rest = crew_swap(first)[1:]
    own_far, own_near, x_in, cotangent, w_gate, w_up, *rest = tie(
        own_far, own_near, x_in, cotangent, w_gate, w_up, *rest
    )

    rest = jnp.concatenate(rest, axis=0)
    own_both = send(own_far, NEAR)
    rest_far = send(rest, FAR)
    rest_near = send(rest, NEAR)
    live = jnp.arange(rows) < live_rows_of(send_counts, recv_counts)
    cotangent = jnp.where(live[:, None], cotangent, jnp.zeros((), BF))
    x_half = lax.dynamic_slice_in_dim(x_in, core * (rows // 2), rows // 2, 0)
    parcels = []
    for q in places:
        cot = columns(cotangent, q, 0, quarter)
        parcels.append(
            jnp.concatenate(
                [x_half, cot[: rows // 2], cot[rows // 2 :], piece_of_weights(q, 1)], axis=1
            )
        )
    parcels = crew_swap(parcels)
    rest_far, rest_near, own_both, *parcels = tie(rest_far, rest_near, own_both, *parcels)

    rest_both = send(rest_far, NEAR)
    mine = jnp.stack(parcels)
    other = lax.ppermute(mine[:, :, :width], "mp", swap)
    second = mine[:, :, width + 2 * quarter :].reshape(crew * depth, 2 * chunks[1])
    rest_both, other, second = tie(rest_both, other, second)

    common = dict(cot=width, quarter=quarter)
    second_near = send(second, NEAR)
    second_far = send(second, FAR)
    gx, parts = chunk_call(
        scalars, mine, other,
        [(own, own_near, own_far, own_both), (rest, rest_near, rest_far, rest_both)],
        None, chunks[0], offset=0, last=False, **common,
    )
    second_near, second_far, *values = tie(second_near, second_far, *gx, *parts)
    gx, (p0, p1, p2, p3) = values[:2], values[2:]

    middle = along(second, INNER)
    ends = along(second_far, TO_ENDS)
    r1 = along(p3, FROM_ENDS)
    r1, middle, ends, p2, p3 = tie(r1, middle, ends, p2, p3)
    r2b = along(p2, FROM_ENDS)
    r2a = along(add(p3, r1), INNER)
    (keep, give), (lasts,) = chunk_call(
        scalars, mine, other, [(second, second_near, second_far, middle, ends)], gx, chunks[1],
        offset=offsets[1], last=True, **common,
    )
    r2a, r2b, keep, give, lasts = tie(r2a, r2b, keep, give, lasts)

    lasts = lax.all_to_all(lasts, "dp", split_axis=0, concat_axis=0, tiled=True)
    theirs = lax.ppermute(give, "mp", swap)
    r3b = along(add(p2, r2b), INNER)
    r3a = along(add(p1, r2a), OUTER)
    rows_x = crew_swap(
        [
            add(keep[s * rows : (s + 1) * rows], theirs[s * rows : (s + 1) * rows])
            for s in range(crew)
        ]
    )
    r3a, r3b, *rows_x = tie(r3a, r3b, *rows_x)

    sums = add(p0, r3a, r3b)
    firsts = crew_swap([sums[s * depth : (s + 1) * depth] for s in range(crew)])
    grad_gate = join_call(scalars, firsts, lasts, chunks[0], quarter)
    return add(*rows_x), grad_gate


def solution(mesh):
    sizes = dict(mesh.shape)
    splits = sizes["dp"] == DEVS and sizes["mp"] == 2
    return jax.shard_map(
        split_plan if splits else general_plan,
        mesh=mesh,
        in_specs=(
            P("dp", None),
            P("dp", "mp"),
            P("dp", "mp"),
            P("dp", "mp"),
            P("dp", None),
            P("dp", None),
        ),
        out_specs=(P("dp", "mp"), P("dp", "mp")),
        check_vma=False,
    )
```

time: 250 us -> 242 us (0.968)
  starting transfers between devices: 58 us -> 43.3 us
  waiting for transfers between devices: 121 us -> 126 us
    ppermute x33 -> x29, starting transfers between devices: 54.1 us -> 39.6 us  [the longest x20 22.7 us: send(): return lax.ppermute(value, 'dp', [(i, i ^ mask) for i in range(DEVS)])]
    ppermute x33 -> x29, waiting for transfers between devices: 121 us -> 126 us  [the longest x20 92.2 us: send(): return lax.ppermute(value, 'dp', [(i, i ^ mask) for i in range(DEVS)])]
    unnamed x62 -> x44, local copies, waits for them, and re-layouts: 8.99 us -> 11 us
  transfers between devices with their start and end apart: 34 -> 30, of which waited for: 13 -> 12; matrix products, arithmetic and copies ran while one was open for 5% -> 4% of each run, Pallas kernels for 17% -> 18%
where the time goes in v3:
time: 242 us
  waiting for transfers between devices  126 us (52%)
  Pallas kernels  45.3 us (19%)
  starting transfers between devices  43.3 us (18%)
  local copies, waits for them, and re-layouts  16.4 us (7%)
  other arithmetic  7.93 us (3%)
    ppermute x20, waiting for transfers between devices, send(): return lax.ppermute(value, 'dp', [(i, i ^ mask) for i in range(DEVS)])  92.2 us
    pallas_call x2, Pallas kernels, chunk_call(): pl.pallas_call(lambda *a: chunk_kernel(*a, plan=plan), grid_spec=pltpu.Pr...  43.4 us
    ppermute x7, waiting for transfers between devices, along(): lax.ppermute(value, 'dp', [(crew * a + q, crew * b + q) for a, b in moves...  34.2 us
    ppermute x20, starting transfers between devices, send(): return lax.ppermute(value, 'dp', [(i, i ^ mask) for i in range(DEVS)])  22.7 us
    ppermute x7, starting transfers between devices, along(): lax.ppermute(value, 'dp', [(crew * a + q, crew * b + q) for a, b in moves...  16.9 us
    unnamed x44, local copies, waits for them, and re-layouts  11 us
    convert_element_type x6, other arithmetic, add(): return total.astype(BF)  5.72 us
  transfers between devices with their start and end apart: 30, of which 12 were waited for; matrix products, arithmetic and copies ran while one was open for 4% of the time, Pallas kernels for 18%

profile of v3, /device:TPU:0, one launch (start us, length us, event | category | flops | bytes accessed | tf_op | source)
XLA Modules:
  0.0 241.7 jit_solution(4556168615425866508)
XLA Ops:
  0.7 1.5 constant_dynamic-slice_fusion
  2.3 3.1 %collective-permute-start.1 = (bf16[128,1280]{1,0:T(8,128)(2,1)S(1)}, bf16[128,1280]{1,0:T(8,128)(2,1)S(1)}, u32[]{:S(2)}, u32[]{:S(2)}) collective-permute-start(bf16[128,1280]{1,0:T(8,128)(2,1)S(1)} %pad_maximum_fusion.1.a_3_), channel_id=1, source_target_pairs={{0,8},{2,10},{4,12},{6,14},{8,0},{10,2},{12,4},{14,6},{16,24},{18,... | collective-permute-start | bytes 983048 | tf_op jit(solution)/shard_map/ppermute | solution.py:73
  5.4 2.6 %collective-permute-start = (bf16[128,1280]{1,0:T(8,128)(2,1)S(1)}, bf16[128,1280]{1,0:T(8,128)(2,1)S(1)}, u32[]{:S(2)}, u32[]{:S(2)}) collective-permute-start(bf16[128,1280]{1,0:T(8,128)(2,1)S(1)} %pad_maximum_fusion.1.a_3_), channel_id=1, source_target_pairs={{0,16},{2,18},{4,20},{6,22},{8,24},{10,26},{12,28},{14,30},{16,0},... | collective-permute-start | bytes 983048 | tf_op jit(solution)/shard_map/ppermute | solution.py:73
  8.0 1.6 collective-permute-start.2
  9.6 1.6 collective-permute-start.3
  11.2 0.5 collective-permute-start.4
  11.7 0.7 reduce_sum.19
  12.4 0.6 reduce_sum.18
  14.3 4.4 %collective-permute-done.2 = bf16[128,1280]{1,0:T(8,128)(2,1)S(1)} collective-permute-done((bf16[128,1280]{1,0:T(8,128)(2,1)S(1)}, bf16[128,1280]{1,0:T(8,128)(2,1)S(1)}, u32[]{:S(2)}, u32[]{:S(2)}) %collective-permute-start.2) | collective-permute-done | bytes 327712 | tf_op jit(solution)/shard_map/ppermute | solution.py:73
  18.7 6.6 %collective-permute-done.3 = bf16[128,1280]{1,0:T(8,128)(2,1)S(1)} collective-permute-done((bf16[128,1280]{1,0:T(8,128)(2,1)S(1)}, bf16[128,1280]{1,0:T(8,128)(2,1)S(1)}, u32[]{:S(2)}, u32[]{:S(2)}) %collective-permute-start.3) | collective-permute-done | bytes 327712 | tf_op jit(solution)/shard_map/ppermute | solution.py:73
  25.3 1.1 dynamic-slice_dynamic-update-slice_fusion.3
  26.5 0.9 copy-done.6
  27.4 0.4 collective-permute-start.7
  27.8 1.0 copy-done.11
  29.1 1.0 copy-done.9
  30.1 0.3 copy-done.8
  30.5 0.5 copy-done.7
  31.2 1.0 dynamic-slice_dynamic-update-slice_fusion.13
  32.2 1.0 dynamic-slice_dynamic-update-slice_fusion.12
  33.1 1.6 collective-permute-start.10
  34.7 1.1 collective-permute-start.9
  35.8 0.9 collective-permute-start.8
  36.7 0.6 collective-permute-start.6
  37.4 0.3 collective-permute-start.5
  37.7 39.8 %collective-permute-done.6.a_8_ = bf16[384,1280]{1,0:T(8,128)(2,1)S(1)} collective-permute-done((bf16[384,1280]{1,0:T(8,128)(2,1)S(1)}, bf16[384,1280]{1,0:T(8,128)(2,1)S(1)}, u32[]{:S(2)}, u32[]{:S(2)}) %collective-permute-start.6) | collective-permute-done | bytes 983072 | tf_op jit(solution)/shard_map/ppermute | solution.py:73
  77.5 2.5 %collective-permute-done.5.a_9_ = bf16[384,1280]{1,0:T(8,128)(2,1)} collective-permute-done((bf16[384,1280]{1,0:T(8,128)(2,1)S(1)}, bf16[384,1280]{1,0:T(8,128)(2,1)}, u32[]{:S(2)}, u32[]{:S(2)}) %collective-permute-start.5) | collective-permute-done | bytes 983072 | tf_op jit(solution)/shard_map/ppermute | solution.py:73
  79.9 2.5 %collective-permute-done.9 = bf16[128,4352]{1,0:T(8,128)(2,1)S(1)} collective-permute-done((bf16[128,4352]{1,0:T(8,128)(2,1)S(1)}, bf16[128,4352]{1,0:T(8,128)(2,1)S(1)}, u32[]{:S(2)}, u32[]{:S(2)}) %collective-permute-start.9) | collective-permute-done | bytes 1114144 | tf_op jit(solution)/shard_map/ppermute | solution.py:73
  82.5 0.6 pad_maximum_fusion.a_1_
  83.1 2.1 copy-done.10
  85.1 1.7 slice.88
  86.8 0.4 collective-permute-start.11
  87.4 1.1 slice.89
  88.5 22.8 %collective-permute-done.11.a_10_ = bf16[384,1280]{1,0:T(8,128)(2,1)} collective-permute-done((bf16[384,1280]{1,0:T(8,128)(2,1)}, bf16[384,1280]{1,0:T(8,128)(2,1)}, u32[]{:S(2)}, u32[]{:S(2)}) %collective-permute-start.11) | collective-permute-done | bytes 983072 | tf_op jit(solution)/shard_map/ppermute | solution.py:73
  111.3 0.3 collective-permute-start.14
  111.6 0.4 collective-permute-start.13
  112.1 25.0 %swiglu_chunk.2 = (bf16[1024,1024]{1,0:T(8,128)(2,1)}, bf16[1024,1024]{1,0:T(8,128)(2,1)}, bf16[512,640]{1,0:T(8,128)(2,1)S(1)}, bf16[512,640]{1,0:T(8,128)(2,1)...) custom-call(s32[48]{0:T(128)S(1)} %stack.179.a_0_, bf16[4,128,4352]{2,1,0:T(8,128)(2,1)} %copy-done.10, ...), custom_call_target="tpu_custom_call" | custom-call | flops 13421772800 | bytes 16777216 | tf_op jit(solution)/shard_map/swiglu_chunk/pallas_call | solution.py:211
  137.2 3.5 %collective-permute-start.15 = (bf16[512,640]{1,0:T(8,128)(2,1)S(1)}, bf16[512,640]{1,0:T(8,128)(2,1)S(1)}, u32[]{:S(2)}, u32[]{:S(2)}) collective-permute-start(bf16[512,640]{1,0:T(8,128)(2,1)S(1)} %get-tuple-element.83), channel_id=1, source_target_pairs={{0,8},{2,10},{4,12},{6,14},{24,16},{26,18},{28,20},{30,22},{1,9},{... | collective-permute-start | bytes 1966088 | tf_op jit(solution)/shard_map/ppermute | solution.py:78
  140.7 0.7 collective-permute-start.16
  141.4 1.3 collective-permute-start.17
  142.7 13.3 %collective-permute-done.17.a_7_ = bf16[512,512]{1,0:T(8,128)(2,1)S(1)} collective-permute-done((bf16[512,512]{1,0:T(8,128)(2,1)S(1)}, bf16[512,512]{1,0:T(8,128)(2,1)S(1)}, u32[]{:S(2)}, u32[]{:S(2)}) %collective-permute-start.17) | collective-permute-done | bytes 524320 | tf_op jit(solution)/shard_map/ppermute | solution.py:78
  156.1 0.7 collective-permute-start.18
  156.9 5.3 %collective-permute-start.19 = (bf16[512,640]{1,0:T(8,128)(2,1)S(1)}, bf16[512,640]{1,0:T(8,128)(2,1)S(1)}, u32[]{:S(2)}, u32[]{:S(2)}) collective-permute-start(bf16[512,640]{1,0:T(8,128)(2,1)S(1)} %get-tuple-element.85), channel_id=1, source_target_pairs={{0,8},{2,10},{4,12},{6,14},{24,16},{26,18},{28,20},{30,22},{1,9},{... | collective-permute-start | bytes 1966088 | tf_op jit(solution)/shard_map/ppermute | solution.py:78
  162.2 18.3 %swiglu_chunk.3 = (bf16[1024,1024]{1,0:T(8,128)(2,1)S(1)}, bf16[1024,1024]{1,0:T(8,128)(2,1)}, bf16[16,128,256]{2,1,0:T(8,128)(2,1)S(1)}) custom-call(s32[48]{0:T(128)S(1)} %stack.179.a_0_, bf16[4,128,4352]{2,1,0:T(8,128)(2,1)} %copy-done.10, bf16[4,128,2048]{2,1,0:T(8,128)(2,1)} %collective-permute-done.12.a_2_, bf16[512,512]{1,0:T(8,128)(2,1)S(1)} %bitcast.46, ...), custom_call_target="tpu_custom_call" | custom-call | flops 5368709120 | bytes 16777216 | tf_op jit(solution)/shard_map/swiglu_chunk/pallas_call | solution.py:211
  180.6 1.0 copy-done
  181.6 0.8 copy-done.12
  182.4 0.9 copy-done.14
  183.2 3.7 %all-to-all-start = ((bf16[16,128,256]{2,1,0:T(8,128)(2,1)}), bf16[16,128,256]{2,1,0:T(8,128)(2,1)S(1)}, u32[]{:S(2)}, u32[]{:S(2)}) async-start(bf16[16,128,256]{2,1,0:T(8,128)(2,1)} %copy-done), calls=%async_computation | async-start | bytes 2097152 | tf_op jit(solution)/shard_map/all_to_all | solution.py:352
  186.9 1.5 add_convert_fusion.1
  188.5 0.7 collective-permute-start.21
  189.4 4.6 %collective-permute-start.20 = (bf16[512,640]{1,0:T(8,128)(2,1)S(1)}, bf16[512,640]{1,0:T(8,128)(2,1)S(1)}, u32[]{:S(2)}, u32[]{:S(2)}) collective-permute-start(bf16[512,640]{1,0:T(8,128)(2,1)S(1)} %add_convert_fusion.2), channel_id=1, source_target_pairs={{0,8},{2,10},{4,12},{6,14},{8,0},{10,2},{12,4},{14,6},{16,24},{18,... | collective-permute-start | bytes 1966088 | tf_op jit(solution)/shard_map/ppermute | solution.py:78
  194.0 2.5 %add_convert_fusion.5 = (bf16[256,1024]{1,0:T(8,128)(2,1)S(1)}, bf16[256,1024]{1,0:T(8,128)(2,1)S(1)}, bf16[256,1024]{1,0:T(8,128)(2,1)S(1)}, bf16[256,1024]{1,0:T(8,128)(2,1)S(1)}) fusion(bf16[1024,1024]{1,0:T(8,128)(2,1)} %collective-permute-done.22, bf16[1024,1024]{1,0:T(8,128)(2,1)S(1)} %get-tuple-element.96), kind=kLoop, calls=%fused_computation.7 | loop fusion | flops 4194304 | bytes 6291456 | tf_op jit(solution)/shard_map/convert_element_type | solution.py:97
  196.5 2.4 %collective-permute-start.25 = (bf16[256,1024]{1,0:T(8,128)(2,1)S(1)}, bf16[256,1024]{1,0:T(8,128)(2,1)S(1)}, u32[]{:S(2)}, u32[]{:S(2)}) collective-permute-start(bf16[256,1024]{1,0:T(8,128)(2,1)S(1)} %get-tuple-element.106), channel_id=1, source_target_pairs={{0,6},{2,4},{4,2},{6,0},{8,14},{10,12},{12,10},{14,8},{16,22},{18,... | collective-permute-start | bytes 1572872 | tf_op jit(solution)/shard_map/ppermute | solution.py:73
  198.9 0.6 collective-permute-start.24
  199.5 0.6 collective-permute-start.23
  200.1 20.9 %collective-permute-done.20 = bf16[512,640]{1,0:T(8,128)(2,1)S(1)} collective-permute-done((bf16[512,640]{1,0:T(8,128)(2,1)S(1)}, bf16[512,640]{1,0:T(8,128)(2,1)S(1)}, u32[]{:S(2)}, u32[]{:S(2)}) %collective-permute-start.20) | collective-permute-done | bytes 655392 | tf_op jit(solution)/shard_map/ppermute | solution.py:78
  221.0 6.0 %collective-permute-done.24 = bf16[256,1024]{1,0:T(8,128)(2,1)S(1)} collective-permute-done((bf16[256,1024]{1,0:T(8,128)(2,1)S(1)}, bf16[256,1024]{1,0:T(8,128)(2,1)S(1)}, u32[]{:S(2)}, u32[]{:S(2)}) %collective-permute-start.24) | collective-permute-done | bytes 524320 | tf_op jit(solution)/shard_map/ppermute | solution.py:73
  226.9 2.7 %collective-permute-done.23 = bf16[256,1024]{1,0:T(8,128)(2,1)S(1)} collective-permute-done((bf16[256,1024]{1,0:T(8,128)(2,1)S(1)}, bf16[256,1024]{1,0:T(8,128)(2,1)S(1)}, u32[]{:S(2)}, u32[]{:S(2)}) %collective-permute-start.23) | collective-permute-done | bytes 524320 | tf_op jit(solution)/shard_map/ppermute | solution.py:73
  229.9 1.9 collective-permute-start.28
  231.8 0.8 collective-permute-start.27
  232.6 0.8 collective-permute-start.26
  233.5 1.2 add_convert_fusion.4
  234.6 3.0 %collective-permute-done.28.a_4_ = bf16[128,640]{1,0:T(8,128)(2,1)S(1)} collective-permute-done((bf16[128,640]{1,0:T(8,128)(2,1)S(1)}, bf16[128,640]{1,0:T(8,128)(2,1)S(1)}, u32[]{:S(2)}, u32[]{:S(2)}) %collective-permute-start.28) | collective-permute-done | bytes 163872 | tf_op jit(solution)/shard_map/ppermute | solution.py:73
  237.6 2.1 collective-permute-done.27.a_3_
  239.7 2.0 join_chunks.1
  (67 shorter events, 1.6 us)
Async XLA Ops:
  2.2 9.5 %copy-start.15 = (s32[1,16]{1,0:T(1,128)S(1)}, s32[1,16]{1,0:T(1,128)}, u32[]{:S(2)}) copy-start(s32[1,16]{1,0:T(1,128)} %param.11) | copy-start | bytes 196
  2.3 10.2 %copy-start.16 = (s32[1,16]{1,0:T(1,128)S(1)}, s32[1,16]{1,0:T(1,128)}, u32[]{:S(2)}) copy-start(s32[1,16]{1,0:T(1,128)} %param.10) | copy-start | bytes 196
  2.3 23.0 %collective-permute-start.1 = (bf16[128,1280]{1,0:T(8,128)(2,1)S(1)}, bf16[128,1280]{1,0:T(8,128)(2,1)S(1)}, u32[]{:S(2)}, u32[]{:S(2)}) collective-permute-start(bf16[128,1280]{1,0:T(8,128)(2,1)S(1)} %pad_maximum_fusion.1.a_3_), channel_id=1, source_target_pairs={{0,8},{2,10},{4,12},{6,14},{8,0},{10,2},{12,4},{14,6},{16,24},{18,... | collective-permute-start | bytes 983048 | tf_op jit(solution)/shard_map/ppermute | solution.py:73
  5.4 19.9 %collective-permute-start = (bf16[128,1280]{1,0:T(8,128)(2,1)S(1)}, bf16[128,1280]{1,0:T(8,128)(2,1)S(1)}, u32[]{:S(2)}, u32[]{:S(2)}) collective-permute-start(bf16[128,1280]{1,0:T(8,128)(2,1)S(1)} %pad_maximum_fusion.1.a_3_), channel_id=1, source_target_pairs={{0,16},{2,18},{4,20},{6,22},{8,24},{10,26},{12,28},{14,30},{16,0},... | collective-permute-start | bytes 983048 | tf_op jit(solution)/shard_map/ppermute | solution.py:73
  8.0 10.7 %collective-permute-start.2 = (bf16[128,1280]{1,0:T(8,128)(2,1)S(1)}, bf16[128,1280]{1,0:T(8,128)(2,1)S(1)}, u32[]{:S(2)}, u32[]{:S(2)}) collective-permute-start(bf16[128,1280]{1,0:T(8,128)(2,1)S(1)} %pad_maximum_fusion.2), channel_id=1, source_target_pairs={{0,2},{2,0},{4,6},{6,4},{8,10},{10,8},{12,14},{14,12},{16,18},{18,... | collective-permute-start | bytes 983048 | tf_op jit(solution)/shard_map/ppermute | solution.py:73
  9.6 15.7 %collective-permute-start.3 = (bf16[128,1280]{1,0:T(8,128)(2,1)S(1)}, bf16[128,1280]{1,0:T(8,128)(2,1)S(1)}, u32[]{:S(2)}, u32[]{:S(2)}) collective-permute-start(bf16[128,1280]{1,0:T(8,128)(2,1)S(1)} %pad_maximum_fusion.3), channel_id=1, source_target_pairs={{0,4},{2,6},{4,0},{6,2},{8,12},{10,14},{12,8},{14,10},{16,20},{18,... | collective-permute-start | bytes 983048 | tf_op jit(solution)/shard_map/ppermute | solution.py:73
  11.2 14.1 %collective-permute-start.4 = (bf16[128,1280]{1,0:T(8,128)(2,1)S(1)}, bf16[128,1280]{1,0:T(8,128)(2,1)S(1)}, u32[]{:S(2)}, u32[]{:S(2)}) collective-permute-start(bf16[128,1280]{1,0:T(8,128)(2,1)S(1)} %pad_maximum_fusion.4), channel_id=1, source_target_pairs={{0,6},{2,4},{4,2},{6,0},{8,14},{10,12},{12,10},{14,8},{16,22},{18,... | collective-permute-start | bytes 983048 | tf_op jit(solution)/shard_map/ppermute | solution.py:73
  26.4 1.0 copy-start.6
  27.4 1.5 copy-start.11
  27.4 10.0 %collective-permute-start.7 = (bf16[128,1280]{1,0:T(8,128)(2,1)S(1)}, bf16[128,1280]{1,0:T(8,128)(2,1)S(1)}, u32[]{:S(2)}, u32[]{:S(2)}) collective-permute-start(bf16[128,1280]{1,0:T(8,128)(2,1)S(1)} %collective-permute-done.a_5_), channel_id=1, source_target_pairs={{0,8},{2,10},{4,12},{6,14},{8,0},{10,2},{12,4},{14,6},{16,24},{18,... | collective-permute-start | bytes 983048 | tf_op jit(solution)/shard_map/ppermute | solution.py:73
  28.9 1.2 copy-start.9
  28.9 1.6 copy-start.8
  28.9 2.1 copy-start.7
  33.1 46.8 %collective-permute-start.10 = (bf16[128,4352]{1,0:T(8,128)(2,1)S(1)}, bf16[128,4352]{1,0:T(8,128)(2,1)S(1)}, u32[]{:S(2)}, u32[]{:S(2)}) collective-permute-start(bf16[128,4352]{1,0:T(8,128)(2,1)S(1)} %get-tuple-element.114), channel_id=1, source_target_pairs={{0,6},{2,4},{4,2},{6,0},{8,14},{10,12},{12,10},{14,8},{16,22},{18,... | collective-permute-start | bytes 3342344 | tf_op jit(solution)/shard_map/ppermute | solution.py:73
  34.7 47.8 %collective-permute-start.9 = (bf16[128,4352]{1,0:T(8,128)(2,1)S(1)}, bf16[128,4352]{1,0:T(8,128)(2,1)S(1)}, u32[]{:S(2)}, u32[]{:S(2)}) collective-permute-start(bf16[128,4352]{1,0:T(8,128)(2,1)S(1)} %get-tuple-element.115), channel_id=1, source_target_pairs={{0,4},{2,6},{4,0},{6,2},{8,12},{10,14},{12,8},{14,10},{16,20},{18,... | collective-permute-start | bytes 3342344 | tf_op jit(solution)/shard_map/ppermute | solution.py:73
  35.8 46.7 %collective-permute-start.8 = (bf16[128,4352]{1,0:T(8,128)(2,1)S(1)}, bf16[128,4352]{1,0:T(8,128)(2,1)S(1)}, u32[]{:S(2)}, u32[]{:S(2)}) collective-permute-start(bf16[128,4352]{1,0:T(8,128)(2,1)S(1)} %get-tuple-element.116), channel_id=1, source_target_pairs={{0,2},{2,0},{4,6},{6,4},{8,10},{10,8},{12,14},{14,12},{16,18},{18,... | collective-permute-start | bytes 3342344 | tf_op jit(solution)/shard_map/ppermute | solution.py:73
  36.7 40.7 %collective-permute-start.6 = (bf16[384,1280]{1,0:T(8,128)(2,1)S(1)}, bf16[384,1280]{1,0:T(8,128)(2,1)S(1)}, u32[]{:S(2)}, u32[]{:S(2)}) collective-permute-start(bf16[384,1280]{1,0:T(8,128)(2,1)S(1)} %constant_dynamic-update-slice_fusion.a_7_), channel_id=1, source_target_pairs={{0,8},{2,10},{4,12},{6,14},{8,0},{10,2},{12,4},{14,6},{16,24},{18,... | collective-permute-start | bytes 2949128 | tf_op jit(solution)/shard_map/ppermute | solution.py:73
  37.4 42.6 %collective-permute-start.5 = (bf16[384,1280]{1,0:T(8,128)(2,1)S(1)}, bf16[384,1280]{1,0:T(8,128)(2,1)}, u32[]{:S(2)}, u32[]{:S(2)}) collective-permute-start(bf16[384,1280]{1,0:T(8,128)(2,1)S(1)} %constant_dynamic-update-slice_fusion.a_7_), channel_id=1, source_target_pairs={{0,16},{2,18},{4,20},{6,22},{8,24},{10,26},{12,28},{14,30},{16,0},... | collective-permute-start | bytes 2949128 | tf_op jit(solution)/shard_map/ppermute | solution.py:73
  83.1 2.1 copy-start.10
  86.8 24.5 %collective-permute-start.12 = (bf16[4,128,2048]{2,1,0:T(8,128)(2,1)}, bf16[4,128,2048]{2,1,0:T(8,128)(2,1)}, u32[]{:S(2)}, u32[]{:S(2)}) collective-permute-start(bf16[4,128,2048]{2,1,0:T(8,128)(2,1)} %slice.88), channel_id=1, source_target_pairs={{0,1},{1,0},{2,3},{3,2},{4,5},{5,4},{6,7},{7,6},{8,9},{9,8},{10,11... | collective-permute-start | bytes 6291464 | tf_op jit(solution)/shard_map/ppermute | solution.py:325
  86.8 24.5 %collective-permute-start.11 = (bf16[384,1280]{1,0:T(8,128)(2,1)}, bf16[384,1280]{1,0:T(8,128)(2,1)}, u32[]{:S(2)}, u32[]{:S(2)}) collective-permute-start(bf16[384,1280]{1,0:T(8,128)(2,1)} %collective-permute-done.5.a_9_), channel_id=1, source_target_pairs={{0,8},{2,10},{4,12},{6,14},{8,0},{10,2},{12,4},{14,6},{16,24},{18,... | collective-permute-start | bytes 2949128 | tf_op jit(solution)/shard_map/ppermute | solution.py:73
  111.3 25.9 %collective-permute-start.14 = (bf16[512,512]{1,0:T(8,128)(2,1)S(1)}, bf16[512,512]{1,0:T(8,128)(2,1)S(1)}, u32[]{:S(2)}, u32[]{:S(2)}) collective-permute-start(bf16[512,512]{1,0:T(8,128)(2,1)S(1)} %bitcast.43), channel_id=1, source_target_pairs={{0,16},{2,18},{4,20},{6,22},{8,24},{10,26},{12,28},{14,30},{16,0},... | collective-permute-start | bytes 1572872 | tf_op jit(solution)/shard_map/ppermute | solution.py:73
  111.6 25.5 %collective-permute-start.13 = (bf16[512,512]{1,0:T(8,128)(2,1)S(1)}, bf16[512,512]{1,0:T(8,128)(2,1)S(1)}, u32[]{:S(2)}, u32[]{:S(2)}) collective-permute-start(bf16[512,512]{1,0:T(8,128)(2,1)S(1)} %bitcast.44), channel_id=1, source_target_pairs={{0,8},{2,10},{4,12},{6,14},{8,0},{10,2},{12,4},{14,6},{16,24},{18,... | collective-permute-start | bytes 1572872 | tf_op jit(solution)/shard_map/ppermute | solution.py:73
  137.1 19.8 %copy-start.1 = (bf16[512,640]{1,0:T(8,128)(2,1)}, bf16[512,640]{1,0:T(8,128)(2,1)S(1)}, u32[]{:S(2)}) copy-start(bf16[512,640]{1,0:T(8,128)(2,1)S(1)} %get-tuple-element.102) | copy-start | bytes 1966084
  137.1 19.8 %copy-start.3 = (bf16[512,640]{1,0:T(8,128)(2,1)}, bf16[512,640]{1,0:T(8,128)(2,1)S(1)}, u32[]{:S(2)}) copy-start(bf16[512,640]{1,0:T(8,128)(2,1)S(1)} %get-tuple-element.79) | copy-start | bytes 1966084
  137.1 43.4 %copy-start.5 = (bf16[512,640]{1,0:T(8,128)(2,1)}, bf16[512,640]{1,0:T(8,128)(2,1)S(1)}, u32[]{:S(2)}) copy-start(bf16[512,640]{1,0:T(8,128)(2,1)S(1)} %get-tuple-element.85) | copy-start | bytes 1966084
  137.2 18.8 %collective-permute-start.15 = (bf16[512,640]{1,0:T(8,128)(2,1)S(1)}, bf16[512,640]{1,0:T(8,128)(2,1)S(1)}, u32[]{:S(2)}, u32[]{:S(2)}) collective-permute-start(bf16[512,640]{1,0:T(8,128)(2,1)S(1)} %get-tuple-element.83), channel_id=1, source_target_pairs={{0,8},{2,10},{4,12},{6,14},{24,16},{26,18},{28,20},{30,22},{1,9},{... | collective-permute-start | bytes 1966088 | tf_op jit(solution)/shard_map/ppermute | solution.py:78
  140.7 2.0 collective-permute-start.16
  141.4 14.6 %collective-permute-start.17 = (bf16[512,512]{1,0:T(8,128)(2,1)S(1)}, bf16[512,512]{1,0:T(8,128)(2,1)S(1)}, u32[]{:S(2)}, u32[]{:S(2)}) collective-permute-start(bf16[512,512]{1,0:T(8,128)(2,1)S(1)} %collective-permute-done.14.a_5_), channel_id=1, source_target_pairs={{8,0},{10,2},{12,4},{14,6},{16,24},{18,26},{20,28},{22,30},{9,1},{... | collective-permute-start | bytes 1572872 | tf_op jit(solution)/shard_map/ppermute | solution.py:78
  156.1 25.4 %collective-permute-start.18 = (bf16[512,640]{1,0:T(8,128)(2,1)S(1)}, bf16[512,640]{1,0:T(8,128)(2,1)S(1)}, u32[]{:S(2)}, u32[]{:S(2)}) collective-permute-start(bf16[512,640]{1,0:T(8,128)(2,1)S(1)} %add_convert_fusion.3), channel_id=1, source_target_pairs={{8,16},{10,18},{12,20},{14,22},{16,8},{18,10},{20,12},{22,14},{9,1... | collective-permute-start | bytes 1966088 | tf_op jit(solution)/shard_map/ppermute | solution.py:78
  156.9 24.7 %collective-permute-start.19 = (bf16[512,640]{1,0:T(8,128)(2,1)S(1)}, bf16[512,640]{1,0:T(8,128)(2,1)S(1)}, u32[]{:S(2)}, u32[]{:S(2)}) collective-permute-start(bf16[512,640]{1,0:T(8,128)(2,1)S(1)} %get-tuple-element.85), channel_id=1, source_target_pairs={{0,8},{2,10},{4,12},{6,14},{24,16},{26,18},{28,20},{30,22},{1,9},{... | collective-permute-start | bytes 1966088 | tf_op jit(solution)/shard_map/ppermute | solution.py:78
  180.6 1.0 copy-start
  181.5 0.8 copy-start.12
  182.4 0.9 copy-start.14
  183.2 10.8 %collective-permute-start.22 = (bf16[1024,1024]{1,0:T(8,128)(2,1)}, bf16[1024,1024]{1,0:T(8,128)(2,1)}, u32[]{:S(2)}, u32[]{:S(2)}) collective-permute-start(bf16[1024,1024]{1,0:T(8,128)(2,1)} %get-tuple-element.97), channel_id=1, source_target_pairs={{0,1},{1,0},{2,3},{3,2},{4,5},{5,4},{6,7},{7,6},{8,9},{9,8},{10,11... | collective-permute-start | bytes 6291464 | tf_op jit(solution)/shard_map/ppermute | solution.py:353
  183.2 51.4 %all-to-all-start = ((bf16[16,128,256]{2,1,0:T(8,128)(2,1)}), bf16[16,128,256]{2,1,0:T(8,128)(2,1)S(1)}, u32[]{:S(2)}, u32[]{:S(2)}) async-start(bf16[16,128,256]{2,1,0:T(8,128)(2,1)} %copy-done), calls=%async_computation | async-start | bytes 2097152 | tf_op jit(solution)/shard_map/all_to_all | solution.py:352
  186.9 2.3 copy-start.4
  186.9 2.3 copy-start.13
  188.5 11.6 %collective-permute-start.21 = (bf16[512,640]{1,0:T(8,128)(2,1)S(1)}, bf16[512,640]{1,0:T(8,128)(2,1)S(1)}, u32[]{:S(2)}, u32[]{:S(2)}) collective-permute-start(bf16[512,640]{1,0:T(8,128)(2,1)S(1)} %add_convert_fusion.1), channel_id=1, source_target_pairs={{8,16},{10,18},{12,20},{14,22},{16,8},{18,10},{20,12},{22,14},{9,1... | collective-permute-start | bytes 1966088 | tf_op jit(solution)/shard_map/ppermute | solution.py:78
  189.4 40.2 %copy-start.2 = (bf16[512,640]{1,0:T(8,128)(2,1)S(1)}, bf16[512,640]{1,0:T(8,128)(2,1)}, u32[]{:S(2)}) copy-start(bf16[512,640]{1,0:T(8,128)(2,1)} %copy-done.1) | copy-start | bytes 1966084
  189.4 31.6 %collective-permute-start.20 = (bf16[512,640]{1,0:T(8,128)(2,1)S(1)}, bf16[512,640]{1,0:T(8,128)(2,1)S(1)}, u32[]{:S(2)}, u32[]{:S(2)}) collective-permute-start(bf16[512,640]{1,0:T(8,128)(2,1)S(1)} %add_convert_fusion.2), channel_id=1, source_target_pairs={{0,8},{2,10},{4,12},{6,14},{8,0},{10,2},{12,4},{14,6},{16,24},{18,... | collective-permute-start | bytes 1966088 | tf_op jit(solution)/shard_map/ppermute | solution.py:78
  196.5 24.5 %collective-permute-start.25 = (bf16[256,1024]{1,0:T(8,128)(2,1)S(1)}, bf16[256,1024]{1,0:T(8,128)(2,1)S(1)}, u32[]{:S(2)}, u32[]{:S(2)}) collective-permute-start(bf16[256,1024]{1,0:T(8,128)(2,1)S(1)} %get-tuple-element.106), channel_id=1, source_target_pairs={{0,6},{2,4},{4,2},{6,0},{8,14},{10,12},{12,10},{14,8},{16,22},{18,... | collective-permute-start | bytes 1572872 | tf_op jit(solution)/shard_map/ppermute | solution.py:73
  198.9 28.0 %collective-permute-start.24 = (bf16[256,1024]{1,0:T(8,128)(2,1)S(1)}, bf16[256,1024]{1,0:T(8,128)(2,1)S(1)}, u32[]{:S(2)}, u32[]{:S(2)}) collective-permute-start(bf16[256,1024]{1,0:T(8,128)(2,1)S(1)} %get-tuple-element.107), channel_id=1, source_target_pairs={{0,4},{2,6},{4,0},{6,2},{8,12},{10,14},{12,8},{14,10},{16,20},{18,... | collective-permute-start | bytes 1572872 | tf_op jit(solution)/shard_map/ppermute | solution.py:73
  199.5 30.1 %collective-permute-start.23 = (bf16[256,1024]{1,0:T(8,128)(2,1)S(1)}, bf16[256,1024]{1,0:T(8,128)(2,1)S(1)}, u32[]{:S(2)}, u32[]{:S(2)}) collective-permute-start(bf16[256,1024]{1,0:T(8,128)(2,1)S(1)} %get-tuple-element.108), channel_id=1, source_target_pairs={{0,2},{2,0},{4,6},{6,4},{8,10},{10,8},{12,14},{14,12},{16,18},{18,... | collective-permute-start | bytes 1572872 | tf_op jit(solution)/shard_map/ppermute | solution.py:73
  229.9 7.7 %collective-permute-start.28 = (bf16[128,640]{1,0:T(8,128)(2,1)S(1)}, bf16[128,640]{1,0:T(8,128)(2,1)S(1)}, u32[]{:S(2)}, u32[]{:S(2)}) collective-permute-start(bf16[128,640]{1,0:T(8,128)(2,1)S(1)} %get-tuple-element.130), channel_id=1, source_target_pairs={{0,6},{2,4},{4,2},{6,0},{8,14},{10,12},{12,10},{14,8},{16,22},{18,... | collective-permute-start | bytes 491528 | tf_op jit(solution)/shard_map/ppermute | solution.py:73
  231.8 7.9 %collective-permute-start.27 = (bf16[128,640]{1,0:T(8,128)(2,1)S(1)}, bf16[128,640]{1,0:T(8,128)(2,1)S(1)}, u32[]{:S(2)}, u32[]{:S(2)}) collective-permute-start(bf16[128,640]{1,0:T(8,128)(2,1)S(1)} %get-tuple-element.131), channel_id=1, source_target_pairs={{0,4},{2,6},{4,0},{6,2},{8,12},{10,14},{12,8},{14,10},{16,20},{18,... | collective-permute-start | bytes 491528 | tf_op jit(solution)/shard_map/ppermute | solution.py:73
  232.6 7.1 %collective-permute-start.26 = (bf16[128,640]{1,0:T(8,128)(2,1)S(1)}, bf16[128,640]{1,0:T(8,128)(2,1)S(1)}, u32[]{:S(2)}, u32[]{:S(2)}) collective-permute-start(bf16[128,640]{1,0:T(8,128)(2,1)S(1)} %get-tuple-element.132), channel_id=1, source_target_pairs={{0,2},{2,0},{4,6},{6,4},{8,10},{10,8},{12,14},{14,12},{16,18},{18,... | collective-permute-start | bytes 491528 | tf_op jit(solution)/shard_map/ppermute | solution.py:73

commit v4 on v3

v4 whole, which is shorter than its diff:
```python
import jax
import jax.numpy as jnp
from jax import lax
from jax.experimental import pallas as pl
from jax.experimental.pallas import tpu as pltpu
from jax.sharding import PartitionSpec as P

BAL = 208
BF = jnp.bfloat16
F32 = jnp.float32


def contract_last(left, right):
    return lax.dot_general(
        left, right, (((1,), (1,)), ((), ())), preferred_element_type=F32
    )


def contract_first(left, right):
    return lax.dot_general(
        left, right, (((0,), (0,)), ((), ())), preferred_element_type=F32
    )


def swiglu_back(x_rows, cot_rows, gate_full, up_full, live_mask):
    gate_val = jnp.dot(x_rows, gate_full, preferred_element_type=F32)
    up_val = jnp.dot(x_rows, up_full, preferred_element_type=F32)
    sig = jax.nn.sigmoid(gate_val)
    cot_val = cot_rows.astype(F32)
    d_gate = jnp.where(
        live_mask[:, None], cot_val * up_val * sig * (1.0 + gate_val * (1.0 - sig)), 0.0
    ).astype(BF)
    d_up = jnp.where(live_mask[:, None], cot_val * gate_val * sig, 0.0).astype(BF)
    return contract_last(d_gate, gate_full) + contract_last(d_up, up_full), d_gate


def live_rows_of(send_counts, recv_counts):
    return BAL + jnp.sum(send_counts[0]) - jnp.sum(recv_counts[0])


def general_plan(x_in, cotangent, w_gate, w_up, send_counts, recv_counts):
    dev_count = lax.axis_size("dp")
    gate_full = lax.all_gather(w_gate, "dp", axis=0, tiled=True)
    up_full = lax.all_gather(w_up, "dp", axis=0, tiled=True)
    live_mask = jnp.arange(x_in.shape[0]) < live_rows_of(send_counts, recv_counts)
    partial_value, d_gate = swiglu_back(x_in, cotangent, gate_full, up_full, live_mask)
    grad_x = lax.psum_scatter(
        partial_value.astype(BF), "mp", scatter_dimension=1, tiled=True
    )
    whole = contract_first(x_in, d_gate)
    pieces = lax.all_to_all(
        whole.reshape(dev_count, x_in.shape[1] // dev_count, whole.shape[1]),
        "dp",
        split_axis=0,
        concat_axis=0,
        tiled=True,
    )
    return grad_x, jnp.sum(pieces, axis=0)


CREW = (0, 1, 2, 3)
NEAR, FAR = 4, 8
CHAIN = (0, NEAR, FAR, NEAR | FAR)
DEVS = 16
TILE = 256


def tie(*values):
    return lax.optimization_barrier(values)


def send(value, mask):
    return lax.ppermute(value, "dp", [(i, i ^ mask) for i in range(DEVS)])


def along(value, moves):
    crew = len(CREW)
    return lax.ppermute(
        value, "dp", [(crew * a + q, crew * b + q) for a, b in moves for q in range(crew)]
    )


OUTER = [(0, 1), (1, 0), (2, 3), (3, 2)]
INNER = [(1, 2), (2, 1)]
TO_ENDS = [(1, 0), (2, 3)]
FROM_ENDS = [(0, 1), (3, 2)]


def crew_swap(pieces):
    return [send(p, m) if m else p for p, m in zip(pieces, CREW)]


def add(*terms):
    total = terms[0].astype(F32)
    for term in terms[1:]:
        total = total + term.astype(F32)
    return total.astype(BF)


def place_weights(scalars, groups, w_all, sems, act):
    blk = w_all.shape[0] // DEVS
    crew = len(CREW)
    inner = scalars[DEVS + 1]
    base = 0
    for n, members in groups:
        for c, member in enumerate(members):
            for i in range(n // blk):
                j = min(c, len(CHAIN) - 1) * crew + base + i
                start = pl.multiple_of(scalars[j] * blk, blk)
                copy = pltpu.make_async_copy(
                    member.at[pl.ds(i * blk, blk), :], w_all.at[pl.ds(start, blk), :], sems.at[j]
                )
                if len(members) > len(CHAIN) and c >= len(CHAIN) - 1:
                    pl.when(inner == (1 if c == len(CHAIN) - 1 else 0))(
                        lambda copy=copy: act(copy)
                    )
                else:
                    act(copy)
        base += n // blk


def grouped(refs, counts):
    groups = []
    for n, members in counts:
        groups.append((n, refs[:members]))
        refs = refs[members:]
    return groups, refs


def place_rows(core, tile, mine_ref, other_ref, cols=slice(None)):
    rows = TILE // 2
    lower = pl.ds(pl.multiple_of(core * rows, rows), rows)
    upper = pl.ds(pl.multiple_of((1 - core) * rows, rows), rows)
    tile[lower, :] = mine_ref[0, :, cols]
    tile[upper, :] = other_ref[0, :, cols]


def store_rows_grad(core, gx, gx_refs, prev):
    half = gx.shape[1] // 2
    low, high = gx[:, :half], gx[:, half:]
    for keep in range(2):

        @pl.when(core == keep)
        def _():
            for i, value in enumerate(((low, high)[keep], (high, low)[keep])):
                if prev is not None:
                    value = value + prev[i][...].astype(F32)
                gx_refs[i][...] = value.astype(BF)


def front(x, w_all, cot_lower, cot_upper):
    ck = w_all.shape[1] // 2
    both = jnp.dot(x, w_all[...], preferred_element_type=F32)
    gate, up = both[:, :ck], both[:, ck:]
    cot = jnp.concatenate([cot_lower, cot_upper], axis=0).astype(F32)
    sig = jax.nn.sigmoid(gate)
    d_gate = (cot * up * sig * (1.0 + gate * (1.0 - sig))).astype(BF)
    d_up = (cot * gate * sig).astype(BF)
    return d_gate, d_up


def first_kernel(scalars, mine_ref, other_ref, low_ref, high_ref, *refs, counts):
    groups, refs = grouped(refs, counts)
    d_ref, refs = refs[0], refs[1:]
    gg_refs, (w_all, x_all, d_all, acc, sems) = refs[: len(CHAIN)], refs[len(CHAIN) :]
    step = pl.program_id(0)
    width = w_all.shape[0]
    blk = width // DEVS
    crew = len(CREW)

    @pl.when(step == 0)
    def _():
        place_weights(scalars, groups, w_all, sems, lambda copy: copy.start())

    here = pl.ds(pl.multiple_of(step * TILE, TILE), TILE)
    place_rows(scalars[DEVS], x_all.at[here], mine_ref, other_ref)

    @pl.when(step == 0)
    def _():
        place_weights(scalars, groups, w_all, sems, lambda copy: copy.wait())

    d_gate, d_up = front(x_all[here, :], w_all, low_ref[0], high_ref[0])
    d_all[here, :] = d_gate
    d_ref[...] = jnp.concatenate([d_gate, d_up], axis=1)

    @pl.when(step == pl.num_programs(0) - 1)
    def _():
        d = d_all[...]
        deep = crew * blk
        for r in range(len(CHAIN)):
            cols = slice(r * deep, (r + 1) * deep)
            acc[cols, :] = contract_first(x_all[:, cols], d).astype(BF)
        for j in range(DEVS):
            row = (j % crew) * blk
            at_row = pl.multiple_of(scalars[2 * DEVS + j] * blk, blk)
            gg_refs[j // crew][row : row + blk, :] = acc[pl.ds(at_row, blk), :]


def rows_grad_kernel(scalars, d_ref, *refs, counts):
    groups, refs = grouped(refs, counts)
    gx_refs, (w_all, sems) = refs[:2], refs[2:]

    @pl.when(pl.program_id(0) == 0)
    def _():
        place_weights(scalars, groups, w_all, sems, lambda copy: copy.start())
        place_weights(scalars, groups, w_all, sems, lambda copy: copy.wait())

    store_rows_grad(scalars[DEVS], contract_last(d_ref[...], w_all[...]), gx_refs, None)


def second_kernel(scalars, mine_ref, other_ref, cot_ref, *refs, counts):
    groups, refs = grouped(refs, counts)
    prev, gx_refs, (d_ref, w_all, x_tile, sems) = refs[:2], refs[2:4], refs[4:]
    step = pl.program_id(0)
    ck = d_ref.shape[1]

    @pl.when(step == 0)
    def _():
        place_weights(scalars, groups, w_all, sems, lambda copy: copy.start())

    place_rows(scalars[DEVS], x_tile, mine_ref, other_ref)

    @pl.when(step == 0)
    def _():
        place_weights(scalars, groups, w_all, sems, lambda copy: copy.wait())

    d_gate, d_up = front(x_tile[...], w_all, cot_ref[0, :, :ck], cot_ref[0, :, ck:])
    d_ref[...] = d_gate
    gx = contract_last(jnp.concatenate([d_gate, d_up], axis=1), w_all[...])
    store_rows_grad(scalars[DEVS], gx, gx_refs, prev)


def gate_grad_kernel(scalars, mine_ref, other_ref, d_ref, *refs):
    out_refs, (x_all, acc) = refs[: len(CHAIN)], refs[len(CHAIN) :]
    step = pl.program_id(0)
    core = scalars[DEVS]
    crew = len(CREW)
    for s in range(crew):
        tile = x_all.at[s * TILE : (s + 1) * TILE]
        place_rows(core, tile, mine_ref.at[s : s + 1], other_ref.at[s : s + 1])
    deep = x_all.shape[1]
    here = pl.ds(pl.multiple_of(step * deep, deep), deep)
    acc[here, :] = contract_first(x_all[...], d_ref[...]).astype(BF)

    @pl.when(step == pl.num_programs(0) - 1)
    def _():
        blk = deep // crew
        for j in range(DEVS):
            row = (j % crew) * blk
            at_row = pl.multiple_of(scalars[j] * blk, blk)
            out_refs[j // crew][row : row + blk, :] = acc[pl.ds(at_row, blk), :]


def kernel_call(body, name, scalars, operands, in_specs, out_specs, out_shape, scratch, flops, limit):
    return pl.pallas_call(
        body,
        grid_spec=pltpu.PrefetchScalarGridSpec(
            num_scalar_prefetch=1,
            grid=(len(CREW),),
            in_specs=in_specs,
            out_specs=out_specs,
            scratch_shapes=scratch,
        ),
        out_shape=out_shape,
        compiler_params=pltpu.CompilerParams(vmem_limit_bytes=limit * 1024 * 1024),
        cost_estimate=pl.CostEstimate(flops=flops, bytes_accessed=2**23, transcendentals=0),
        name=name,
    )(scalars, *operands)


def spec_of_cols(wide, col):
    return pl.BlockSpec((1, TILE // 2, wide), lambda i, o: (i, 0, col))


def flat_of(groups):
    counts = [(g[0].shape[0], len(g)) for g in groups]
    return counts, [v for g in groups for v in g]


def first_chunk(scalars, mine, other, groups, width, ck, cot_col):
    counts, flat = flat_of(groups)
    rows = len(CREW) * TILE
    deep = width // len(CHAIN)
    d, *parts = kernel_call(
        lambda *a: first_kernel(*a, counts=counts),
        "first_chunk",
        scalars,
        [mine, other, mine, mine] + flat,
        [
            spec_of_cols(width, 0),
            spec_of_cols(width, 0),
            spec_of_cols(ck, cot_col // ck),
            spec_of_cols(ck, cot_col // ck + 1),
        ]
        + [pl.BlockSpec(memory_space=pltpu.HBM)] * len(flat),
        [pl.BlockSpec((TILE, 2 * ck), lambda i, o: (i, 0))]
        + [pl.BlockSpec((deep, ck), lambda i, o: (0, 0))] * len(CHAIN),
        [jax.ShapeDtypeStruct((rows, 2 * ck), BF)]
        + [jax.ShapeDtypeStruct((deep, ck), BF)] * len(CHAIN),
        [
            pltpu.VMEM((width, 2 * ck), BF),
            pltpu.VMEM((rows, width), BF),
            pltpu.VMEM((rows, ck), BF),
            pltpu.VMEM((width, ck), BF),
            pltpu.SemaphoreType.DMA((DEVS,)),
        ],
        6 * rows * width * ck,
        56,
    )
    return d, parts


def rows_grad(scalars, d, groups, width):
    counts, flat = flat_of(groups)
    rows, wide = d.shape
    gx_spec = pl.BlockSpec((TILE, width // 2), lambda i, o: (i, 0))
    return kernel_call(
        lambda *a: rows_grad_kernel(*a, counts=counts),
        "rows_grad",
        scalars,
        [d] + flat,
        [pl.BlockSpec((TILE, wide), lambda i, o: (i, 0))]
        + [pl.BlockSpec(memory_space=pltpu.HBM)] * len(flat),
        [gx_spec] * 2,
        [jax.ShapeDtypeStruct((rows, width // 2), BF)] * 2,
        [pltpu.VMEM((width, wide), BF), pltpu.SemaphoreType.DMA((DEVS,))],
        2 * rows * width * wide,
        56,
    )


def second_chunk(scalars, mine, other, groups, prev, width, ck, cot_col):
    counts, flat = flat_of(groups)
    rows = len(CREW) * TILE
    gx_spec = pl.BlockSpec((TILE, width // 2), lambda i, o: (i, 0))
    return kernel_call(
        lambda *a: second_kernel(*a, counts=counts),
        "second_chunk",
        scalars,
        [mine, other, mine] + flat + list(prev),
        [
            spec_of_cols(width, 0),
            spec_of_cols(width, 0),
            spec_of_cols(2 * ck, cot_col // (2 * ck)),
        ]
        + [pl.BlockSpec(memory_space=pltpu.HBM)] * len(flat)
        + [gx_spec] * 2,
        [gx_spec] * 2 + [pl.BlockSpec((TILE, ck), lambda i, o: (i, 0))],
        [jax.ShapeDtypeStruct((rows, width // 2), BF)] * 2
        + [jax.ShapeDtypeStruct((rows, ck), BF)],
        [
            pltpu.VMEM((width, 2 * ck), BF),
            pltpu.VMEM((TILE, width), BF),
            pltpu.SemaphoreType.DMA((DEVS,)),
        ],
        8 * rows * width * ck,
        56,
    )


def gate_grad(scalars, mine, other, d, width):
    rows, ck = d.shape
    steps = len(CREW)
    deep = width // steps
    x_spec = pl.BlockSpec((steps, TILE // 2, width // steps), lambda i, o: (0, 0, i))
    return kernel_call(
        gate_grad_kernel,
        "gate_grad",
        scalars,
        [mine, other, d],
        [x_spec, x_spec, pl.BlockSpec((rows, ck), lambda i, o: (0, 0))],
        [pl.BlockSpec((deep, ck), lambda i, o: (0, 0))] * len(CHAIN),
        [jax.ShapeDtypeStruct((deep, ck), BF)] * len(CHAIN),
        [pltpu.VMEM((rows, deep), BF), pltpu.VMEM((width, ck), BF)],
        2 * rows * width * ck,
        56,
    )


def join_kernel(scalars, *refs, quarter):
    out = refs[-1]
    for s in range(len(CREW)):
        start = scalars[DEVS + 2 + s] * quarter
        out[:, pl.ds(pl.multiple_of(start, 128), quarter)] = refs[s][...].astype(F32)


def join_call(scalars, pieces):
    depth, quarter = pieces[0].shape
    vmem = pl.BlockSpec(memory_space=pltpu.VMEM)
    return pl.pallas_call(
        lambda *a: join_kernel(*a, quarter=quarter),
        in_specs=[pl.BlockSpec(memory_space=pltpu.SMEM)] + [vmem] * len(CREW),
        out_specs=vmem,
        out_shape=jax.ShapeDtypeStruct((depth, len(CREW) * quarter), F32),
        compiler_params=pltpu.CompilerParams(vmem_limit_bytes=16 * 1024 * 1024),
        name="join_quarters",
    )(scalars, *pieces)


def split_plan(x_in, cotangent, w_gate, w_up, send_counts, recv_counts):
    rows, width = x_in.shape
    depth, hidden = w_gate.shape
    crew = len(CREW)
    quarter = hidden // crew
    core = lax.axis_index("mp")
    index = lax.axis_index("dp")
    z, place = index // crew, index % crew
    places = [place ^ m for m in CREW]
    chunks = [640, 256]
    offsets = [0, chunks[0]]
    swap = [(0, 1), (1, 0)]

    def columns(array, q, offset, count):
        return lax.dynamic_slice_in_dim(array, q * quarter + offset, count, 1)

    def piece_of_weights(q, k):
        return jnp.concatenate(
            [columns(w, q, offsets[k], chunks[k]) for w in (w_gate, w_up)], axis=1
        )

    order = [z, z ^ 1, jnp.where(z < 2, 2, 1), jnp.where(z < 2, 3, 0)]
    inner = ((z == 1) | (z == 2)).astype(jnp.int32)
    scalars = [index ^ c ^ m for c in CHAIN for m in CREW] + [core, inner] + places
    scalars += [0] * (2 * DEVS - len(scalars)) + [p * crew + q for p in order for q in places]
    scalars = jnp.stack([jnp.asarray(v, jnp.int32) for v in scalars])

    first = [piece_of_weights(q, 0) for q in places]
    own = first[0]
    own_far = send(own, FAR)
    own_near = send(own, NEAR)
    rest = crew_swap(first)[1:]
    own_far, own_near, x_in, cotangent, w_gate, w_up = tie(
        own_far, own_near, x_in, cotangent, w_gate, w_up
    )

    live = jnp.arange(rows) < live_rows_of(send_counts, recv_counts)
    cotangent = jnp.where(live[:, None], cotangent, jnp.zeros((), BF))
    x_half = lax.dynamic_slice_in_dim(x_in, core * (rows // 2), rows // 2, 0)
    parcels = []
    for q in places:
        cot = [columns(cotangent, q, offsets[k], chunks[k]) for k in (1, 0)]
        halves = [c[h : h + rows // 2] for c in cot for h in (0, rows // 2)]
        parcels.append(jnp.concatenate([x_half, *halves, piece_of_weights(q, 1)], axis=1))
    rest = jnp.concatenate(rest, axis=0)
    rest, own_far, *parcels = tie(rest, own_far, *parcels)

    own_both = send(own_far, NEAR)
    rest_far = send(rest, FAR)
    rest_near = send(rest, NEAR)
    parcels = crew_swap(parcels)
    rest_far, rest_near, own_both, *parcels = tie(rest_far, rest_near, own_both, *parcels)

    rest_both = send(rest_far, NEAR)
    mine = jnp.stack(parcels)
    other = lax.ppermute(mine, "mp", swap)
    rest_both, other, mine = tie(rest_both, other, mine)
    second = mine[:, :, width + 2 * quarter :].reshape(crew * depth, 2 * chunks[1])

    cot_second = width
    cot_first = width + 2 * chunks[1]

    second_near = send(second, NEAR)
    second_far = send(second, FAR)
    groups = [(own, own_near, own_far, own_both), (rest, rest_near, rest_far, rest_both)]
    d_first, parts = first_chunk(scalars, mine, other, groups, width, chunks[0], cot_first)
    second_near, second_far, d_first, p0, p1, p2, p3 = tie(second_near, second_far, d_first, *parts)

    middle = along(second, INNER)
    ends = along(second_far, TO_ENDS)
    r1 = along(p3, FROM_ENDS)
    gx = rows_grad(scalars, d_first, groups, width)
    r1, middle, ends, p2, p3, *gx = tie(r1, middle, ends, p2, p3, *gx)
    r2b = along(p2, FROM_ENDS)
    r2a = along(add(p3, r1), INNER)
    keep, give, d_second = second_chunk(
        scalars, mine, other, [(second, second_near, second_far, middle, ends)], gx,
        width, chunks[1], cot_second,
    )
    r2a, r2b, keep, give, d_second = tie(r2a, r2b, keep, give, d_second)

    theirs = lax.ppermute(give, "mp", swap)
    q_parts = gate_grad(scalars, mine, other, d_second, width)
    theirs, *q_parts = tie(theirs, *q_parts)
    q_own, q_near, q_far, q_both = q_parts
    from_near = send(q_both, NEAR)
    r3b = along(add(p2, r2b), INNER)
    r3a = along(add(p1, r2a), OUTER)
    rows_x = crew_swap(
        [
            add(keep[s * rows : (s + 1) * rows], theirs[s * rows : (s + 1) * rows])
            for s in range(crew)
        ]
    )
    sum_far = send(add(q_far, from_near), FAR)
    sum_near = send(q_near, NEAR)
    r3a, r3b, sum_far, sum_near, *rows_x = tie(r3a, r3b, sum_far, sum_near, *rows_x)
    sums = jnp.concatenate([add(p0, r3a, r3b), add(q_own, sum_near, sum_far)], axis=1)
    pieces = crew_swap([sums[s * depth : (s + 1) * depth] for s in range(crew)])
    return add(*rows_x), join_call(scalars, pieces)


def solution(mesh):
    sizes = dict(mesh.shape)
    splits = sizes["dp"] == DEVS and sizes["mp"] == 2
    return jax.shard_map(
        split_plan if splits else general_plan,
        mesh=mesh,
        in_specs=(
            P("dp", None),
            P("dp", "mp"),
            P("dp", "mp"),
            P("dp", "mp"),
            P("dp", None),
            P("dp", None),
        ),
        out_specs=(P("dp", "mp"), P("dp", "mp")),
        check_vma=False,
    )
```

time: 242 us -> 231 us (0.955)
  waiting for transfers between devices: 126 us -> 109 us
  starting transfers between devices: 43.3 us -> 51.1 us
  local copies, waits for them, and re-layouts: 16.4 us -> 11.6 us
  Pallas kernels: 45.3 us -> 49.4 us
    ppermute x7, waiting for transfers between devices: 34.2 us -> 0.97 us  [along(): lax.ppermute(value, 'dp', [(crew * a + q, crew * b + q) for a, b in moves...]
    ppermute x20 -> x23, waiting for transfers between devices: 92.2 us -> 108 us  [send(): return lax.ppermute(value, 'dp', [(i, i ^ mask) for i in range(DEVS)])]
    ppermute x20 -> x23, starting transfers between devices: 22.7 us -> 34.2 us  [send(): return lax.ppermute(value, 'dp', [(i, i ^ mask) for i in range(DEVS)])]
    pallas_call x3 -> x5, Pallas kernels: 45.3 us -> 49.4 us  [the longest x4 47.5 us: kernel_call(): pl.pallas_call(body, grid_spec=pltpu.PrefetchScalarGridSpec(num_scalar_pr...]
    unnamed x44 -> x67, local copies, waits for them, and re-layouts: 11 us -> 6.95 us
    all_to_all x1 -> x0, starting transfers between devices: 3.66 us -> none  [split_plan(): lasts = lax.all_to_all(lasts, 'dp', split_axis=0, concat_axis=0, tiled=True)]
    convert_element_type x6 -> x8, other arithmetic: 5.72 us -> 3.04 us  [add(): return total.astype(BF)]
  transfers between devices with their start and end apart: 30 -> 32, of which waited for: 12 -> 18; matrix products, arithmetic and copies ran while one was open for 4% -> 3% of each run, Pallas kernels for 18% -> 21%
where the time goes in v4:
time: 231 us; the launch traced here: 230 us
  waiting for transfers between devices  109 us (47%)
  starting transfers between devices  51.1 us (22%)
  Pallas kernels  49.4 us (21%)
  local copies, waits for them, and re-layouts  11.6 us (5%)
  other arithmetic  7.15 us (3%)
  between operations  2.44 us (1%)
    ppermute x23, waiting for transfers between devices, send(): return lax.ppermute(value, 'dp', [(i, i ^ mask) for i in range(DEVS)])  108 us
    pallas_call x4, Pallas kernels, kernel_call(): pl.pallas_call(body, grid_spec=pltpu.PrefetchScalarGridSpec(num_scalar_pr...  47.5 us
    ppermute x23, starting transfers between devices, send(): return lax.ppermute(value, 'dp', [(i, i ^ mask) for i in range(DEVS)])  34.2 us
    ppermute x7, starting transfers between devices, along(): lax.ppermute(value, 'dp', [(crew * a + q, crew * b + q) for a, b in moves...  16.9 us
    unnamed x67, local copies, waits for them, and re-layouts  6.95 us
  transfers between devices with their start and end apart: 32, of which 18 were waited for; matrix products, arithmetic and copies ran while one was open for 3% of the time, Pallas kernels for 21%

profile of v4, /device:TPU:0, one launch (start us, length us, event | category | flops | bytes accessed | tf_op | source)
XLA Modules:
  0.0 230.5 jit_solution(3131769969910055144)
XLA Ops:
  0.7 1.5 constant_dynamic-slice_fusion
  2.3 4.1 %collective-permute-start.3 = (bf16[128,1280]{1,0:T(8,128)(2,1)S(1)}, bf16[128,1280]{1,0:T(8,128)(2,1)}, u32[]{:S(2)}, u32[]{:S(2)}) collective-permute-start(bf16[128,1280]{1,0:T(8,128)(2,1)S(1)} %pad_maximum_fusion.5.a_5_.a_2_), channel_id=1, source_target_pairs={{0,16},{2,18},{4,20},{6,22},{8,24},{10,26},{12,28},{14,30},{16,0},... | collective-permute-start | bytes 983048 | tf_op jit(solution)/shard_map/ppermute | solution.py:73
  6.4 1.6 collective-permute-start.4
  8.0 1.6 collective-permute-start
  9.6 1.6 collective-permute-start.1
  11.2 0.5 collective-permute-start.2
  11.7 0.6 reduce_sum.18
  12.4 0.7 reduce_sum.19
  14.3 7.0 %collective-permute-done.3.a_7_.a_4_ = bf16[128,1280]{1,0:T(8,128)(2,1)} collective-permute-done((bf16[128,1280]{1,0:T(8,128)(2,1)S(1)}, bf16[128,1280]{1,0:T(8,128)(2,1)}, u32[]{:S(2)}, u32[]{:S(2)}) %collective-permute-start.3) | collective-permute-done | bytes 327712 | tf_op jit(solution)/shard_map/ppermute | solution.py:73
  21.6 1.0 copy-done.1
  22.7 1.4 copy-done.7
  24.3 1.0 copy-done.3
  25.7 0.5 copy-done.2
  26.6 1.0 dynamic-slice_dynamic-update-slice_fusion.21
  27.5 1.0 dynamic-slice_dynamic-update-slice_fusion.20
  28.6 1.6 collective-permute-start.7
  30.2 2.4 %collective-permute-start.10 = (bf16[128,4352]{1,0:T(8,128)(2,1)S(1)}, bf16[128,4352]{1,0:T(8,128)(2,1)S(1)}, u32[]{:S(2)}, u32[]{:S(2)}) collective-permute-start(bf16[128,4352]{1,0:T(8,128)(2,1)S(1)} %get-tuple-element.80), channel_id=1, source_target_pairs={{0,6},{2,4},{4,2},{6,0},{8,14},{10,12},{12,10},{14,8},{16,22},{18,... | collective-permute-start | bytes 3342344 | tf_op jit(solution)/shard_map/ppermute | solution.py:73
  32.6 0.5 collective-permute-start.8
  33.1 0.5 collective-permute-start.9
  33.7 2.3 %collective-permute-start.5 = (bf16[384,1280]{1,0:T(8,128)(2,1)S(1)}, bf16[384,1280]{1,0:T(8,128)(2,1)S(1)}, u32[]{:S(2)}, u32[]{:S(2)}) collective-permute-start(bf16[384,1280]{1,0:T(8,128)(2,1)S(1)} %pad_maximum_fusion.1.a_9_.a_6_), channel_id=1, source_target_pairs={{0,16},{2,18},{4,20},{6,22},{8,24},{10,26},{12,28},{14,30},{16,0},... | collective-permute-start | bytes 2949128 | tf_op jit(solution)/shard_map/ppermute | solution.py:73
  36.0 7.6 %collective-permute-done.7.a_8_.a_5_ = bf16[128,1280]{1,0:T(8,128)(2,1)S(1)} collective-permute-done((bf16[128,1280]{1,0:T(8,128)(2,1)}, bf16[128,1280]{1,0:T(8,128)(2,1)S(1)}, u32[]{:S(2)}, u32[]{:S(2)}) %collective-permute-start.7) | collective-permute-done | bytes 327712 | tf_op jit(solution)/shard_map/ppermute | solution.py:73
  43.5 34.5 %collective-permute-done.5.a_11_.a_8_ = bf16[384,1280]{1,0:T(8,128)(2,1)S(1)} collective-permute-done((bf16[384,1280]{1,0:T(8,128)(2,1)S(1)}, bf16[384,1280]{1,0:T(8,128)(2,1)S(1)}, u32[]{:S(2)}, u32[]{:S(2)}) %collective-permute-start.5) | collective-permute-done | bytes 983072 | tf_op jit(solution)/shard_map/ppermute | solution.py:73
  78.0 1.7 collective-permute-done.6.a_10_.a_7_
  79.7 0.5 collective-permute-done.8
  80.2 0.4 copy-done.22
  80.6 2.4 %pad_maximum_fusion.a_1_.a_3_.a_4_.mine_ref = bf16[4,128,4352]{2,1,0:T(8,128)(2,1)} fusion(bf16[1,128,4352]{2,1,0:T(8,128)(2,1)S(1)} %bitcast.48, bf16[1,128,4352]{2,1,0:T(8,128)(2,1)S(1)} %bitcast.50, bf16[1,128,4352]{2,1,0:T(8,128)(2,1)S(1)} %bitcast.49, bf16[1,128,4352]{2,1,0:T(8,128)(2,1)S(1)} %bitcast.43), kind=kLoop, calls=%fused_computation | loop fusion | flops 6684672 | bytes 8912896 | tf_op jit(solution)/shard_map/stack | solution.py:454
  83.0 1.5 collective-permute-start.11
  84.5 0.7 stack.179.a_0_.scalars
  85.3 21.9 %collective-permute-done.11.a_12_.a_9_ = bf16[384,1280]{1,0:T(8,128)(2,1)S(1)} collective-permute-done((bf16[384,1280]{1,0:T(8,128)(2,1)S(1)}, bf16[384,1280]{1,0:T(8,128)(2,1)S(1)}, u32[]{:S(2)}, u32[]{:S(2)}) %collective-permute-start.11) | collective-permute-done | bytes 983072 | tf_op jit(solution)/shard_map/ppermute | solution.py:73
  107.2 1.4 slice.103
  108.6 1.5 collective-permute-start.13
  110.2 5.1 %collective-permute-start.14 = (bf16[512,512]{1,0:T(8,128)(2,1)S(1)}, bf16[512,512]{1,0:T(8,128)(2,1)S(1)}, u32[]{:S(2)}, u32[]{:S(2)}) collective-permute-start(bf16[512,512]{1,0:T(8,128)(2,1)S(1)} %bitcast.45), channel_id=1, source_target_pairs={{0,16},{2,18},{4,20},{6,22},{8,24},{10,26},{12,28},{14,30},{16,0},... | collective-permute-start | bytes 1572872 | tf_op jit(solution)/shard_map/ppermute | solution.py:73
  115.3 17.0 %first_chunk.1 = (bf16[1024,1280]{1,0:T(8,128)(2,1)}, bf16[512,640]{1,0:T(8,128)(2,1)}, bf16[512,640]{1,0:T(8,128)(2,1)}, bf16[512,640]{1,0:T(8,128)(2,1)}, bf16[512,640]{1,0:T(8,128)(2,1)}) custom-call(s32[48]{0:T(128)} %stack.179.a_0_.scalars, bf16[4,128,4352]{2,1,0:T(8,128)(2,1)} %pad_maximum_fusion.a_1_.a_3_.a_4_.mine_ref, ...), custom_call_target="tpu_custom_call" | custom-call | flops 8053063680 | bytes 8388608 | tf_op jit(solution)/shard_map/first_chunk/pallas_call | solution.py:255
  132.3 1.1 collective-permute-done.13.a_5_
  133.4 4.6 %collective-permute-done.14.a_6_ = bf16[512,512]{1,0:T(8,128)(2,1)S(1)} collective-permute-done((bf16[512,512]{1,0:T(8,128)(2,1)S(1)}, bf16[512,512]{1,0:T(8,128)(2,1)S(1)}, u32[]{:S(2)}, u32[]{:S(2)}) %collective-permute-start.14) | collective-permute-done | bytes 524320 | tf_op jit(solution)/shard_map/ppermute | solution.py:73
  138.0 2.6 %collective-permute-start.15 = (bf16[512,640]{1,0:T(8,128)(2,1)}, bf16[512,640]{1,0:T(8,128)(2,1)S(1)}, u32[]{:S(2)}, u32[]{:S(2)}) collective-permute-start(bf16[512,640]{1,0:T(8,128)(2,1)} %get-tuple-element.104), channel_id=1, source_target_pairs={{0,8},{2,10},{4,12},{6,14},{24,16},{26,18},{28,20},{30,22},{1,9},{... | collective-permute-start | bytes 1966088 | tf_op jit(solution)/shard_map/ppermute | solution.py:78
  140.6 0.7 collective-permute-start.16
  141.3 1.3 collective-permute-start.17
  142.6 12.1 %rows_grad.1 = (bf16[1024,1024]{1,0:T(8,128)(2,1)}, bf16[1024,1024]{1,0:T(8,128)(2,1)}) custom-call(s32[48]{0:T(128)} %stack.179.a_0_.scalars, bf16[1024,1280]{1,0:T(8,128)(2,1)} %get-tuple-element.101.a_1_, bf16[128,1280]{1,0:T(8,128)(2,1)} %copy-done.17, bf16[128,1280]{1,0:T(8,128)(2,1)} %collective-permute-done.4.a_6_.a_3_, ...), custom_call_target="tpu_custom_call" | custom-call | flops 5368709120 | bytes 8388608 | tf_op jit(solution)/shard_map/rows_grad/pallas_call | solution.py:255
  154.8 0.9 collective-permute-done.17.a_8_
  155.9 0.7 collective-permute-start.18
  156.6 5.6 %collective-permute-start.19 = (bf16[512,640]{1,0:T(8,128)(2,1)S(1)}, bf16[512,640]{1,0:T(8,128)(2,1)S(1)}, u32[]{:S(2)}, u32[]{:S(2)}) collective-permute-start(bf16[512,640]{1,0:T(8,128)(2,1)S(1)} %copy-done.11), channel_id=1, source_target_pairs={{0,8},{2,10},{4,12},{6,14},{24,16},{26,18},{28,20},{30,22},{1,9},{... | collective-permute-start | bytes 1966088 | tf_op jit(solution)/shard_map/ppermute | solution.py:78
  162.2 12.1 %second_chunk.1 = (bf16[1024,1024]{1,0:T(8,128)(2,1)}, bf16[1024,1024]{1,0:T(8,128)(2,1)}, bf16[1024,256]{1,0:T(8,128)(2,1)}) custom-call(s32[48]{0:T(128)} %stack.179.a_0_.scalars, bf16[4,128,4352]{2,1,0:T(8,128)(2,1)} %pad_maximum_fusion.a_1_.a_3_.a_4_.mine_ref, bf16[4,128,4352]{2,1,0:T(8,128)(2,1)} %collective-permute-done.12.a_2_.other_ref, ...), custom_call_target="tpu_custom_call" | custom-call | flops 4294967296 | bytes 8388608 | tf_op jit(solution)/shard_map/second_chunk/pallas_call | solution.py:255
  174.6 0.9 collective-permute-start.21
  175.7 5.2 %collective-permute-start.20 = (bf16[512,640]{1,0:T(8,128)(2,1)S(1)}, bf16[512,640]{1,0:T(8,128)(2,1)S(1)}, u32[]{:S(2)}, u32[]{:S(2)}) collective-permute-start(bf16[512,640]{1,0:T(8,128)(2,1)S(1)} %add_convert_fusion.2), channel_id=1, source_target_pairs={{0,8},{2,10},{4,12},{6,14},{8,0},{10,2},{12,4},{14,6},{16,24},{18,... | collective-permute-start | bytes 1966088 | tf_op jit(solution)/shard_map/ppermute | solution.py:78
  180.9 6.2 %gate_grad.1 = (bf16[512,256]{1,0:T(8,128)(2,1)}, bf16[512,256]{1,0:T(8,128)(2,1)}, bf16[512,256]{1,0:T(8,128)(2,1)}, bf16[512,256]{1,0:T(8,128)(2,1)}) custom-call(s32[48]{0:T(128)} %stack.179.a_0_.scalars, bf16[4,128,4352]{2,1,0:T(8,128)(2,1)} %pad_maximum_fusion.a_1_.a_3_.a_4_.mine_ref, bf16[4,128,4352]{2,1,0:T(8,128)(2,1)} %collective-permute-done.12.a_2_.other_ref, ...), custom_call_target="tpu_custom_call" | custom-call | flops 1073741824 | bytes 8388608 | tf_op jit(solution)/shard_map/gate_grad/pallas_call | solution.py:255
  187.2 1.0 add_convert_fusion.5
  188.2 1.6 collective-permute-start.26
  189.8 1.5 collective-permute-start.27
  191.3 0.5 collective-permute-start.28
  191.8 9.8 %collective-permute-done.23 = bf16[512,256]{1,0:T(8,128)(2,1)S(1)} collective-permute-done((bf16[512,256]{1,0:T(8,128)(2,1)}, bf16[512,256]{1,0:T(8,128)(2,1)S(1)}, u32[]{:S(2)}, u32[]{:S(2)}) %collective-permute-start.23) | collective-permute-done | bytes 262176 | tf_op jit(solution)/shard_map/ppermute | solution.py:73
  201.6 1.7 collective-permute-start.25
  203.8 10.1 %collective-permute-done.25 = bf16[512,256]{1,0:T(8,128)(2,1)S(1)} collective-permute-done((bf16[512,256]{1,0:T(8,128)(2,1)S(1)}, bf16[512,256]{1,0:T(8,128)(2,1)S(1)}, u32[]{:S(2)}, u32[]{:S(2)}) %collective-permute-start.25) | collective-permute-done | bytes 262176 | tf_op jit(solution)/shard_map/ppermute | solution.py:73
  213.9 0.6 collective-permute-done.27
  214.5 2.9 %collective-permute-done.24 = bf16[512,256]{1,0:T(8,128)(2,1)S(1)} collective-permute-done((bf16[512,256]{1,0:T(8,128)(2,1)S(1)}, bf16[512,256]{1,0:T(8,128)(2,1)S(1)}, u32[]{:S(2)}, u32[]{:S(2)}) %collective-permute-start.24) | collective-permute-done | bytes 262176 | tf_op jit(solution)/shard_map/ppermute | solution.py:73
  217.7 0.7 copy-done.20
  218.5 1.6 collective-permute-start.29
  220.1 1.5 collective-permute-start.30
  221.6 0.5 collective-permute-start.31
  222.1 1.2 add_convert_fusion.4
  223.3 1.4 collective-permute-done.29.a_2_
  224.6 3.0 %collective-permute-done.30.a_3_ = bf16[128,896]{1,0:T(8,128)(2,1)S(1)} collective-permute-done((bf16[128,896]{1,0:T(8,128)(2,1)S(1)}, bf16[128,896]{1,0:T(8,128)(2,1)S(1)}, u32[]{:S(2)}, u32[]{:S(2)}) %collective-permute-start.30) | collective-permute-done | bytes 229408 | tf_op jit(solution)/shard_map/ppermute | solution.py:73
  227.6 1.0 collective-permute-done.31.a_4_
  228.6 1.9 join_quarters.1
  (97 shorter events, 3.0 us)
Async XLA Ops:
  2.2 19.3 %copy-start.17 = (bf16[128,1280]{1,0:T(8,128)(2,1)}, bf16[128,1280]{1,0:T(8,128)(2,1)S(1)}, u32[]{:S(2)}) copy-start(bf16[128,1280]{1,0:T(8,128)(2,1)S(1)} %pad_maximum_fusion.5.a_5_.a_2_) | copy-start | bytes 983044
  2.3 9.5 %copy-start.26 = (s32[1,16]{1,0:T(1,128)S(1)}, s32[1,16]{1,0:T(1,128)}, u32[]{:S(2)}) copy-start(s32[1,16]{1,0:T(1,128)} %param.10) | copy-start | bytes 196
  2.3 10.1 %copy-start.27 = (s32[1,16]{1,0:T(1,128)S(1)}, s32[1,16]{1,0:T(1,128)}, u32[]{:S(2)}) copy-start(s32[1,16]{1,0:T(1,128)} %param.11) | copy-start | bytes 196
  2.3 19.3 %copy-start.19 = (bf16[256,2048]{1,0:T(8,128)(2,1)S(1)}, bf16[256,2048]{1,0:T(8,128)(2,1)}, u32[]{:S(2)}) copy-start(bf16[256,2048]{1,0:T(8,128)(2,1)} %param.6) | copy-start | bytes 3145732
  2.3 19.0 %collective-permute-start.3 = (bf16[128,1280]{1,0:T(8,128)(2,1)S(1)}, bf16[128,1280]{1,0:T(8,128)(2,1)}, u32[]{:S(2)}, u32[]{:S(2)}) collective-permute-start(bf16[128,1280]{1,0:T(8,128)(2,1)S(1)} %pad_maximum_fusion.5.a_5_.a_2_), channel_id=1, source_target_pairs={{0,16},{2,18},{4,20},{6,22},{8,24},{10,26},{12,28},{14,30},{16,0},... | collective-permute-start | bytes 983048 | tf_op jit(solution)/shard_map/ppermute | solution.py:73
  6.4 15.1 %collective-permute-start.4 = (bf16[128,1280]{1,0:T(8,128)(2,1)S(1)}, bf16[128,1280]{1,0:T(8,128)(2,1)}, u32[]{:S(2)}, u32[]{:S(2)}) collective-permute-start(bf16[128,1280]{1,0:T(8,128)(2,1)S(1)} %pad_maximum_fusion.5.a_5_.a_2_), channel_id=1, source_target_pairs={{0,8},{2,10},{4,12},{6,14},{8,0},{10,2},{12,4},{14,6},{16,24},{18,... | collective-permute-start | bytes 983048 | tf_op jit(solution)/shard_map/ppermute | solution.py:73
  8.0 20.5 %collective-permute-start = (bf16[128,1280]{1,0:T(8,128)(2,1)S(1)}, bf16[128,1280]{1,0:T(8,128)(2,1)S(1)}, u32[]{:S(2)}, u32[]{:S(2)}) collective-permute-start(bf16[128,1280]{1,0:T(8,128)(2,1)S(1)} %pad_maximum_fusion.2), channel_id=1, source_target_pairs={{0,2},{2,0},{4,6},{6,4},{8,10},{10,8},{12,14},{14,12},{16,18},{18,... | collective-permute-start | bytes 983048 | tf_op jit(solution)/shard_map/ppermute | solution.py:73
  9.6 18.9 %collective-permute-start.1 = (bf16[128,1280]{1,0:T(8,128)(2,1)S(1)}, bf16[128,1280]{1,0:T(8,128)(2,1)S(1)}, u32[]{:S(2)}, u32[]{:S(2)}) collective-permute-start(bf16[128,1280]{1,0:T(8,128)(2,1)S(1)} %pad_maximum_fusion.3), channel_id=1, source_target_pairs={{0,4},{2,6},{4,0},{6,2},{8,12},{10,14},{12,8},{14,10},{16,20},{18,... | collective-permute-start | bytes 983048 | tf_op jit(solution)/shard_map/ppermute | solution.py:73
  11.2 17.3 %collective-permute-start.2 = (bf16[128,1280]{1,0:T(8,128)(2,1)S(1)}, bf16[128,1280]{1,0:T(8,128)(2,1)S(1)}, u32[]{:S(2)}, u32[]{:S(2)}) collective-permute-start(bf16[128,1280]{1,0:T(8,128)(2,1)S(1)} %pad_maximum_fusion.4), channel_id=1, source_target_pairs={{0,6},{2,4},{4,2},{6,0},{8,14},{10,12},{12,10},{14,8},{16,22},{18,... | collective-permute-start | bytes 983048 | tf_op jit(solution)/shard_map/ppermute | solution.py:73
  21.6 1.0 copy-start.1
  22.6 1.5 copy-start.7
  24.1 1.2 copy-start.3
  24.1 1.6 copy-start.4
  24.1 2.2 copy-start.2
  28.6 54.4 %copy-start.8 = (bf16[384,1280]{1,0:T(8,128)(2,1)}, bf16[384,1280]{1,0:T(8,128)(2,1)S(1)}, u32[]{:S(2)}) copy-start(bf16[384,1280]{1,0:T(8,128)(2,1)S(1)} %pad_maximum_fusion.1.a_9_.a_6_) | copy-start | bytes 2949124
  28.6 14.9 %collective-permute-start.7 = (bf16[128,1280]{1,0:T(8,128)(2,1)}, bf16[128,1280]{1,0:T(8,128)(2,1)S(1)}, u32[]{:S(2)}, u32[]{:S(2)}) collective-permute-start(bf16[128,1280]{1,0:T(8,128)(2,1)} %collective-permute-done.3.a_7_.a_4_), channel_id=1, source_target_pairs={{0,8},{2,10},{4,12},{6,14},{8,0},{10,2},{12,4},{14,6},{16,24},{18,... | collective-permute-start | bytes 983048 | tf_op jit(solution)/shard_map/ppermute | solution.py:73
  30.2 49.5 %collective-permute-start.10 = (bf16[128,4352]{1,0:T(8,128)(2,1)S(1)}, bf16[128,4352]{1,0:T(8,128)(2,1)S(1)}, u32[]{:S(2)}, u32[]{:S(2)}) collective-permute-start(bf16[128,4352]{1,0:T(8,128)(2,1)S(1)} %get-tuple-element.80), channel_id=1, source_target_pairs={{0,6},{2,4},{4,2},{6,0},{8,14},{10,12},{12,10},{14,8},{16,22},{18,... | collective-permute-start | bytes 3342344 | tf_op jit(solution)/shard_map/ppermute | solution.py:73
  32.6 47.6 %collective-permute-start.8 = (bf16[128,4352]{1,0:T(8,128)(2,1)S(1)}, bf16[128,4352]{1,0:T(8,128)(2,1)S(1)}, u32[]{:S(2)}, u32[]{:S(2)}) collective-permute-start(bf16[128,4352]{1,0:T(8,128)(2,1)S(1)} %get-tuple-element.78), channel_id=1, source_target_pairs={{0,2},{2,0},{4,6},{6,4},{8,10},{10,8},{12,14},{14,12},{16,18},{18,... | collective-permute-start | bytes 3342344 | tf_op jit(solution)/shard_map/ppermute | solution.py:73
  33.1 47.0 %collective-permute-start.9 = (bf16[128,4352]{1,0:T(8,128)(2,1)S(1)}, bf16[128,4352]{1,0:T(8,128)(2,1)S(1)}, u32[]{:S(2)}, u32[]{:S(2)}) collective-permute-start(bf16[128,4352]{1,0:T(8,128)(2,1)S(1)} %get-tuple-element.79), channel_id=1, source_target_pairs={{0,4},{2,6},{4,0},{6,2},{8,12},{10,14},{12,8},{14,10},{16,20},{18,... | collective-permute-start | bytes 3342344 | tf_op jit(solution)/shard_map/ppermute | solution.py:73
  33.7 44.4 %collective-permute-start.5 = (bf16[384,1280]{1,0:T(8,128)(2,1)S(1)}, bf16[384,1280]{1,0:T(8,128)(2,1)S(1)}, u32[]{:S(2)}, u32[]{:S(2)}) collective-permute-start(bf16[384,1280]{1,0:T(8,128)(2,1)S(1)} %pad_maximum_fusion.1.a_9_.a_6_), channel_id=1, source_target_pairs={{0,16},{2,18},{4,20},{6,22},{8,24},{10,26},{12,28},{14,30},{16,0},... | collective-permute-start | bytes 2949128 | tf_op jit(solution)/shard_map/ppermute | solution.py:73
  43.5 39.5 %copy-start.24 = (bf16[128,1280]{1,0:T(8,128)(2,1)}, bf16[128,1280]{1,0:T(8,128)(2,1)S(1)}, u32[]{:S(2)}) copy-start(bf16[128,1280]{1,0:T(8,128)(2,1)S(1)} %collective-permute-done.7.a_8_.a_5_) | copy-start | bytes 983044
  43.5 36.1 %collective-permute-start.6 = (bf16[384,1280]{1,0:T(8,128)(2,1)S(1)}, bf16[384,1280]{1,0:T(8,128)(2,1)S(1)}, u32[]{:S(2)}, u32[]{:S(2)}) collective-permute-start(bf16[384,1280]{1,0:T(8,128)(2,1)S(1)} %pad_maximum_fusion.1.a_9_.a_6_), channel_id=1, source_target_pairs={{0,8},{2,10},{4,12},{6,14},{8,0},{10,2},{12,4},{14,6},{16,24},{18,... | collective-permute-start | bytes 2949128 | tf_op jit(solution)/shard_map/ppermute | solution.py:73
  78.0 5.0 %copy-start.21 = (bf16[384,1280]{1,0:T(8,128)(2,1)}, bf16[384,1280]{1,0:T(8,128)(2,1)S(1)}, u32[]{:S(2)}) copy-start(bf16[384,1280]{1,0:T(8,128)(2,1)S(1)} %collective-permute-done.5.a_11_.a_8_) | copy-start | bytes 2949124
  79.7 1.0 copy-start.22
  83.0 24.2 %collective-permute-start.12 = (bf16[4,128,4352]{2,1,0:T(8,128)(2,1)}, bf16[4,128,4352]{2,1,0:T(8,128)(2,1)}, u32[]{:S(2)}, u32[]{:S(2)}) collective-permute-start(bf16[4,128,4352]{2,1,0:T(8,128)(2,1)} %pad_maximum_fusion.a_1_.a_3_.a_4_.mine_ref), channel_id=1, source_target_pairs={{0,1},{1,0},{2,3},{3,2},{4,5},{5,4},{6,7},{7,6},{8,9},{9,8},{10,11... | collective-permute-start | bytes 13369352 | tf_op jit(solution)/shard_map/ppermute | solution.py:455
  83.0 24.2 %collective-permute-start.11 = (bf16[384,1280]{1,0:T(8,128)(2,1)S(1)}, bf16[384,1280]{1,0:T(8,128)(2,1)S(1)}, u32[]{:S(2)}, u32[]{:S(2)}) collective-permute-start(bf16[384,1280]{1,0:T(8,128)(2,1)S(1)} %collective-permute-done.5.a_11_.a_8_), channel_id=1, source_target_pairs={{0,8},{2,10},{4,12},{6,14},{8,0},{10,2},{12,4},{14,6},{16,24},{18,... | collective-permute-start | bytes 2949128 | tf_op jit(solution)/shard_map/ppermute | solution.py:73
  107.2 8.1 %copy-start.23 = (bf16[384,1280]{1,0:T(8,128)(2,1)}, bf16[384,1280]{1,0:T(8,128)(2,1)S(1)}, u32[]{:S(2)}) copy-start(bf16[384,1280]{1,0:T(8,128)(2,1)S(1)} %collective-permute-done.11.a_12_.a_9_) | copy-start | bytes 2949124
  108.6 32.0 %copy-start.6 = (bf16[4,128,512]{2,1,0:T(8,128)(2,1)}, bf16[4,128,512]{2,1,0:T(8,128)(2,1)S(1)}, u32[]{:S(2)}) copy-start(bf16[4,128,512]{2,1,0:T(8,128)(2,1)S(1)} %slice.103) | copy-start | bytes 1572868
  108.6 24.7 %collective-permute-start.13 = (bf16[512,512]{1,0:T(8,128)(2,1)S(1)}, bf16[512,512]{1,0:T(8,128)(2,1)S(1)}, u32[]{:S(2)}, u32[]{:S(2)}) collective-permute-start(bf16[512,512]{1,0:T(8,128)(2,1)S(1)} %bitcast.44), channel_id=1, source_target_pairs={{0,8},{2,10},{4,12},{6,14},{8,0},{10,2},{12,4},{14,6},{16,24},{18,... | collective-permute-start | bytes 1572872 | tf_op jit(solution)/shard_map/ppermute | solution.py:73
  110.2 27.8 %collective-permute-start.14 = (bf16[512,512]{1,0:T(8,128)(2,1)S(1)}, bf16[512,512]{1,0:T(8,128)(2,1)S(1)}, u32[]{:S(2)}, u32[]{:S(2)}) collective-permute-start(bf16[512,512]{1,0:T(8,128)(2,1)S(1)} %bitcast.45), channel_id=1, source_target_pairs={{0,16},{2,18},{4,20},{6,22},{8,24},{10,26},{12,28},{14,30},{16,0},... | collective-permute-start | bytes 1572872 | tf_op jit(solution)/shard_map/ppermute | solution.py:73
  133.4 21.4 %copy-start.13 = (bf16[512,512]{1,0:T(8,128)(2,1)}, bf16[512,512]{1,0:T(8,128)(2,1)S(1)}, u32[]{:S(2)}) copy-start(bf16[512,512]{1,0:T(8,128)(2,1)S(1)} %collective-permute-done.13.a_5_) | copy-start | bytes 1572868
  138.0 16.7 %copy-start.14 = (bf16[512,512]{1,0:T(8,128)(2,1)}, bf16[512,512]{1,0:T(8,128)(2,1)S(1)}, u32[]{:S(2)}) copy-start(bf16[512,512]{1,0:T(8,128)(2,1)S(1)} %collective-permute-done.14.a_6_) | copy-start | bytes 1572868
  138.0 17.7 %copy-start.12 = (bf16[512,640]{1,0:T(8,128)(2,1)S(1)}, bf16[512,640]{1,0:T(8,128)(2,1)}, u32[]{:S(2)}) copy-start(bf16[512,640]{1,0:T(8,128)(2,1)} %get-tuple-element.104) | copy-start | bytes 1966084
  138.0 17.7 %collective-permute-start.15 = (bf16[512,640]{1,0:T(8,128)(2,1)}, bf16[512,640]{1,0:T(8,128)(2,1)S(1)}, u32[]{:S(2)}, u32[]{:S(2)}) collective-permute-start(bf16[512,640]{1,0:T(8,128)(2,1)} %get-tuple-element.104), channel_id=1, source_target_pairs={{0,8},{2,10},{4,12},{6,14},{24,16},{26,18},{28,20},{30,22},{1,9},{... | collective-permute-start | bytes 1966088 | tf_op jit(solution)/shard_map/ppermute | solution.py:78
  140.6 14.2 %collective-permute-start.16 = (bf16[512,512]{1,0:T(8,128)(2,1)S(1)}, bf16[512,512]{1,0:T(8,128)(2,1)S(1)}, u32[]{:S(2)}, u32[]{:S(2)}) collective-permute-start(bf16[512,512]{1,0:T(8,128)(2,1)S(1)} %bitcast.46), channel_id=1, source_target_pairs={{8,16},{10,18},{12,20},{14,22},{16,8},{18,10},{20,12},{22,14},{9,1... | collective-permute-start | bytes 1572872 | tf_op jit(solution)/shard_map/ppermute | solution.py:78
  141.3 14.4 %collective-permute-start.17 = (bf16[512,512]{1,0:T(8,128)(2,1)S(1)}, bf16[512,512]{1,0:T(8,128)(2,1)S(1)}, u32[]{:S(2)}, u32[]{:S(2)}) collective-permute-start(bf16[512,512]{1,0:T(8,128)(2,1)S(1)} %collective-permute-done.14.a_6_), channel_id=1, source_target_pairs={{8,0},{10,2},{12,4},{14,6},{16,24},{18,26},{20,28},{22,30},{9,1},{... | collective-permute-start | bytes 1572872 | tf_op jit(solution)/shard_map/ppermute | solution.py:78
  154.8 1.8 copy-start.11
  154.8 7.4 %copy-start.15 = (bf16[512,512]{1,0:T(8,128)(2,1)}, bf16[512,512]{1,0:T(8,128)(2,1)S(1)}, u32[]{:S(2)}) copy-start(bf16[512,512]{1,0:T(8,128)(2,1)S(1)} %collective-permute-done.16.a_7_) | copy-start | bytes 1572868
  155.7 6.5 %copy-start.16 = (bf16[512,512]{1,0:T(8,128)(2,1)}, bf16[512,512]{1,0:T(8,128)(2,1)S(1)}, u32[]{:S(2)}) copy-start(bf16[512,512]{1,0:T(8,128)(2,1)S(1)} %collective-permute-done.17.a_8_) | copy-start | bytes 1572868
  155.9 18.5 %collective-permute-start.18 = (bf16[512,640]{1,0:T(8,128)(2,1)S(1)}, bf16[512,640]{1,0:T(8,128)(2,1)S(1)}, u32[]{:S(2)}, u32[]{:S(2)}) collective-permute-start(bf16[512,640]{1,0:T(8,128)(2,1)S(1)} %add_convert_fusion.3), channel_id=1, source_target_pairs={{8,16},{10,18},{12,20},{14,22},{16,8},{18,10},{20,12},{22,14},{9,1... | collective-permute-start | bytes 1966088 | tf_op jit(solution)/shard_map/ppermute | solution.py:78
  156.6 17.8 %collective-permute-start.19 = (bf16[512,640]{1,0:T(8,128)(2,1)S(1)}, bf16[512,640]{1,0:T(8,128)(2,1)S(1)}, u32[]{:S(2)}, u32[]{:S(2)}) collective-permute-start(bf16[512,640]{1,0:T(8,128)(2,1)S(1)} %copy-done.11), channel_id=1, source_target_pairs={{0,8},{2,10},{4,12},{6,14},{24,16},{26,18},{28,20},{30,22},{1,9},{... | collective-permute-start | bytes 1966088 | tf_op jit(solution)/shard_map/ppermute | solution.py:78
  174.3 1.2 copy-start.10
  174.4 12.7 %collective-permute-start.22 = (bf16[1024,1024]{1,0:T(8,128)(2,1)}, bf16[1024,1024]{1,0:T(8,128)(2,1)S(1)}, u32[]{:S(2)}, u32[]{:S(2)}) collective-permute-start(bf16[1024,1024]{1,0:T(8,128)(2,1)} %get-tuple-element.117), channel_id=1, source_target_pairs={{0,1},{1,0},{2,3},{3,2},{4,5},{5,4},{6,7},{7,6},{8,9},{9,8},{10,11... | collective-permute-start | bytes 6291464 | tf_op jit(solution)/shard_map/ppermute | solution.py:481
  174.6 16.7 %collective-permute-start.21 = (bf16[512,640]{1,0:T(8,128)(2,1)S(1)}, bf16[512,640]{1,0:T(8,128)(2,1)S(1)}, u32[]{:S(2)}, u32[]{:S(2)}) collective-permute-start(bf16[512,640]{1,0:T(8,128)(2,1)S(1)} %add_convert_fusion.1), channel_id=1, source_target_pairs={{8,16},{10,18},{12,20},{14,22},{16,8},{18,10},{20,12},{22,14},{9,1... | collective-permute-start | bytes 1966088 | tf_op jit(solution)/shard_map/ppermute | solution.py:78
  175.7 27.7 %collective-permute-start.20 = (bf16[512,640]{1,0:T(8,128)(2,1)S(1)}, bf16[512,640]{1,0:T(8,128)(2,1)S(1)}, u32[]{:S(2)}, u32[]{:S(2)}) collective-permute-start(bf16[512,640]{1,0:T(8,128)(2,1)S(1)} %add_convert_fusion.2), channel_id=1, source_target_pairs={{0,8},{2,10},{4,12},{6,14},{8,0},{10,2},{12,4},{14,6},{16,24},{18,... | collective-permute-start | bytes 1966088 | tf_op jit(solution)/shard_map/ppermute | solution.py:78
  180.9 6.4 %copy-start.5 = (bf16[1024,1024]{1,0:T(8,128)(2,1)S(1)}, bf16[1024,1024]{1,0:T(8,128)(2,1)}, u32[]{:S(2)}) copy-start(bf16[1024,1024]{1,0:T(8,128)(2,1)} %get-tuple-element.126) | copy-start | bytes 6291460
  187.1 14.5 %copy-start.25 = (bf16[512,256]{1,0:T(8,128)(2,1)S(1)}, bf16[512,256]{1,0:T(8,128)(2,1)}, u32[]{:S(2)}) copy-start(bf16[512,256]{1,0:T(8,128)(2,1)} %get-tuple-element.125) | copy-start | bytes 786436
  187.1 16.2 %copy-start.18 = (bf16[512,256]{1,0:T(8,128)(2,1)S(1)}, bf16[512,256]{1,0:T(8,128)(2,1)}, u32[]{:S(2)}) copy-start(bf16[512,256]{1,0:T(8,128)(2,1)} %get-tuple-element.123) | copy-start | bytes 786436
  187.1 14.5 %collective-permute-start.23 = (bf16[512,256]{1,0:T(8,128)(2,1)}, bf16[512,256]{1,0:T(8,128)(2,1)S(1)}, u32[]{:S(2)}, u32[]{:S(2)}) collective-permute-start(bf16[512,256]{1,0:T(8,128)(2,1)} %get-tuple-element.124), channel_id=1, source_target_pairs={{0,8},{2,10},{4,12},{6,14},{8,0},{10,2},{12,4},{14,6},{16,24},{18,... | collective-permute-start | bytes 786440 | tf_op jit(solution)/shard_map/ppermute | solution.py:73
  188.2 29.2 %copy-start.9 = (bf16[512,640]{1,0:T(8,128)(2,1)S(1)}, bf16[512,640]{1,0:T(8,128)(2,1)}, u32[]{:S(2)}) copy-start(bf16[512,640]{1,0:T(8,128)(2,1)} %get-tuple-element.132) | copy-start | bytes 1966084
  188.2 25.7 %collective-permute-start.26 = (bf16[256,1024]{1,0:T(8,128)(2,1)S(1)}, bf16[256,1024]{1,0:T(8,128)(2,1)S(1)}, u32[]{:S(2)}, u32[]{:S(2)}) collective-permute-start(bf16[256,1024]{1,0:T(8,128)(2,1)S(1)} %get-tuple-element.140), channel_id=1, source_target_pairs={{0,2},{2,0},{4,6},{6,4},{8,10},{10,8},{12,14},{14,12},{16,18},{18,... | collective-permute-start | bytes 1572872 | tf_op jit(solution)/shard_map/ppermute | solution.py:73
  189.8 24.7 %collective-permute-start.27 = (bf16[256,1024]{1,0:T(8,128)(2,1)S(1)}, bf16[256,1024]{1,0:T(8,128)(2,1)S(1)}, u32[]{:S(2)}, u32[]{:S(2)}) collective-permute-start(bf16[256,1024]{1,0:T(8,128)(2,1)S(1)} %get-tuple-element.139), channel_id=1, source_target_pairs={{0,4},{2,6},{4,0},{6,2},{8,12},{10,14},{12,8},{14,10},{16,20},{18,... | collective-permute-start | bytes 1572872 | tf_op jit(solution)/shard_map/ppermute | solution.py:73
  191.3 23.2 %collective-permute-start.28 = (bf16[256,1024]{1,0:T(8,128)(2,1)S(1)}, bf16[256,1024]{1,0:T(8,128)(2,1)S(1)}, u32[]{:S(2)}, u32[]{:S(2)}) collective-permute-start(bf16[256,1024]{1,0:T(8,128)(2,1)S(1)} %get-tuple-element.138), channel_id=1, source_target_pairs={{0,6},{2,4},{4,2},{6,0},{8,14},{10,12},{12,10},{14,8},{16,22},{18,... | collective-permute-start | bytes 1572872 | tf_op jit(solution)/shard_map/ppermute | solution.py:73
  201.6 12.3 %collective-permute-start.25 = (bf16[512,256]{1,0:T(8,128)(2,1)S(1)}, bf16[512,256]{1,0:T(8,128)(2,1)S(1)}, u32[]{:S(2)}, u32[]{:S(2)}) collective-permute-start(bf16[512,256]{1,0:T(8,128)(2,1)S(1)} %copy-done.25), channel_id=1, source_target_pairs={{0,8},{2,10},{4,12},{6,14},{8,0},{10,2},{12,4},{14,6},{16,24},{18,... | collective-permute-start | bytes 786440 | tf_op jit(solution)/shard_map/ppermute | solution.py:73
  203.4 14.0 %collective-permute-start.24 = (bf16[512,256]{1,0:T(8,128)(2,1)S(1)}, bf16[512,256]{1,0:T(8,128)(2,1)S(1)}, u32[]{:S(2)}, u32[]{:S(2)}) collective-permute-start(bf16[512,256]{1,0:T(8,128)(2,1)S(1)} %add_convert_fusion.10), channel_id=1, source_target_pairs={{0,16},{2,18},{4,20},{6,22},{8,24},{10,26},{12,28},{14,30},{16,0},... | collective-permute-start | bytes 786440 | tf_op jit(solution)/shard_map/ppermute | solution.py:73
  217.4 1.0 copy-start.20
  218.5 6.1 %collective-permute-start.29 = (bf16[128,896]{1,0:T(8,128)(2,1)S(1)}, bf16[128,896]{1,0:T(8,128)(2,1)S(1)}, u32[]{:S(2)}, u32[]{:S(2)}) collective-permute-start(bf16[128,896]{1,0:T(8,128)(2,1)S(1)} %get-tuple-element.155), channel_id=1, source_target_pairs={{0,2},{2,0},{4,6},{6,4},{8,10},{10,8},{12,14},{14,12},{16,18},{18,... | collective-permute-start | bytes 688136 | tf_op jit(solution)/shard_map/ppermute | solution.py:73
  220.1 7.5 %collective-permute-start.30 = (bf16[128,896]{1,0:T(8,128)(2,1)S(1)}, bf16[128,896]{1,0:T(8,128)(2,1)S(1)}, u32[]{:S(2)}, u32[]{:S(2)}) collective-permute-start(bf16[128,896]{1,0:T(8,128)(2,1)S(1)} %get-tuple-element.156), channel_id=1, source_target_pairs={{0,4},{2,6},{4,0},{6,2},{8,12},{10,14},{12,8},{14,10},{16,20},{18,... | collective-permute-start | bytes 688136 | tf_op jit(solution)/shard_map/ppermute | solution.py:73
  221.6 7.0 %copy-start = (s32[48]{0:T(128)S(1)}, s32[48]{0:T(128)}, u32[]{:S(2)}) copy-start(s32[48]{0:T(128)} %stack.179.a_0_.scalars) | copy-start | bytes 580
  221.6 7.0 %collective-permute-start.31 = (bf16[128,896]{1,0:T(8,128)(2,1)S(1)}, bf16[128,896]{1,0:T(8,128)(2,1)S(1)}, u32[]{:S(2)}, u32[]{:S(2)}) collective-permute-start(bf16[128,896]{1,0:T(8,128)(2,1)S(1)} %get-tuple-element.153), channel_id=1, source_target_pairs={{0,6},{2,4},{4,2},{6,0},{8,14},{10,12},{12,10},{14,8},{16,22},{18,... | collective-permute-start | bytes 688136 | tf_op jit(solution)/shard_map/ppermute | solution.py:73

commit v5 on v4

--- a/solution.py
+++ b/solution.py
@@ -157,6 +157,47 @@
     d_gate = (cot * up * sig * (1.0 + gate * (1.0 - sig))).astype(BF)
     d_up = (cot * gate * sig).astype(BF)
     return d_gate, d_up
+
+
+def pack_kernel(scalars, sent, got, x_ref, cot_ref, gate_ref, up_ref, *outs, chunks, quarter):
+    rows, width = x_ref.shape
+    half = rows // 2
+    live = BAL
+    for i in range(sent.shape[1]):
+        live = live + sent[0, i] - got[0, i]
+    is_live = lax.broadcasted_iota(jnp.int32, (rows, 1), 0) < live
+    x_half = x_ref[pl.ds(pl.multiple_of(scalars[DEVS] * half, half), half), :]
+    for s, out in enumerate(outs):
+        start = scalars[DEVS + 2 + s] * quarter
+        out[:, :width] = x_half
+        col = width
+        for k in (1, 0):
+            spot = pl.ds(pl.multiple_of(start + sum(chunks[:k]), 128), chunks[k])
+            cot = jnp.where(is_live, cot_ref[:, spot].astype(F32), 0.0).astype(BF)
+            for part in (cot[:half], cot[half:]):
+                out[:, col : col + chunks[k]] = part
+                col += chunks[k]
+        spot = pl.ds(pl.multiple_of(start + chunks[0], 128), chunks[1])
+        for ref in (gate_ref, up_ref):
+            out[:, col : col + chunks[1]] = ref[:, spot]
+            col += chunks[1]
+
+
+def pack_parcels(scalars, sent, got, x_in, cotangent, w_gate, w_up, chunks):
+    rows, width = x_in.shape
+    quarter = sum(chunks)
+    vmem = pl.BlockSpec(memory_space=pltpu.VMEM)
+    smem = pl.BlockSpec(memory_space=pltpu.SMEM)
+    wide = width + 2 * quarter + 2 * chunks[1]
+    return pl.pallas_call(
+        lambda *a: pack_kernel(*a, chunks=chunks, quarter=quarter),
+        in_specs=[smem] * 3 + [vmem] * 4,
+        out_specs=[vmem] * len(CREW),
+        out_shape=[jax.ShapeDtypeStruct((rows // 2, wide), BF)] * len(CREW),
+        compiler_params=pltpu.CompilerParams(vmem_limit_bytes=32 * 1024 * 1024),
+        cost_estimate=pl.CostEstimate(flops=0, bytes_accessed=2**23, transcendentals=0),
+        name="pack_parcels",
+    )(scalars, sent, got, x_in, cotangent, w_gate, w_up)
 
 
 def first_kernel(scalars, mine_ref, other_ref, low_ref, high_ref, *refs, counts):
@@ -305,7 +346,7 @@
             pltpu.SemaphoreType.DMA((DEVS,)),
         ],
         6 * rows * width * ck,
-        56,
+        32,
     )
     return d, parts
 
@@ -325,7 +366,7 @@
         [jax.ShapeDtypeStruct((rows, width // 2), BF)] * 2,
         [pltpu.VMEM((width, wide), BF), pltpu.SemaphoreType.DMA((DEVS,))],
         2 * rows * width * wide,
-        56,
+        24,
     )
 
 
@@ -354,7 +395,7 @@
             pltpu.SemaphoreType.DMA((DEVS,)),
         ],
         8 * rows * width * ck,
-        56,
+        24,
     )
 
 
@@ -373,23 +414,27 @@
         [jax.ShapeDtypeStruct((deep, ck), BF)] * len(CHAIN),
         [pltpu.VMEM((rows, deep), BF), pltpu.VMEM((width, ck), BF)],
         2 * rows * width * ck,
-        56,
+        24,
     )
 
 
 def join_kernel(scalars, *refs, quarter):
     out = refs[-1]
-    for s in range(len(CREW)):
-        start = scalars[DEVS + 2 + s] * quarter
-        out[:, pl.ds(pl.multiple_of(start, 128), quarter)] = refs[s][...].astype(F32)
+    for i, ref in enumerate(refs[:-1]):
+        ck = ref.shape[1]
+        start = scalars[DEVS + 2 + i % len(CREW)] * quarter
+        if i >= len(CREW):
+            start = start + refs[0].shape[1]
+        out[:, pl.ds(pl.multiple_of(start, 128), ck)] = ref[...].astype(F32)
 
 
 def join_call(scalars, pieces):
-    depth, quarter = pieces[0].shape
+    depth = pieces[0].shape[0]
+    quarter = pieces[0].shape[1] + pieces[-1].shape[1]
     vmem = pl.BlockSpec(memory_space=pltpu.VMEM)
     return pl.pallas_call(
         lambda *a: join_kernel(*a, quarter=quarter),
-        in_specs=[pl.BlockSpec(memory_space=pltpu.SMEM)] + [vmem] * len(CREW),
+        in_specs=[pl.BlockSpec(memory_space=pltpu.SMEM)] + [vmem] * len(pieces),
         out_specs=vmem,
         out_shape=jax.ShapeDtypeStruct((depth, len(CREW) * quarter), F32),
         compiler_params=pltpu.CompilerParams(vmem_limit_bytes=16 * 1024 * 1024),
@@ -432,15 +477,9 @@
     own_far, own_near, x_in, cotangent, w_gate, w_up = tie(
         own_far, own_near, x_in, cotangent, w_gate, w_up
     )
-
-    live = jnp.arange(rows) < live_rows_of(send_counts, recv_counts)
-    cotangent = jnp.where(live[:, None], cotangent, jnp.zeros((), BF))
-    x_half = lax.dynamic_slice_in_dim(x_in, core * (rows // 2), rows // 2, 0)
-    parcels = []
-    for q in places:
-        cot = [columns(cotangent, q, offsets[k], chunks[k]) for k in (1, 0)]
-        halves = [c[h : h + rows // 2] for c in cot for h in (0, rows // 2)]
-        parcels.append(jnp.concatenate([x_half, *halves, piece_of_weights(q, 1)], axis=1))
+    parcels = pack_parcels(
+        scalars, send_counts, recv_counts, x_in, cotangent, w_gate, w_up, chunks
+    )
     rest = jnp.concatenate(rest, axis=0)
     rest, own_far, *parcels = tie(rest, own_far, *parcels)
 
@@ -453,8 +492,8 @@
     rest_both = send(rest_far, NEAR)
     mine = jnp.stack(parcels)
     other = lax.ppermute(mine, "mp", swap)
-    rest_both, other, mine = tie(rest_both, other, mine)
     second = mine[:, :, width + 2 * quarter :].reshape(crew * depth, 2 * chunks[1])
+    rest_both, other, second = tie(rest_both, other, second)
 
     cot_second = width
     cot_first = width + 2 * chunks[1]
@@ -491,12 +530,15 @@
             for s in range(crew)
         ]
     )
+    from_near, r3a, r3b = tie(from_near, r3a, r3b)
     sum_far = send(add(q_far, from_near), FAR)
     sum_near = send(q_near, NEAR)
-    r3a, r3b, sum_far, sum_near, *rows_x = tie(r3a, r3b, sum_far, sum_near, *rows_x)
-    sums = jnp.concatenate([add(p0, r3a, r3b), add(q_own, sum_near, sum_far)], axis=1)
-    pieces = crew_swap([sums[s * depth : (s + 1) * depth] for s in range(crew)])
-    return add(*rows_x), join_call(scalars, pieces)
+    sums = add(p0, r3a, r3b)
+    firsts = crew_swap([sums[s * depth : (s + 1) * depth] for s in range(crew)])
+    sum_far, sum_near, *rows_x = tie(sum_far, sum_near, *rows_x)
+    sums = add(q_own, sum_near, sum_far)
+    lasts = crew_swap([sums[s * depth : (s + 1) * depth] for s in range(crew)])
+    return add(*rows_x), join_call(scalars, firsts + lasts)
 
 
 def solution(mesh):

time: 231 us -> 217 us (0.939)
  Pallas kernels: 49.4 us -> 39.4 us
  local copies, waits for them, and re-layouts: 11.6 us -> 4.53 us
  waiting for transfers between devices: 109 us -> 113 us
    ppermute x7, waiting for transfers between devices: 0.97 us -> 12.6 us  [along(): lax.ppermute(value, 'dp', [(crew * a + q, crew * b + q) for a, b in moves...]
    pallas_call x4, Pallas kernels: 47.5 us -> 36.5 us  [kernel_call(): pl.pallas_call(body, grid_spec=pltpu.PrefetchScalarGridSpec(num_scalar_pr...]
    ppermute x23 -> x26, waiting for transfers between devices: 108 us -> 101 us  [send(): return lax.ppermute(value, 'dp', [(i, i ^ mask) for i in range(DEVS)])]
    unnamed x67 -> x12, local copies, waits for them, and re-layouts: 6.95 us -> 1.52 us
    ppermute x23 -> x26, starting transfers between devices: 34.2 us -> 36 us  [send(): return lax.ppermute(value, 'dp', [(i, i ^ mask) for i in range(DEVS)])]
  transfers between devices with their start and end apart: 32 -> 35, of which waited for: 18 -> 19; matrix products, arithmetic and copies ran while one was open for 3% -> 3% of each run, Pallas kernels for 21% -> 17%
where the time goes in v5:
time: 217 us
  waiting for transfers between devices  113 us (52%)
  starting transfers between devices  51.4 us (24%)
  Pallas kernels  39.4 us (18%)
  other arithmetic  7.11 us (3%)
  local copies, waits for them, and re-layouts  4.53 us (2%)
    ppermute x26, waiting for transfers between devices, send(): return lax.ppermute(value, 'dp', [(i, i ^ mask) for i in range(DEVS)])  101 us
    pallas_call x4, Pallas kernels, kernel_call(): pl.pallas_call(body, grid_spec=pltpu.PrefetchScalarGridSpec(num_scalar_pr...  36.5 us
    ppermute x26, starting transfers between devices, send(): return lax.ppermute(value, 'dp', [(i, i ^ mask) for i in range(DEVS)])  36 us
    ppermute x7, starting transfers between devices, along(): lax.ppermute(value, 'dp', [(crew * a + q, crew * b + q) for a, b in moves...  15.3 us
    ppermute x7, waiting for transfers between devices, along(): lax.ppermute(value, 'dp', [(crew * a + q, crew * b + q) for a, b in moves...  12.6 us
  transfers between devices with their start and end apart: 35, of which 19 were waited for; matrix products, arithmetic and copies ran while one was open for 3% of the time, Pallas kernels for 17%

profile of v5, /device:TPU:0, one launch (start us, length us, event | category | flops | bytes accessed | tf_op | source)
XLA Modules:
  0.0 216.9 jit_solution(11051690803436805267)
XLA Ops:
  0.7 1.6 constant_dynamic-slice_fusion
  2.4 4.1 %collective-permute-start.3 = (bf16[128,1280]{1,0:T(8,128)(2,1)S(1)}, bf16[128,1280]{1,0:T(8,128)(2,1)S(1)}, u32[]{:S(2)}, u32[]{:S(2)}) collective-permute-start(bf16[128,1280]{1,0:T(8,128)(2,1)S(1)} %pad_maximum_fusion.5.a_5_.a_2_), channel_id=1, source_target_pairs={{0,16},{2,18},{4,20},{6,22},{8,24},{10,26},{12,28},{14,30},{16,0},... | collective-permute-start | bytes 983048 | tf_op jit(solution)/shard_map/ppermute | solution.py:73
  6.5 1.6 collective-permute-start.4
  8.0 0.7 pad_maximum_fusion.2
  8.8 1.5 collective-permute-start
  10.3 0.7 pad_maximum_fusion.3
  11.0 1.5 collective-permute-start.1
  12.6 0.7 pad_maximum_fusion.4
  13.3 0.5 collective-permute-start.2
  13.8 0.5 broadcast.9
  14.3 0.7 stack.174.a_0_.scalars
  15.1 6.2 %collective-permute-done.3.a_7_.a_4_ = bf16[128,1280]{1,0:T(8,128)(2,1)S(1)} collective-permute-done((bf16[128,1280]{1,0:T(8,128)(2,1)S(1)}, bf16[128,1280]{1,0:T(8,128)(2,1)S(1)}, u32[]{:S(2)}, u32[]{:S(2)}) %collective-permute-start.3) | collective-permute-done | bytes 327712 | tf_op jit(solution)/shard_map/ppermute | solution.py:73
  21.6 1.5 copy-done.2
  23.1 1.0 pack_parcels.1
  24.2 2.8 %collective-permute-done.1 = bf16[128,1280]{1,0:T(8,128)(2,1)} collective-permute-done((bf16[128,1280]{1,0:T(8,128)(2,1)}, bf16[128,1280]{1,0:T(8,128)(2,1)}, u32[]{:S(2)}, u32[]{:S(2)}) %collective-permute-start.1) | collective-permute-done | bytes 327712 | tf_op jit(solution)/shard_map/ppermute | solution.py:73
  27.0 1.2 pad_maximum_fusion.1.a_9_.a_6_
  28.2 0.5 collective-permute-start.7
  28.7 1.5 collective-permute-start.10
  30.2 1.5 collective-permute-start.8
  31.7 0.5 collective-permute-start.9
  32.7 9.5 %collective-permute-done.7.a_8_.a_5_ = bf16[128,1280]{1,0:T(8,128)(2,1)S(1)} collective-permute-done((bf16[128,1280]{1,0:T(8,128)(2,1)S(1)}, bf16[128,1280]{1,0:T(8,128)(2,1)S(1)}, u32[]{:S(2)}, u32[]{:S(2)}) %collective-permute-start.7) | collective-permute-done | bytes 327712 | tf_op jit(solution)/shard_map/ppermute | solution.py:73
  42.2 32.7 %collective-permute-done.5.a_11_.a_8_ = bf16[384,1280]{1,0:T(8,128)(2,1)S(1)} collective-permute-done((bf16[384,1280]{1,0:T(8,128)(2,1)S(1)}, bf16[384,1280]{1,0:T(8,128)(2,1)S(1)}, u32[]{:S(2)}, u32[]{:S(2)}) %collective-permute-start.5) | collective-permute-done | bytes 983072 | tf_op jit(solution)/shard_map/ppermute | solution.py:73
  74.8 2.7 %collective-permute-done.6.a_10_.a_7_ = bf16[384,1280]{1,0:T(8,128)(2,1)S(1)} collective-permute-done((bf16[384,1280]{1,0:T(8,128)(2,1)S(1)}, bf16[384,1280]{1,0:T(8,128)(2,1)S(1)}, u32[]{:S(2)}, u32[]{:S(2)}) %collective-permute-start.6) | collective-permute-done | bytes 983072 | tf_op jit(solution)/shard_map/ppermute | solution.py:73
  77.5 0.6 pad_maximum_fusion.a_1_.a_3_.a_4_.mine_ref
  78.2 1.2 collective-permute-start.11
  79.4 22.9 %collective-permute-done.11.a_12_.a_9_ = bf16[384,1280]{1,0:T(8,128)(2,1)S(1)} collective-permute-done((bf16[384,1280]{1,0:T(8,128)(2,1)S(1)}, bf16[384,1280]{1,0:T(8,128)(2,1)S(1)}, u32[]{:S(2)}, u32[]{:S(2)}) %collective-permute-start.11) | collective-permute-done | bytes 983072 | tf_op jit(solution)/shard_map/ppermute | solution.py:73
  102.4 1.1 collective-permute-start.13
  103.5 4.3 %collective-permute-start.14 = (bf16[512,512]{1,0:T(8,128)(2,1)S(1)}, bf16[512,512]{1,0:T(8,128)(2,1)S(1)}, u32[]{:S(2)}, u32[]{:S(2)}) collective-permute-start(bf16[512,512]{1,0:T(8,128)(2,1)S(1)} %bitcast.44), channel_id=1, source_target_pairs={{0,16},{2,18},{4,20},{6,22},{8,24},{10,26},{12,28},{14,30},{16,0},... | collective-permute-start | bytes 1572872 | tf_op jit(solution)/shard_map/ppermute | solution.py:73
  107.8 13.5 %first_chunk.1 = (bf16[1024,1280]{1,0:T(8,128)(2,1)S(1)}, bf16[512,640]{1,0:T(8,128)(2,1)S(1)}, bf16[512,640]{1,0:T(8,128)(2,1)S(1)}, bf16[512,640]{1,0:T(8,128)(2,1)S(1)}, bf16[512,640]{1,0:T(8,128)(2,1)S(1)}) custom-call(s32[48]{0:T(128)S(1)} %stack.174.a_0_.scalars, bf16[4,128,4352]{2,1,0:T(8,128)(2,1)S(1)} %pad_maximum_fusion.a_1_.a_3_.a_4_.mine_ref, ...), custom_call_target="tpu_custom_call" | custom-call | flops 8053063680 | bytes 8388608 | tf_op jit(solution)/shard_map/first_chunk/pallas_call | solution.py:296
  121.3 5.7 %collective-permute-done.13.a_5_ = bf16[512,512]{1,0:T(8,128)(2,1)S(1)} collective-permute-done((bf16[512,512]{1,0:T(8,128)(2,1)S(1)}, bf16[512,512]{1,0:T(8,128)(2,1)S(1)}, u32[]{:S(2)}, u32[]{:S(2)}) %collective-permute-start.13) | collective-permute-done | bytes 524320 | tf_op jit(solution)/shard_map/ppermute | solution.py:73
  127.1 3.5 %collective-permute-done.14.a_6_ = bf16[512,512]{1,0:T(8,128)(2,1)S(1)} collective-permute-done((bf16[512,512]{1,0:T(8,128)(2,1)S(1)}, bf16[512,512]{1,0:T(8,128)(2,1)S(1)}, u32[]{:S(2)}, u32[]{:S(2)}) %collective-permute-start.14) | collective-permute-done | bytes 524320 | tf_op jit(solution)/shard_map/ppermute | solution.py:73
  130.6 2.4 %collective-permute-start.15 = (bf16[512,640]{1,0:T(8,128)(2,1)S(1)}, bf16[512,640]{1,0:T(8,128)(2,1)S(1)}, u32[]{:S(2)}, u32[]{:S(2)}) collective-permute-start(bf16[512,640]{1,0:T(8,128)(2,1)S(1)} %get-tuple-element.112), channel_id=1, source_target_pairs={{0,8},{2,10},{4,12},{6,14},{24,16},{26,18},{28,20},{30,22},{1,9},{... | collective-permute-start | bytes 1966088 | tf_op jit(solution)/shard_map/ppermute | solution.py:78
  133.0 0.7 collective-permute-start.16
  133.7 1.3 collective-permute-start.17
  135.0 9.0 %rows_grad.1 = (bf16[1024,1024]{1,0:T(8,128)(2,1)S(1)}, bf16[1024,1024]{1,0:T(8,128)(2,1)S(1)}) custom-call(s32[48]{0:T(128)S(1)} %stack.174.a_0_.scalars, bf16[1024,1280]{1,0:T(8,128)(2,1)S(1)} %get-tuple-element.109.a_1_, bf16[128,1280]{1,0:T(8,128)(2,1)S(1)} %pad_maximum_fusion.5.a_5_.a_2_, bf16[128,1280]{1,0:T(8,128)(2,1)} %collective-permute-done.4.a_6_.a_3_, ...), custom_call_target="tpu_custom_call" | custom-call | flops 5368709120 | bytes 8388608 | tf_op jit(solution)/shard_map/rows_grad/pallas_call | solution.py:296
  144.0 4.1 %collective-permute-done.17.a_8_ = bf16[512,512]{1,0:T(8,128)(2,1)S(1)} collective-permute-done((bf16[512,512]{1,0:T(8,128)(2,1)S(1)}, bf16[512,512]{1,0:T(8,128)(2,1)S(1)}, u32[]{:S(2)}, u32[]{:S(2)}) %collective-permute-start.17) | collective-permute-done | bytes 524320 | tf_op jit(solution)/shard_map/ppermute | solution.py:78
  148.3 0.7 collective-permute-start.18
  149.0 4.3 %collective-permute-start.19 = (bf16[512,640]{1,0:T(8,128)(2,1)S(1)}, bf16[512,640]{1,0:T(8,128)(2,1)S(1)}, u32[]{:S(2)}, u32[]{:S(2)}) collective-permute-start(bf16[512,640]{1,0:T(8,128)(2,1)S(1)} %get-tuple-element.114), channel_id=1, source_target_pairs={{0,8},{2,10},{4,12},{6,14},{24,16},{26,18},{28,20},{30,22},{1,9},{... | collective-permute-start | bytes 1966088 | tf_op jit(solution)/shard_map/ppermute | solution.py:78
  153.3 10.7 %second_chunk.1 = (bf16[1024,1024]{1,0:T(8,128)(2,1)S(1)}, bf16[1024,1024]{1,0:T(8,128)(2,1)S(1)}, bf16[1024,256]{1,0:T(8,128)(2,1)S(1)}) custom-call(s32[48]{0:T(128)S(1)} %stack.174.a_0_.scalars, bf16[4,128,4352]{2,1,0:T(8,128)(2,1)S(1)} %pad_maximum_fusion.a_1_.a_3_.a_4_.mine_ref, bf16[4,128,4352]{2,1,0:T(8,128)(2,1)S(1)} %collective-permute-done.12.a_2_.other_ref, ...), custom_call_target="tpu_custom_call" | custom-call | flops 4294967296 | bytes 8388608 | tf_op jit(solution)/shard_map/second_chunk/pallas_call | solution.py:296
  164.0 1.0 collective-permute-done.19
  165.2 0.7 collective-permute-start.23
  166.1 5.1 %collective-permute-start.22 = (bf16[512,640]{1,0:T(8,128)(2,1)S(1)}, bf16[512,640]{1,0:T(8,128)(2,1)S(1)}, u32[]{:S(2)}, u32[]{:S(2)}) collective-permute-start(bf16[512,640]{1,0:T(8,128)(2,1)S(1)} %add_convert_fusion.2), channel_id=1, source_target_pairs={{0,8},{2,10},{4,12},{6,14},{8,0},{10,2},{12,4},{14,6},{16,24},{18,... | collective-permute-start | bytes 1966088 | tf_op jit(solution)/shard_map/ppermute | solution.py:78
  171.2 3.4 %gate_grad.1 = (bf16[512,256]{1,0:T(8,128)(2,1)S(1)}, bf16[512,256]{1,0:T(8,128)(2,1)S(1)}, bf16[512,256]{1,0:T(8,128)(2,1)S(1)}, bf16[512,256]{1,0:T(8,128)(2,1)S(1)}) custom-call(s32[48]{0:T(128)S(1)} %stack.174.a_0_.scalars, bf16[4,128,4352]{2,1,0:T(8,128)(2,1)S(1)} %pad_maximum_fusion.a_1_.a_3_.a_4_.mine_ref, ...), custom_call_target="tpu_custom_call" | custom-call | flops 1073741824 | bytes 8388608 | tf_op jit(solution)/shard_map/gate_grad/pallas_call | solution.py:296
  174.7 1.0 add_convert_fusion.5
  175.6 1.6 collective-permute-start.26
  177.2 1.5 collective-permute-start.27
  178.7 0.5 collective-permute-start.28
  179.2 7.5 %collective-permute-done.22 = bf16[512,640]{1,0:T(8,128)(2,1)S(1)} collective-permute-done((bf16[512,640]{1,0:T(8,128)(2,1)S(1)}, bf16[512,640]{1,0:T(8,128)(2,1)S(1)}, u32[]{:S(2)}, u32[]{:S(2)}) %collective-permute-start.22) | collective-permute-done | bytes 655392 | tf_op jit(solution)/shard_map/ppermute | solution.py:78
  186.7 2.4 %collective-permute-start.25 = (bf16[512,256]{1,0:T(8,128)(2,1)S(1)}, bf16[512,256]{1,0:T(8,128)(2,1)S(1)}, u32[]{:S(2)}, u32[]{:S(2)}) collective-permute-start(bf16[512,256]{1,0:T(8,128)(2,1)S(1)} %get-tuple-element.135), channel_id=1, source_target_pairs={{0,8},{2,10},{4,12},{6,14},{8,0},{10,2},{12,4},{14,6},{16,24},{18,... | collective-permute-start | bytes 786440 | tf_op jit(solution)/shard_map/ppermute | solution.py:73
  189.2 3.2 %collective-permute-done.21 = bf16[512,256]{1,0:T(8,128)(2,1)S(1)} collective-permute-done((bf16[512,256]{1,0:T(8,128)(2,1)S(1)}, bf16[512,256]{1,0:T(8,128)(2,1)S(1)}, u32[]{:S(2)}, u32[]{:S(2)}) %collective-permute-start.21) | collective-permute-done | bytes 262176 | tf_op jit(solution)/shard_map/ppermute | solution.py:73
  192.4 2.2 %collective-permute-start.24 = (bf16[512,256]{1,0:T(8,128)(2,1)S(1)}, bf16[512,256]{1,0:T(8,128)(2,1)S(1)}, u32[]{:S(2)}, u32[]{:S(2)}) collective-permute-start(bf16[512,256]{1,0:T(8,128)(2,1)S(1)} %add_convert_fusion.10), channel_id=1, source_target_pairs={{0,16},{2,18},{4,20},{6,22},{8,24},{10,26},{12,28},{14,30},{16,0},... | collective-permute-start | bytes 786440 | tf_op jit(solution)/shard_map/ppermute | solution.py:73
  194.9 6.2 %collective-permute-done.25 = bf16[512,256]{1,0:T(8,128)(2,1)S(1)} collective-permute-done((bf16[512,256]{1,0:T(8,128)(2,1)S(1)}, bf16[512,256]{1,0:T(8,128)(2,1)S(1)}, u32[]{:S(2)}, u32[]{:S(2)}) %collective-permute-start.25) | collective-permute-done | bytes 262176 | tf_op jit(solution)/shard_map/ppermute | solution.py:73
  201.1 1.5 collective-permute-start.29
  202.6 1.5 collective-permute-start.30
  204.2 0.5 collective-permute-start.31
  204.6 2.0 collective-permute-done.24
  206.7 1.6 collective-permute-start.32
  208.3 1.5 collective-permute-start.33
  209.8 0.9 collective-permute-start.34
  210.7 1.2 add_convert_fusion.4
  212.1 0.5 collective-permute-done.31.a_4_
  212.6 1.2 collective-permute-done.33.a_7_
  213.8 1.2 collective-permute-done.34.a_8_
  215.0 1.9 join_quarters.1
  (45 shorter events, 2.3 us)
Async XLA Ops:
  0.7 20.9 %copy-start.3 = (bf16[256,2048]{1,0:T(8,128)(2,1)S(1)}, bf16[256,2048]{1,0:T(8,128)(2,1)}, u32[]{:S(2)}) copy-start(bf16[256,2048]{1,0:T(8,128)(2,1)} %a_3_) | copy-start | bytes 3145732
  2.3 19.3 %copy-start = (bf16[128,3584]{1,0:T(8,128)(2,1)S(1)}, bf16[128,3584]{1,0:T(8,128)(2,1)}, u32[]{:S(2)}) copy-start(bf16[128,3584]{1,0:T(8,128)(2,1)} %a_5_) | copy-start | bytes 2752516
  2.3 19.3 %copy-start.1 = (bf16[128,3584]{1,0:T(8,128)(2,1)S(1)}, bf16[128,3584]{1,0:T(8,128)(2,1)}, u32[]{:S(2)}) copy-start(bf16[128,3584]{1,0:T(8,128)(2,1)} %a_6_) | copy-start | bytes 2752516
  2.3 19.3 %copy-start.4 = (s32[1,16]{1,0:T(1,128)S(1)}, s32[1,16]{1,0:T(1,128)}, u32[]{:S(2)}) copy-start(s32[1,16]{1,0:T(1,128)} %a_1_.1) | copy-start | bytes 196
  2.3 19.3 %copy-start.5 = (s32[1,16]{1,0:T(1,128)S(1)}, s32[1,16]{1,0:T(1,128)}, u32[]{:S(2)}) copy-start(s32[1,16]{1,0:T(1,128)} %a_2_.1) | copy-start | bytes 196
  2.4 18.9 %collective-permute-start.3 = (bf16[128,1280]{1,0:T(8,128)(2,1)S(1)}, bf16[128,1280]{1,0:T(8,128)(2,1)S(1)}, u32[]{:S(2)}, u32[]{:S(2)}) collective-permute-start(bf16[128,1280]{1,0:T(8,128)(2,1)S(1)} %pad_maximum_fusion.5.a_5_.a_2_), channel_id=1, source_target_pairs={{0,16},{2,18},{4,20},{6,22},{8,24},{10,26},{12,28},{14,30},{16,0},... | collective-permute-start | bytes 983048 | tf_op jit(solution)/shard_map/ppermute | solution.py:73
  6.5 15.1 %collective-permute-start.4 = (bf16[128,1280]{1,0:T(8,128)(2,1)S(1)}, bf16[128,1280]{1,0:T(8,128)(2,1)}, u32[]{:S(2)}, u32[]{:S(2)}) collective-permute-start(bf16[128,1280]{1,0:T(8,128)(2,1)S(1)} %pad_maximum_fusion.5.a_5_.a_2_), channel_id=1, source_target_pairs={{0,8},{2,10},{4,12},{6,14},{8,0},{10,2},{12,4},{14,6},{16,24},{18,... | collective-permute-start | bytes 983048 | tf_op jit(solution)/shard_map/ppermute | solution.py:73
  8.8 15.4 %collective-permute-start = (bf16[128,1280]{1,0:T(8,128)(2,1)}, bf16[128,1280]{1,0:T(8,128)(2,1)}, u32[]{:S(2)}, u32[]{:S(2)}) collective-permute-start(bf16[128,1280]{1,0:T(8,128)(2,1)} %pad_maximum_fusion.2), channel_id=1, source_target_pairs={{0,2},{2,0},{4,6},{6,4},{8,10},{10,8},{12,14},{14,12},{16,18},{18,... | collective-permute-start | bytes 983048 | tf_op jit(solution)/shard_map/ppermute | solution.py:73
  11.0 15.9 %collective-permute-start.1 = (bf16[128,1280]{1,0:T(8,128)(2,1)}, bf16[128,1280]{1,0:T(8,128)(2,1)}, u32[]{:S(2)}, u32[]{:S(2)}) collective-permute-start(bf16[128,1280]{1,0:T(8,128)(2,1)} %pad_maximum_fusion.3), channel_id=1, source_target_pairs={{0,4},{2,6},{4,0},{6,2},{8,12},{10,14},{12,8},{14,10},{16,20},{18,... | collective-permute-start | bytes 983048 | tf_op jit(solution)/shard_map/ppermute | solution.py:73
  13.3 13.7 %collective-permute-start.2 = (bf16[128,1280]{1,0:T(8,128)(2,1)}, bf16[128,1280]{1,0:T(8,128)(2,1)}, u32[]{:S(2)}, u32[]{:S(2)}) collective-permute-start(bf16[128,1280]{1,0:T(8,128)(2,1)} %pad_maximum_fusion.4), channel_id=1, source_target_pairs={{0,6},{2,4},{4,2},{6,0},{8,14},{10,12},{12,10},{14,8},{16,22},{18,... | collective-permute-start | bytes 983048 | tf_op jit(solution)/shard_map/ppermute | solution.py:73
  21.6 1.5 copy-start.2
  28.2 13.9 %collective-permute-start.7 = (bf16[128,1280]{1,0:T(8,128)(2,1)S(1)}, bf16[128,1280]{1,0:T(8,128)(2,1)S(1)}, u32[]{:S(2)}, u32[]{:S(2)}) collective-permute-start(bf16[128,1280]{1,0:T(8,128)(2,1)S(1)} %collective-permute-done.3.a_7_.a_4_), channel_id=1, source_target_pairs={{0,8},{2,10},{4,12},{6,14},{8,0},{10,2},{12,4},{14,6},{16,24},{18,... | collective-permute-start | bytes 983048 | tf_op jit(solution)/shard_map/ppermute | solution.py:73
  28.7 48.8 %collective-permute-start.10 = (bf16[128,4352]{1,0:T(8,128)(2,1)S(1)}, bf16[128,4352]{1,0:T(8,128)(2,1)S(1)}, u32[]{:S(2)}, u32[]{:S(2)}) collective-permute-start(bf16[128,4352]{1,0:T(8,128)(2,1)S(1)} %get-tuple-element.89), channel_id=1, source_target_pairs={{0,6},{2,4},{4,2},{6,0},{8,14},{10,12},{12,10},{14,8},{16,22},{18,... | collective-permute-start | bytes 3342344 | tf_op jit(solution)/shard_map/ppermute | solution.py:73
  30.2 47.3 %collective-permute-start.8 = (bf16[128,4352]{1,0:T(8,128)(2,1)S(1)}, bf16[128,4352]{1,0:T(8,128)(2,1)S(1)}, u32[]{:S(2)}, u32[]{:S(2)}) collective-permute-start(bf16[128,4352]{1,0:T(8,128)(2,1)S(1)} %get-tuple-element.87), channel_id=1, source_target_pairs={{0,2},{2,0},{4,6},{6,4},{8,10},{10,8},{12,14},{14,12},{16,18},{18,... | collective-permute-start | bytes 3342344 | tf_op jit(solution)/shard_map/ppermute | solution.py:73
  31.7 45.8 %collective-permute-start.9 = (bf16[128,4352]{1,0:T(8,128)(2,1)S(1)}, bf16[128,4352]{1,0:T(8,128)(2,1)S(1)}, u32[]{:S(2)}, u32[]{:S(2)}) collective-permute-start(bf16[128,4352]{1,0:T(8,128)(2,1)S(1)} %get-tuple-element.88), channel_id=1, source_target_pairs={{0,4},{2,6},{4,0},{6,2},{8,12},{10,14},{12,8},{14,10},{16,20},{18,... | collective-permute-start | bytes 3342344 | tf_op jit(solution)/shard_map/ppermute | solution.py:73
  32.2 42.6 %collective-permute-start.5 = (bf16[384,1280]{1,0:T(8,128)(2,1)S(1)}, bf16[384,1280]{1,0:T(8,128)(2,1)S(1)}, u32[]{:S(2)}, u32[]{:S(2)}) collective-permute-start(bf16[384,1280]{1,0:T(8,128)(2,1)S(1)} %pad_maximum_fusion.1.a_9_.a_6_), channel_id=1, source_target_pairs={{0,16},{2,18},{4,20},{6,22},{8,24},{10,26},{12,28},{14,30},{16,0},... | collective-permute-start | bytes 2949128 | tf_op jit(solution)/shard_map/ppermute | solution.py:73
  42.2 35.3 %collective-permute-start.6 = (bf16[384,1280]{1,0:T(8,128)(2,1)S(1)}, bf16[384,1280]{1,0:T(8,128)(2,1)S(1)}, u32[]{:S(2)}, u32[]{:S(2)}) collective-permute-start(bf16[384,1280]{1,0:T(8,128)(2,1)S(1)} %pad_maximum_fusion.1.a_9_.a_6_), channel_id=1, source_target_pairs={{0,8},{2,10},{4,12},{6,14},{8,0},{10,2},{12,4},{14,6},{16,24},{18,... | collective-permute-start | bytes 2949128 | tf_op jit(solution)/shard_map/ppermute | solution.py:73
  78.1 24.3 %collective-permute-start.12 = (bf16[4,128,4352]{2,1,0:T(8,128)(2,1)S(1)}, bf16[4,128,4352]{2,1,0:T(8,128)(2,1)S(1)}, u32[]{:S(2)}, u32[]{:S(2)}) collective-permute-start(bf16[4,128,4352]{2,1,0:T(8,128)(2,1)S(1)} %pad_maximum_fusion.a_1_.a_3_.a_4_.mine_ref), channel_id=1, source_target_pairs={{0,1},{1,0},{2,3},{3,2},{4,5},{5,4},{6,7},{7,6},{8,9},{9,8},{10,11... | collective-permute-start | bytes 13369352 | tf_op jit(solution)/shard_map/ppermute | solution.py:494
  78.2 24.2 %collective-permute-start.11 = (bf16[384,1280]{1,0:T(8,128)(2,1)S(1)}, bf16[384,1280]{1,0:T(8,128)(2,1)S(1)}, u32[]{:S(2)}, u32[]{:S(2)}) collective-permute-start(bf16[384,1280]{1,0:T(8,128)(2,1)S(1)} %collective-permute-done.5.a_11_.a_8_), channel_id=1, source_target_pairs={{0,8},{2,10},{4,12},{6,14},{8,0},{10,2},{12,4},{14,6},{16,24},{18,... | collective-permute-start | bytes 2949128 | tf_op jit(solution)/shard_map/ppermute | solution.py:73
  102.4 24.7 %collective-permute-start.13 = (bf16[512,512]{1,0:T(8,128)(2,1)S(1)}, bf16[512,512]{1,0:T(8,128)(2,1)S(1)}, u32[]{:S(2)}, u32[]{:S(2)}) collective-permute-start(bf16[512,512]{1,0:T(8,128)(2,1)S(1)} %bitcast.43), channel_id=1, source_target_pairs={{0,8},{2,10},{4,12},{6,14},{8,0},{10,2},{12,4},{14,6},{16,24},{18,... | collective-permute-start | bytes 1572872 | tf_op jit(solution)/shard_map/ppermute | solution.py:73
  103.5 27.1 %collective-permute-start.14 = (bf16[512,512]{1,0:T(8,128)(2,1)S(1)}, bf16[512,512]{1,0:T(8,128)(2,1)S(1)}, u32[]{:S(2)}, u32[]{:S(2)}) collective-permute-start(bf16[512,512]{1,0:T(8,128)(2,1)S(1)} %bitcast.44), channel_id=1, source_target_pairs={{0,16},{2,18},{4,20},{6,22},{8,24},{10,26},{12,28},{14,30},{16,0},... | collective-permute-start | bytes 1572872 | tf_op jit(solution)/shard_map/ppermute | solution.py:73
  130.6 17.5 %collective-permute-start.15 = (bf16[512,640]{1,0:T(8,128)(2,1)S(1)}, bf16[512,640]{1,0:T(8,128)(2,1)S(1)}, u32[]{:S(2)}, u32[]{:S(2)}) collective-permute-start(bf16[512,640]{1,0:T(8,128)(2,1)S(1)} %get-tuple-element.112), channel_id=1, source_target_pairs={{0,8},{2,10},{4,12},{6,14},{24,16},{26,18},{28,20},{30,22},{1,9},{... | collective-permute-start | bytes 1966088 | tf_op jit(solution)/shard_map/ppermute | solution.py:78
  133.0 11.0 %collective-permute-start.16 = (bf16[512,512]{1,0:T(8,128)(2,1)S(1)}, bf16[512,512]{1,0:T(8,128)(2,1)S(1)}, u32[]{:S(2)}, u32[]{:S(2)}) collective-permute-start(bf16[512,512]{1,0:T(8,128)(2,1)S(1)} %bitcast.45), channel_id=1, source_target_pairs={{8,16},{10,18},{12,20},{14,22},{16,8},{18,10},{20,12},{22,14},{9,1... | collective-permute-start | bytes 1572872 | tf_op jit(solution)/shard_map/ppermute | solution.py:78
  133.7 14.4 %collective-permute-start.17 = (bf16[512,512]{1,0:T(8,128)(2,1)S(1)}, bf16[512,512]{1,0:T(8,128)(2,1)S(1)}, u32[]{:S(2)}, u32[]{:S(2)}) collective-permute-start(bf16[512,512]{1,0:T(8,128)(2,1)S(1)} %collective-permute-done.14.a_6_), channel_id=1, source_target_pairs={{8,0},{10,2},{12,4},{14,6},{16,24},{18,26},{20,28},{22,30},{9,1},{... | collective-permute-start | bytes 1572872 | tf_op jit(solution)/shard_map/ppermute | solution.py:78
  148.3 15.7 %collective-permute-start.18 = (bf16[512,640]{1,0:T(8,128)(2,1)S(1)}, bf16[512,640]{1,0:T(8,128)(2,1)S(1)}, u32[]{:S(2)}, u32[]{:S(2)}) collective-permute-start(bf16[512,640]{1,0:T(8,128)(2,1)S(1)} %add_convert_fusion.3), channel_id=1, source_target_pairs={{8,16},{10,18},{12,20},{14,22},{16,8},{18,10},{20,12},{22,14},{9,1... | collective-permute-start | bytes 1966088 | tf_op jit(solution)/shard_map/ppermute | solution.py:78
  149.0 16.0 %collective-permute-start.19 = (bf16[512,640]{1,0:T(8,128)(2,1)S(1)}, bf16[512,640]{1,0:T(8,128)(2,1)S(1)}, u32[]{:S(2)}, u32[]{:S(2)}) collective-permute-start(bf16[512,640]{1,0:T(8,128)(2,1)S(1)} %get-tuple-element.114), channel_id=1, source_target_pairs={{0,8},{2,10},{4,12},{6,14},{24,16},{26,18},{28,20},{30,22},{1,9},{... | collective-permute-start | bytes 1966088 | tf_op jit(solution)/shard_map/ppermute | solution.py:78
  165.0 9.6 %collective-permute-start.20 = (bf16[1024,1024]{1,0:T(8,128)(2,1)S(1)}, bf16[1024,1024]{1,0:T(8,128)(2,1)S(1)}, u32[]{:S(2)}, u32[]{:S(2)}) collective-permute-start(bf16[1024,1024]{1,0:T(8,128)(2,1)S(1)} %get-tuple-element.123), channel_id=1, source_target_pairs={{0,1},{1,0},{2,3},{3,2},{4,5},{5,4},{6,7},{7,6},{8,9},{9,8},{10,11... | collective-permute-start | bytes 6291464 | tf_op jit(solution)/shard_map/ppermute | solution.py:520
  165.2 13.5 %collective-permute-start.23 = (bf16[512,640]{1,0:T(8,128)(2,1)S(1)}, bf16[512,640]{1,0:T(8,128)(2,1)S(1)}, u32[]{:S(2)}, u32[]{:S(2)}) collective-permute-start(bf16[512,640]{1,0:T(8,128)(2,1)S(1)} %add_convert_fusion.1), channel_id=1, source_target_pairs={{8,16},{10,18},{12,20},{14,22},{16,8},{18,10},{20,12},{22,14},{9,1... | collective-permute-start | bytes 1966088 | tf_op jit(solution)/shard_map/ppermute | solution.py:78
  166.1 20.6 %collective-permute-start.22 = (bf16[512,640]{1,0:T(8,128)(2,1)S(1)}, bf16[512,640]{1,0:T(8,128)(2,1)S(1)}, u32[]{:S(2)}, u32[]{:S(2)}) collective-permute-start(bf16[512,640]{1,0:T(8,128)(2,1)S(1)} %add_convert_fusion.2), channel_id=1, source_target_pairs={{0,8},{2,10},{4,12},{6,14},{8,0},{10,2},{12,4},{14,6},{16,24},{18,... | collective-permute-start | bytes 1966088 | tf_op jit(solution)/shard_map/ppermute | solution.py:78
  174.6 17.7 %collective-permute-start.21 = (bf16[512,256]{1,0:T(8,128)(2,1)S(1)}, bf16[512,256]{1,0:T(8,128)(2,1)S(1)}, u32[]{:S(2)}, u32[]{:S(2)}) collective-permute-start(bf16[512,256]{1,0:T(8,128)(2,1)S(1)} %get-tuple-element.130), channel_id=1, source_target_pairs={{0,8},{2,10},{4,12},{6,14},{8,0},{10,2},{12,4},{14,6},{16,24},{18,... | collective-permute-start | bytes 786440 | tf_op jit(solution)/shard_map/ppermute | solution.py:73
  175.6 27.0 %collective-permute-start.26 = (bf16[256,1024]{1,0:T(8,128)(2,1)S(1)}, bf16[256,1024]{1,0:T(8,128)(2,1)S(1)}, u32[]{:S(2)}, u32[]{:S(2)}) collective-permute-start(bf16[256,1024]{1,0:T(8,128)(2,1)S(1)} %get-tuple-element.150), channel_id=1, source_target_pairs={{0,2},{2,0},{4,6},{6,4},{8,10},{10,8},{12,14},{14,12},{16,18},{18,... | collective-permute-start | bytes 1572872 | tf_op jit(solution)/shard_map/ppermute | solution.py:73
  177.2 27.0 %collective-permute-start.27 = (bf16[256,1024]{1,0:T(8,128)(2,1)S(1)}, bf16[256,1024]{1,0:T(8,128)(2,1)S(1)}, u32[]{:S(2)}, u32[]{:S(2)}) collective-permute-start(bf16[256,1024]{1,0:T(8,128)(2,1)S(1)} %get-tuple-element.149), channel_id=1, source_target_pairs={{0,4},{2,6},{4,0},{6,2},{8,12},{10,14},{12,8},{14,10},{16,20},{18,... | collective-permute-start | bytes 1572872 | tf_op jit(solution)/shard_map/ppermute | solution.py:73
  178.7 25.9 %collective-permute-start.28 = (bf16[256,1024]{1,0:T(8,128)(2,1)S(1)}, bf16[256,1024]{1,0:T(8,128)(2,1)S(1)}, u32[]{:S(2)}, u32[]{:S(2)}) collective-permute-start(bf16[256,1024]{1,0:T(8,128)(2,1)S(1)} %get-tuple-element.148), channel_id=1, source_target_pairs={{0,6},{2,4},{4,2},{6,0},{8,14},{10,12},{12,10},{14,8},{16,22},{18,... | collective-permute-start | bytes 1572872 | tf_op jit(solution)/shard_map/ppermute | solution.py:73
  186.7 14.4 %collective-permute-start.25 = (bf16[512,256]{1,0:T(8,128)(2,1)S(1)}, bf16[512,256]{1,0:T(8,128)(2,1)S(1)}, u32[]{:S(2)}, u32[]{:S(2)}) collective-permute-start(bf16[512,256]{1,0:T(8,128)(2,1)S(1)} %get-tuple-element.135), channel_id=1, source_target_pairs={{0,8},{2,10},{4,12},{6,14},{8,0},{10,2},{12,4},{14,6},{16,24},{18,... | collective-permute-start | bytes 786440 | tf_op jit(solution)/shard_map/ppermute | solution.py:73
  192.4 14.2 %collective-permute-start.24 = (bf16[512,256]{1,0:T(8,128)(2,1)S(1)}, bf16[512,256]{1,0:T(8,128)(2,1)S(1)}, u32[]{:S(2)}, u32[]{:S(2)}) collective-permute-start(bf16[512,256]{1,0:T(8,128)(2,1)S(1)} %add_convert_fusion.10), channel_id=1, source_target_pairs={{0,16},{2,18},{4,20},{6,22},{8,24},{10,26},{12,28},{14,30},{16,0},... | collective-permute-start | bytes 786440 | tf_op jit(solution)/shard_map/ppermute | solution.py:73
  201.1 8.7 %collective-permute-start.29 = (bf16[128,640]{1,0:T(8,128)(2,1)S(1)}, bf16[128,640]{1,0:T(8,128)(2,1)S(1)}, u32[]{:S(2)}, u32[]{:S(2)}) collective-permute-start(bf16[128,640]{1,0:T(8,128)(2,1)S(1)} %get-tuple-element.162), channel_id=1, source_target_pairs={{0,2},{2,0},{4,6},{6,4},{8,10},{10,8},{12,14},{14,12},{16,18},{18,... | collective-permute-start | bytes 491528 | tf_op jit(solution)/shard_map/ppermute | solution.py:73
  202.6 9.5 %collective-permute-start.30 = (bf16[128,640]{1,0:T(8,128)(2,1)S(1)}, bf16[128,640]{1,0:T(8,128)(2,1)S(1)}, u32[]{:S(2)}, u32[]{:S(2)}) collective-permute-start(bf16[128,640]{1,0:T(8,128)(2,1)S(1)} %get-tuple-element.161), channel_id=1, source_target_pairs={{0,4},{2,6},{4,0},{6,2},{8,12},{10,14},{12,8},{14,10},{16,20},{18,... | collective-permute-start | bytes 491528 | tf_op jit(solution)/shard_map/ppermute | solution.py:73
  204.2 8.5 %collective-permute-start.31 = (bf16[128,640]{1,0:T(8,128)(2,1)S(1)}, bf16[128,640]{1,0:T(8,128)(2,1)S(1)}, u32[]{:S(2)}, u32[]{:S(2)}) collective-permute-start(bf16[128,640]{1,0:T(8,128)(2,1)S(1)} %get-tuple-element.160), channel_id=1, source_target_pairs={{0,6},{2,4},{4,2},{6,0},{8,14},{10,12},{12,10},{14,8},{16,22},{18,... | collective-permute-start | bytes 491528 | tf_op jit(solution)/shard_map/ppermute | solution.py:73
  206.7 5.9 %collective-permute-start.32 = (bf16[128,256]{1,0:T(8,128)(2,1)S(1)}, bf16[128,256]{1,0:T(8,128)(2,1)S(1)}, u32[]{:S(2)}, u32[]{:S(2)}) collective-permute-start(bf16[128,256]{1,0:T(8,128)(2,1)S(1)} %get-tuple-element.166), channel_id=1, source_target_pairs={{0,2},{2,0},{4,6},{6,4},{8,10},{10,8},{12,14},{14,12},{16,18},{18,... | collective-permute-start | bytes 196616 | tf_op jit(solution)/shard_map/ppermute | solution.py:73
  208.3 5.5 %collective-permute-start.33 = (bf16[128,256]{1,0:T(8,128)(2,1)S(1)}, bf16[128,256]{1,0:T(8,128)(2,1)S(1)}, u32[]{:S(2)}, u32[]{:S(2)}) collective-permute-start(bf16[128,256]{1,0:T(8,128)(2,1)S(1)} %get-tuple-element.165), channel_id=1, source_target_pairs={{0,4},{2,6},{4,0},{6,2},{8,12},{10,14},{12,8},{14,10},{16,20},{18,... | collective-permute-start | bytes 196616 | tf_op jit(solution)/shard_map/ppermute | solution.py:73
  209.8 5.2 %collective-permute-start.34 = (bf16[128,256]{1,0:T(8,128)(2,1)S(1)}, bf16[128,256]{1,0:T(8,128)(2,1)S(1)}, u32[]{:S(2)}, u32[]{:S(2)}) collective-permute-start(bf16[128,256]{1,0:T(8,128)(2,1)S(1)} %get-tuple-element.164), channel_id=1, source_target_pairs={{0,6},{2,4},{4,2},{6,0},{8,14},{10,12},{12,10},{14,8},{16,22},{18,... | collective-permute-start | bytes 196616 | tf_op jit(solution)/shard_map/ppermute | solution.py:73

commit v6 on v5

--- a/solution.py
+++ b/solution.py
@@ -474,9 +474,7 @@
     own_far = send(own, FAR)
     own_near = send(own, NEAR)
     rest = crew_swap(first)[1:]
-    own_far, own_near, x_in, cotangent, w_gate, w_up = tie(
-        own_far, own_near, x_in, cotangent, w_gate, w_up
-    )
+    own_near, x_in, cotangent, w_gate, w_up = tie(own_near, x_in, cotangent, w_gate, w_up)
     parcels = pack_parcels(
         scalars, send_counts, recv_counts, x_in, cotangent, w_gate, w_up, chunks
     )
@@ -502,7 +500,8 @@
     second_far = send(second, FAR)
     groups = [(own, own_near, own_far, own_both), (rest, rest_near, rest_far, rest_both)]
     d_first, parts = first_chunk(scalars, mine, other, groups, width, chunks[0], cot_first)
-    second_near, second_far, d_first, p0, p1, p2, p3 = tie(second_near, second_far, d_first, *parts)
+    second_near, second_far, d_first = tie(second_near, second_far, d_first)
+    p0, p1, p2, p3 = parts
 
     middle = along(second, INNER)
     ends = along(second_far, TO_ENDS)

time: 217 us -> 213 us (0.982)
  waiting for transfers between devices: 113 us -> 104 us
  starting transfers between devices: 51.4 us -> 56.8 us
    ppermute x26, waiting for transfers between devices: 101 us -> 92.4 us  [send(): return lax.ppermute(value, 'dp', [(i, i ^ mask) for i in range(DEVS)])]
    ppermute x26, starting transfers between devices: 36 us -> 39.9 us  [send(): return lax.ppermute(value, 'dp', [(i, i ^ mask) for i in range(DEVS)])]
  transfers between devices with their start and end apart: 35 -> 35, of which waited for: 19 -> 17; matrix products, arithmetic and copies ran while one was open for 3% -> 4% of each run, Pallas kernels for 17% -> 18%
where the time goes in v6:
time: 213 us
  waiting for transfers between devices  104 us (49%)
  starting transfers between devices  56.8 us (27%)
  Pallas kernels  39.4 us (18%)
  other arithmetic  7.08 us (3%)
  local copies, waits for them, and re-layouts  4.53 us (2%)
    ppermute x26, waiting for transfers between devices, send(): return lax.ppermute(value, 'dp', [(i, i ^ mask) for i in range(DEVS)])  92.4 us
    ppermute x26, starting transfers between devices, send(): return lax.ppermute(value, 'dp', [(i, i ^ mask) for i in range(DEVS)])  39.9 us
    pallas_call x4, Pallas kernels, kernel_call(): pl.pallas_call(body, grid_spec=pltpu.PrefetchScalarGridSpec(num_scalar_pr...  36.5 us
    ppermute x7, starting transfers between devices, along(): lax.ppermute(value, 'dp', [(crew * a + q, crew * b + q) for a, b in moves...  16.8 us
    ppermute x7, waiting for transfers between devices, along(): lax.ppermute(value, 'dp', [(crew * a + q, crew * b + q) for a, b in moves...  11.6 us
  transfers between devices with their start and end apart: 35, of which 17 were waited for; matrix products, arithmetic and copies ran while one was open for 4% of the time, Pallas kernels for 18%

profile of v6, /device:TPU:0, one launch (start us, length us, event | category | flops | bytes accessed | tf_op | source)
XLA Modules:
  0.0 212.9 jit_solution(6558943685892518847)
XLA Ops:
  0.7 1.6 constant_dynamic-slice_fusion
  2.4 3.1 %collective-permute-start.4 = (bf16[128,1280]{1,0:T(8,128)(2,1)S(1)}, bf16[128,1280]{1,0:T(8,128)(2,1)S(1)}, u32[]{:S(2)}, u32[]{:S(2)}) collective-permute-start(bf16[128,1280]{1,0:T(8,128)(2,1)S(1)} %pad_maximum_fusion.5.a_5_.a_2_), channel_id=1, source_target_pairs={{0,8},{2,10},{4,12},{6,14},{8,0},{10,2},{12,4},{14,6},{16,24},{18,... | collective-permute-start | bytes 983048 | tf_op jit(solution)/shard_map/ppermute | solution.py:73
  5.5 0.7 pad_maximum_fusion.2
  6.2 1.5 collective-permute-start
  7.7 0.7 pad_maximum_fusion.3
  8.4 1.5 collective-permute-start.1
  10.0 0.7 pad_maximum_fusion.4
  10.7 0.5 collective-permute-start.2
  11.2 2.6 %collective-permute-start.3 = (bf16[128,1280]{1,0:T(8,128)(2,1)S(1)}, bf16[128,1280]{1,0:T(8,128)(2,1)}, u32[]{:S(2)}, u32[]{:S(2)}) collective-permute-start(bf16[128,1280]{1,0:T(8,128)(2,1)S(1)} %pad_maximum_fusion.5.a_5_.a_2_), channel_id=1, source_target_pairs={{0,16},{2,18},{4,20},{6,22},{8,24},{10,26},{12,28},{14,30},{16,0},... | collective-permute-start | bytes 983048 | tf_op jit(solution)/shard_map/ppermute | solution.py:73
  13.8 0.5 broadcast.9
  14.3 0.7 stack.174.a_0_.scalars
  15.2 1.5 copy-done.2
  16.6 1.0 pack_parcels.1
  17.7 7.0 %collective-permute-done.1 = bf16[128,1280]{1,0:T(8,128)(2,1)} collective-permute-done((bf16[128,1280]{1,0:T(8,128)(2,1)}, bf16[128,1280]{1,0:T(8,128)(2,1)}, u32[]{:S(2)}, u32[]{:S(2)}) %collective-permute-start.1) | collective-permute-done | bytes 327712 | tf_op jit(solution)/shard_map/ppermute | solution.py:73
  24.7 1.2 pad_maximum_fusion.1.a_9_.a_6_
  25.9 1.6 collective-permute-done.3.a_7_.a_4_
  27.6 2.4 %collective-permute-start.10 = (bf16[128,4352]{1,0:T(8,128)(2,1)S(1)}, bf16[128,4352]{1,0:T(8,128)(2,1)S(1)}, u32[]{:S(2)}, u32[]{:S(2)}) collective-permute-start(bf16[128,4352]{1,0:T(8,128)(2,1)S(1)} %get-tuple-element.83), channel_id=1, source_target_pairs={{0,6},{2,4},{4,2},{6,0},{8,14},{10,12},{12,10},{14,8},{16,22},{18,... | collective-permute-start | bytes 3342344 | tf_op jit(solution)/shard_map/ppermute | solution.py:73
  30.0 0.5 collective-permute-start.8
  30.5 0.5 collective-permute-start.9
  31.0 3.1 %collective-permute-start.5 = (bf16[384,1280]{1,0:T(8,128)(2,1)S(1)}, bf16[384,1280]{1,0:T(8,128)(2,1)S(1)}, u32[]{:S(2)}, u32[]{:S(2)}) collective-permute-start(bf16[384,1280]{1,0:T(8,128)(2,1)S(1)} %pad_maximum_fusion.1.a_9_.a_6_), channel_id=1, source_target_pairs={{0,16},{2,18},{4,20},{6,22},{8,24},{10,26},{12,28},{14,30},{16,0},... | collective-permute-start | bytes 2949128 | tf_op jit(solution)/shard_map/ppermute | solution.py:73
  34.1 7.3 %collective-permute-done.7.a_8_.a_5_ = bf16[128,1280]{1,0:T(8,128)(2,1)S(1)} collective-permute-done((bf16[128,1280]{1,0:T(8,128)(2,1)}, bf16[128,1280]{1,0:T(8,128)(2,1)S(1)}, u32[]{:S(2)}, u32[]{:S(2)}) %collective-permute-start.7) | collective-permute-done | bytes 327712 | tf_op jit(solution)/shard_map/ppermute | solution.py:73
  41.4 33.7 %collective-permute-done.5.a_11_.a_8_ = bf16[384,1280]{1,0:T(8,128)(2,1)S(1)} collective-permute-done((bf16[384,1280]{1,0:T(8,128)(2,1)S(1)}, bf16[384,1280]{1,0:T(8,128)(2,1)S(1)}, u32[]{:S(2)}, u32[]{:S(2)}) %collective-permute-start.5) | collective-permute-done | bytes 983072 | tf_op jit(solution)/shard_map/ppermute | solution.py:73
  75.1 2.9 %collective-permute-done.6.a_10_.a_7_ = bf16[384,1280]{1,0:T(8,128)(2,1)S(1)} collective-permute-done((bf16[384,1280]{1,0:T(8,128)(2,1)S(1)}, bf16[384,1280]{1,0:T(8,128)(2,1)S(1)}, u32[]{:S(2)}, u32[]{:S(2)}) %collective-permute-start.6) | collective-permute-done | bytes 983072 | tf_op jit(solution)/shard_map/ppermute | solution.py:73
  78.0 0.6 pad_maximum_fusion.a_1_.a_3_.a_4_.mine_ref
  78.7 1.2 collective-permute-start.11
  79.9 23.0 %collective-permute-done.11.a_12_.a_9_ = bf16[384,1280]{1,0:T(8,128)(2,1)S(1)} collective-permute-done((bf16[384,1280]{1,0:T(8,128)(2,1)S(1)}, bf16[384,1280]{1,0:T(8,128)(2,1)S(1)}, u32[]{:S(2)}, u32[]{:S(2)}) %collective-permute-start.11) | collective-permute-done | bytes 983072 | tf_op jit(solution)/shard_map/ppermute | solution.py:73
  102.9 1.1 collective-permute-start.15
  104.0 3.1 %collective-permute-start.16 = (bf16[512,512]{1,0:T(8,128)(2,1)S(1)}, bf16[512,512]{1,0:T(8,128)(2,1)S(1)}, u32[]{:S(2)}, u32[]{:S(2)}) collective-permute-start(bf16[512,512]{1,0:T(8,128)(2,1)S(1)} %bitcast.44), channel_id=1, source_target_pairs={{0,16},{2,18},{4,20},{6,22},{8,24},{10,26},{12,28},{14,30},{16,0},... | collective-permute-start | bytes 1572872 | tf_op jit(solution)/shard_map/ppermute | solution.py:73
  107.1 13.5 %first_chunk.1 = (bf16[1024,1280]{1,0:T(8,128)(2,1)S(1)}, bf16[512,640]{1,0:T(8,128)(2,1)S(1)}, bf16[512,640]{1,0:T(8,128)(2,1)S(1)}, bf16[512,640]{1,0:T(8,128)(2,1)S(1)}, bf16[512,640]{1,0:T(8,128)(2,1)S(1)}) custom-call(s32[48]{0:T(128)S(1)} %stack.174.a_0_.scalars, bf16[4,128,4352]{2,1,0:T(8,128)(2,1)S(1)} %pad_maximum_fusion.a_1_.a_3_.a_4_.mine_ref, ...), custom_call_target="tpu_custom_call" | custom-call | flops 8053063680 | bytes 8388608 | tf_op jit(solution)/shard_map/first_chunk/pallas_call | solution.py:296
  120.6 2.4 %collective-permute-start.13 = (bf16[512,640]{1,0:T(8,128)(2,1)S(1)}, bf16[512,640]{1,0:T(8,128)(2,1)S(1)}, u32[]{:S(2)}, u32[]{:S(2)}) collective-permute-start(bf16[512,640]{1,0:T(8,128)(2,1)S(1)} %get-tuple-element.102), channel_id=1, source_target_pairs={{0,8},{2,10},{4,12},{6,14},{24,16},{26,18},{28,20},{30,22},{1,9},{... | collective-permute-start | bytes 1966088 | tf_op jit(solution)/shard_map/ppermute | solution.py:78
  123.0 0.7 collective-permute-start.14
  123.7 3.8 %collective-permute-done.15.a_5_ = bf16[512,512]{1,0:T(8,128)(2,1)S(1)} collective-permute-done((bf16[512,512]{1,0:T(8,128)(2,1)S(1)}, bf16[512,512]{1,0:T(8,128)(2,1)S(1)}, u32[]{:S(2)}, u32[]{:S(2)}) %collective-permute-start.15) | collective-permute-done | bytes 524320 | tf_op jit(solution)/shard_map/ppermute | solution.py:73
  127.6 1.1 collective-permute-done.16.a_6_
  128.6 1.3 collective-permute-start.17
  129.9 9.0 %rows_grad.1 = (bf16[1024,1024]{1,0:T(8,128)(2,1)S(1)}, bf16[1024,1024]{1,0:T(8,128)(2,1)S(1)}) custom-call(s32[48]{0:T(128)S(1)} %stack.174.a_0_.scalars, bf16[1024,1280]{1,0:T(8,128)(2,1)S(1)} %get-tuple-element.99.a_1_, bf16[128,1280]{1,0:T(8,128)(2,1)S(1)} %pad_maximum_fusion.5.a_5_.a_2_, bf16[128,1280]{1,0:T(8,128)(2,1)S(1)} %collective-permute-done.4.a_6_.a_3_, ...), custom_call_target="tpu_custom_call" | custom-call | flops 5368709120 | bytes 8388608 | tf_op jit(solution)/shard_map/rows_grad/pallas_call | solution.py:296
  138.9 1.4 collective-permute-done.13
  140.3 2.1 collective-permute-done.17.a_8_
  142.6 0.7 collective-permute-start.18
  143.3 7.0 %collective-permute-start.19 = (bf16[512,640]{1,0:T(8,128)(2,1)S(1)}, bf16[512,640]{1,0:T(8,128)(2,1)S(1)}, u32[]{:S(2)}, u32[]{:S(2)}) collective-permute-start(bf16[512,640]{1,0:T(8,128)(2,1)S(1)} %get-tuple-element.104), channel_id=1, source_target_pairs={{0,8},{2,10},{4,12},{6,14},{24,16},{26,18},{28,20},{30,22},{1,9},{... | collective-permute-start | bytes 1966088 | tf_op jit(solution)/shard_map/ppermute | solution.py:78
  150.3 10.7 %second_chunk.1 = (bf16[1024,1024]{1,0:T(8,128)(2,1)S(1)}, bf16[1024,1024]{1,0:T(8,128)(2,1)S(1)}, bf16[1024,256]{1,0:T(8,128)(2,1)S(1)}) custom-call(s32[48]{0:T(128)S(1)} %stack.174.a_0_.scalars, bf16[4,128,4352]{2,1,0:T(8,128)(2,1)S(1)} %pad_maximum_fusion.a_1_.a_3_.a_4_.mine_ref, bf16[4,128,4352]{2,1,0:T(8,128)(2,1)S(1)} %collective-permute-done.12.a_2_.other_ref, ...), custom_call_target="tpu_custom_call" | custom-call | flops 4294967296 | bytes 8388608 | tf_op jit(solution)/shard_map/second_chunk/pallas_call | solution.py:296
  161.0 0.6 collective-permute-done.19
  161.7 0.7 collective-permute-start.23
  162.6 4.0 %collective-permute-start.22 = (bf16[512,640]{1,0:T(8,128)(2,1)S(1)}, bf16[512,640]{1,0:T(8,128)(2,1)S(1)}, u32[]{:S(2)}, u32[]{:S(2)}) collective-permute-start(bf16[512,640]{1,0:T(8,128)(2,1)S(1)} %add_convert_fusion.2), channel_id=1, source_target_pairs={{0,8},{2,10},{4,12},{6,14},{8,0},{10,2},{12,4},{14,6},{16,24},{18,... | collective-permute-start | bytes 1966088 | tf_op jit(solution)/shard_map/ppermute | solution.py:78
  166.6 3.4 %gate_grad.1 = (bf16[512,256]{1,0:T(8,128)(2,1)S(1)}, bf16[512,256]{1,0:T(8,128)(2,1)S(1)}, bf16[512,256]{1,0:T(8,128)(2,1)S(1)}, bf16[512,256]{1,0:T(8,128)(2,1)S(1)}) custom-call(s32[48]{0:T(128)S(1)} %stack.174.a_0_.scalars, bf16[4,128,4352]{2,1,0:T(8,128)(2,1)S(1)} %pad_maximum_fusion.a_1_.a_3_.a_4_.mine_ref, ...), custom_call_target="tpu_custom_call" | custom-call | flops 1073741824 | bytes 8388608 | tf_op jit(solution)/shard_map/gate_grad/pallas_call | solution.py:296
  170.1 0.9 add_convert_fusion.5
  171.0 1.6 collective-permute-start.26
  172.6 1.4 collective-permute-start.27
  174.0 0.6 collective-permute-start.28
  174.6 7.5 %collective-permute-done.22 = bf16[512,640]{1,0:T(8,128)(2,1)S(1)} collective-permute-done((bf16[512,640]{1,0:T(8,128)(2,1)S(1)}, bf16[512,640]{1,0:T(8,128)(2,1)S(1)}, u32[]{:S(2)}, u32[]{:S(2)}) %collective-permute-start.22) | collective-permute-done | bytes 655392 | tf_op jit(solution)/shard_map/ppermute | solution.py:78
  182.1 3.4 %collective-permute-start.25 = (bf16[512,256]{1,0:T(8,128)(2,1)S(1)}, bf16[512,256]{1,0:T(8,128)(2,1)S(1)}, u32[]{:S(2)}, u32[]{:S(2)}) collective-permute-start(bf16[512,256]{1,0:T(8,128)(2,1)S(1)} %get-tuple-element.125), channel_id=1, source_target_pairs={{0,8},{2,10},{4,12},{6,14},{8,0},{10,2},{12,4},{14,6},{16,24},{18,... | collective-permute-start | bytes 786440 | tf_op jit(solution)/shard_map/ppermute | solution.py:73
  185.6 2.2 %collective-permute-done.21 = bf16[512,256]{1,0:T(8,128)(2,1)S(1)} collective-permute-done((bf16[512,256]{1,0:T(8,128)(2,1)S(1)}, bf16[512,256]{1,0:T(8,128)(2,1)S(1)}, u32[]{:S(2)}, u32[]{:S(2)}) %collective-permute-start.21) | collective-permute-done | bytes 262176 | tf_op jit(solution)/shard_map/ppermute | solution.py:73
  187.8 3.3 %collective-permute-start.24 = (bf16[512,256]{1,0:T(8,128)(2,1)S(1)}, bf16[512,256]{1,0:T(8,128)(2,1)S(1)}, u32[]{:S(2)}, u32[]{:S(2)}) collective-permute-start(bf16[512,256]{1,0:T(8,128)(2,1)S(1)} %add_convert_fusion.10), channel_id=1, source_target_pairs={{0,16},{2,18},{4,20},{6,22},{8,24},{10,26},{12,28},{14,30},{16,0},... | collective-permute-start | bytes 786440 | tf_op jit(solution)/shard_map/ppermute | solution.py:73
  191.4 6.2 %collective-permute-done.25 = bf16[512,256]{1,0:T(8,128)(2,1)S(1)} collective-permute-done((bf16[512,256]{1,0:T(8,128)(2,1)S(1)}, bf16[512,256]{1,0:T(8,128)(2,1)S(1)}, u32[]{:S(2)}, u32[]{:S(2)}) %collective-permute-start.25) | collective-permute-done | bytes 262176 | tf_op jit(solution)/shard_map/ppermute | solution.py:73
  197.6 1.5 collective-permute-start.29
  199.1 1.4 collective-permute-start.30
  200.5 0.6 collective-permute-start.31
  201.1 0.8 collective-permute-done.24
  202.1 1.6 collective-permute-start.32
  203.7 1.4 collective-permute-start.33
  205.1 2.0 collective-permute-start.34
  207.1 1.2 add_convert_fusion.4
  208.2 1.4 collective-permute-done.30.a_3_
  209.6 1.4 collective-permute-done.33.a_7_
  211.0 1.9 join_quarters.1
  (45 shorter events, 1.3 us)
Async XLA Ops:
  0.7 14.4 %copy-start.3 = (bf16[256,2048]{1,0:T(8,128)(2,1)S(1)}, bf16[256,2048]{1,0:T(8,128)(2,1)}, u32[]{:S(2)}) copy-start(bf16[256,2048]{1,0:T(8,128)(2,1)} %a_3_) | copy-start | bytes 3145732
  2.3 12.8 %copy-start = (bf16[128,3584]{1,0:T(8,128)(2,1)S(1)}, bf16[128,3584]{1,0:T(8,128)(2,1)}, u32[]{:S(2)}) copy-start(bf16[128,3584]{1,0:T(8,128)(2,1)} %a_5_) | copy-start | bytes 2752516
  2.3 12.8 %copy-start.1 = (bf16[128,3584]{1,0:T(8,128)(2,1)S(1)}, bf16[128,3584]{1,0:T(8,128)(2,1)}, u32[]{:S(2)}) copy-start(bf16[128,3584]{1,0:T(8,128)(2,1)} %a_6_) | copy-start | bytes 2752516
  2.3 12.8 %copy-start.4 = (s32[1,16]{1,0:T(1,128)S(1)}, s32[1,16]{1,0:T(1,128)}, u32[]{:S(2)}) copy-start(s32[1,16]{1,0:T(1,128)} %a_1_.1) | copy-start | bytes 196
  2.3 12.8 %copy-start.5 = (s32[1,16]{1,0:T(1,128)S(1)}, s32[1,16]{1,0:T(1,128)}, u32[]{:S(2)}) copy-start(s32[1,16]{1,0:T(1,128)} %a_2_.1) | copy-start | bytes 196
  2.4 12.7 %collective-permute-start.4 = (bf16[128,1280]{1,0:T(8,128)(2,1)S(1)}, bf16[128,1280]{1,0:T(8,128)(2,1)S(1)}, u32[]{:S(2)}, u32[]{:S(2)}) collective-permute-start(bf16[128,1280]{1,0:T(8,128)(2,1)S(1)} %pad_maximum_fusion.5.a_5_.a_2_), channel_id=1, source_target_pairs={{0,8},{2,10},{4,12},{6,14},{8,0},{10,2},{12,4},{14,6},{16,24},{18,... | collective-permute-start | bytes 983048 | tf_op jit(solution)/shard_map/ppermute | solution.py:73
  6.2 11.5 %collective-permute-start = (bf16[128,1280]{1,0:T(8,128)(2,1)}, bf16[128,1280]{1,0:T(8,128)(2,1)}, u32[]{:S(2)}, u32[]{:S(2)}) collective-permute-start(bf16[128,1280]{1,0:T(8,128)(2,1)} %pad_maximum_fusion.2), channel_id=1, source_target_pairs={{0,2},{2,0},{4,6},{6,4},{8,10},{10,8},{12,14},{14,12},{16,18},{18,... | collective-permute-start | bytes 983048 | tf_op jit(solution)/shard_map/ppermute | solution.py:73
  8.4 16.2 %collective-permute-start.1 = (bf16[128,1280]{1,0:T(8,128)(2,1)}, bf16[128,1280]{1,0:T(8,128)(2,1)}, u32[]{:S(2)}, u32[]{:S(2)}) collective-permute-start(bf16[128,1280]{1,0:T(8,128)(2,1)} %pad_maximum_fusion.3), channel_id=1, source_target_pairs={{0,4},{2,6},{4,0},{6,2},{8,12},{10,14},{12,8},{14,10},{16,20},{18,... | collective-permute-start | bytes 983048 | tf_op jit(solution)/shard_map/ppermute | solution.py:73
  10.7 14.0 %collective-permute-start.2 = (bf16[128,1280]{1,0:T(8,128)(2,1)}, bf16[128,1280]{1,0:T(8,128)(2,1)}, u32[]{:S(2)}, u32[]{:S(2)}) collective-permute-start(bf16[128,1280]{1,0:T(8,128)(2,1)} %pad_maximum_fusion.4), channel_id=1, source_target_pairs={{0,6},{2,4},{4,2},{6,0},{8,14},{10,12},{12,10},{14,8},{16,22},{18,... | collective-permute-start | bytes 983048 | tf_op jit(solution)/shard_map/ppermute | solution.py:73
  11.2 16.4 %collective-permute-start.3 = (bf16[128,1280]{1,0:T(8,128)(2,1)S(1)}, bf16[128,1280]{1,0:T(8,128)(2,1)}, u32[]{:S(2)}, u32[]{:S(2)}) collective-permute-start(bf16[128,1280]{1,0:T(8,128)(2,1)S(1)} %pad_maximum_fusion.5.a_5_.a_2_), channel_id=1, source_target_pairs={{0,16},{2,18},{4,20},{6,22},{8,24},{10,26},{12,28},{14,30},{16,0},... | collective-permute-start | bytes 983048 | tf_op jit(solution)/shard_map/ppermute | solution.py:73
  15.1 1.5 copy-start.2
  27.6 13.8 %collective-permute-start.7 = (bf16[128,1280]{1,0:T(8,128)(2,1)}, bf16[128,1280]{1,0:T(8,128)(2,1)S(1)}, u32[]{:S(2)}, u32[]{:S(2)}) collective-permute-start(bf16[128,1280]{1,0:T(8,128)(2,1)} %collective-permute-done.3.a_7_.a_4_), channel_id=1, source_target_pairs={{0,8},{2,10},{4,12},{6,14},{8,0},{10,2},{12,4},{14,6},{16,24},{18,... | collective-permute-start | bytes 983048 | tf_op jit(solution)/shard_map/ppermute | solution.py:73
  27.6 50.5 %collective-permute-start.10 = (bf16[128,4352]{1,0:T(8,128)(2,1)S(1)}, bf16[128,4352]{1,0:T(8,128)(2,1)S(1)}, u32[]{:S(2)}, u32[]{:S(2)}) collective-permute-start(bf16[128,4352]{1,0:T(8,128)(2,1)S(1)} %get-tuple-element.83), channel_id=1, source_target_pairs={{0,6},{2,4},{4,2},{6,0},{8,14},{10,12},{12,10},{14,8},{16,22},{18,... | collective-permute-start | bytes 3342344 | tf_op jit(solution)/shard_map/ppermute | solution.py:73
  30.0 48.0 %collective-permute-start.8 = (bf16[128,4352]{1,0:T(8,128)(2,1)S(1)}, bf16[128,4352]{1,0:T(8,128)(2,1)S(1)}, u32[]{:S(2)}, u32[]{:S(2)}) collective-permute-start(bf16[128,4352]{1,0:T(8,128)(2,1)S(1)} %get-tuple-element.81), channel_id=1, source_target_pairs={{0,2},{2,0},{4,6},{6,4},{8,10},{10,8},{12,14},{14,12},{16,18},{18,... | collective-permute-start | bytes 3342344 | tf_op jit(solution)/shard_map/ppermute | solution.py:73
  30.5 47.5 %collective-permute-start.9 = (bf16[128,4352]{1,0:T(8,128)(2,1)S(1)}, bf16[128,4352]{1,0:T(8,128)(2,1)S(1)}, u32[]{:S(2)}, u32[]{:S(2)}) collective-permute-start(bf16[128,4352]{1,0:T(8,128)(2,1)S(1)} %get-tuple-element.82), channel_id=1, source_target_pairs={{0,4},{2,6},{4,0},{6,2},{8,12},{10,14},{12,8},{14,10},{16,20},{18,... | collective-permute-start | bytes 3342344 | tf_op jit(solution)/shard_map/ppermute | solution.py:73
  31.0 44.1 %collective-permute-start.5 = (bf16[384,1280]{1,0:T(8,128)(2,1)S(1)}, bf16[384,1280]{1,0:T(8,128)(2,1)S(1)}, u32[]{:S(2)}, u32[]{:S(2)}) collective-permute-start(bf16[384,1280]{1,0:T(8,128)(2,1)S(1)} %pad_maximum_fusion.1.a_9_.a_6_), channel_id=1, source_target_pairs={{0,16},{2,18},{4,20},{6,22},{8,24},{10,26},{12,28},{14,30},{16,0},... | collective-permute-start | bytes 2949128 | tf_op jit(solution)/shard_map/ppermute | solution.py:73
  41.4 36.6 %collective-permute-start.6 = (bf16[384,1280]{1,0:T(8,128)(2,1)S(1)}, bf16[384,1280]{1,0:T(8,128)(2,1)S(1)}, u32[]{:S(2)}, u32[]{:S(2)}) collective-permute-start(bf16[384,1280]{1,0:T(8,128)(2,1)S(1)} %pad_maximum_fusion.1.a_9_.a_6_), channel_id=1, source_target_pairs={{0,8},{2,10},{4,12},{6,14},{8,0},{10,2},{12,4},{14,6},{16,24},{18,... | collective-permute-start | bytes 2949128 | tf_op jit(solution)/shard_map/ppermute | solution.py:73
  78.7 24.3 %collective-permute-start.12 = (bf16[4,128,4352]{2,1,0:T(8,128)(2,1)S(1)}, bf16[4,128,4352]{2,1,0:T(8,128)(2,1)S(1)}, u32[]{:S(2)}, u32[]{:S(2)}) collective-permute-start(bf16[4,128,4352]{2,1,0:T(8,128)(2,1)S(1)} %pad_maximum_fusion.a_1_.a_3_.a_4_.mine_ref), channel_id=1, source_target_pairs={{0,1},{1,0},{2,3},{3,2},{4,5},{5,4},{6,7},{7,6},{8,9},{9,8},{10,11... | collective-permute-start | bytes 13369352 | tf_op jit(solution)/shard_map/ppermute | solution.py:492
  78.7 24.2 %collective-permute-start.11 = (bf16[384,1280]{1,0:T(8,128)(2,1)S(1)}, bf16[384,1280]{1,0:T(8,128)(2,1)S(1)}, u32[]{:S(2)}, u32[]{:S(2)}) collective-permute-start(bf16[384,1280]{1,0:T(8,128)(2,1)S(1)} %collective-permute-done.5.a_11_.a_8_), channel_id=1, source_target_pairs={{0,8},{2,10},{4,12},{6,14},{8,0},{10,2},{12,4},{14,6},{16,24},{18,... | collective-permute-start | bytes 2949128 | tf_op jit(solution)/shard_map/ppermute | solution.py:73
  102.9 24.7 %collective-permute-start.15 = (bf16[512,512]{1,0:T(8,128)(2,1)S(1)}, bf16[512,512]{1,0:T(8,128)(2,1)S(1)}, u32[]{:S(2)}, u32[]{:S(2)}) collective-permute-start(bf16[512,512]{1,0:T(8,128)(2,1)S(1)} %bitcast.43), channel_id=1, source_target_pairs={{0,8},{2,10},{4,12},{6,14},{8,0},{10,2},{12,4},{14,6},{16,24},{18,... | collective-permute-start | bytes 1572872 | tf_op jit(solution)/shard_map/ppermute | solution.py:73
  104.0 24.6 %collective-permute-start.16 = (bf16[512,512]{1,0:T(8,128)(2,1)S(1)}, bf16[512,512]{1,0:T(8,128)(2,1)S(1)}, u32[]{:S(2)}, u32[]{:S(2)}) collective-permute-start(bf16[512,512]{1,0:T(8,128)(2,1)S(1)} %bitcast.44), channel_id=1, source_target_pairs={{0,16},{2,18},{4,20},{6,22},{8,24},{10,26},{12,28},{14,30},{16,0},... | collective-permute-start | bytes 1572872 | tf_op jit(solution)/shard_map/ppermute | solution.py:73
  120.6 19.7 %collective-permute-start.13 = (bf16[512,640]{1,0:T(8,128)(2,1)S(1)}, bf16[512,640]{1,0:T(8,128)(2,1)S(1)}, u32[]{:S(2)}, u32[]{:S(2)}) collective-permute-start(bf16[512,640]{1,0:T(8,128)(2,1)S(1)} %get-tuple-element.102), channel_id=1, source_target_pairs={{0,8},{2,10},{4,12},{6,14},{24,16},{26,18},{28,20},{30,22},{1,9},{... | collective-permute-start | bytes 1966088 | tf_op jit(solution)/shard_map/ppermute | solution.py:78
  123.0 15.9 %collective-permute-start.14 = (bf16[512,512]{1,0:T(8,128)(2,1)S(1)}, bf16[512,512]{1,0:T(8,128)(2,1)S(1)}, u32[]{:S(2)}, u32[]{:S(2)}) collective-permute-start(bf16[512,512]{1,0:T(8,128)(2,1)S(1)} %bitcast.45), channel_id=1, source_target_pairs={{8,16},{10,18},{12,20},{14,22},{16,8},{18,10},{20,12},{22,14},{9,1... | collective-permute-start | bytes 1572872 | tf_op jit(solution)/shard_map/ppermute | solution.py:78
  128.6 13.8 %collective-permute-start.17 = (bf16[512,512]{1,0:T(8,128)(2,1)S(1)}, bf16[512,512]{1,0:T(8,128)(2,1)S(1)}, u32[]{:S(2)}, u32[]{:S(2)}) collective-permute-start(bf16[512,512]{1,0:T(8,128)(2,1)S(1)} %collective-permute-done.16.a_6_), channel_id=1, source_target_pairs={{8,0},{10,2},{12,4},{14,6},{16,24},{18,26},{20,28},{22,30},{9,1},{... | collective-permute-start | bytes 1572872 | tf_op jit(solution)/shard_map/ppermute | solution.py:78
  142.6 18.4 %collective-permute-start.18 = (bf16[512,640]{1,0:T(8,128)(2,1)S(1)}, bf16[512,640]{1,0:T(8,128)(2,1)S(1)}, u32[]{:S(2)}, u32[]{:S(2)}) collective-permute-start(bf16[512,640]{1,0:T(8,128)(2,1)S(1)} %add_convert_fusion.3), channel_id=1, source_target_pairs={{8,16},{10,18},{12,20},{14,22},{16,8},{18,10},{20,12},{22,14},{9,1... | collective-permute-start | bytes 1966088 | tf_op jit(solution)/shard_map/ppermute | solution.py:78
  143.3 18.2 %collective-permute-start.19 = (bf16[512,640]{1,0:T(8,128)(2,1)S(1)}, bf16[512,640]{1,0:T(8,128)(2,1)S(1)}, u32[]{:S(2)}, u32[]{:S(2)}) collective-permute-start(bf16[512,640]{1,0:T(8,128)(2,1)S(1)} %get-tuple-element.104), channel_id=1, source_target_pairs={{0,8},{2,10},{4,12},{6,14},{24,16},{26,18},{28,20},{30,22},{1,9},{... | collective-permute-start | bytes 1966088 | tf_op jit(solution)/shard_map/ppermute | solution.py:78
  161.5 8.5 %collective-permute-start.20 = (bf16[1024,1024]{1,0:T(8,128)(2,1)S(1)}, bf16[1024,1024]{1,0:T(8,128)(2,1)S(1)}, u32[]{:S(2)}, u32[]{:S(2)}) collective-permute-start(bf16[1024,1024]{1,0:T(8,128)(2,1)S(1)} %get-tuple-element.113), channel_id=1, source_target_pairs={{0,1},{1,0},{2,3},{3,2},{4,5},{5,4},{6,7},{7,6},{8,9},{9,8},{10,11... | collective-permute-start | bytes 6291464 | tf_op jit(solution)/shard_map/ppermute | solution.py:519
  161.7 12.3 %collective-permute-start.23 = (bf16[512,640]{1,0:T(8,128)(2,1)S(1)}, bf16[512,640]{1,0:T(8,128)(2,1)S(1)}, u32[]{:S(2)}, u32[]{:S(2)}) collective-permute-start(bf16[512,640]{1,0:T(8,128)(2,1)S(1)} %add_convert_fusion.1), channel_id=1, source_target_pairs={{8,16},{10,18},{12,20},{14,22},{16,8},{18,10},{20,12},{22,14},{9,1... | collective-permute-start | bytes 1966088 | tf_op jit(solution)/shard_map/ppermute | solution.py:78
  162.6 19.6 %collective-permute-start.22 = (bf16[512,640]{1,0:T(8,128)(2,1)S(1)}, bf16[512,640]{1,0:T(8,128)(2,1)S(1)}, u32[]{:S(2)}, u32[]{:S(2)}) collective-permute-start(bf16[512,640]{1,0:T(8,128)(2,1)S(1)} %add_convert_fusion.2), channel_id=1, source_target_pairs={{0,8},{2,10},{4,12},{6,14},{8,0},{10,2},{12,4},{14,6},{16,24},{18,... | collective-permute-start | bytes 1966088 | tf_op jit(solution)/shard_map/ppermute | solution.py:78
  170.0 17.8 %collective-permute-start.21 = (bf16[512,256]{1,0:T(8,128)(2,1)S(1)}, bf16[512,256]{1,0:T(8,128)(2,1)S(1)}, u32[]{:S(2)}, u32[]{:S(2)}) collective-permute-start(bf16[512,256]{1,0:T(8,128)(2,1)S(1)} %get-tuple-element.120), channel_id=1, source_target_pairs={{0,8},{2,10},{4,12},{6,14},{8,0},{10,2},{12,4},{14,6},{16,24},{18,... | collective-permute-start | bytes 786440 | tf_op jit(solution)/shard_map/ppermute | solution.py:73
  171.0 28.1 %collective-permute-start.26 = (bf16[256,1024]{1,0:T(8,128)(2,1)S(1)}, bf16[256,1024]{1,0:T(8,128)(2,1)S(1)}, u32[]{:S(2)}, u32[]{:S(2)}) collective-permute-start(bf16[256,1024]{1,0:T(8,128)(2,1)S(1)} %get-tuple-element.140), channel_id=1, source_target_pairs={{0,2},{2,0},{4,6},{6,4},{8,10},{10,8},{12,14},{14,12},{16,18},{18,... | collective-permute-start | bytes 1572872 | tf_op jit(solution)/shard_map/ppermute | solution.py:73
  172.6 28.0 %collective-permute-start.27 = (bf16[256,1024]{1,0:T(8,128)(2,1)S(1)}, bf16[256,1024]{1,0:T(8,128)(2,1)S(1)}, u32[]{:S(2)}, u32[]{:S(2)}) collective-permute-start(bf16[256,1024]{1,0:T(8,128)(2,1)S(1)} %get-tuple-element.139), channel_id=1, source_target_pairs={{0,4},{2,6},{4,0},{6,2},{8,12},{10,14},{12,8},{14,10},{16,20},{18,... | collective-permute-start | bytes 1572872 | tf_op jit(solution)/shard_map/ppermute | solution.py:73
  174.0 27.1 %collective-permute-start.28 = (bf16[256,1024]{1,0:T(8,128)(2,1)S(1)}, bf16[256,1024]{1,0:T(8,128)(2,1)S(1)}, u32[]{:S(2)}, u32[]{:S(2)}) collective-permute-start(bf16[256,1024]{1,0:T(8,128)(2,1)S(1)} %get-tuple-element.138), channel_id=1, source_target_pairs={{0,6},{2,4},{4,2},{6,0},{8,14},{10,12},{12,10},{14,8},{16,22},{18,... | collective-permute-start | bytes 1572872 | tf_op jit(solution)/shard_map/ppermute | solution.py:73
  182.1 15.5 %collective-permute-start.25 = (bf16[512,256]{1,0:T(8,128)(2,1)S(1)}, bf16[512,256]{1,0:T(8,128)(2,1)S(1)}, u32[]{:S(2)}, u32[]{:S(2)}) collective-permute-start(bf16[512,256]{1,0:T(8,128)(2,1)S(1)} %get-tuple-element.125), channel_id=1, source_target_pairs={{0,8},{2,10},{4,12},{6,14},{8,0},{10,2},{12,4},{14,6},{16,24},{18,... | collective-permute-start | bytes 786440 | tf_op jit(solution)/shard_map/ppermute | solution.py:73
  187.8 14.2 %collective-permute-start.24 = (bf16[512,256]{1,0:T(8,128)(2,1)S(1)}, bf16[512,256]{1,0:T(8,128)(2,1)S(1)}, u32[]{:S(2)}, u32[]{:S(2)}) collective-permute-start(bf16[512,256]{1,0:T(8,128)(2,1)S(1)} %add_convert_fusion.10), channel_id=1, source_target_pairs={{0,16},{2,18},{4,20},{6,22},{8,24},{10,26},{12,28},{14,30},{16,0},... | collective-permute-start | bytes 786440 | tf_op jit(solution)/shard_map/ppermute | solution.py:73
  197.6 7.4 %collective-permute-start.29 = (bf16[128,640]{1,0:T(8,128)(2,1)S(1)}, bf16[128,640]{1,0:T(8,128)(2,1)S(1)}, u32[]{:S(2)}, u32[]{:S(2)}) collective-permute-start(bf16[128,640]{1,0:T(8,128)(2,1)S(1)} %get-tuple-element.152), channel_id=1, source_target_pairs={{0,2},{2,0},{4,6},{6,4},{8,10},{10,8},{12,14},{14,12},{16,18},{18,... | collective-permute-start | bytes 491528 | tf_op jit(solution)/shard_map/ppermute | solution.py:73
  199.1 10.5 %collective-permute-start.30 = (bf16[128,640]{1,0:T(8,128)(2,1)S(1)}, bf16[128,640]{1,0:T(8,128)(2,1)S(1)}, u32[]{:S(2)}, u32[]{:S(2)}) collective-permute-start(bf16[128,640]{1,0:T(8,128)(2,1)S(1)} %get-tuple-element.151), channel_id=1, source_target_pairs={{0,4},{2,6},{4,0},{6,2},{8,12},{10,14},{12,8},{14,10},{16,20},{18,... | collective-permute-start | bytes 491528 | tf_op jit(solution)/shard_map/ppermute | solution.py:73
  200.5 9.1 %collective-permute-start.31 = (bf16[128,640]{1,0:T(8,128)(2,1)S(1)}, bf16[128,640]{1,0:T(8,128)(2,1)S(1)}, u32[]{:S(2)}, u32[]{:S(2)}) collective-permute-start(bf16[128,640]{1,0:T(8,128)(2,1)S(1)} %get-tuple-element.150), channel_id=1, source_target_pairs={{0,6},{2,4},{4,2},{6,0},{8,14},{10,12},{12,10},{14,8},{16,22},{18,... | collective-permute-start | bytes 491528 | tf_op jit(solution)/shard_map/ppermute | solution.py:73
  202.1 7.5 %collective-permute-start.32 = (bf16[128,256]{1,0:T(8,128)(2,1)S(1)}, bf16[128,256]{1,0:T(8,128)(2,1)S(1)}, u32[]{:S(2)}, u32[]{:S(2)}) collective-permute-start(bf16[128,256]{1,0:T(8,128)(2,1)S(1)} %get-tuple-element.156), channel_id=1, source_target_pairs={{0,2},{2,0},{4,6},{6,4},{8,10},{10,8},{12,14},{14,12},{16,18},{18,... | collective-permute-start | bytes 196616 | tf_op jit(solution)/shard_map/ppermute | solution.py:73
  203.7 7.3 %collective-permute-start.33 = (bf16[128,256]{1,0:T(8,128)(2,1)S(1)}, bf16[128,256]{1,0:T(8,128)(2,1)S(1)}, u32[]{:S(2)}, u32[]{:S(2)}) collective-permute-start(bf16[128,256]{1,0:T(8,128)(2,1)S(1)} %get-tuple-element.155), channel_id=1, source_target_pairs={{0,4},{2,6},{4,0},{6,2},{8,12},{10,14},{12,8},{14,10},{16,20},{18,... | collective-permute-start | bytes 196616 | tf_op jit(solution)/shard_map/ppermute | solution.py:73
  205.1 5.9 %collective-permute-start.34 = (bf16[128,256]{1,0:T(8,128)(2,1)S(1)}, bf16[128,256]{1,0:T(8,128)(2,1)S(1)}, u32[]{:S(2)}, u32[]{:S(2)}) collective-permute-start(bf16[128,256]{1,0:T(8,128)(2,1)S(1)} %get-tuple-element.154), channel_id=1, source_target_pairs={{0,6},{2,4},{4,2},{6,0},{8,14},{10,12},{12,10},{14,8},{16,22},{18,... | collective-permute-start | bytes 196616 | tf_op jit(solution)/shard_map/ppermute | solution.py:73

commit v7 on v6

--- a/solution.py
+++ b/solution.py
@@ -198,6 +198,27 @@
         cost_estimate=pl.CostEstimate(flops=0, bytes_accessed=2**23, transcendentals=0),
         name="pack_parcels",
     )(scalars, sent, got, x_in, cotangent, w_gate, w_up)
+
+
+def pieces_kernel(scalars, gate_ref, up_ref, *outs, ck, quarter):
+    for s, out in enumerate(outs):
+        start = scalars[DEVS + 2 + s] * quarter
+        spot = pl.ds(pl.multiple_of(start, 128), ck)
+        out[:, :ck] = gate_ref[:, spot]
+        out[:, ck:] = up_ref[:, spot]
+
+
+def pieces_of_first(scalars, w_gate, w_up, ck, quarter):
+    vmem = pl.BlockSpec(memory_space=pltpu.VMEM)
+    return pl.pallas_call(
+        lambda *a: pieces_kernel(*a, ck=ck, quarter=quarter),
+        in_specs=[pl.BlockSpec(memory_space=pltpu.SMEM), vmem, vmem],
+        out_specs=[vmem] * len(CREW),
+        out_shape=[jax.ShapeDtypeStruct((w_gate.shape[0], 2 * ck), BF)] * len(CREW),
+        compiler_params=pltpu.CompilerParams(vmem_limit_bytes=16 * 1024 * 1024),
+        cost_estimate=pl.CostEstimate(flops=0, bytes_accessed=2**22, transcendentals=0),
+        name="pieces_of_first",
+    )(scalars, w_gate, w_up)
 
 
 def first_kernel(scalars, mine_ref, other_ref, low_ref, high_ref, *refs, counts):
@@ -452,16 +473,7 @@
     z, place = index // crew, index % crew
     places = [place ^ m for m in CREW]
     chunks = [640, 256]
-    offsets = [0, chunks[0]]
     swap = [(0, 1), (1, 0)]
-
-    def columns(array, q, offset, count):
-        return lax.dynamic_slice_in_dim(array, q * quarter + offset, count, 1)
-
-    def piece_of_weights(q, k):
-        return jnp.concatenate(
-            [columns(w, q, offsets[k], chunks[k]) for w in (w_gate, w_up)], axis=1
-        )
 
     order = [z, z ^ 1, jnp.where(z < 2, 2, 1), jnp.where(z < 2, 3, 0)]
     inner = ((z == 1) | (z == 2)).astype(jnp.int32)
@@ -469,7 +481,7 @@
     scalars += [0] * (2 * DEVS - len(scalars)) + [p * crew + q for p in order for q in places]
     scalars = jnp.stack([jnp.asarray(v, jnp.int32) for v in scalars])
 
-    first = [piece_of_weights(q, 0) for q in places]
+    first = pieces_of_first(scalars, w_gate, w_up, chunks[0], quarter)
     own = first[0]
     own_far = send(own, FAR)
     own_near = send(own, NEAR)

time: 213 us -> 211 us (level)
  other arithmetic: 7.08 us -> 3.75 us
    unnamed x12 -> x16, local copies, waits for them, and re-layouts: 1.52 us -> 5.09 us
    concatenate x4 -> x0, other arithmetic: 2.27 us -> none  [piece_of_weights(): jnp.concatenate([columns(w, q, offsets[k], chunks[k]) for w in (w_gate, w...]
  transfers between devices with their start and end apart: 35 -> 35, of which waited for: 17 -> 18; matrix products, arithmetic and copies ran while one was open for 4% -> 1% of each run, Pallas kernels for 18% -> 18%
where the time goes in v7:
time: 211 us
  waiting for transfers between devices  104 us (49%)
  starting transfers between devices  56.7 us (27%)
  Pallas kernels  40.4 us (19%)
  local copies, waits for them, and re-layouts  5.33 us (3%)
  other arithmetic  3.75 us (2%)
    ppermute x26, waiting for transfers between devices, send(): return lax.ppermute(value, 'dp', [(i, i ^ mask) for i in range(DEVS)])  91.9 us
    ppermute x26, starting transfers between devices, send(): return lax.ppermute(value, 'dp', [(i, i ^ mask) for i in range(DEVS)])  39.1 us
    pallas_call x4, Pallas kernels, kernel_call(): pl.pallas_call(body, grid_spec=pltpu.PrefetchScalarGridSpec(num_scalar_pr...  36.9 us
    ppermute x7, starting transfers between devices, along(): lax.ppermute(value, 'dp', [(crew * a + q, crew * b + q) for a, b in moves...  17.5 us
    ppermute x7, waiting for transfers between devices, along(): lax.ppermute(value, 'dp', [(crew * a + q, crew * b + q) for a, b in moves...  12 us
    unnamed x16, local copies, waits for them, and re-layouts  5.09 us
  transfers between devices with their start and end apart: 35, of which 18 were waited for; matrix products, arithmetic and copies ran while one was open for 1% of the time, Pallas kernels for 18%

profile of v7, /device:TPU:0, one launch (start us, length us, event | category | flops | bytes accessed | tf_op | source)
XLA Modules:
  0.0 211.1 jit_solution(5176310073853994286)
XLA Ops:
  0.9 1.2 copy-done
  2.0 1.2 copy-done.2
  3.2 0.6 pieces_of_first.1
  3.9 3.1 %collective-permute-start.4 = (bf16[128,1280]{1,0:T(8,128)(2,1)S(1)}, bf16[128,1280]{1,0:T(8,128)(2,1)S(1)}, u32[]{:S(2)}, u32[]{:S(2)}) collective-permute-start(bf16[128,1280]{1,0:T(8,128)(2,1)S(1)} %get-tuple-element.77.a_5_.a_2_), channel_id=1, source_target_pairs={{0,8},{2,10},{4,12},{6,14},{8,0},{10,2},{12,4},{14,6},{16,24},{18,... | collective-permute-start | bytes 983048 | tf_op jit(solution)/shard_map/ppermute | solution.py:73
  7.0 1.5 collective-permute-start
  8.5 1.5 collective-permute-start.1
  10.0 0.5 collective-permute-start.2
  10.4 2.6 %collective-permute-start.3 = (bf16[128,1280]{1,0:T(8,128)(2,1)S(1)}, bf16[128,1280]{1,0:T(8,128)(2,1)S(1)}, u32[]{:S(2)}, u32[]{:S(2)}) collective-permute-start(bf16[128,1280]{1,0:T(8,128)(2,1)S(1)} %get-tuple-element.77.a_5_.a_2_), channel_id=1, source_target_pairs={{0,16},{2,18},{4,20},{6,22},{8,24},{10,26},{12,28},{14,30},{16,0},... | collective-permute-start | bytes 983048 | tf_op jit(solution)/shard_map/ppermute | solution.py:73
  13.0 5.9 %collective-permute-done.4.a_6_.a_3_ = bf16[128,1280]{1,0:T(8,128)(2,1)S(1)} collective-permute-done((bf16[128,1280]{1,0:T(8,128)(2,1)S(1)}, bf16[128,1280]{1,0:T(8,128)(2,1)S(1)}, u32[]{:S(2)}, u32[]{:S(2)}) %collective-permute-start.4) | collective-permute-done | bytes 327712 | tf_op jit(solution)/shard_map/ppermute | solution.py:73
  19.0 1.5 copy-done.4
  20.5 1.2 copy-done.5
  21.7 1.0 pack_parcels.1
  22.7 1.7 collective-permute-done.1
  24.4 2.3 %collective-permute-done.3.a_7_.a_4_ = bf16[128,1280]{1,0:T(8,128)(2,1)S(1)} collective-permute-done((bf16[128,1280]{1,0:T(8,128)(2,1)S(1)}, bf16[128,1280]{1,0:T(8,128)(2,1)S(1)}, u32[]{:S(2)}, u32[]{:S(2)}) %collective-permute-start.3) | collective-permute-done | bytes 327712 | tf_op jit(solution)/shard_map/ppermute | solution.py:73
  26.8 2.4 %collective-permute-start.10 = (bf16[128,4352]{1,0:T(8,128)(2,1)S(1)}, bf16[128,4352]{1,0:T(8,128)(2,1)S(1)}, u32[]{:S(2)}, u32[]{:S(2)}) collective-permute-start(bf16[128,4352]{1,0:T(8,128)(2,1)S(1)} %get-tuple-element.91), channel_id=1, source_target_pairs={{0,6},{2,4},{4,2},{6,0},{8,14},{10,12},{12,10},{14,8},{16,22},{18,... | collective-permute-start | bytes 3342344 | tf_op jit(solution)/shard_map/ppermute | solution.py:73
  29.2 0.5 collective-permute-start.8
  29.7 0.5 collective-permute-start.9
  30.2 3.0 %collective-permute-start.5 = (bf16[384,1280]{1,0:T(8,128)(2,1)S(1)}, bf16[384,1280]{1,0:T(8,128)(2,1)S(1)}, u32[]{:S(2)}, u32[]{:S(2)}) collective-permute-start(bf16[384,1280]{1,0:T(8,128)(2,1)S(1)} %pad_maximum_fusion.1.a_9_.a_6_), channel_id=1, source_target_pairs={{0,16},{2,18},{4,20},{6,22},{8,24},{10,26},{12,28},{14,30},{16,0},... | collective-permute-start | bytes 2949128 | tf_op jit(solution)/shard_map/ppermute | solution.py:73
  33.3 7.5 %collective-permute-done.7.a_8_.a_5_ = bf16[128,1280]{1,0:T(8,128)(2,1)S(1)} collective-permute-done((bf16[128,1280]{1,0:T(8,128)(2,1)S(1)}, bf16[128,1280]{1,0:T(8,128)(2,1)S(1)}, u32[]{:S(2)}, u32[]{:S(2)}) %collective-permute-start.7) | collective-permute-done | bytes 327712 | tf_op jit(solution)/shard_map/ppermute | solution.py:73
  40.7 32.5 %collective-permute-done.5.a_11_.a_8_ = bf16[384,1280]{1,0:T(8,128)(2,1)S(1)} collective-permute-done((bf16[384,1280]{1,0:T(8,128)(2,1)S(1)}, bf16[384,1280]{1,0:T(8,128)(2,1)S(1)}, u32[]{:S(2)}, u32[]{:S(2)}) %collective-permute-start.5) | collective-permute-done | bytes 983072 | tf_op jit(solution)/shard_map/ppermute | solution.py:73
  73.3 3.0 %collective-permute-done.6.a_10_.a_7_ = bf16[384,1280]{1,0:T(8,128)(2,1)S(1)} collective-permute-done((bf16[384,1280]{1,0:T(8,128)(2,1)S(1)}, bf16[384,1280]{1,0:T(8,128)(2,1)S(1)}, u32[]{:S(2)}, u32[]{:S(2)}) %collective-permute-start.6) | collective-permute-done | bytes 983072 | tf_op jit(solution)/shard_map/ppermute | solution.py:73
  76.3 0.6 pad_maximum_fusion.a_1_.a_3_.a_4_.mine_ref
  77.0 1.4 collective-permute-start.11
  78.5 22.8 %collective-permute-done.11.a_12_.a_9_ = bf16[384,1280]{1,0:T(8,128)(2,1)S(1)} collective-permute-done((bf16[384,1280]{1,0:T(8,128)(2,1)S(1)}, bf16[384,1280]{1,0:T(8,128)(2,1)S(1)}, u32[]{:S(2)}, u32[]{:S(2)}) %collective-permute-start.11) | collective-permute-done | bytes 983072 | tf_op jit(solution)/shard_map/ppermute | solution.py:73
  101.2 1.3 collective-permute-start.15
  102.5 1.9 collective-permute-start.16
  104.4 13.6 %first_chunk.1 = (bf16[1024,1280]{1,0:T(8,128)(2,1)S(1)}, bf16[512,640]{1,0:T(8,128)(2,1)S(1)}, bf16[512,640]{1,0:T(8,128)(2,1)S(1)}, bf16[512,640]{1,0:T(8,128)(2,1)S(1)}, bf16[512,640]{1,0:T(8,128)(2,1)S(1)}) custom-call(s32[48]{0:T(128)S(1)} %stack.174.a_0_.scalars, bf16[4,128,4352]{2,1,0:T(8,128)(2,1)S(1)} %pad_maximum_fusion.a_1_.a_3_.a_4_.mine_ref, ...), custom_call_target="tpu_custom_call" | custom-call | flops 8053063680 | bytes 8388608 | tf_op jit(solution)/shard_map/first_chunk/pallas_call | solution.py:317
  118.0 3.3 %collective-permute-start.13 = (bf16[512,640]{1,0:T(8,128)(2,1)S(1)}, bf16[512,640]{1,0:T(8,128)(2,1)S(1)}, u32[]{:S(2)}, u32[]{:S(2)}) collective-permute-start(bf16[512,640]{1,0:T(8,128)(2,1)S(1)} %get-tuple-element.110), channel_id=1, source_target_pairs={{0,8},{2,10},{4,12},{6,14},{24,16},{26,18},{28,20},{30,22},{1,9},{... | collective-permute-start | bytes 1966088 | tf_op jit(solution)/shard_map/ppermute | solution.py:78
  121.3 0.7 collective-permute-start.14
  122.0 3.9 %collective-permute-done.15.a_5_ = bf16[512,512]{1,0:T(8,128)(2,1)S(1)} collective-permute-done((bf16[512,512]{1,0:T(8,128)(2,1)S(1)}, bf16[512,512]{1,0:T(8,128)(2,1)S(1)}, u32[]{:S(2)}, u32[]{:S(2)}) %collective-permute-start.15) | collective-permute-done | bytes 524320 | tf_op jit(solution)/shard_map/ppermute | solution.py:73
  125.9 0.2 collective-permute-done.16.a_6_
  126.2 1.3 collective-permute-start.17
  127.5 9.1 %rows_grad.1 = (bf16[1024,1024]{1,0:T(8,128)(2,1)S(1)}, bf16[1024,1024]{1,0:T(8,128)(2,1)S(1)}) custom-call(s32[48]{0:T(128)S(1)} %stack.174.a_0_.scalars, bf16[1024,1280]{1,0:T(8,128)(2,1)S(1)} %get-tuple-element.107.a_1_, bf16[128,1280]{1,0:T(8,128)(2,1)S(1)} %get-tuple-element.77.a_5_.a_2_, bf16[128,1280]{1,0:T(8,128)(2,1)S(1)} %collective-permute-done.4.a_6_.a_3_, ...), custom_call_target="tpu_custom_call" | custom-call | flops 5368709120 | bytes 8388608 | tf_op jit(solution)/shard_map/rows_grad/pallas_call | solution.py:317
  136.6 2.3 %collective-permute-done.13 = bf16[512,640]{1,0:T(8,128)(2,1)S(1)} collective-permute-done((bf16[512,640]{1,0:T(8,128)(2,1)S(1)}, bf16[512,640]{1,0:T(8,128)(2,1)S(1)}, u32[]{:S(2)}, u32[]{:S(2)}) %collective-permute-start.13) | collective-permute-done | bytes 655392 | tf_op jit(solution)/shard_map/ppermute | solution.py:78
  138.9 1.7 collective-permute-done.17.a_8_
  140.7 0.7 collective-permute-start.18
  141.5 6.8 %collective-permute-start.19 = (bf16[512,640]{1,0:T(8,128)(2,1)S(1)}, bf16[512,640]{1,0:T(8,128)(2,1)S(1)}, u32[]{:S(2)}, u32[]{:S(2)}) collective-permute-start(bf16[512,640]{1,0:T(8,128)(2,1)S(1)} %get-tuple-element.112), channel_id=1, source_target_pairs={{0,8},{2,10},{4,12},{6,14},{24,16},{26,18},{28,20},{30,22},{1,9},{... | collective-permute-start | bytes 1966088 | tf_op jit(solution)/shard_map/ppermute | solution.py:78
  148.3 10.8 %second_chunk.1 = (bf16[1024,1024]{1,0:T(8,128)(2,1)S(1)}, bf16[1024,1024]{1,0:T(8,128)(2,1)S(1)}, bf16[1024,256]{1,0:T(8,128)(2,1)S(1)}) custom-call(s32[48]{0:T(128)S(1)} %stack.174.a_0_.scalars, bf16[4,128,4352]{2,1,0:T(8,128)(2,1)S(1)} %pad_maximum_fusion.a_1_.a_3_.a_4_.mine_ref, bf16[4,128,4352]{2,1,0:T(8,128)(2,1)S(1)} %collective-permute-done.12.a_2_.other_ref, ...), custom_call_target="tpu_custom_call" | custom-call | flops 4294967296 | bytes 8388608 | tf_op jit(solution)/shard_map/second_chunk/pallas_call | solution.py:317
  159.1 0.6 collective-permute-done.19
  159.7 0.2 add_convert_fusion.1
  159.9 0.7 collective-permute-start.23
  160.7 4.0 %collective-permute-start.22 = (bf16[512,640]{1,0:T(8,128)(2,1)S(1)}, bf16[512,640]{1,0:T(8,128)(2,1)S(1)}, u32[]{:S(2)}, u32[]{:S(2)}) collective-permute-start(bf16[512,640]{1,0:T(8,128)(2,1)S(1)} %add_convert_fusion.2), channel_id=1, source_target_pairs={{0,8},{2,10},{4,12},{6,14},{8,0},{10,2},{12,4},{14,6},{16,24},{18,... | collective-permute-start | bytes 1966088 | tf_op jit(solution)/shard_map/ppermute | solution.py:78
  164.8 3.4 %gate_grad.1 = (bf16[512,256]{1,0:T(8,128)(2,1)S(1)}, bf16[512,256]{1,0:T(8,128)(2,1)S(1)}, bf16[512,256]{1,0:T(8,128)(2,1)S(1)}, bf16[512,256]{1,0:T(8,128)(2,1)S(1)}) custom-call(s32[48]{0:T(128)S(1)} %stack.174.a_0_.scalars, bf16[4,128,4352]{2,1,0:T(8,128)(2,1)S(1)} %pad_maximum_fusion.a_1_.a_3_.a_4_.mine_ref, ...), custom_call_target="tpu_custom_call" | custom-call | flops 1073741824 | bytes 8388608 | tf_op jit(solution)/shard_map/gate_grad/pallas_call | solution.py:317
  168.2 1.0 add_convert_fusion.5
  169.3 1.6 collective-permute-start.26
  170.8 1.4 collective-permute-start.27
  172.2 0.6 collective-permute-start.28
  172.8 7.5 %collective-permute-done.22 = bf16[512,640]{1,0:T(8,128)(2,1)S(1)} collective-permute-done((bf16[512,640]{1,0:T(8,128)(2,1)S(1)}, bf16[512,640]{1,0:T(8,128)(2,1)S(1)}, u32[]{:S(2)}, u32[]{:S(2)}) %collective-permute-start.22) | collective-permute-done | bytes 655392 | tf_op jit(solution)/shard_map/ppermute | solution.py:78
  180.3 3.4 %collective-permute-start.25 = (bf16[512,256]{1,0:T(8,128)(2,1)S(1)}, bf16[512,256]{1,0:T(8,128)(2,1)S(1)}, u32[]{:S(2)}, u32[]{:S(2)}) collective-permute-start(bf16[512,256]{1,0:T(8,128)(2,1)S(1)} %get-tuple-element.133), channel_id=1, source_target_pairs={{0,8},{2,10},{4,12},{6,14},{8,0},{10,2},{12,4},{14,6},{16,24},{18,... | collective-permute-start | bytes 786440 | tf_op jit(solution)/shard_map/ppermute | solution.py:73
  183.7 2.2 %collective-permute-done.21 = bf16[512,256]{1,0:T(8,128)(2,1)S(1)} collective-permute-done((bf16[512,256]{1,0:T(8,128)(2,1)S(1)}, bf16[512,256]{1,0:T(8,128)(2,1)S(1)}, u32[]{:S(2)}, u32[]{:S(2)}) %collective-permute-start.21) | collective-permute-done | bytes 262176 | tf_op jit(solution)/shard_map/ppermute | solution.py:73
  186.0 3.3 %collective-permute-start.24 = (bf16[512,256]{1,0:T(8,128)(2,1)S(1)}, bf16[512,256]{1,0:T(8,128)(2,1)S(1)}, u32[]{:S(2)}, u32[]{:S(2)}) collective-permute-start(bf16[512,256]{1,0:T(8,128)(2,1)S(1)} %add_convert_fusion.10), channel_id=1, source_target_pairs={{0,16},{2,18},{4,20},{6,22},{8,24},{10,26},{12,28},{14,30},{16,0},... | collective-permute-start | bytes 786440 | tf_op jit(solution)/shard_map/ppermute | solution.py:73
  189.3 0.2 add_convert_fusion
  189.6 6.2 %collective-permute-done.25 = bf16[512,256]{1,0:T(8,128)(2,1)S(1)} collective-permute-done((bf16[512,256]{1,0:T(8,128)(2,1)S(1)}, bf16[512,256]{1,0:T(8,128)(2,1)S(1)}, u32[]{:S(2)}, u32[]{:S(2)}) %collective-permute-start.25) | collective-permute-done | bytes 262176 | tf_op jit(solution)/shard_map/ppermute | solution.py:73
  195.8 1.5 collective-permute-start.29
  197.3 1.4 collective-permute-start.30
  198.7 0.6 collective-permute-start.31
  199.3 0.8 collective-permute-done.24
  200.3 1.6 collective-permute-start.32
  201.8 1.4 collective-permute-start.33
  203.3 2.0 collective-permute-start.34
  205.3 1.2 add_convert_fusion.4
  206.4 1.4 collective-permute-done.30.a_3_
  207.8 1.4 collective-permute-done.33.a_7_
  209.2 1.9 join_quarters.1
  (45 shorter events, 1.0 us)
Async XLA Ops:
  0.6 18.3 %copy-start.6 = (s32[1,16]{1,0:T(1,128)S(1)}, s32[1,16]{1,0:T(1,128)}, u32[]{:S(2)}) copy-start(s32[1,16]{1,0:T(1,128)} %a_1_.3) | copy-start | bytes 196
  0.6 18.3 %copy-start.7 = (s32[1,16]{1,0:T(1,128)S(1)}, s32[1,16]{1,0:T(1,128)}, u32[]{:S(2)}) copy-start(s32[1,16]{1,0:T(1,128)} %a_2_.3) | copy-start | bytes 196
  0.8 1.2 copy-start
  2.0 1.2 copy-start.2
  3.2 15.7 %copy-start.1 = (bf16[128,3584]{1,0:T(8,128)(2,1)S(1)}, bf16[128,3584]{1,0:T(8,128)(2,1)}, u32[]{:S(2)}) copy-start(bf16[128,3584]{1,0:T(8,128)(2,1)} %a_5_) | copy-start | bytes 2752516
  3.2 15.7 %copy-start.3 = (bf16[128,3584]{1,0:T(8,128)(2,1)S(1)}, bf16[128,3584]{1,0:T(8,128)(2,1)}, u32[]{:S(2)}) copy-start(bf16[128,3584]{1,0:T(8,128)(2,1)} %a_6_) | copy-start | bytes 2752516
  3.9 15.1 %collective-permute-start.4 = (bf16[128,1280]{1,0:T(8,128)(2,1)S(1)}, bf16[128,1280]{1,0:T(8,128)(2,1)S(1)}, u32[]{:S(2)}, u32[]{:S(2)}) collective-permute-start(bf16[128,1280]{1,0:T(8,128)(2,1)S(1)} %get-tuple-element.77.a_5_.a_2_), channel_id=1, source_target_pairs={{0,8},{2,10},{4,12},{6,14},{8,0},{10,2},{12,4},{14,6},{16,24},{18,... | collective-permute-start | bytes 983048 | tf_op jit(solution)/shard_map/ppermute | solution.py:73
  7.0 15.7 %collective-permute-start = (bf16[128,1280]{1,0:T(8,128)(2,1)S(1)}, bf16[128,1280]{1,0:T(8,128)(2,1)S(1)}, u32[]{:S(2)}, u32[]{:S(2)}) collective-permute-start(bf16[128,1280]{1,0:T(8,128)(2,1)S(1)} %get-tuple-element.74), channel_id=1, source_target_pairs={{0,2},{2,0},{4,6},{6,4},{8,10},{10,8},{12,14},{14,12},{16,18},{18,... | collective-permute-start | bytes 983048 | tf_op jit(solution)/shard_map/ppermute | solution.py:73
  8.5 15.9 %collective-permute-start.1 = (bf16[128,1280]{1,0:T(8,128)(2,1)S(1)}, bf16[128,1280]{1,0:T(8,128)(2,1)S(1)}, u32[]{:S(2)}, u32[]{:S(2)}) collective-permute-start(bf16[128,1280]{1,0:T(8,128)(2,1)S(1)} %get-tuple-element.75), channel_id=1, source_target_pairs={{0,4},{2,6},{4,0},{6,2},{8,12},{10,14},{12,8},{14,10},{16,20},{18,... | collective-permute-start | bytes 983048 | tf_op jit(solution)/shard_map/ppermute | solution.py:73
  10.0 14.4 %collective-permute-start.2 = (bf16[128,1280]{1,0:T(8,128)(2,1)S(1)}, bf16[128,1280]{1,0:T(8,128)(2,1)S(1)}, u32[]{:S(2)}, u32[]{:S(2)}) collective-permute-start(bf16[128,1280]{1,0:T(8,128)(2,1)S(1)} %get-tuple-element.76), channel_id=1, source_target_pairs={{0,6},{2,4},{4,2},{6,0},{8,14},{10,12},{12,10},{14,8},{16,22},{18,... | collective-permute-start | bytes 983048 | tf_op jit(solution)/shard_map/ppermute | solution.py:73
  10.4 16.3 %collective-permute-start.3 = (bf16[128,1280]{1,0:T(8,128)(2,1)S(1)}, bf16[128,1280]{1,0:T(8,128)(2,1)S(1)}, u32[]{:S(2)}, u32[]{:S(2)}) collective-permute-start(bf16[128,1280]{1,0:T(8,128)(2,1)S(1)} %get-tuple-element.77.a_5_.a_2_), channel_id=1, source_target_pairs={{0,16},{2,18},{4,20},{6,22},{8,24},{10,26},{12,28},{14,30},{16,0},... | collective-permute-start | bytes 983048 | tf_op jit(solution)/shard_map/ppermute | solution.py:73
  18.9 1.5 copy-start.4
  20.4 1.2 copy-start.5
  26.7 14.0 %collective-permute-start.7 = (bf16[128,1280]{1,0:T(8,128)(2,1)S(1)}, bf16[128,1280]{1,0:T(8,128)(2,1)S(1)}, u32[]{:S(2)}, u32[]{:S(2)}) collective-permute-start(bf16[128,1280]{1,0:T(8,128)(2,1)S(1)} %collective-permute-done.3.a_7_.a_4_), channel_id=1, source_target_pairs={{0,8},{2,10},{4,12},{6,14},{8,0},{10,2},{12,4},{14,6},{16,24},{18,... | collective-permute-start | bytes 983048 | tf_op jit(solution)/shard_map/ppermute | solution.py:73
  26.8 49.6 %collective-permute-start.10 = (bf16[128,4352]{1,0:T(8,128)(2,1)S(1)}, bf16[128,4352]{1,0:T(8,128)(2,1)S(1)}, u32[]{:S(2)}, u32[]{:S(2)}) collective-permute-start(bf16[128,4352]{1,0:T(8,128)(2,1)S(1)} %get-tuple-element.91), channel_id=1, source_target_pairs={{0,6},{2,4},{4,2},{6,0},{8,14},{10,12},{12,10},{14,8},{16,22},{18,... | collective-permute-start | bytes 3342344 | tf_op jit(solution)/shard_map/ppermute | solution.py:73
  29.2 47.1 %collective-permute-start.8 = (bf16[128,4352]{1,0:T(8,128)(2,1)S(1)}, bf16[128,4352]{1,0:T(8,128)(2,1)S(1)}, u32[]{:S(2)}, u32[]{:S(2)}) collective-permute-start(bf16[128,4352]{1,0:T(8,128)(2,1)S(1)} %get-tuple-element.89), channel_id=1, source_target_pairs={{0,2},{2,0},{4,6},{6,4},{8,10},{10,8},{12,14},{14,12},{16,18},{18,... | collective-permute-start | bytes 3342344 | tf_op jit(solution)/shard_map/ppermute | solution.py:73
  29.7 46.6 %collective-permute-start.9 = (bf16[128,4352]{1,0:T(8,128)(2,1)S(1)}, bf16[128,4352]{1,0:T(8,128)(2,1)S(1)}, u32[]{:S(2)}, u32[]{:S(2)}) collective-permute-start(bf16[128,4352]{1,0:T(8,128)(2,1)S(1)} %get-tuple-element.90), channel_id=1, source_target_pairs={{0,4},{2,6},{4,0},{6,2},{8,12},{10,14},{12,8},{14,10},{16,20},{18,... | collective-permute-start | bytes 3342344 | tf_op jit(solution)/shard_map/ppermute | solution.py:73
  30.2 43.0 %collective-permute-start.5 = (bf16[384,1280]{1,0:T(8,128)(2,1)S(1)}, bf16[384,1280]{1,0:T(8,128)(2,1)S(1)}, u32[]{:S(2)}, u32[]{:S(2)}) collective-permute-start(bf16[384,1280]{1,0:T(8,128)(2,1)S(1)} %pad_maximum_fusion.1.a_9_.a_6_), channel_id=1, source_target_pairs={{0,16},{2,18},{4,20},{6,22},{8,24},{10,26},{12,28},{14,30},{16,0},... | collective-permute-start | bytes 2949128 | tf_op jit(solution)/shard_map/ppermute | solution.py:73
  40.7 35.6 %collective-permute-start.6 = (bf16[384,1280]{1,0:T(8,128)(2,1)S(1)}, bf16[384,1280]{1,0:T(8,128)(2,1)S(1)}, u32[]{:S(2)}, u32[]{:S(2)}) collective-permute-start(bf16[384,1280]{1,0:T(8,128)(2,1)S(1)} %pad_maximum_fusion.1.a_9_.a_6_), channel_id=1, source_target_pairs={{0,8},{2,10},{4,12},{6,14},{8,0},{10,2},{12,4},{14,6},{16,24},{18,... | collective-permute-start | bytes 2949128 | tf_op jit(solution)/shard_map/ppermute | solution.py:73
  77.0 24.3 %collective-permute-start.12 = (bf16[4,128,4352]{2,1,0:T(8,128)(2,1)S(1)}, bf16[4,128,4352]{2,1,0:T(8,128)(2,1)S(1)}, u32[]{:S(2)}, u32[]{:S(2)}) collective-permute-start(bf16[4,128,4352]{2,1,0:T(8,128)(2,1)S(1)} %pad_maximum_fusion.a_1_.a_3_.a_4_.mine_ref), channel_id=1, source_target_pairs={{0,1},{1,0},{2,3},{3,2},{4,5},{5,4},{6,7},{7,6},{8,9},{9,8},{10,11... | collective-permute-start | bytes 13369352 | tf_op jit(solution)/shard_map/ppermute | solution.py:504
  77.0 24.2 %collective-permute-start.11 = (bf16[384,1280]{1,0:T(8,128)(2,1)S(1)}, bf16[384,1280]{1,0:T(8,128)(2,1)S(1)}, u32[]{:S(2)}, u32[]{:S(2)}) collective-permute-start(bf16[384,1280]{1,0:T(8,128)(2,1)S(1)} %collective-permute-done.5.a_11_.a_8_), channel_id=1, source_target_pairs={{0,8},{2,10},{4,12},{6,14},{8,0},{10,2},{12,4},{14,6},{16,24},{18,... | collective-permute-start | bytes 2949128 | tf_op jit(solution)/shard_map/ppermute | solution.py:73
  101.2 24.7 %collective-permute-start.15 = (bf16[512,512]{1,0:T(8,128)(2,1)S(1)}, bf16[512,512]{1,0:T(8,128)(2,1)S(1)}, u32[]{:S(2)}, u32[]{:S(2)}) collective-permute-start(bf16[512,512]{1,0:T(8,128)(2,1)S(1)} %bitcast.43), channel_id=1, source_target_pairs={{0,8},{2,10},{4,12},{6,14},{8,0},{10,2},{12,4},{14,6},{16,24},{18,... | collective-permute-start | bytes 1572872 | tf_op jit(solution)/shard_map/ppermute | solution.py:73
  102.5 23.6 %collective-permute-start.16 = (bf16[512,512]{1,0:T(8,128)(2,1)S(1)}, bf16[512,512]{1,0:T(8,128)(2,1)S(1)}, u32[]{:S(2)}, u32[]{:S(2)}) collective-permute-start(bf16[512,512]{1,0:T(8,128)(2,1)S(1)} %bitcast.44), channel_id=1, source_target_pairs={{0,16},{2,18},{4,20},{6,22},{8,24},{10,26},{12,28},{14,30},{16,0},... | collective-permute-start | bytes 1572872 | tf_op jit(solution)/shard_map/ppermute | solution.py:73
  118.0 20.8 %collective-permute-start.13 = (bf16[512,640]{1,0:T(8,128)(2,1)S(1)}, bf16[512,640]{1,0:T(8,128)(2,1)S(1)}, u32[]{:S(2)}, u32[]{:S(2)}) collective-permute-start(bf16[512,640]{1,0:T(8,128)(2,1)S(1)} %get-tuple-element.110), channel_id=1, source_target_pairs={{0,8},{2,10},{4,12},{6,14},{24,16},{26,18},{28,20},{30,22},{1,9},{... | collective-permute-start | bytes 1966088 | tf_op jit(solution)/shard_map/ppermute | solution.py:78
  121.3 15.3 %collective-permute-start.14 = (bf16[512,512]{1,0:T(8,128)(2,1)S(1)}, bf16[512,512]{1,0:T(8,128)(2,1)S(1)}, u32[]{:S(2)}, u32[]{:S(2)}) collective-permute-start(bf16[512,512]{1,0:T(8,128)(2,1)S(1)} %bitcast.45), channel_id=1, source_target_pairs={{8,16},{10,18},{12,20},{14,22},{16,8},{18,10},{20,12},{22,14},{9,1... | collective-permute-start | bytes 1572872 | tf_op jit(solution)/shard_map/ppermute | solution.py:78
  126.2 14.4 %collective-permute-start.17 = (bf16[512,512]{1,0:T(8,128)(2,1)S(1)}, bf16[512,512]{1,0:T(8,128)(2,1)S(1)}, u32[]{:S(2)}, u32[]{:S(2)}) collective-permute-start(bf16[512,512]{1,0:T(8,128)(2,1)S(1)} %collective-permute-done.16.a_6_), channel_id=1, source_target_pairs={{8,0},{10,2},{12,4},{14,6},{16,24},{18,26},{20,28},{22,30},{9,1},{... | collective-permute-start | bytes 1572872 | tf_op jit(solution)/shard_map/ppermute | solution.py:78
  140.7 18.4 %collective-permute-start.18 = (bf16[512,640]{1,0:T(8,128)(2,1)S(1)}, bf16[512,640]{1,0:T(8,128)(2,1)S(1)}, u32[]{:S(2)}, u32[]{:S(2)}) collective-permute-start(bf16[512,640]{1,0:T(8,128)(2,1)S(1)} %add_convert_fusion.3), channel_id=1, source_target_pairs={{8,16},{10,18},{12,20},{14,22},{16,8},{18,10},{20,12},{22,14},{9,1... | collective-permute-start | bytes 1966088 | tf_op jit(solution)/shard_map/ppermute | solution.py:78
  141.5 18.2 %collective-permute-start.19 = (bf16[512,640]{1,0:T(8,128)(2,1)S(1)}, bf16[512,640]{1,0:T(8,128)(2,1)S(1)}, u32[]{:S(2)}, u32[]{:S(2)}) collective-permute-start(bf16[512,640]{1,0:T(8,128)(2,1)S(1)} %get-tuple-element.112), channel_id=1, source_target_pairs={{0,8},{2,10},{4,12},{6,14},{24,16},{26,18},{28,20},{30,22},{1,9},{... | collective-permute-start | bytes 1966088 | tf_op jit(solution)/shard_map/ppermute | solution.py:78
  159.7 8.5 %collective-permute-start.20 = (bf16[1024,1024]{1,0:T(8,128)(2,1)S(1)}, bf16[1024,1024]{1,0:T(8,128)(2,1)S(1)}, u32[]{:S(2)}, u32[]{:S(2)}) collective-permute-start(bf16[1024,1024]{1,0:T(8,128)(2,1)S(1)} %get-tuple-element.121), channel_id=1, source_target_pairs={{0,1},{1,0},{2,3},{3,2},{4,5},{5,4},{6,7},{7,6},{8,9},{9,8},{10,11... | collective-permute-start | bytes 6291464 | tf_op jit(solution)/shard_map/ppermute | solution.py:531
  159.9 12.4 %collective-permute-start.23 = (bf16[512,640]{1,0:T(8,128)(2,1)S(1)}, bf16[512,640]{1,0:T(8,128)(2,1)S(1)}, u32[]{:S(2)}, u32[]{:S(2)}) collective-permute-start(bf16[512,640]{1,0:T(8,128)(2,1)S(1)} %add_convert_fusion.1), channel_id=1, source_target_pairs={{8,16},{10,18},{12,20},{14,22},{16,8},{18,10},{20,12},{22,14},{9,1... | collective-permute-start | bytes 1966088 | tf_op jit(solution)/shard_map/ppermute | solution.py:78
  160.7 19.6 %collective-permute-start.22 = (bf16[512,640]{1,0:T(8,128)(2,1)S(1)}, bf16[512,640]{1,0:T(8,128)(2,1)S(1)}, u32[]{:S(2)}, u32[]{:S(2)}) collective-permute-start(bf16[512,640]{1,0:T(8,128)(2,1)S(1)} %add_convert_fusion.2), channel_id=1, source_target_pairs={{0,8},{2,10},{4,12},{6,14},{8,0},{10,2},{12,4},{14,6},{16,24},{18,... | collective-permute-start | bytes 1966088 | tf_op jit(solution)/shard_map/ppermute | solution.py:78
  168.2 17.8 %collective-permute-start.21 = (bf16[512,256]{1,0:T(8,128)(2,1)S(1)}, bf16[512,256]{1,0:T(8,128)(2,1)S(1)}, u32[]{:S(2)}, u32[]{:S(2)}) collective-permute-start(bf16[512,256]{1,0:T(8,128)(2,1)S(1)} %get-tuple-element.128), channel_id=1, source_target_pairs={{0,8},{2,10},{4,12},{6,14},{8,0},{10,2},{12,4},{14,6},{16,24},{18,... | collective-permute-start | bytes 786440 | tf_op jit(solution)/shard_map/ppermute | solution.py:73
  169.3 28.0 %collective-permute-start.26 = (bf16[256,1024]{1,0:T(8,128)(2,1)S(1)}, bf16[256,1024]{1,0:T(8,128)(2,1)S(1)}, u32[]{:S(2)}, u32[]{:S(2)}) collective-permute-start(bf16[256,1024]{1,0:T(8,128)(2,1)S(1)} %get-tuple-element.148), channel_id=1, source_target_pairs={{0,2},{2,0},{4,6},{6,4},{8,10},{10,8},{12,14},{14,12},{16,18},{18,... | collective-permute-start | bytes 1572872 | tf_op jit(solution)/shard_map/ppermute | solution.py:73
  170.8 27.9 %collective-permute-start.27 = (bf16[256,1024]{1,0:T(8,128)(2,1)S(1)}, bf16[256,1024]{1,0:T(8,128)(2,1)S(1)}, u32[]{:S(2)}, u32[]{:S(2)}) collective-permute-start(bf16[256,1024]{1,0:T(8,128)(2,1)S(1)} %get-tuple-element.147), channel_id=1, source_target_pairs={{0,4},{2,6},{4,0},{6,2},{8,12},{10,14},{12,8},{14,10},{16,20},{18,... | collective-permute-start | bytes 1572872 | tf_op jit(solution)/shard_map/ppermute | solution.py:73
  172.2 27.1 %collective-permute-start.28 = (bf16[256,1024]{1,0:T(8,128)(2,1)S(1)}, bf16[256,1024]{1,0:T(8,128)(2,1)S(1)}, u32[]{:S(2)}, u32[]{:S(2)}) collective-permute-start(bf16[256,1024]{1,0:T(8,128)(2,1)S(1)} %get-tuple-element.146), channel_id=1, source_target_pairs={{0,6},{2,4},{4,2},{6,0},{8,14},{10,12},{12,10},{14,8},{16,22},{18,... | collective-permute-start | bytes 1572872 | tf_op jit(solution)/shard_map/ppermute | solution.py:73
  180.3 15.5 %collective-permute-start.25 = (bf16[512,256]{1,0:T(8,128)(2,1)S(1)}, bf16[512,256]{1,0:T(8,128)(2,1)S(1)}, u32[]{:S(2)}, u32[]{:S(2)}) collective-permute-start(bf16[512,256]{1,0:T(8,128)(2,1)S(1)} %get-tuple-element.133), channel_id=1, source_target_pairs={{0,8},{2,10},{4,12},{6,14},{8,0},{10,2},{12,4},{14,6},{16,24},{18,... | collective-permute-start | bytes 786440 | tf_op jit(solution)/shard_map/ppermute | solution.py:73
  186.0 14.2 %collective-permute-start.24 = (bf16[512,256]{1,0:T(8,128)(2,1)S(1)}, bf16[512,256]{1,0:T(8,128)(2,1)S(1)}, u32[]{:S(2)}, u32[]{:S(2)}) collective-permute-start(bf16[512,256]{1,0:T(8,128)(2,1)S(1)} %add_convert_fusion.10), channel_id=1, source_target_pairs={{0,16},{2,18},{4,20},{6,22},{8,24},{10,26},{12,28},{14,30},{16,0},... | collective-permute-start | bytes 786440 | tf_op jit(solution)/shard_map/ppermute | solution.py:73
  195.8 7.5 %collective-permute-start.29 = (bf16[128,640]{1,0:T(8,128)(2,1)S(1)}, bf16[128,640]{1,0:T(8,128)(2,1)S(1)}, u32[]{:S(2)}, u32[]{:S(2)}) collective-permute-start(bf16[128,640]{1,0:T(8,128)(2,1)S(1)} %get-tuple-element.152), channel_id=1, source_target_pairs={{0,2},{2,0},{4,6},{6,4},{8,10},{10,8},{12,14},{14,12},{16,18},{18,... | collective-permute-start | bytes 491528 | tf_op jit(solution)/shard_map/ppermute | solution.py:73
  197.3 10.5 %collective-permute-start.30 = (bf16[128,640]{1,0:T(8,128)(2,1)S(1)}, bf16[128,640]{1,0:T(8,128)(2,1)S(1)}, u32[]{:S(2)}, u32[]{:S(2)}) collective-permute-start(bf16[128,640]{1,0:T(8,128)(2,1)S(1)} %get-tuple-element.151), channel_id=1, source_target_pairs={{0,4},{2,6},{4,0},{6,2},{8,12},{10,14},{12,8},{14,10},{16,20},{18,... | collective-permute-start | bytes 491528 | tf_op jit(solution)/shard_map/ppermute | solution.py:73
  198.7 9.1 %collective-permute-start.31 = (bf16[128,640]{1,0:T(8,128)(2,1)S(1)}, bf16[128,640]{1,0:T(8,128)(2,1)S(1)}, u32[]{:S(2)}, u32[]{:S(2)}) collective-permute-start(bf16[128,640]{1,0:T(8,128)(2,1)S(1)} %get-tuple-element.150), channel_id=1, source_target_pairs={{0,6},{2,4},{4,2},{6,0},{8,14},{10,12},{12,10},{14,8},{16,22},{18,... | collective-permute-start | bytes 491528 | tf_op jit(solution)/shard_map/ppermute | solution.py:73
  200.3 7.5 %collective-permute-start.32 = (bf16[128,256]{1,0:T(8,128)(2,1)S(1)}, bf16[128,256]{1,0:T(8,128)(2,1)S(1)}, u32[]{:S(2)}, u32[]{:S(2)}) collective-permute-start(bf16[128,256]{1,0:T(8,128)(2,1)S(1)} %get-tuple-element.156), channel_id=1, source_target_pairs={{0,2},{2,0},{4,6},{6,4},{8,10},{10,8},{12,14},{14,12},{16,18},{18,... | collective-permute-start | bytes 196616 | tf_op jit(solution)/shard_map/ppermute | solution.py:73
  201.8 7.3 %collective-permute-start.33 = (bf16[128,256]{1,0:T(8,128)(2,1)S(1)}, bf16[128,256]{1,0:T(8,128)(2,1)S(1)}, u32[]{:S(2)}, u32[]{:S(2)}) collective-permute-start(bf16[128,256]{1,0:T(8,128)(2,1)S(1)} %get-tuple-element.155), channel_id=1, source_target_pairs={{0,4},{2,6},{4,0},{6,2},{8,12},{10,14},{12,8},{14,10},{16,20},{18,... | collective-permute-start | bytes 196616 | tf_op jit(solution)/shard_map/ppermute | solution.py:73
  203.3 5.9 %collective-permute-start.34 = (bf16[128,256]{1,0:T(8,128)(2,1)S(1)}, bf16[128,256]{1,0:T(8,128)(2,1)S(1)}, u32[]{:S(2)}, u32[]{:S(2)}) collective-permute-start(bf16[128,256]{1,0:T(8,128)(2,1)S(1)} %get-tuple-element.154), channel_id=1, source_target_pairs={{0,6},{2,4},{4,2},{6,0},{8,14},{10,12},{12,10},{14,8},{16,22},{18,... | collective-permute-start | bytes 196616 | tf_op jit(solution)/shard_map/ppermute | solution.py:73

commit v8 on v7

--- a/solution.py
+++ b/solution.py
@@ -159,9 +159,20 @@
     return d_gate, d_up
 
 
-def pack_kernel(scalars, sent, got, x_ref, cot_ref, gate_ref, up_ref, *outs, chunks, quarter):
+def pack_kernel(scalars, sent, got, x_ref, cot_ref, gate_ref, up_ref, *refs, chunks, quarter):
+    outs, sems = refs[: len(CREW)], refs[len(CREW)]
     rows, width = x_ref.shape
     half = rows // 2
+    copies = []
+    for s, out in enumerate(outs):
+        start = scalars[DEVS + 2 + s] * quarter + chunks[0]
+        spot = pl.ds(pl.multiple_of(start, 128), chunks[1])
+        for i, ref in enumerate((gate_ref, up_ref)):
+            col = width + 2 * quarter + i * chunks[1]
+            there = out.at[:, col : col + chunks[1]]
+            copies.append(pltpu.make_async_copy(ref.at[:, spot], there, sems.at[2 * s + i]))
+    for copy in copies:
+        copy.start()
     live = BAL
     for i in range(sent.shape[1]):
         live = live + sent[0, i] - got[0, i]
@@ -177,10 +188,8 @@
             for part in (cot[:half], cot[half:]):
                 out[:, col : col + chunks[k]] = part
                 col += chunks[k]
-        spot = pl.ds(pl.multiple_of(start + chunks[0], 128), chunks[1])
-        for ref in (gate_ref, up_ref):
-            out[:, col : col + chunks[1]] = ref[:, spot]
-            col += chunks[1]
+    for copy in copies:
+        copy.wait()
 
 
 def pack_parcels(scalars, sent, got, x_in, cotangent, w_gate, w_up, chunks):
@@ -191,8 +200,9 @@
     wide = width + 2 * quarter + 2 * chunks[1]
     return pl.pallas_call(
         lambda *a: pack_kernel(*a, chunks=chunks, quarter=quarter),
-        in_specs=[smem] * 3 + [vmem] * 4,
+        in_specs=[smem] * 3 + [vmem] * 2 + [pl.BlockSpec(memory_space=pltpu.HBM)] * 2,
         out_specs=[vmem] * len(CREW),
+        scratch_shapes=[pltpu.SemaphoreType.DMA((2 * len(CREW),))],
         out_shape=[jax.ShapeDtypeStruct((rows // 2, wide), BF)] * len(CREW),
         compiler_params=pltpu.CompilerParams(vmem_limit_bytes=32 * 1024 * 1024),
         cost_estimate=pl.CostEstimate(flops=0, bytes_accessed=2**23, transcendentals=0),
@@ -200,20 +210,29 @@
     )(scalars, sent, got, x_in, cotangent, w_gate, w_up)
 
 
-def pieces_kernel(scalars, gate_ref, up_ref, *outs, ck, quarter):
+def pieces_kernel(scalars, gate_ref, up_ref, *refs, ck, quarter):
+    outs, sems = refs[: len(CREW)], refs[len(CREW)]
+    copies = []
     for s, out in enumerate(outs):
         start = scalars[DEVS + 2 + s] * quarter
         spot = pl.ds(pl.multiple_of(start, 128), ck)
-        out[:, :ck] = gate_ref[:, spot]
-        out[:, ck:] = up_ref[:, spot]
+        for i, ref in enumerate((gate_ref, up_ref)):
+            there = out.at[:, i * ck : (i + 1) * ck]
+            copies.append(pltpu.make_async_copy(ref.at[:, spot], there, sems.at[2 * s + i]))
+    for copy in copies:
+        copy.start()
+    for copy in copies:
+        copy.wait()
 
 
 def pieces_of_first(scalars, w_gate, w_up, ck, quarter):
     vmem = pl.BlockSpec(memory_space=pltpu.VMEM)
     return pl.pallas_call(
         lambda *a: pieces_kernel(*a, ck=ck, quarter=quarter),
-        in_specs=[pl.BlockSpec(memory_space=pltpu.SMEM), vmem, vmem],
+        in_specs=[pl.BlockSpec(memory_space=pltpu.SMEM)]
+        + [pl.BlockSpec(memory_space=pltpu.HBM)] * 2,
         out_specs=[vmem] * len(CREW),
+        scratch_shapes=[pltpu.SemaphoreType.DMA((2 * len(CREW),))],
         out_shape=[jax.ShapeDtypeStruct((w_gate.shape[0], 2 * ck), BF)] * len(CREW),
         compiler_params=pltpu.CompilerParams(vmem_limit_bytes=16 * 1024 * 1024),
         cost_estimate=pl.CostEstimate(flops=0, bytes_accessed=2**22, transcendentals=0),
@@ -486,7 +505,7 @@
     own_far = send(own, FAR)
     own_near = send(own, NEAR)
     rest = crew_swap(first)[1:]
-    own_near, x_in, cotangent, w_gate, w_up = tie(own_near, x_in, cotangent, w_gate, w_up)
+    own_near, x_in, cotangent = tie(own_near, x_in, cotangent)
     parcels = pack_parcels(
         scalars, send_counts, recv_counts, x_in, cotangent, w_gate, w_up, chunks
     )

time: 211 us -> 212 us (level)
  no operation moved by 1% of the time
where the time goes in v8:
time: 212 us; the launch traced here: 211 us
  waiting for transfers between devices  104 us (49%)
  starting transfers between devices  56.6 us (27%)
  Pallas kernels  40.7 us (19%)
  local copies, waits for them, and re-layouts  5.33 us (3%)
  other arithmetic  3.75 us (2%)
    ppermute x26, waiting for transfers between devices, send(): return lax.ppermute(value, 'dp', [(i, i ^ mask) for i in range(DEVS)])  91.7 us
    ppermute x26, starting transfers between devices, send(): return lax.ppermute(value, 'dp', [(i, i ^ mask) for i in range(DEVS)])  39.1 us
    pallas_call x4, Pallas kernels, kernel_call(): pl.pallas_call(body, grid_spec=pltpu.PrefetchScalarGridSpec(num_scalar_pr...  36.9 us
    ppermute x7, starting transfers between devices, along(): lax.ppermute(value, 'dp', [(crew * a + q, crew * b + q) for a, b in moves...  17.5 us
    ppermute x7, waiting for transfers between devices, along(): lax.ppermute(value, 'dp', [(crew * a + q, crew * b + q) for a, b in moves...  12 us
    unnamed x16, local copies, waits for them, and re-layouts  5.09 us
  transfers between devices with their start and end apart: 35, of which 18 were waited for; matrix products, arithmetic and copies ran while one was open for 1% of the time, Pallas kernels for 18%

profile of v8, /device:TPU:0, one launch (start us, length us, event | category | flops | bytes accessed | tf_op | source)
XLA Modules:
  0.0 211.2 jit_solution(343235231421814926)
XLA Ops:
  0.9 1.2 copy-done
  2.0 1.2 copy-done.2
  3.2 0.8 pieces_of_first.1
  4.0 3.1 %collective-permute-start.4 = (bf16[128,1280]{1,0:T(8,128)(2,1)S(1)}, bf16[128,1280]{1,0:T(8,128)(2,1)S(1)}, u32[]{:S(2)}, u32[]{:S(2)}) collective-permute-start(bf16[128,1280]{1,0:T(8,128)(2,1)S(1)} %get-tuple-element.75.a_5_.a_2_), channel_id=1, source_target_pairs={{0,8},{2,10},{4,12},{6,14},{8,0},{10,2},{12,4},{14,6},{16,24},{18,... | collective-permute-start | bytes 983048 | tf_op jit(solution)/shard_map/ppermute | solution.py:73
  7.1 1.5 collective-permute-start
  8.6 1.5 collective-permute-start.1
  10.1 0.5 collective-permute-start.2
  10.6 2.6 %collective-permute-start.3 = (bf16[128,1280]{1,0:T(8,128)(2,1)S(1)}, bf16[128,1280]{1,0:T(8,128)(2,1)S(1)}, u32[]{:S(2)}, u32[]{:S(2)}) collective-permute-start(bf16[128,1280]{1,0:T(8,128)(2,1)S(1)} %get-tuple-element.75.a_5_.a_2_), channel_id=1, source_target_pairs={{0,16},{2,18},{4,20},{6,22},{8,24},{10,26},{12,28},{14,30},{16,0},... | collective-permute-start | bytes 983048 | tf_op jit(solution)/shard_map/ppermute | solution.py:73
  13.2 5.9 %collective-permute-done.4.a_6_.a_3_ = bf16[128,1280]{1,0:T(8,128)(2,1)S(1)} collective-permute-done((bf16[128,1280]{1,0:T(8,128)(2,1)S(1)}, bf16[128,1280]{1,0:T(8,128)(2,1)S(1)}, u32[]{:S(2)}, u32[]{:S(2)}) %collective-permute-start.4) | collective-permute-done | bytes 327712 | tf_op jit(solution)/shard_map/ppermute | solution.py:73
  19.1 1.5 copy-done.4
  20.6 1.2 copy-done.5
  21.8 1.2 pack_parcels.1
  23.0 1.5 collective-permute-done.1
  24.6 2.3 %collective-permute-done.3.a_7_.a_4_ = bf16[128,1280]{1,0:T(8,128)(2,1)S(1)} collective-permute-done((bf16[128,1280]{1,0:T(8,128)(2,1)S(1)}, bf16[128,1280]{1,0:T(8,128)(2,1)S(1)}, u32[]{:S(2)}, u32[]{:S(2)}) %collective-permute-start.3) | collective-permute-done | bytes 327712 | tf_op jit(solution)/shard_map/ppermute | solution.py:73
  26.9 2.4 %collective-permute-start.10 = (bf16[128,4352]{1,0:T(8,128)(2,1)S(1)}, bf16[128,4352]{1,0:T(8,128)(2,1)S(1)}, u32[]{:S(2)}, u32[]{:S(2)}) collective-permute-start(bf16[128,4352]{1,0:T(8,128)(2,1)S(1)} %get-tuple-element.87), channel_id=1, source_target_pairs={{0,6},{2,4},{4,2},{6,0},{8,14},{10,12},{12,10},{14,8},{16,22},{18,... | collective-permute-start | bytes 3342344 | tf_op jit(solution)/shard_map/ppermute | solution.py:73
  29.3 0.5 collective-permute-start.8
  29.9 0.5 collective-permute-start.9
  30.4 3.0 %collective-permute-start.5 = (bf16[384,1280]{1,0:T(8,128)(2,1)S(1)}, bf16[384,1280]{1,0:T(8,128)(2,1)S(1)}, u32[]{:S(2)}, u32[]{:S(2)}) collective-permute-start(bf16[384,1280]{1,0:T(8,128)(2,1)S(1)} %pad_maximum_fusion.1.a_9_.a_6_), channel_id=1, source_target_pairs={{0,16},{2,18},{4,20},{6,22},{8,24},{10,26},{12,28},{14,30},{16,0},... | collective-permute-start | bytes 2949128 | tf_op jit(solution)/shard_map/ppermute | solution.py:73
  33.4 7.5 %collective-permute-done.7.a_8_.a_5_ = bf16[128,1280]{1,0:T(8,128)(2,1)S(1)} collective-permute-done((bf16[128,1280]{1,0:T(8,128)(2,1)S(1)}, bf16[128,1280]{1,0:T(8,128)(2,1)S(1)}, u32[]{:S(2)}, u32[]{:S(2)}) %collective-permute-start.7) | collective-permute-done | bytes 327712 | tf_op jit(solution)/shard_map/ppermute | solution.py:73
  40.9 32.5 %collective-permute-done.5.a_11_.a_8_ = bf16[384,1280]{1,0:T(8,128)(2,1)S(1)} collective-permute-done((bf16[384,1280]{1,0:T(8,128)(2,1)S(1)}, bf16[384,1280]{1,0:T(8,128)(2,1)S(1)}, u32[]{:S(2)}, u32[]{:S(2)}) %collective-permute-start.5) | collective-permute-done | bytes 983072 | tf_op jit(solution)/shard_map/ppermute | solution.py:73
  73.4 3.0 %collective-permute-done.6.a_10_.a_7_ = bf16[384,1280]{1,0:T(8,128)(2,1)S(1)} collective-permute-done((bf16[384,1280]{1,0:T(8,128)(2,1)S(1)}, bf16[384,1280]{1,0:T(8,128)(2,1)S(1)}, u32[]{:S(2)}, u32[]{:S(2)}) %collective-permute-start.6) | collective-permute-done | bytes 983072 | tf_op jit(solution)/shard_map/ppermute | solution.py:73
  76.5 0.6 pad_maximum_fusion.a_1_.a_3_.a_4_.mine_ref
  77.2 1.4 collective-permute-start.11
  78.6 22.8 %collective-permute-done.11.a_12_.a_9_ = bf16[384,1280]{1,0:T(8,128)(2,1)S(1)} collective-permute-done((bf16[384,1280]{1,0:T(8,128)(2,1)S(1)}, bf16[384,1280]{1,0:T(8,128)(2,1)S(1)}, u32[]{:S(2)}, u32[]{:S(2)}) %collective-permute-start.11) | collective-permute-done | bytes 983072 | tf_op jit(solution)/shard_map/ppermute | solution.py:73
  101.3 1.3 collective-permute-start.15
  102.6 1.9 collective-permute-start.16
  104.5 13.6 %first_chunk.1 = (bf16[1024,1280]{1,0:T(8,128)(2,1)S(1)}, bf16[512,640]{1,0:T(8,128)(2,1)S(1)}, bf16[512,640]{1,0:T(8,128)(2,1)S(1)}, bf16[512,640]{1,0:T(8,128)(2,1)S(1)}, bf16[512,640]{1,0:T(8,128)(2,1)S(1)}) custom-call(s32[48]{0:T(128)S(1)} %stack.174.a_0_.scalars, bf16[4,128,4352]{2,1,0:T(8,128)(2,1)S(1)} %pad_maximum_fusion.a_1_.a_3_.a_4_.mine_ref, ...), custom_call_target="tpu_custom_call" | custom-call | flops 8053063680 | bytes 8388608 | tf_op jit(solution)/shard_map/first_chunk/pallas_call | solution.py:336
  118.2 3.2 %collective-permute-start.13 = (bf16[512,640]{1,0:T(8,128)(2,1)S(1)}, bf16[512,640]{1,0:T(8,128)(2,1)S(1)}, u32[]{:S(2)}, u32[]{:S(2)}) collective-permute-start(bf16[512,640]{1,0:T(8,128)(2,1)S(1)} %get-tuple-element.106), channel_id=1, source_target_pairs={{0,8},{2,10},{4,12},{6,14},{24,16},{26,18},{28,20},{30,22},{1,9},{... | collective-permute-start | bytes 1966088 | tf_op jit(solution)/shard_map/ppermute | solution.py:78
  121.4 0.7 collective-permute-start.14
  122.1 4.0 %collective-permute-done.15.a_5_ = bf16[512,512]{1,0:T(8,128)(2,1)S(1)} collective-permute-done((bf16[512,512]{1,0:T(8,128)(2,1)S(1)}, bf16[512,512]{1,0:T(8,128)(2,1)S(1)}, u32[]{:S(2)}, u32[]{:S(2)}) %collective-permute-start.15) | collective-permute-done | bytes 524320 | tf_op jit(solution)/shard_map/ppermute | solution.py:73
  126.1 0.2 collective-permute-done.16.a_6_
  126.3 1.3 collective-permute-start.17
  127.6 9.1 %rows_grad.1 = (bf16[1024,1024]{1,0:T(8,128)(2,1)S(1)}, bf16[1024,1024]{1,0:T(8,128)(2,1)S(1)}) custom-call(s32[48]{0:T(128)S(1)} %stack.174.a_0_.scalars, bf16[1024,1280]{1,0:T(8,128)(2,1)S(1)} %get-tuple-element.103.a_1_, bf16[128,1280]{1,0:T(8,128)(2,1)S(1)} %get-tuple-element.75.a_5_.a_2_, bf16[128,1280]{1,0:T(8,128)(2,1)S(1)} %collective-permute-done.4.a_6_.a_3_, ...), custom_call_target="tpu_custom_call" | custom-call | flops 5368709120 | bytes 8388608 | tf_op jit(solution)/shard_map/rows_grad/pallas_call | solution.py:336
  136.7 2.3 %collective-permute-done.13 = bf16[512,640]{1,0:T(8,128)(2,1)S(1)} collective-permute-done((bf16[512,640]{1,0:T(8,128)(2,1)S(1)}, bf16[512,640]{1,0:T(8,128)(2,1)S(1)}, u32[]{:S(2)}, u32[]{:S(2)}) %collective-permute-start.13) | collective-permute-done | bytes 655392 | tf_op jit(solution)/shard_map/ppermute | solution.py:78
  139.0 1.7 collective-permute-done.17.a_8_
  140.7 0.2 add_convert_fusion.3
  140.9 0.7 collective-permute-start.18
  141.6 6.8 %collective-permute-start.19 = (bf16[512,640]{1,0:T(8,128)(2,1)S(1)}, bf16[512,640]{1,0:T(8,128)(2,1)S(1)}, u32[]{:S(2)}, u32[]{:S(2)}) collective-permute-start(bf16[512,640]{1,0:T(8,128)(2,1)S(1)} %get-tuple-element.108), channel_id=1, source_target_pairs={{0,8},{2,10},{4,12},{6,14},{24,16},{26,18},{28,20},{30,22},{1,9},{... | collective-permute-start | bytes 1966088 | tf_op jit(solution)/shard_map/ppermute | solution.py:78
  148.4 10.8 %second_chunk.1 = (bf16[1024,1024]{1,0:T(8,128)(2,1)S(1)}, bf16[1024,1024]{1,0:T(8,128)(2,1)S(1)}, bf16[1024,256]{1,0:T(8,128)(2,1)S(1)}) custom-call(s32[48]{0:T(128)S(1)} %stack.174.a_0_.scalars, bf16[4,128,4352]{2,1,0:T(8,128)(2,1)S(1)} %pad_maximum_fusion.a_1_.a_3_.a_4_.mine_ref, bf16[4,128,4352]{2,1,0:T(8,128)(2,1)S(1)} %collective-permute-done.12.a_2_.other_ref, ...), custom_call_target="tpu_custom_call" | custom-call | flops 4294967296 | bytes 8388608 | tf_op jit(solution)/shard_map/second_chunk/pallas_call | solution.py:336
  159.3 0.5 collective-permute-done.19
  160.0 0.7 collective-permute-start.23
  160.9 4.0 %collective-permute-start.22 = (bf16[512,640]{1,0:T(8,128)(2,1)S(1)}, bf16[512,640]{1,0:T(8,128)(2,1)S(1)}, u32[]{:S(2)}, u32[]{:S(2)}) collective-permute-start(bf16[512,640]{1,0:T(8,128)(2,1)S(1)} %add_convert_fusion.2), channel_id=1, source_target_pairs={{0,8},{2,10},{4,12},{6,14},{8,0},{10,2},{12,4},{14,6},{16,24},{18,... | collective-permute-start | bytes 1966088 | tf_op jit(solution)/shard_map/ppermute | solution.py:78
  164.9 3.4 %gate_grad.1 = (bf16[512,256]{1,0:T(8,128)(2,1)S(1)}, bf16[512,256]{1,0:T(8,128)(2,1)S(1)}, bf16[512,256]{1,0:T(8,128)(2,1)S(1)}, bf16[512,256]{1,0:T(8,128)(2,1)S(1)}) custom-call(s32[48]{0:T(128)S(1)} %stack.174.a_0_.scalars, bf16[4,128,4352]{2,1,0:T(8,128)(2,1)S(1)} %pad_maximum_fusion.a_1_.a_3_.a_4_.mine_ref, ...), custom_call_target="tpu_custom_call" | custom-call | flops 1073741824 | bytes 8388608 | tf_op jit(solution)/shard_map/gate_grad/pallas_call | solution.py:336
  168.4 1.0 add_convert_fusion.5
  169.4 1.6 collective-permute-start.26
  170.9 1.4 collective-permute-start.27
  172.4 0.6 collective-permute-start.28
  172.9 7.5 %collective-permute-done.22 = bf16[512,640]{1,0:T(8,128)(2,1)S(1)} collective-permute-done((bf16[512,640]{1,0:T(8,128)(2,1)S(1)}, bf16[512,640]{1,0:T(8,128)(2,1)S(1)}, u32[]{:S(2)}, u32[]{:S(2)}) %collective-permute-start.22) | collective-permute-done | bytes 655392 | tf_op jit(solution)/shard_map/ppermute | solution.py:78
  180.4 3.4 %collective-permute-start.25 = (bf16[512,256]{1,0:T(8,128)(2,1)S(1)}, bf16[512,256]{1,0:T(8,128)(2,1)S(1)}, u32[]{:S(2)}, u32[]{:S(2)}) collective-permute-start(bf16[512,256]{1,0:T(8,128)(2,1)S(1)} %get-tuple-element.129), channel_id=1, source_target_pairs={{0,8},{2,10},{4,12},{6,14},{8,0},{10,2},{12,4},{14,6},{16,24},{18,... | collective-permute-start | bytes 786440 | tf_op jit(solution)/shard_map/ppermute | solution.py:73
  183.8 2.2 %collective-permute-done.21 = bf16[512,256]{1,0:T(8,128)(2,1)S(1)} collective-permute-done((bf16[512,256]{1,0:T(8,128)(2,1)S(1)}, bf16[512,256]{1,0:T(8,128)(2,1)S(1)}, u32[]{:S(2)}, u32[]{:S(2)}) %collective-permute-start.21) | collective-permute-done | bytes 262176 | tf_op jit(solution)/shard_map/ppermute | solution.py:73
  186.1 3.3 %collective-permute-start.24 = (bf16[512,256]{1,0:T(8,128)(2,1)S(1)}, bf16[512,256]{1,0:T(8,128)(2,1)S(1)}, u32[]{:S(2)}, u32[]{:S(2)}) collective-permute-start(bf16[512,256]{1,0:T(8,128)(2,1)S(1)} %add_convert_fusion.10), channel_id=1, source_target_pairs={{0,16},{2,18},{4,20},{6,22},{8,24},{10,26},{12,28},{14,30},{16,0},... | collective-permute-start | bytes 786440 | tf_op jit(solution)/shard_map/ppermute | solution.py:73
  189.4 0.2 add_convert_fusion
  189.7 6.2 %collective-permute-done.25 = bf16[512,256]{1,0:T(8,128)(2,1)S(1)} collective-permute-done((bf16[512,256]{1,0:T(8,128)(2,1)S(1)}, bf16[512,256]{1,0:T(8,128)(2,1)S(1)}, u32[]{:S(2)}, u32[]{:S(2)}) %collective-permute-start.25) | collective-permute-done | bytes 262176 | tf_op jit(solution)/shard_map/ppermute | solution.py:73
  195.9 1.5 collective-permute-start.29
  197.4 1.4 collective-permute-start.30
  198.8 0.6 collective-permute-start.31
  199.4 0.8 collective-permute-done.24
  200.4 1.6 collective-permute-start.32
  202.0 1.4 collective-permute-start.33
  203.4 2.0 collective-permute-start.34
  205.4 1.2 add_convert_fusion.4
  206.5 1.4 collective-permute-done.30.a_3_
  207.9 1.4 collective-permute-done.33.a_7_
  209.3 1.9 join_quarters.1
  (45 shorter events, 1.0 us)
Async XLA Ops:
  0.6 18.4 %copy-start.6 = (s32[1,16]{1,0:T(1,128)S(1)}, s32[1,16]{1,0:T(1,128)}, u32[]{:S(2)}) copy-start(s32[1,16]{1,0:T(1,128)} %a_1_.3) | copy-start | bytes 196
  0.6 18.4 %copy-start.7 = (s32[1,16]{1,0:T(1,128)S(1)}, s32[1,16]{1,0:T(1,128)}, u32[]{:S(2)}) copy-start(s32[1,16]{1,0:T(1,128)} %a_2_.3) | copy-start | bytes 196
  0.8 1.2 copy-start
  2.0 1.2 copy-start.2
  3.2 15.8 %copy-start.1 = (bf16[128,3584]{1,0:T(8,128)(2,1)S(1)}, bf16[128,3584]{1,0:T(8,128)(2,1)}, u32[]{:S(2)}) copy-start(bf16[128,3584]{1,0:T(8,128)(2,1)} %a_5_.1) | copy-start | bytes 2752516
  3.2 15.8 %copy-start.3 = (bf16[128,3584]{1,0:T(8,128)(2,1)S(1)}, bf16[128,3584]{1,0:T(8,128)(2,1)}, u32[]{:S(2)}) copy-start(bf16[128,3584]{1,0:T(8,128)(2,1)} %a_6_.1) | copy-start | bytes 2752516
  4.0 15.1 %collective-permute-start.4 = (bf16[128,1280]{1,0:T(8,128)(2,1)S(1)}, bf16[128,1280]{1,0:T(8,128)(2,1)S(1)}, u32[]{:S(2)}, u32[]{:S(2)}) collective-permute-start(bf16[128,1280]{1,0:T(8,128)(2,1)S(1)} %get-tuple-element.75.a_5_.a_2_), channel_id=1, source_target_pairs={{0,8},{2,10},{4,12},{6,14},{8,0},{10,2},{12,4},{14,6},{16,24},{18,... | collective-permute-start | bytes 983048 | tf_op jit(solution)/shard_map/ppermute | solution.py:73
  7.1 15.9 %collective-permute-start = (bf16[128,1280]{1,0:T(8,128)(2,1)S(1)}, bf16[128,1280]{1,0:T(8,128)(2,1)S(1)}, u32[]{:S(2)}, u32[]{:S(2)}) collective-permute-start(bf16[128,1280]{1,0:T(8,128)(2,1)S(1)} %get-tuple-element.72), channel_id=1, source_target_pairs={{0,2},{2,0},{4,6},{6,4},{8,10},{10,8},{12,14},{14,12},{16,18},{18,... | collective-permute-start | bytes 983048 | tf_op jit(solution)/shard_map/ppermute | solution.py:73
  8.6 15.9 %collective-permute-start.1 = (bf16[128,1280]{1,0:T(8,128)(2,1)S(1)}, bf16[128,1280]{1,0:T(8,128)(2,1)S(1)}, u32[]{:S(2)}, u32[]{:S(2)}) collective-permute-start(bf16[128,1280]{1,0:T(8,128)(2,1)S(1)} %get-tuple-element.73), channel_id=1, source_target_pairs={{0,4},{2,6},{4,0},{6,2},{8,12},{10,14},{12,8},{14,10},{16,20},{18,... | collective-permute-start | bytes 983048 | tf_op jit(solution)/shard_map/ppermute | solution.py:73
  10.1 14.4 %collective-permute-start.2 = (bf16[128,1280]{1,0:T(8,128)(2,1)S(1)}, bf16[128,1280]{1,0:T(8,128)(2,1)S(1)}, u32[]{:S(2)}, u32[]{:S(2)}) collective-permute-start(bf16[128,1280]{1,0:T(8,128)(2,1)S(1)} %get-tuple-element.74), channel_id=1, source_target_pairs={{0,6},{2,4},{4,2},{6,0},{8,14},{10,12},{12,10},{14,8},{16,22},{18,... | collective-permute-start | bytes 983048 | tf_op jit(solution)/shard_map/ppermute | solution.py:73
  10.6 16.3 %collective-permute-start.3 = (bf16[128,1280]{1,0:T(8,128)(2,1)S(1)}, bf16[128,1280]{1,0:T(8,128)(2,1)S(1)}, u32[]{:S(2)}, u32[]{:S(2)}) collective-permute-start(bf16[128,1280]{1,0:T(8,128)(2,1)S(1)} %get-tuple-element.75.a_5_.a_2_), channel_id=1, source_target_pairs={{0,16},{2,18},{4,20},{6,22},{8,24},{10,26},{12,28},{14,30},{16,0},... | collective-permute-start | bytes 983048 | tf_op jit(solution)/shard_map/ppermute | solution.py:73
  19.1 1.5 copy-start.4
  20.6 1.2 copy-start.5
  26.9 14.0 %collective-permute-start.7 = (bf16[128,1280]{1,0:T(8,128)(2,1)S(1)}, bf16[128,1280]{1,0:T(8,128)(2,1)S(1)}, u32[]{:S(2)}, u32[]{:S(2)}) collective-permute-start(bf16[128,1280]{1,0:T(8,128)(2,1)S(1)} %collective-permute-done.3.a_7_.a_4_), channel_id=1, source_target_pairs={{0,8},{2,10},{4,12},{6,14},{8,0},{10,2},{12,4},{14,6},{16,24},{18,... | collective-permute-start | bytes 983048 | tf_op jit(solution)/shard_map/ppermute | solution.py:73
  26.9 49.6 %collective-permute-start.10 = (bf16[128,4352]{1,0:T(8,128)(2,1)S(1)}, bf16[128,4352]{1,0:T(8,128)(2,1)S(1)}, u32[]{:S(2)}, u32[]{:S(2)}) collective-permute-start(bf16[128,4352]{1,0:T(8,128)(2,1)S(1)} %get-tuple-element.87), channel_id=1, source_target_pairs={{0,6},{2,4},{4,2},{6,0},{8,14},{10,12},{12,10},{14,8},{16,22},{18,... | collective-permute-start | bytes 3342344 | tf_op jit(solution)/shard_map/ppermute | solution.py:73
  29.3 47.1 %collective-permute-start.8 = (bf16[128,4352]{1,0:T(8,128)(2,1)S(1)}, bf16[128,4352]{1,0:T(8,128)(2,1)S(1)}, u32[]{:S(2)}, u32[]{:S(2)}) collective-permute-start(bf16[128,4352]{1,0:T(8,128)(2,1)S(1)} %get-tuple-element.85), channel_id=1, source_target_pairs={{0,2},{2,0},{4,6},{6,4},{8,10},{10,8},{12,14},{14,12},{16,18},{18,... | collective-permute-start | bytes 3342344 | tf_op jit(solution)/shard_map/ppermute | solution.py:73
  29.9 46.6 %collective-permute-start.9 = (bf16[128,4352]{1,0:T(8,128)(2,1)S(1)}, bf16[128,4352]{1,0:T(8,128)(2,1)S(1)}, u32[]{:S(2)}, u32[]{:S(2)}) collective-permute-start(bf16[128,4352]{1,0:T(8,128)(2,1)S(1)} %get-tuple-element.86), channel_id=1, source_target_pairs={{0,4},{2,6},{4,0},{6,2},{8,12},{10,14},{12,8},{14,10},{16,20},{18,... | collective-permute-start | bytes 3342344 | tf_op jit(solution)/shard_map/ppermute | solution.py:73
  30.4 43.0 %collective-permute-start.5 = (bf16[384,1280]{1,0:T(8,128)(2,1)S(1)}, bf16[384,1280]{1,0:T(8,128)(2,1)S(1)}, u32[]{:S(2)}, u32[]{:S(2)}) collective-permute-start(bf16[384,1280]{1,0:T(8,128)(2,1)S(1)} %pad_maximum_fusion.1.a_9_.a_6_), channel_id=1, source_target_pairs={{0,16},{2,18},{4,20},{6,22},{8,24},{10,26},{12,28},{14,30},{16,0},... | collective-permute-start | bytes 2949128 | tf_op jit(solution)/shard_map/ppermute | solution.py:73
  40.9 35.6 %collective-permute-start.6 = (bf16[384,1280]{1,0:T(8,128)(2,1)S(1)}, bf16[384,1280]{1,0:T(8,128)(2,1)S(1)}, u32[]{:S(2)}, u32[]{:S(2)}) collective-permute-start(bf16[384,1280]{1,0:T(8,128)(2,1)S(1)} %pad_maximum_fusion.1.a_9_.a_6_), channel_id=1, source_target_pairs={{0,8},{2,10},{4,12},{6,14},{8,0},{10,2},{12,4},{14,6},{16,24},{18,... | collective-permute-start | bytes 2949128 | tf_op jit(solution)/shard_map/ppermute | solution.py:73
  77.1 24.3 %collective-permute-start.12 = (bf16[4,128,4352]{2,1,0:T(8,128)(2,1)S(1)}, bf16[4,128,4352]{2,1,0:T(8,128)(2,1)S(1)}, u32[]{:S(2)}, u32[]{:S(2)}) collective-permute-start(bf16[4,128,4352]{2,1,0:T(8,128)(2,1)S(1)} %pad_maximum_fusion.a_1_.a_3_.a_4_.mine_ref), channel_id=1, source_target_pairs={{0,1},{1,0},{2,3},{3,2},{4,5},{5,4},{6,7},{7,6},{8,9},{9,8},{10,11... | collective-permute-start | bytes 13369352 | tf_op jit(solution)/shard_map/ppermute | solution.py:523
  77.2 24.2 %collective-permute-start.11 = (bf16[384,1280]{1,0:T(8,128)(2,1)S(1)}, bf16[384,1280]{1,0:T(8,128)(2,1)S(1)}, u32[]{:S(2)}, u32[]{:S(2)}) collective-permute-start(bf16[384,1280]{1,0:T(8,128)(2,1)S(1)} %collective-permute-done.5.a_11_.a_8_), channel_id=1, source_target_pairs={{0,8},{2,10},{4,12},{6,14},{8,0},{10,2},{12,4},{14,6},{16,24},{18,... | collective-permute-start | bytes 2949128 | tf_op jit(solution)/shard_map/ppermute | solution.py:73
  101.3 24.7 %collective-permute-start.15 = (bf16[512,512]{1,0:T(8,128)(2,1)S(1)}, bf16[512,512]{1,0:T(8,128)(2,1)S(1)}, u32[]{:S(2)}, u32[]{:S(2)}) collective-permute-start(bf16[512,512]{1,0:T(8,128)(2,1)S(1)} %bitcast.43), channel_id=1, source_target_pairs={{0,8},{2,10},{4,12},{6,14},{8,0},{10,2},{12,4},{14,6},{16,24},{18,... | collective-permute-start | bytes 1572872 | tf_op jit(solution)/shard_map/ppermute | solution.py:73
  102.6 23.6 %collective-permute-start.16 = (bf16[512,512]{1,0:T(8,128)(2,1)S(1)}, bf16[512,512]{1,0:T(8,128)(2,1)S(1)}, u32[]{:S(2)}, u32[]{:S(2)}) collective-permute-start(bf16[512,512]{1,0:T(8,128)(2,1)S(1)} %bitcast.44), channel_id=1, source_target_pairs={{0,16},{2,18},{4,20},{6,22},{8,24},{10,26},{12,28},{14,30},{16,0},... | collective-permute-start | bytes 1572872 | tf_op jit(solution)/shard_map/ppermute | solution.py:73
  118.2 20.8 %collective-permute-start.13 = (bf16[512,640]{1,0:T(8,128)(2,1)S(1)}, bf16[512,640]{1,0:T(8,128)(2,1)S(1)}, u32[]{:S(2)}, u32[]{:S(2)}) collective-permute-start(bf16[512,640]{1,0:T(8,128)(2,1)S(1)} %get-tuple-element.106), channel_id=1, source_target_pairs={{0,8},{2,10},{4,12},{6,14},{24,16},{26,18},{28,20},{30,22},{1,9},{... | collective-permute-start | bytes 1966088 | tf_op jit(solution)/shard_map/ppermute | solution.py:78
  121.4 15.3 %collective-permute-start.14 = (bf16[512,512]{1,0:T(8,128)(2,1)S(1)}, bf16[512,512]{1,0:T(8,128)(2,1)S(1)}, u32[]{:S(2)}, u32[]{:S(2)}) collective-permute-start(bf16[512,512]{1,0:T(8,128)(2,1)S(1)} %bitcast.45), channel_id=1, source_target_pairs={{8,16},{10,18},{12,20},{14,22},{16,8},{18,10},{20,12},{22,14},{9,1... | collective-permute-start | bytes 1572872 | tf_op jit(solution)/shard_map/ppermute | solution.py:78
  126.3 14.4 %collective-permute-start.17 = (bf16[512,512]{1,0:T(8,128)(2,1)S(1)}, bf16[512,512]{1,0:T(8,128)(2,1)S(1)}, u32[]{:S(2)}, u32[]{:S(2)}) collective-permute-start(bf16[512,512]{1,0:T(8,128)(2,1)S(1)} %collective-permute-done.16.a_6_), channel_id=1, source_target_pairs={{8,0},{10,2},{12,4},{14,6},{16,24},{18,26},{20,28},{22,30},{9,1},{... | collective-permute-start | bytes 1572872 | tf_op jit(solution)/shard_map/ppermute | solution.py:78
  140.9 18.4 %collective-permute-start.18 = (bf16[512,640]{1,0:T(8,128)(2,1)S(1)}, bf16[512,640]{1,0:T(8,128)(2,1)S(1)}, u32[]{:S(2)}, u32[]{:S(2)}) collective-permute-start(bf16[512,640]{1,0:T(8,128)(2,1)S(1)} %add_convert_fusion.3), channel_id=1, source_target_pairs={{8,16},{10,18},{12,20},{14,22},{16,8},{18,10},{20,12},{22,14},{9,1... | collective-permute-start | bytes 1966088 | tf_op jit(solution)/shard_map/ppermute | solution.py:78
  141.6 18.2 %collective-permute-start.19 = (bf16[512,640]{1,0:T(8,128)(2,1)S(1)}, bf16[512,640]{1,0:T(8,128)(2,1)S(1)}, u32[]{:S(2)}, u32[]{:S(2)}) collective-permute-start(bf16[512,640]{1,0:T(8,128)(2,1)S(1)} %get-tuple-element.108), channel_id=1, source_target_pairs={{0,8},{2,10},{4,12},{6,14},{24,16},{26,18},{28,20},{30,22},{1,9},{... | collective-permute-start | bytes 1966088 | tf_op jit(solution)/shard_map/ppermute | solution.py:78
  159.8 8.5 %collective-permute-start.20 = (bf16[1024,1024]{1,0:T(8,128)(2,1)S(1)}, bf16[1024,1024]{1,0:T(8,128)(2,1)S(1)}, u32[]{:S(2)}, u32[]{:S(2)}) collective-permute-start(bf16[1024,1024]{1,0:T(8,128)(2,1)S(1)} %get-tuple-element.117), channel_id=1, source_target_pairs={{0,1},{1,0},{2,3},{3,2},{4,5},{5,4},{6,7},{7,6},{8,9},{9,8},{10,11... | collective-permute-start | bytes 6291464 | tf_op jit(solution)/shard_map/ppermute | solution.py:550
  160.0 12.4 %collective-permute-start.23 = (bf16[512,640]{1,0:T(8,128)(2,1)S(1)}, bf16[512,640]{1,0:T(8,128)(2,1)S(1)}, u32[]{:S(2)}, u32[]{:S(2)}) collective-permute-start(bf16[512,640]{1,0:T(8,128)(2,1)S(1)} %add_convert_fusion.1), channel_id=1, source_target_pairs={{8,16},{10,18},{12,20},{14,22},{16,8},{18,10},{20,12},{22,14},{9,1... | collective-permute-start | bytes 1966088 | tf_op jit(solution)/shard_map/ppermute | solution.py:78
  160.9 19.6 %collective-permute-start.22 = (bf16[512,640]{1,0:T(8,128)(2,1)S(1)}, bf16[512,640]{1,0:T(8,128)(2,1)S(1)}, u32[]{:S(2)}, u32[]{:S(2)}) collective-permute-start(bf16[512,640]{1,0:T(8,128)(2,1)S(1)} %add_convert_fusion.2), channel_id=1, source_target_pairs={{0,8},{2,10},{4,12},{6,14},{8,0},{10,2},{12,4},{14,6},{16,24},{18,... | collective-permute-start | bytes 1966088 | tf_op jit(solution)/shard_map/ppermute | solution.py:78
  168.3 17.8 %collective-permute-start.21 = (bf16[512,256]{1,0:T(8,128)(2,1)S(1)}, bf16[512,256]{1,0:T(8,128)(2,1)S(1)}, u32[]{:S(2)}, u32[]{:S(2)}) collective-permute-start(bf16[512,256]{1,0:T(8,128)(2,1)S(1)} %get-tuple-element.124), channel_id=1, source_target_pairs={{0,8},{2,10},{4,12},{6,14},{8,0},{10,2},{12,4},{14,6},{16,24},{18,... | collective-permute-start | bytes 786440 | tf_op jit(solution)/shard_map/ppermute | solution.py:73
  169.4 28.0 %collective-permute-start.26 = (bf16[256,1024]{1,0:T(8,128)(2,1)S(1)}, bf16[256,1024]{1,0:T(8,128)(2,1)S(1)}, u32[]{:S(2)}, u32[]{:S(2)}) collective-permute-start(bf16[256,1024]{1,0:T(8,128)(2,1)S(1)} %get-tuple-element.144), channel_id=1, source_target_pairs={{0,2},{2,0},{4,6},{6,4},{8,10},{10,8},{12,14},{14,12},{16,18},{18,... | collective-permute-start | bytes 1572872 | tf_op jit(solution)/shard_map/ppermute | solution.py:73
  170.9 27.9 %collective-permute-start.27 = (bf16[256,1024]{1,0:T(8,128)(2,1)S(1)}, bf16[256,1024]{1,0:T(8,128)(2,1)S(1)}, u32[]{:S(2)}, u32[]{:S(2)}) collective-permute-start(bf16[256,1024]{1,0:T(8,128)(2,1)S(1)} %get-tuple-element.143), channel_id=1, source_target_pairs={{0,4},{2,6},{4,0},{6,2},{8,12},{10,14},{12,8},{14,10},{16,20},{18,... | collective-permute-start | bytes 1572872 | tf_op jit(solution)/shard_map/ppermute | solution.py:73
  172.4 27.1 %collective-permute-start.28 = (bf16[256,1024]{1,0:T(8,128)(2,1)S(1)}, bf16[256,1024]{1,0:T(8,128)(2,1)S(1)}, u32[]{:S(2)}, u32[]{:S(2)}) collective-permute-start(bf16[256,1024]{1,0:T(8,128)(2,1)S(1)} %get-tuple-element.142), channel_id=1, source_target_pairs={{0,6},{2,4},{4,2},{6,0},{8,14},{10,12},{12,10},{14,8},{16,22},{18,... | collective-permute-start | bytes 1572872 | tf_op jit(solution)/shard_map/ppermute | solution.py:73
  180.4 15.5 %collective-permute-start.25 = (bf16[512,256]{1,0:T(8,128)(2,1)S(1)}, bf16[512,256]{1,0:T(8,128)(2,1)S(1)}, u32[]{:S(2)}, u32[]{:S(2)}) collective-permute-start(bf16[512,256]{1,0:T(8,128)(2,1)S(1)} %get-tuple-element.129), channel_id=1, source_target_pairs={{0,8},{2,10},{4,12},{6,14},{8,0},{10,2},{12,4},{14,6},{16,24},{18,... | collective-permute-start | bytes 786440 | tf_op jit(solution)/shard_map/ppermute | solution.py:73
  186.1 14.2 %collective-permute-start.24 = (bf16[512,256]{1,0:T(8,128)(2,1)S(1)}, bf16[512,256]{1,0:T(8,128)(2,1)S(1)}, u32[]{:S(2)}, u32[]{:S(2)}) collective-permute-start(bf16[512,256]{1,0:T(8,128)(2,1)S(1)} %add_convert_fusion.10), channel_id=1, source_target_pairs={{0,16},{2,18},{4,20},{6,22},{8,24},{10,26},{12,28},{14,30},{16,0},... | collective-permute-start | bytes 786440 | tf_op jit(solution)/shard_map/ppermute | solution.py:73
  195.9 7.5 %collective-permute-start.29 = (bf16[128,640]{1,0:T(8,128)(2,1)S(1)}, bf16[128,640]{1,0:T(8,128)(2,1)S(1)}, u32[]{:S(2)}, u32[]{:S(2)}) collective-permute-start(bf16[128,640]{1,0:T(8,128)(2,1)S(1)} %get-tuple-element.148), channel_id=1, source_target_pairs={{0,2},{2,0},{4,6},{6,4},{8,10},{10,8},{12,14},{14,12},{16,18},{18,... | collective-permute-start | bytes 491528 | tf_op jit(solution)/shard_map/ppermute | solution.py:73
  197.4 10.5 %collective-permute-start.30 = (bf16[128,640]{1,0:T(8,128)(2,1)S(1)}, bf16[128,640]{1,0:T(8,128)(2,1)S(1)}, u32[]{:S(2)}, u32[]{:S(2)}) collective-permute-start(bf16[128,640]{1,0:T(8,128)(2,1)S(1)} %get-tuple-element.147), channel_id=1, source_target_pairs={{0,4},{2,6},{4,0},{6,2},{8,12},{10,14},{12,8},{14,10},{16,20},{18,... | collective-permute-start | bytes 491528 | tf_op jit(solution)/shard_map/ppermute | solution.py:73
  198.8 9.1 %collective-permute-start.31 = (bf16[128,640]{1,0:T(8,128)(2,1)S(1)}, bf16[128,640]{1,0:T(8,128)(2,1)S(1)}, u32[]{:S(2)}, u32[]{:S(2)}) collective-permute-start(bf16[128,640]{1,0:T(8,128)(2,1)S(1)} %get-tuple-element.146), channel_id=1, source_target_pairs={{0,6},{2,4},{4,2},{6,0},{8,14},{10,12},{12,10},{14,8},{16,22},{18,... | collective-permute-start | bytes 491528 | tf_op jit(solution)/shard_map/ppermute | solution.py:73
  200.4 7.5 %collective-permute-start.32 = (bf16[128,256]{1,0:T(8,128)(2,1)S(1)}, bf16[128,256]{1,0:T(8,128)(2,1)S(1)}, u32[]{:S(2)}, u32[]{:S(2)}) collective-permute-start(bf16[128,256]{1,0:T(8,128)(2,1)S(1)} %get-tuple-element.152), channel_id=1, source_target_pairs={{0,2},{2,0},{4,6},{6,4},{8,10},{10,8},{12,14},{14,12},{16,18},{18,... | collective-permute-start | bytes 196616 | tf_op jit(solution)/shard_map/ppermute | solution.py:73
  202.0 7.3 %collective-permute-start.33 = (bf16[128,256]{1,0:T(8,128)(2,1)S(1)}, bf16[128,256]{1,0:T(8,128)(2,1)S(1)}, u32[]{:S(2)}, u32[]{:S(2)}) collective-permute-start(bf16[128,256]{1,0:T(8,128)(2,1)S(1)} %get-tuple-element.151), channel_id=1, source_target_pairs={{0,4},{2,6},{4,0},{6,2},{8,12},{10,14},{12,8},{14,10},{16,20},{18,... | collective-permute-start | bytes 196616 | tf_op jit(solution)/shard_map/ppermute | solution.py:73
  203.4 5.9 %collective-permute-start.34 = (bf16[128,256]{1,0:T(8,128)(2,1)S(1)}, bf16[128,256]{1,0:T(8,128)(2,1)S(1)}, u32[]{:S(2)}, u32[]{:S(2)}) collective-permute-start(bf16[128,256]{1,0:T(8,128)(2,1)S(1)} %get-tuple-element.150), channel_id=1, source_target_pairs={{0,6},{2,4},{4,2},{6,0},{8,14},{10,12},{12,10},{14,8},{16,22},{18,... | collective-permute-start | bytes 196616 | tf_op jit(solution)/shard_map/ppermute | solution.py:73
